TPU v7x, 32 devices: a whole 2x2x4 slice. The times are simulated.
32 devices in a mesh: groups: 2 (over x), delta: 4 (over y, core), tensor: 4 (over z).
Axes of the slice: x: 2, y: 2, z: 4, core: 2. Of those that a mesh axis runs over, the one named last changes fastest.
Arguments:
- tokens: bfloat16 [1024, 8192], P('groups', 'delta'), parts along dimension 0, may hold values from -6 to 6
- gate_weight: bfloat16 [8192, 16384], P('delta', 'tensor'), may hold values from -0.0625 to 0.0625
- up_weight: bfloat16 [8192, 16384], P('delta', 'tensor'), may hold values from -0.0625 to 0.0625
- down_weight: bfloat16 [16384, 8192], P('tensor', 'delta'), may hold values from -0.046875 to 0.046875
- gate_tiles: bfloat16 [16, 8, 256, 256], P('delta', 'tensor'), may hold values from -0.375 to 0.375
- up_tiles: bfloat16 [16, 8, 256, 256], P('delta', 'tensor'), may hold values from -0.375 to 0.375
- down_tiles: bfloat16 [16, 8, 256, 256], P('delta', 'tensor'), may hold values from -0.375 to 0.375
- gate_pattern: int32 [16, 8], P('delta', 'tensor'), may hold values from 0 to 511, as said below
- up_pattern: int32 [16, 8], P('delta', 'tensor'), may hold values from 0 to 511, as said below
- down_pattern: int32 [16, 8], P('delta', 'tensor'), may hold values from 0 to 511, as said below
- row_variant: int32 [1024], P('groups'), parts along dimension 0, may hold values from 0 to 15, as said below
- variant_slot: int32 [32], P('groups'), parts along dimension 0, may hold values from 0 to 15, as said below
Outputs:
- mixed: bfloat16 [1024, 8192], P(('groups', 'tensor'), 'delta'), parts along dimension 0
There are 2 independent parts, one for each index of `groups`. A program takes and returns all parts, laid end to end along the dimension named above; an argument that names none is the same for every part. Nothing has to cross between parts.
Inputs may be any that keep to these rules, and one draw needn't show every extreme that they name: `row_variant`: owner k of the delta axis holds the slots k * 4 to k * 4 + 3. The rows whose slot lies with one owner number at most 128; exactly 128 for one owner, which one varies from draw to draw; the other owners' counts differ by at most one. `variant_slot`: A permutation: every slot holds exactly one variant. `gate_pattern`: within one slot and one tensor shard the 2 positions differ; position p stands for row block p // c and column block p % c of that shard's [8192, 4096] grid of tiles. `up_pattern`: as gate_pattern. `down_pattern`: within one slot and one tensor shard the 2 positions differ; position p stands for row block p // e and column block p % e of that shard's [4096, 8192] grid of tiles.
All inputs are finite; a program needn't handle non-finite values.
Results may differ from a plain program's by a relative error of at most 0.005.
Values may be sent and summed in bfloat16 or wider, within the bound.
No kernel may reach another device: no remote copies, remote signals or barrier semaphores. Data moves between devices by JAX's collectives and lax.ppermute only.
A program may use at most 192 MiB of HBM per device.

v0:
```python
import jax
import jax.numpy as jnp
from jax import lax
from jax.sharding import PartitionSpec as P

CAP = 128


def owner_slots(row_variant, variant_slot, owners, per_owner, capacity):
    lookup = row_variant[:, None] == jnp.arange(variant_slot.shape[0], dtype=jnp.int32)[None, :]
    slot_rows = jnp.sum(jnp.where(lookup, variant_slot[None, :], 0), axis=1)
    owner_rows = slot_rows // per_owner
    owner_hits = (owner_rows[:, None] == jnp.arange(owners, dtype=jnp.int32)[None, :]).astype(
        jnp.int32
    )
    position = jnp.sum(jnp.cumsum(owner_hits, axis=0) * owner_hits, axis=1) - 1
    row_number = jnp.arange(row_variant.shape[0], dtype=jnp.int32)
    buffer_rows = jnp.zeros((owners, capacity), jnp.int32).at[owner_rows, position].set(row_number)
    buffer_live = jnp.zeros((owners, capacity), jnp.bool_).at[owner_rows, position].set(True)
    buffer_local = (
        jnp.zeros((owners, capacity), jnp.int32).at[owner_rows, position].set(slot_rows % per_owner)
    )
    return (buffer_rows, buffer_live, buffer_local)


def tile_products(source, tile_set, pattern, slot_local, slot_live, out_tiles):
    capacity = source.shape[0]
    tile_width = tile_set.shape[-1]
    per_owner, per_slot = pattern.shape
    flat_pattern = pattern.reshape(-1)
    in_index = flat_pattern // out_tiles
    out_index = flat_pattern % out_tiles
    blocks = source.reshape(capacity, -1, tile_width)
    picked = jnp.take(blocks, in_index, axis=1)
    flat_tiles = tile_set.reshape(per_owner * per_slot, tile_width, tile_width)
    products = jnp.einsum("cjk,jkf->cjf", picked, flat_tiles, preferred_element_type=jnp.float32)
    tile_slot = jnp.arange(per_owner * per_slot, dtype=jnp.int32) // per_slot
    selected = (slot_local[:, None] == tile_slot[None, :]) & slot_live[:, None]
    products = products * selected[:, :, None].astype(jnp.float32)
    placing = (out_index[:, None] == jnp.arange(out_tiles, dtype=jnp.int32)[None, :]).astype(
        jnp.float32
    )
    placed = jnp.einsum("cjf,jg->cgf", products, placing, precision=lax.Precision.HIGHEST)
    return placed.reshape(capacity, out_tiles * tile_width)


def place_rows(values, row_ids, row_live, row_count):
    inside = row_live & (row_ids >= 0) & (row_ids < row_count)
    target = jnp.where(inside, row_ids, row_count)
    return jnp.zeros((row_count, values.shape[1]), jnp.float32).at[target].add(values, mode="drop")


def activate(summed, hidden_width):
    return (jax.nn.silu(summed[:, :hidden_width]) * summed[:, hidden_width:]).astype(jnp.bfloat16)


def shards(
    tokens,
    gate_weight,
    up_weight,
    down_weight,
    gate_tiles,
    up_tiles,
    down_tiles,
    gate_pattern,
    up_pattern,
    down_pattern,
    row_variant,
    variant_slot,
):
    owners = lax.axis_size("delta")
    self_owner = lax.axis_index("delta")
    per_owner = gate_tiles.shape[0]
    tile_width = gate_tiles.shape[-1]
    all_rows, shard_width = tokens.shape
    full_width = shard_width * owners
    hidden_width = gate_weight.shape[1]
    capacity = CAP
    buffer_rows, buffer_live, buffer_local = owner_slots(
        row_variant, variant_slot, owners, per_owner, capacity
    )
    mine_rows = lax.dynamic_index_in_dim(buffer_rows, self_owner, 0, keepdims=False)
    mine_live = lax.dynamic_index_in_dim(buffer_live, self_owner, 0, keepdims=False)
    mine_local = lax.dynamic_index_in_dim(buffer_local, self_owner, 0, keepdims=False)
    outgoing = jnp.take(tokens, buffer_rows.reshape(-1), axis=0).reshape(
        owners, capacity, shard_width
    )
    received = lax.all_to_all(outgoing, "delta", split_axis=0, concat_axis=2, tiled=True).reshape(
        capacity, full_width
    )
    column_tiles = hidden_width // tile_width
    width_tiles = full_width // tile_width
    gate_delta = tile_products(
        received, gate_tiles, gate_pattern, mine_local, mine_live, column_tiles
    )
    up_delta = tile_products(received, up_tiles, up_pattern, mine_local, mine_live, column_tiles)
    delta_both = jnp.concatenate([gate_delta, up_delta], axis=1)
    base_gate = jnp.dot(tokens, gate_weight, preferred_element_type=jnp.float32)
    base_up = jnp.dot(tokens, up_weight, preferred_element_type=jnp.float32)
    summed = lax.psum_scatter(
        jnp.concatenate([base_gate, base_up], axis=1)
        + place_rows(delta_both, mine_rows, mine_live, all_rows // owners * lax.axis_size("delta")),
        "delta",
        scatter_dimension=0,
        tiled=True,
    )
    hidden_home = activate(summed, hidden_width)
    empty_mine = jnp.zeros((capacity, hidden_width), jnp.bfloat16)
    shard_piece = lax.all_gather(hidden_home, "delta", axis=0, tiled=True)
    mine_acc = empty_mine
    product = jnp.dot(shard_piece, down_weight, preferred_element_type=jnp.float32)
    inside = (mine_rows >= 0) & (mine_rows < shard_piece.shape[0])
    picked = jnp.take(shard_piece, jnp.clip(mine_rows, 0, shard_piece.shape[0] - 1), axis=0)
    mine_acc = jnp.where(inside[:, None], picked, mine_acc)
    base_out = product
    down_delta = tile_products(
        mine_acc, down_tiles, down_pattern, mine_local, mine_live, width_tiles
    )
    spread = down_delta.reshape(capacity, owners, shard_width)
    returned = lax.all_to_all(spread, "delta", split_axis=1, concat_axis=0, tiled=True).reshape(
        owners * capacity, shard_width
    )
    returned = jnp.where(buffer_live.reshape(-1)[:, None], returned, 0.0)
    base_out = base_out.at[buffer_rows.reshape(-1)].add(returned)
    reduced = lax.psum_scatter(base_out, "tensor", scatter_dimension=0, tiled=True)
    return reduced.astype(jnp.bfloat16)


def solution(mesh):
    return jax.shard_map(
        shards,
        mesh=mesh,
        in_specs=(
            P("groups", "delta"),
            P("delta", "tensor"),
            P("delta", "tensor"),
            P("tensor", "delta"),
            P("delta", "tensor", None, None),
            P("delta", "tensor", None, None),
            P("delta", "tensor", None, None),
            P("delta", "tensor"),
            P("delta", "tensor"),
            P("delta", "tensor"),
            P("groups"),
            P("groups"),
        ),
        out_specs=P(("groups", "tensor"), "delta"),
        check_vma=False,
    )
```

profile of v0, /device:TPU:0, one launch (start us, length us, event | category | flops | bytes accessed | tf_op | source)
XLA Modules:
  0.0 516.8 jit_solution(12278220830866452507)
XLA Ops:
  6.5 0.0 copy-start
  6.5 0.9 select_reduce_fusion
  7.5 1.2 reduce-window.6
  8.7 0.2 slice_reduce_fusion
  8.9 0.2 reduce-window.9
  9.1 0.1 add_bitcast_fusion
  9.3 22.5 %scatter_fusion.1 = s32[4,128]{1,0:T(4,128)S(1)} fusion(s32[4,128]{1,0:T(4,128)S(1)} %broadcast.564.clone, s32[512]{0:T(512)S(1)} %bitcast.136, s32[512]{0:T(512)S(1)} %iota.29), kind=kCustom, calls=%fused_computation.6 | custom fusion | bytes 10240 | tf_op jit(solution)/shard_map/scatter | solution.py:18
  31.9 0.0 copy-done
  31.9 3.3 gather_fusion
  35.2 3.9 copy.28
  39.2 3.2 broadcast_select_fusion
  42.4 4.4 all-to-all-start
  46.9 0.0 reduce-scatter.3.cloned.1.call-start
  47.0 23.3 %scatter_fusion = pred[4,128]{1,0:T(4,128)(4,1)S(1)} fusion(pred[4,128]{1,0:T(4,128)(4,1)S(1)} %broadcast_in_dim.77, s32[512]{0:T(512)S(1)} %bitcast.137, pred[512]{0:T(512)(128)(4,1)S(1)} %broadcast.628), kind=kCustom, calls=%fused_computation.5 | custom fusion | bytes 5632 | tf_op jit(solution)/shard_map/scatter | solution.py:19
  70.3 0.0 copy-done.3
  70.3 0.1 copy.27
  70.4 0.1 reshape.496
  70.5 0.0 copy-done.4
  70.5 0.1 copy.31
  70.6 0.1 reshape.500
  70.7 0.0 copy-done.5
  70.8 0.1 copy.34
  70.8 0.1 reshape.503
  71.0 14.3 %fusion.53 = f32[512,4096]{1,0:T(8,128)} fusion(bf16[512,2048]{1,0:T(8,128)(2,1)S(1)} %copy-done, bf16[2048,4096]{1,0:T(8,128)(2,1)} %param.15), kind=kOutput, calls=%fused_computation.152 | convolution fusion | flops 8589934592 | bytes 27262976 | tf_op jit(solution)/shard_map/dot_general | solution.py:98
  85.3 14.4 %fusion.54 = f32[512,4096]{1,0:T(8,128)} fusion(bf16[512,2048]{1,0:T(8,128)(2,1)S(1)} %copy-done, bf16[2048,4096]{1,0:T(8,128)(2,1)} %param.16), kind=kOutput, calls=%fused_computation.153 | convolution fusion | flops 8589934592 | bytes 27262976 | tf_op jit(solution)/shard_map/dot_general | solution.py:99
  99.7 22.5 %scatter_fusion.2 = s32[4,128]{1,0:T(4,128)S(1)} fusion(s32[4,128]{1,0:T(4,128)S(1)} %broadcast.564.clone.1, s32[512]{0:T(512)S(1)} %bitcast.138, s32[512]{0:T(512)S(1)} %get-tuple-element.12), kind=kCustom, calls=%fused_computation.7 | custom fusion | bytes 10240 | tf_op jit(solution)/shard_map/scatter | solution.py:21
  122.3 0.1 and_convert_fusion
  122.3 11.5 %pad_maximum_fusion = f32[512,8192]{1,0:T(8,128)} fusion(f32[512,4096]{1,0:T(8,128)} %fusion.54, f32[512,4096]{1,0:T(8,128)} %fusion.53), kind=kLoop, calls=%fused_computation.10 | loop fusion | flops 4194304 | bytes 33554432 | tf_op jit(solution)/shard_map/concatenate | solution.py:101
  133.9 0.0 all-to-all-done
  133.9 3.4 copy.29
  137.3 0.0 copy-start.2
  137.3 0.6 gather_fusion.4
  137.9 1.7 fusion.6
  139.6 1.5 fusion.10
  141.2 0.0 copy-done.2
  141.2 1.6 copy.42
  142.8 2.2 gather_fusion.3
  145.0 1.6 fusion.7
  146.6 1.5 fusion.12
  148.1 3.0 copy.41
  151.1 18.4 %scatter_custom_fusion.3 = f32[512,8192]{1,0:T(8,128)} fusion(f32[512,8192]{1,0:T(8,128)} %pad_maximum_fusion, s32[128]{0:T(128)S(1)} %get-tuple-element.17, f32[128,4096]{1,0:T(8,128)S(1)} %bitcast.139, f32[]{:T(128)} %constant.248, f32[128,4096]{1,0:T(8,128)} %bitcast.140), kind=kCustom, calls=%fused_computation.11 | custom fusion | flops 2097152 | bytes 20972032 | tf_op jit(solution)/shard_map/scatter-add | solution.py:50
  169.4 0.0 reduce-scatter.3.cloned.1.call-update
  169.5 0.0 all-gather.2.cloned.1.call-start
  169.5 129.3 %reduce-scatter.3.cloned.1.call-done = f32[128,8192]{1,0:T(8,128)} async-done(((f32[512,8192]{1,0:T(8,128)}), f32[128,8192]{1,0:T(8,128)}) %reduce-scatter.3.cloned.1.call-update) | async-done | bytes 4194320 | tf_op jit(solution)/shard_map/reduce_scatter | solution.py:100
  298.8 3.8 fusion.4
  302.6 0.0 all-gather.2.cloned.1.call-update
  302.6 0.1 reshape.504
  302.8 34.5 %all-gather.2.cloned.1.call-done = bf16[512,4096]{1,0:T(8,128)(2,1)} async-done(((bf16[128,4096]{1,0:T(8,128)(2,1)}), bf16[512,4096]{1,0:T(8,128)(2,1)}) %all-gather.2.cloned.1.call-update) | async-done | bytes 4194320 | tf_op jit(solution)/shard_map/all_gather | solution.py:109
  337.3 4.9 gather_fusion.1
  342.2 0.2 fusion.8
  342.5 0.6 gather_fusion.2
  343.1 1.6 fusion.5
  344.7 3.6 convolution_bitcast_fusion
  348.2 5.6 %reshape_reshape.8 = f32[128,4,2048]{2,1,0:T(4,128)} reshape(f32[128,32,256]{2,1,0:T(8,128)} %convolution_bitcast_fusion) | data formatting | bytes 8388608 | tf_op jit(solution)/shard_map/reshape;reshape | solution.py:119
  353.9 6.6 %copy.38 = f32[128,4,2048]{2,0,1:T(8,128)} copy(f32[128,4,2048]{2,1,0:T(4,128)} %reshape_reshape.8) | data formatting | bytes 8388608 | tf_op jit(solution)/shard_map/reshape;reshape | solution.py:119
  360.4 4.9 all-to-all-start.1
  365.4 0.0 reduce-scatter.5.cloned.1.call-start
  365.4 15.2 %fusion.55 = f32[512,2048]{1,0:T(8,128)} fusion(bf16[512,4096]{1,0:T(8,128)(2,1)} %all-gather.2.cloned.1.call-done, bf16[4096,2048]{1,0:T(8,128)(2,1)} %param.17), kind=kOutput, calls=%fused_computation.154 | convolution fusion | flops 8589934592 | bytes 25165824 | tf_op jit(solution)/shard_map/dot_general | solution.py:111
  380.6 33.0 %all-to-all-done.1 = f32[128,4,2048]{2,0,1:T(8,128)} async-done(((f32[128,4,2048]{2,0,1:T(8,128)}), f32[128,4,2048]{2,0,1:T(8,128)}, u32[]{:S(2)}, u32[]{:S(2)}) %all-to-all-start.1) | async-done | bytes 4194336 | tf_op jit(solution)/shard_map/all_to_all | solution.py:120
  413.6 4.5 bitcast_select_fusion
  418.1 12.7 %scatter_fusion.3 = f32[512,2048]{1,0:T(8,128)} fusion(f32[512,2048]{1,0:T(8,128)} %fusion.55, s32[512]{0:T(512)S(1)} %bitcast.150, f32[512,2048]{1,0:T(8,128)} %bitcast_select_fusion), kind=kCustom, calls=%fused_computation.9 | custom fusion | flops 1048576 | bytes 12584960 | tf_op jit(solution)/shard_map/scatter-add | solution.py:124
  430.8 0.0 reduce-scatter.5.cloned.1.call-update
  430.8 76.9 %reduce-scatter.5.cloned.1.call-done = f32[128,2048]{1,0:T(8,128)} async-done(((f32[512,2048]{1,0:T(8,128)}), f32[128,2048]{1,0:T(8,128)}) %reduce-scatter.5.cloned.1.call-update) | async-done | bytes 1048592 | tf_op jit(solution)/shard_map/reduce_scatter | solution.py:125
  507.7 2.1 convert_element_type.27
  (34 shorter events, 0.3 us)
Async XLA Ops:
  6.5 25.4 %copy-start = (bf16[512,2048]{1,0:T(8,128)(2,1)S(1)}, bf16[512,2048]{1,0:T(8,128)(2,1)}, u32[]{:S(2)}) copy-start(bf16[512,2048]{1,0:T(8,128)(2,1)} %param.14) | copy-start | bytes 6291460
  39.2 31.1 %copy-start.3 = (s32[4,2]{0,1:T(2,128)S(1)}, s32[4,2]{0,1:T(2,128)}, u32[]{:S(2)}) copy-start(s32[4,2]{0,1:T(2,128)} %param.21) | copy-start | bytes 100
  39.2 31.3 %copy-start.4 = (s32[4,2]{0,1:T(2,128)S(1)}, s32[4,2]{0,1:T(2,128)}, u32[]{:S(2)}) copy-start(s32[4,2]{0,1:T(2,128)} %param.22) | copy-start | bytes 100
  39.2 31.5 %copy-start.5 = (s32[4,2]{0,1:T(2,128)S(1)}, s32[4,2]{0,1:T(2,128)}, u32[]{:S(2)}) copy-start(s32[4,2]{0,1:T(2,128)} %param.23) | copy-start | bytes 100
  42.4 91.5 %all-to-all-start = ((bf16[4,128,2048]{1,2,0:T(8,128)(2,1)}), bf16[4,128,2048]{1,2,0:T(8,128)(2,1)}, u32[]{:S(2)}, u32[]{:S(2)}) async-start(bf16[4,128,2048]{1,2,0:T(8,128)(2,1)} %broadcast_select_fusion), calls=%async_computation | async-start | bytes 4194304 | tf_op jit(solution)/shard_map/all_to_all | solution.py:88
  46.9 252.0 %reduce-scatter.3.cloned.1.call-start = ((), (), s32[]{:S(2)}) async-start(), calls=%async_computation.4 | async-start | bytes 20971520 | tf_op jit(solution)/shard_map/reduce_scatter | solution.py:100
  137.3 3.8 copy-start.2
  169.5 167.8 %all-gather.2.cloned.1.call-start = ((), (), s32[]{:S(2)}) async-start(), calls=%async_computation.5 | async-start | bytes 5242880 | tf_op jit(solution)/shard_map/all_gather | solution.py:109
  360.4 53.2 %all-to-all-start.1 = ((f32[128,4,2048]{2,0,1:T(8,128)}), f32[128,4,2048]{2,0,1:T(8,128)}, u32[]{:S(2)}, u32[]{:S(2)}) async-start(f32[128,4,2048]{2,0,1:T(8,128)} %copy.38), calls=%async_computation.2 | async-start | bytes 8388608 | tf_op jit(solution)/shard_map/all_to_all | solution.py:120
  365.4 142.3 %reduce-scatter.5.cloned.1.call-start = ((), (), s32[]{:S(2)}) async-start(), calls=%async_computation.6 | async-start | bytes 5242880 | tf_op jit(solution)/shard_map/reduce_scatter | solution.py:125
  418.1 91.7 %copy-start.1 = (bf16[512,2048]{1,0:T(8,128)(2,1)S(1)}, bf16[512,2048]{1,0:T(8,128)(2,1)}, u32[]{:S(2)}) copy-start(bf16[512,2048]{1,0:T(8,128)(2,1)} %param.14) | copy-start | bytes 6291460
Sparse Core Ops, SparseCore 0:
  169.6 129.1 reduce-scatter.2
  302.7 34.4 all-gather.1
  430.9 76.7 reduce-scatter.4
where the time goes:
time: 526 us; the launch traced here: 517 us
  waiting for transfers between devices  274 us (52%)
  local copies, waits for them, and re-layouts  105 us (20%)
  other arithmetic  59.1 us (11%)
  matrix products  55.4 us (11%)
  between operations  13.9 us (3%)
  starting transfers between devices  9.51 us (2%)
    reduce_scatter x1, waiting for transfers between devices, shards(): lax.psum_scatter(jnp.concatenate([base_gate, base_up], axis=1) + place_ro...  129 us
    reduce_scatter x1, waiting for transfers between devices, shards(): lax.psum_scatter(base_out, 'tensor', scatter_dimension=0, tiled=True)  76.9 us
    scatter x2, local copies, waits for them, and re-layouts, owner_slots(): jnp.zeros((owners, capacity), jnp.int32).at[owner_rows, position]  45.1 us
    all_gather x1, waiting for transfers between devices, shards(): shard_piece = lax.all_gather(hidden_home, 'delta', axis=0, tiled=True)  34.5 us
    all_to_all x1, waiting for transfers between devices, shards(): lax.all_to_all(spread, 'delta', split_axis=1, concat_axis=0, tiled=True)  33 us
    scatter x1, local copies, waits for them, and re-layouts, owner_slots(): jnp.zeros((owners, capacity), jnp.bool_).at[owner_rows, position].set(True)  23.3 us
    scatter-add x1, other arithmetic, place_rows(): jnp.zeros((row_count, values.shape[1]), jnp.float32).at[target]  18.4 us
    dot_general x1, matrix products, shards(): jnp.dot(shard_piece, down_weight, preferred_element_type=jnp.float32)  15.2 us
  transfers between devices with their start and end apart: 5, of which 4 were waited for; matrix products, arithmetic and copies ran while one was open for 20% of the time, Pallas kernels for 0%

commit v1 on v0

v1 whole, which is shorter than its diff:
```python
import functools

import jax
import jax.numpy as jnp
from jax import lax
from jax.experimental import pallas as pl
from jax.experimental.pallas import tpu as pltpu
from jax.sharding import PartitionSpec as P

CAP = 128
CHUNKS = (1, 1, 1, 1)
VMEM = 56 * 1024 * 1024
BF = jnp.bfloat16
F32 = jnp.float32


def cost(flops, moved):
    return pl.CostEstimate(flops=int(flops), bytes_accessed=int(moved), transcendentals=0)


def whole(shape):
    zeros = (0,) * len(shape)
    return pl.BlockSpec(shape, lambda *_: zeros)


def ranks(slot_lane, slot_sub, row_lane, row_sub, per_owner):
    same = (slot_sub // per_owner) == (slot_lane // per_owner)
    ahead = same & (row_sub < row_lane)
    return jnp.sum(ahead.astype(jnp.int32), axis=0, keepdims=True)


def pack_body(owners, per_owner, kinds, col_tiles, capacity, scal, x, sl, ss, rl, rs, out):
    tile = 256
    here = x.shape[1] // tile
    me = scal[0]
    pos = ranks(sl[...], ss[...], rl[...], rs[...], per_owner)
    rows = x.shape[0]
    place = lax.broadcasted_iota(jnp.int32, (capacity, rows), 0) == pos
    out[...] = jnp.zeros_like(out)

    def step(i, carry):
        at = i // per_owner
        local = i % per_owner
        owner = scal[1 + at]
        slot = owner * per_owner + local
        hot = jnp.where(place & (sl[...] == slot), 1.0, 0.0).astype(BF)
        top = pl.multiple_of(at * capacity, capacity)
        for j in range(kinds):
            block = scal[1 + owners + slot * kinds + j] // col_tiles

            @pl.when(block // here == me)
            def _():
                col = pl.multiple_of((block % here) * tile, tile)
                got = jnp.dot(hot, x[:, pl.ds(col, tile)], preferred_element_type=F32)
                view = (pl.ds(top, capacity), pl.ds(j * tile, tile))
                out[view] = out[view] + got.astype(BF)

        return carry

    lax.fori_loop(0, owners * per_owner, step, 0)


def pack(scal, xs, sl, ss, rl, rs, owners, per_owner, kinds, col_tiles):
    rows = xs.shape[0]
    width = kinds * 256
    return pl.pallas_call(
        functools.partial(pack_body, owners, per_owner, kinds, col_tiles, CAP),
        grid_spec=pltpu.PrefetchScalarGridSpec(
            num_scalar_prefetch=1,
            grid=(1,),
            in_specs=[whole(xs.shape), whole((1, rows)), whole((rows, 1)), whole((1, rows)), whole((rows, 1))],
            out_specs=whole((owners * CAP, width)),
        ),
        out_shape=jax.ShapeDtypeStruct((owners * CAP, width), BF),
        compiler_params=pltpu.CompilerParams(vmem_limit_bytes=VMEM),
        cost_estimate=cost(2e9, 4e6),
    )(scal, xs, sl, ss, rl, rs)


def product_body(owners, per_owner, per_slot, pieces, scal, x, gt, ut, sl, ss, rl, rs, out):
    tile = 256
    me = scal[0]
    capacity = x.shape[0]
    rows = sl.shape[1]
    pos = ranks(sl[...], ss[...], rl[...], rs[...], per_owner)
    place = lax.broadcasted_iota(jnp.int32, (capacity, rows), 0) == pos
    mine = place & ((sl[...] // per_owner) == me)
    slot = jnp.sum(jnp.where(mine, sl[...] % per_owner + 1, 0), axis=1, keepdims=True) - 1
    hot = jnp.where(mine, 1.0, 0.0).astype(BF)
    for kind, tiles in enumerate((gt, ut)):
        for j in range(per_slot):
            at = (kind * per_slot + j) * tile
            source = x[:, at : at + tile]
            total = jnp.zeros((capacity, tile), F32)
            for s in range(per_owner):
                picked = jnp.where(slot == s, source, jnp.zeros_like(source))
                total = total + jnp.dot(picked, tiles[s, j], preferred_element_type=F32)
            spread = lax.dot_general(
                hot, total.astype(BF), (((0,), (0,)), ((), ())), preferred_element_type=F32
            ).astype(BF)
            for home, offset, size, start in pieces:
                out[home, offset : offset + size, at : at + tile] = spread[start : start + size]


def product(scal, x, gt, ut, sl, ss, rl, rs, owners, per_owner, pieces):
    rows = sl.shape[1]
    per_slot = gt.shape[1]
    shape = (owners, rows // owners, x.shape[1])
    return pl.pallas_call(
        functools.partial(product_body, owners, per_owner, per_slot, pieces),
        grid_spec=pltpu.PrefetchScalarGridSpec(
            num_scalar_prefetch=1,
            grid=(1,),
            in_specs=[
                whole(x.shape),
                whole(gt.shape),
                whole(ut.shape),
                whole((1, rows)),
                whole((rows, 1)),
                whole((1, rows)),
                whole((rows, 1)),
            ],
            out_specs=whole(shape),
        ),
        out_shape=jax.ShapeDtypeStruct(shape, BF),
        compiler_params=pltpu.CompilerParams(vmem_limit_bytes=VMEM),
        cost_estimate=cost(1e9, 4e6),
    )(scal, x, gt, ut, sl, ss, rl, rs)


def gate_up_body(x, wg, wu, send, keep):
    half = send.shape[1]
    for i, w in enumerate((wg, wu)):
        total = jnp.dot(x[...], w[...], preferred_element_type=F32)
        send[i] = total[:half].astype(send.dtype)
        keep[i] = total[half:]


def gate_up(x, wg, wu):
    rows, depth = x.shape
    width = wg.shape[1]
    block = min(1024, width)
    outs = pl.BlockSpec((2, rows // 2, block), lambda i: (0, 0, i))
    weights = pl.BlockSpec((depth, block), lambda i: (0, i))
    return pl.pallas_call(
        gate_up_body,
        grid=(width // block,),
        in_specs=[whole(x.shape), weights, weights],
        out_specs=[outs, outs],
        out_shape=[jax.ShapeDtypeStruct((2, rows // 2, width), F32)] * 2,
        compiler_params=pltpu.CompilerParams(vmem_limit_bytes=VMEM),
        cost_estimate=cost(4 * rows * depth * width, 4 * depth * width),
    )(x, wg, wu)


def activate_body(per_slot, slots, col_tiles, first, scal, mine, got, delta, slot, out):
    tile = 256
    rows = out.shape[0]
    where = []
    for j in range(2 * per_slot):

        def look(s, held):
            return jnp.where(slot[...] == s, scal[first + s * 2 * per_slot + j] % col_tiles, held)

        where.append(lax.fori_loop(0, slots, look, jnp.zeros((rows, 1), jnp.int32)))
    for b in range(col_tiles):
        cols = slice(b * tile, (b + 1) * tile)
        sums = []
        for kind in range(2):
            total = mine[kind, :, cols] + got[kind, :, cols].astype(F32)
            for j in range(per_slot):
                k = kind * per_slot + j
                add = delta[:, k * tile : (k + 1) * tile].astype(F32)
                total = total + jnp.where(where[k] == b, add, 0.0)
            sums.append(total)
        gate, up = sums
        out[:, cols] = (gate / (1.0 + jnp.exp(-gate)) * up).astype(BF)


def activate(scal, mine, got, delta, slot, per_slot, slots, col_tiles, first):
    rows, width = mine.shape[1:]
    return pl.pallas_call(
        functools.partial(activate_body, per_slot, slots, col_tiles, first),
        grid_spec=pltpu.PrefetchScalarGridSpec(
            num_scalar_prefetch=1,
            grid=(1,),
            in_specs=[whole(mine.shape), whole(got.shape), whole(delta.shape), whole((rows, 1))],
            out_specs=whole((rows, width)),
        ),
        out_shape=jax.ShapeDtypeStruct((rows, width), BF),
        compiler_params=pltpu.CompilerParams(vmem_limit_bytes=VMEM),
        cost_estimate=cost(20 * rows * width, 14 * rows * width),
    )(scal, mine, got, delta, slot)


def down_body(width_tiles, here, count, scal, hid, w, tiles, slot, out):
    tile = 256
    me = scal[0]
    across = out.shape[1] // tile
    step = pl.program_id(0)
    out[...] = jnp.dot(hid[...], w[...], preferred_element_type=F32)

    def one(i, carry):
        place = scal[1 + count + i]
        block = place % width_tiles - me * here - step * across

        @pl.when((block >= 0) & (block < across))
        def _():
            source = hid[:, pl.ds(pl.multiple_of((place // width_tiles) * tile, tile), tile)]
            picked = jnp.where(slot[...] == scal[1 + i], source, jnp.zeros_like(source))
            add = jnp.dot(picked, tiles[i], preferred_element_type=F32)
            cols = pl.ds(pl.multiple_of(block * tile, tile), tile)
            out[:, cols] = out[:, cols] + add

        return carry

    lax.fori_loop(0, count, one, 0)


def down(scal, hid, w, tiles, slot, width_tiles):
    rows, depth = hid.shape
    width = w.shape[1]
    block = min(512, width)
    count = tiles.shape[0]
    return pl.pallas_call(
        functools.partial(down_body, width_tiles, width // 256, count),
        grid_spec=pltpu.PrefetchScalarGridSpec(
            num_scalar_prefetch=1,
            grid=(width // block,),
            in_specs=[
                whole(hid.shape),
                pl.BlockSpec((depth, block), lambda i, s: (0, i)),
                whole(tiles.shape),
                whole((rows, 1)),
            ],
            out_specs=pl.BlockSpec((rows, block), lambda i, s: (0, i)),
        ),
        out_shape=jax.ShapeDtypeStruct((rows, width), F32),
        compiler_params=pltpu.CompilerParams(vmem_limit_bytes=VMEM),
        cost_estimate=cost(2 * rows * depth * width, 2 * depth * width),
    )(scal, hid, w, tiles, slot)


def shards(
    tokens,
    gate_weight,
    up_weight,
    down_weight,
    gate_tiles,
    up_tiles,
    down_tiles,
    gate_pattern,
    up_pattern,
    down_pattern,
    row_variant,
    variant_slot,
):
    owners = lax.axis_size("delta")
    shift = lax.axis_size("tensor")
    groups = lax.axis_size("groups")
    me = lax.axis_index("delta")
    here_t = lax.axis_index("tensor")
    my_core, my_y = me % 2, me // 2
    ys = owners // 2
    per_owner, per_slot = gate_pattern.shape
    slots = owners * per_owner
    rows, shard_width = tokens.shape
    width = gate_weight.shape[1]
    col_tiles = width // 256
    width_tiles = shard_width * owners // 256
    unit = rows // sum(CHUNKS)
    sizes = [unit * c for c in CHUNKS]

    def core_swap(x):
        return lax.ppermute(x, "delta", [(i, i ^ 1) for i in range(owners)])

    def y_move(x, k):
        return lax.ppermute(x, "delta", [(i, (i + 2 * k) % owners) for i in range(owners)])

    order_y = [(my_y + k) % ys for k in range(1, ys)] + [my_y]
    homes = jnp.stack([y * 2 + c for c in (1 - my_core, my_core) for y in order_y]).astype(jnp.int32)

    def reduce_homes(x, axis):
        half = owners // 2
        kept = x[half:] + core_swap(x[:half])
        total = kept[ys - 1]
        for k in range(1, ys):
            total = total + y_move(kept[k - 1], k)
        return total

    row_ids = []
    offset = 0
    for size in sizes:
        each = size // (owners * shift)
        ids = (
            jnp.arange(shift, dtype=jnp.int32)[None, :, None] * (rows // shift)
            + offset
            + homes[:, None, None] * each
            + jnp.arange(each, dtype=jnp.int32)[None, None, :]
        )
        row_ids.append(ids.reshape(-1))
        offset += owners * each
    row_of = jnp.concatenate(row_ids)

    hit = row_variant[:, None] == jnp.arange(variant_slot.shape[0], dtype=jnp.int32)[None, :]
    slot_rows = jnp.sum(jnp.where(hit, variant_slot[None, :], 0), axis=1)
    slot_q = jnp.sum(
        jnp.where(row_of[:, None] == jnp.arange(rows, dtype=jnp.int32)[None, :], slot_rows[None, :], 0), axis=1
    )
    sl, ss = slot_q[None, :], slot_q[:, None]
    rl, rs = row_of[None, :], row_of[:, None]

    own = jnp.concatenate([gate_pattern, up_pattern, down_pattern], axis=1)
    seen = jnp.stack([own] + [lax.ppermute(own, "delta", [(i, (i - k) % owners) for i in range(owners)]) for k in range(1, owners)])
    back = (jnp.arange(owners, dtype=jnp.int32) - me) % owners
    by_owner = jnp.sum(
        jnp.where(
            (back[:, None] == jnp.arange(owners, dtype=jnp.int32)[None, :])[:, :, None, None], seen[None], 0
        ),
        axis=1,
    ).reshape(slots, 3 * per_slot)
    kinds = 2 * per_slot
    in_places = by_owner[:, :kinds].reshape(-1)
    scal = jnp.concatenate([me.astype(jnp.int32)[None], homes, in_places])

    if groups == 2 and per_owner % 2 == 0:
        part = per_owner // 2
        mine_g = lax.axis_index("groups")
        piece = lax.dynamic_slice_in_dim(down_tiles, mine_g * part, part, 0)
        gathered = jnp.stack([y_move(piece, -k) for k in range(1, ys)] + [piece])
        other = lax.ppermute(gathered, "groups", [(0, 1), (1, 0)])
        both = jnp.stack([gathered, other])
        starts = [mine_g * part, (1 - mine_g) * part]
    else:
        part = per_owner
        both = jnp.stack([y_move(down_tiles, -k) for k in range(1, ys)] + [down_tiles])[None]
        starts = [0]
    all_tiles = jnp.stack([core_swap(both), both]).reshape(-1, 256, 256)
    tile_slots = jnp.stack(
        [
            (y * 2 + c) * per_owner + start + s
            for c in (1 - my_core, my_core)
            for start in starts
            for y in order_y
            for s in range(part)
        ]
    ).astype(jnp.int32)
    picked = tile_slots[:, None] == jnp.arange(slots, dtype=jnp.int32)[None, :]
    places = jnp.sum(jnp.where(picked[:, :, None], by_owner[None, :, kinds:], 0), axis=1).reshape(-1)
    down_scal = jnp.concatenate([me.astype(jnp.int32)[None], jnp.repeat(tile_slots, per_slot), places])

    xs = jnp.take(tokens, row_of, axis=0)

    packed = pack(scal, xs, sl, ss, rl, rs, owners, per_owner, kinds, col_tiles)
    features = reduce_homes(packed.reshape(owners, CAP, -1), 0)
    pieces = []
    start, inner = 0, 0
    for size in sizes:
        each = size // owners
        for home in range(owners):
            pieces.append((home, inner, each, start + home * each))
        start += size
        inner += each
    spread = product(scal, features, gate_tiles, up_tiles, sl, ss, rl, rs, owners, per_owner, tuple(pieces))
    home_delta = reduce_homes(spread, 0)

    result = []
    start, inner = 0, 0
    for size in sizes:
        each = size // owners
        x = xs[start : start + size]
        send, keep = gate_up(x, gate_weight, up_weight)
        summed = keep + core_swap(send)
        mine = summed[:, (ys - 1) * each :]
        got = None
        for k in range(1, ys):
            moved = y_move(summed[:, (k - 1) * each : k * each].astype(BF), k)
            if got is None:
                got = moved
            else:
                mine = mine + moved.astype(F32)
        slot_home = ss[start + size - each : start + size]
        hid = activate(
            scal, mine, got, home_delta[inner : inner + each], slot_home, per_slot, slots, col_tiles, 1 + owners
        )
        chip = jnp.concatenate([y_move(hid, -k) for k in range(1, ys)] + [hid])
        full = jnp.concatenate([core_swap(chip), chip])
        out = down(down_scal, full, down_weight, all_tiles, ss[start : start + size], width_tiles)
        blocks = out.reshape(owners, shift, size // (owners * shift), shard_width).transpose(1, 0, 2, 3)
        total = lax.dynamic_index_in_dim(blocks, here_t, 0, keepdims=False)
        for k in range(1, shift):
            gone = lax.dynamic_index_in_dim(blocks, (here_t + k) % shift, 0, keepdims=False).astype(BF)
            total = total + lax.ppermute(
                gone, "tensor", [(i, (i + k) % shift) for i in range(shift)]
            ).astype(F32)
        result.append(total.astype(BF))
        start += size
        inner += each

    at = jnp.stack([((d // 2) - my_y - 1) % ys + ys * jnp.where(d % 2 == my_core, 1, 0) for d in range(owners)])
    placed = [jnp.take(r, at, axis=0).reshape(-1, shard_width) for r in result]
    return jnp.concatenate(placed, axis=0)


def solution(mesh):
    return jax.shard_map(
        shards,
        mesh=mesh,
        in_specs=(
            P("groups", "delta"),
            P("delta", "tensor"),
            P("delta", "tensor"),
            P("tensor", "delta"),
            P("delta", "tensor", None, None),
            P("delta", "tensor", None, None),
            P("delta", "tensor", None, None),
            P("delta", "tensor"),
            P("delta", "tensor"),
            P("delta", "tensor"),
            P("groups"),
            P("groups"),
        ),
        out_specs=P(("groups", "tensor"), "delta"),
        check_vma=False,
    )
```

time: 526 us -> 286 us (0.54); the launches traced: 517 us -> 285 us
  waiting for transfers between devices: 274 us -> 33.8 us
  Pallas kernels: 0 us -> 141 us
  local copies, waits for them, and re-layouts: 105 us -> 34.7 us
  matrix products: 55.4 us -> 0 us
  starting transfers between devices: 9.51 us -> 41.7 us
  other arithmetic: 59.1 us -> 33.1 us
  between operations: 13.9 us -> 0.51 us
    reduce_scatter x2 -> x0, waiting for transfers between devices: 206 us -> none  [the longest x1 129 us: shards(): lax.psum_scatter(jnp.concatenate([base_gate, base_up], axis=1) + place_ro...]
    pallas_call x0 -> x14, Pallas kernels: none -> 141 us  [the longest x4 56.8 us: gate_up(): pl.pallas_call(gate_up_body, grid=(width // block,), in_specs=[whole(x.sh...]
    scatter x3 -> x0, local copies, waits for them, and re-layouts: 68.4 us -> none  [the longest x2 45.1 us: owner_slots(): jnp.zeros((owners, capacity), jnp.int32).at[owner_rows, position]]
    dot_general x9 -> x0, matrix products: 55.4 us -> none  [the longest x1 15.2 us: shards(): jnp.dot(shard_piece, down_weight, preferred_element_type=jnp.float32)]
    ppermute x0 -> x38, starting transfers between devices: none -> 41.7 us  [the longest x12 23.1 us: shards(): lax.ppermute(gone, 'tensor', [(i, (i + k) % shift) for i in range(shift)])]
    all_gather x1 -> x0, waiting for transfers between devices: 34.5 us -> none  [shards(): shard_piece = lax.all_gather(hidden_home, 'delta', axis=0, tiled=True)]
    ppermute x0 -> x38, waiting for transfers between devices: none -> 33.8 us  [the longest x11 26.8 us: y_move(): lax.ppermute(x, 'delta', [(i, (i + 2 * k) % owners) for i in range(owners)])]
    all_to_all x2 -> x0, waiting for transfers between devices: 33 us -> none  [the longest x1 33 us: shards(): lax.all_to_all(spread, 'delta', split_axis=1, concat_axis=0, tiled=True)]
  transfers between devices with their start and end apart: 5 -> 38, of which waited for: 4 -> 8; matrix products, arithmetic and copies ran while one was open for 20% -> 21% of each run, Pallas kernels for 0% -> 45%
where the time goes in v1:
time: 286 us; the launch traced here: 285 us
  Pallas kernels  141 us (49%)
  starting transfers between devices  41.7 us (15%)
  local copies, waits for them, and re-layouts  34.7 us (12%)
  waiting for transfers between devices  33.8 us (12%)
  other arithmetic  33.1 us (12%)
    pallas_call x4, Pallas kernels, gate_up(): pl.pallas_call(gate_up_body, grid=(width // block,), in_specs=[whole(x.sh...  56.8 us
    pallas_call x4, Pallas kernels, down(): pl.pallas_call(functools.partial(down_body, width_tiles, width // 256, co...  54.6 us
    ppermute x11, waiting for transfers between devices, y_move(): lax.ppermute(x, 'delta', [(i, (i + 2 * k) % owners) for i in range(owners)])  26.8 us
    ppermute x12, starting transfers between devices, shards(): lax.ppermute(gone, 'tensor', [(i, (i + k) % shift) for i in range(shift)])  23.1 us
    pallas_call x4, Pallas kernels, activate(): pl.pallas_call(functools.partial(activate_body, per_slot, slots, col_tile...  16.1 us
    ppermute x11, starting transfers between devices, y_move(): lax.ppermute(x, 'delta', [(i, (i + 2 * k) % owners) for i in range(owners)])  11.1 us
    add x4, other arithmetic, shards(): summed = keep + core_swap(send)  9.03 us
    pallas_call x1, Pallas kernels, pack(): pl.pallas_call(functools.partial(pack_body, owners, per_owner, kinds, col...  8.65 us
  transfers between devices with their start and end apart: 38, of which 8 were waited for; matrix products, arithmetic and copies ran while one was open for 21% of the time, Pallas kernels for 45%

profile of v1, /device:TPU:0, one launch (start us, length us, event | category | flops | bytes accessed | tf_op | source)
XLA Modules:
  0.0 285.0 jit_solution(16855997030191512014)
XLA Ops:
  1.4 2.6 collective-permute-start.1
  4.0 1.4 collective-permute-start
  6.6 3.3 %gather_fusion = bf16[512,2048]{1,0:T(8,128)(2,1)} fusion(bf16[512,2048]{1,0:T(8,128)(2,1)S(1)} %copy-done, s32[1024]{0:T(1024)S(1)} %pad_clamp_fusion.1), kind=kCustom, calls=%fused_computation.4 | custom fusion | bytes 4196352 | tf_op jit(solution)/shard_map/jit(_take)/gather | solution.py:352
  9.9 1.8 broadcast_select_fusion.x
  11.8 1.6 fusion.29
  13.8 14.4 %shard_map.118 = (f32[2,64,4096]{2,1,0:T(8,128)}, f32[2,64,4096]{2,1,0:T(8,128)}) custom-call(bf16[128,2048]{1,0:T(8,128)(2,1)} %get-tuple-element.24.x, bf16[2048,4096]{1,0:T(8,128)(2,1)} %wg.7, bf16[2048,4096]{1,0:T(8,128)(2,1)} %wu.7), custom_call_target="tpu_custom_call" | custom-call | flops 4294967296 | bytes 33554432 | tf_op jit(solution)/shard_map/pallas_call | solution.py:145
  32.1 8.6 %shard_map.119 = bf16[512,1024]{1,0:T(8,128)(2,1)} custom-call(s32[69]{0:T(128)} %concatenate.81.scal, bf16[512,2048]{1,0:T(8,128)(2,1)} %copy-done.2, s32[1,512]{1,0:T(1,128)} %bitcast.193, s32[512,1]{1,0:T(8,128)} %copy.63.ss, s32[1,512]{1,0:T(1,128)} %bitcast.196, s32[512,1]{1,0:T(8,128)} %copy.64.rs), custom_call_target="tpu_custom_call" | custom-call | flops 2000000000 | bytes 4000000 | tf_op jit(solution)/shard_map/pallas_call | solution.py:66
  40.7 1.3 fusion.30
  42.2 14.1 %shard_map.123 = (f32[2,64,4096]{2,1,0:T(8,128)}, f32[2,64,4096]{2,1,0:T(8,128)}) custom-call(bf16[128,2048]{1,0:T(8,128)(2,1)} %get-tuple-element.27.x, bf16[2048,4096]{1,0:T(8,128)(2,1)} %wg.7, bf16[2048,4096]{1,0:T(8,128)(2,1)} %wu.7), custom_call_target="tpu_custom_call" | custom-call | flops 4294967296 | bytes 33554432 | tf_op jit(solution)/shard_map/pallas_call | solution.py:145
  56.6 14.1 %shard_map.126 = (f32[2,64,4096]{2,1,0:T(8,128)}, f32[2,64,4096]{2,1,0:T(8,128)}) custom-call(bf16[128,2048]{1,0:T(8,128)(2,1)} %get-tuple-element.26.x, bf16[2048,4096]{1,0:T(8,128)(2,1)} %wg.7, bf16[2048,4096]{1,0:T(8,128)(2,1)} %wu.7), custom_call_target="tpu_custom_call" | custom-call | flops 4294967296 | bytes 33554432 | tf_op jit(solution)/shard_map/pallas_call | solution.py:145
  71.1 1.4 collective-permute-start.6
  72.5 14.2 %shard_map.129 = (f32[2,64,4096]{2,1,0:T(8,128)}, f32[2,64,4096]{2,1,0:T(8,128)}) custom-call(bf16[128,2048]{1,0:T(8,128)(2,1)} %get-tuple-element.25.x, bf16[2048,4096]{1,0:T(8,128)(2,1)} %wg.7, bf16[2048,4096]{1,0:T(8,128)(2,1)} %wu.7), custom_call_target="tpu_custom_call" | custom-call | flops 4294967296 | bytes 33554432 | tf_op jit(solution)/shard_map/pallas_call | solution.py:145
  87.8 5.1 %shard_map.120 = bf16[4,128,1024]{2,1,0:T(8,128)(2,1)} custom-call(s32[69]{0:T(128)} %concatenate.81.scal, bf16[128,1024]{1,0:T(8,128)(2,1)} %fusion.1.x, bf16[4,2,256,256]{3,2,1,0:T(8,128)(2,1)} %gt.1, bf16[4,2,256,256]{3,2,1,0:T(8,128)(2,1)} %ut.1, s32[1,512]{1,0:T(1,128)} %bitcast.194, s32[512,1]{1,0:T(8,128)} %copy.63.ss, s32[1,512]{1,0:T(1,128)} %bitcast.197, ...), custom_call_target="tpu_custom_call" | custom-call | flops 1000000000 | bytes 4000000 | tf_op jit(solution)/shard_map/pallas_call | solution.py:109
  92.9 1.9 slice.200
  95.3 2.2 fusion.27
  97.6 1.5 collective-permute-start.12
  106.8 2.5 add.539
  110.1 1.2 collective-permute-start.4
  111.6 2.6 add.564
  116.0 2.0 add.568
  118.8 1.2 collective-permute-start.25
  120.0 1.9 add.572
  124.5 1.1 slice.193.mine
  125.6 4.0 %shard_map.121 = bf16[32,4096]{1,0:T(8,128)(2,1)} custom-call(s32[69]{0:T(128)} %concatenate.81.scal, f32[2,32,4096]{2,1,0:T(8,128)} %slice.193.mine, bf16[2,32,4096]{2,1,0:T(8,128)(2,1)} %collective-permute-done.4.got, bf16[32,1024]{1,0:T(8,128)(2,1)} %get-tuple-element.46.delta, s32[32,1]{1,0:T(8,128)} %copy.67.slot), custom_call_target="tpu_custom_call" | custom-call | flops 2621440 | bytes 1835008 | tf_op jit(solution)/shard_map/pallas_call | solution.py:182
  129.6 1.2 collective-permute-start.9
  131.3 2.8 pad_maximum_fusion.1
  134.1 1.1 slice.205.mine
  135.3 1.1 slice.209.mine
  136.3 1.1 slice.213.mine
  137.4 4.0 %shard_map.124 = bf16[32,4096]{1,0:T(8,128)(2,1)} custom-call(s32[69]{0:T(128)} %concatenate.81.scal, f32[2,32,4096]{2,1,0:T(8,128)} %slice.205.mine, bf16[2,32,4096]{2,1,0:T(8,128)(2,1)} %collective-permute-done.18.got, bf16[32,1024]{1,0:T(8,128)(2,1)} %get-tuple-element.49.delta, s32[32,1]{1,0:T(8,128)} %copy.71.slot), custom_call_target="tpu_custom_call" | custom-call | flops 2621440 | bytes 1835008 | tf_op jit(solution)/shard_map/pallas_call | solution.py:182
  142.2 5.6 %collective-permute-done.25.got = bf16[2,32,4096]{2,1,0:T(8,128)(2,1)} collective-permute-done((bf16[2,32,4096]{2,1,0:T(8,128)(2,1)}, bf16[2,32,4096]{2,1,0:T(8,128)(2,1)}, u32[]{:S(2)}, u32[]{:S(2)}) %collective-permute-start.25) | collective-permute-done | bytes 524320 | tf_op jit(solution)/shard_map/ppermute | solution.py:278
  147.8 4.1 %shard_map.127 = bf16[32,4096]{1,0:T(8,128)(2,1)} custom-call(s32[69]{0:T(128)} %concatenate.81.scal, f32[2,32,4096]{2,1,0:T(8,128)} %slice.209.mine, bf16[2,32,4096]{2,1,0:T(8,128)(2,1)} %collective-permute-done.25.got, bf16[32,1024]{1,0:T(8,128)(2,1)} %get-tuple-element.48.delta, s32[32,1]{1,0:T(8,128)} %copy.75.slot), custom_call_target="tpu_custom_call" | custom-call | flops 2621440 | bytes 1835008 | tf_op jit(solution)/shard_map/pallas_call | solution.py:182
  151.9 1.2 collective-permute-start.26
  153.1 6.0 %collective-permute-done.32.got = bf16[2,32,4096]{2,1,0:T(8,128)(2,1)} collective-permute-done((bf16[2,32,4096]{2,1,0:T(8,128)(2,1)}, bf16[2,32,4096]{2,1,0:T(8,128)(2,1)}, u32[]{:S(2)}, u32[]{:S(2)}) %collective-permute-start.32) | collective-permute-done | bytes 524320 | tf_op jit(solution)/shard_map/ppermute | solution.py:278
  159.0 4.0 %shard_map.130 = bf16[32,4096]{1,0:T(8,128)(2,1)} custom-call(s32[69]{0:T(128)} %concatenate.81.scal, f32[2,32,4096]{2,1,0:T(8,128)} %slice.213.mine, bf16[2,32,4096]{2,1,0:T(8,128)(2,1)} %collective-permute-done.32.got, bf16[32,1024]{1,0:T(8,128)(2,1)} %get-tuple-element.47.delta, s32[32,1]{1,0:T(8,128)} %copy.79.slot), custom_call_target="tpu_custom_call" | custom-call | flops 2621440 | bytes 1835008 | tf_op jit(solution)/shard_map/pallas_call | solution.py:182
  163.0 1.2 collective-permute-start.33
  164.6 5.5 %collective-permute-done.19 = bf16[32,4096]{1,0:T(8,128)(2,1)S(1)} collective-permute-done((bf16[32,4096]{1,0:T(8,128)(2,1)}, bf16[32,4096]{1,0:T(8,128)(2,1)S(1)}, u32[]{:S(2)}, u32[]{:S(2)}) %collective-permute-start.19) | collective-permute-done | bytes 262176 | tf_op jit(solution)/shard_map/ppermute | solution.py:278
  170.3 5.5 %collective-permute-done.26 = bf16[32,4096]{1,0:T(8,128)(2,1)S(1)} collective-permute-done((bf16[32,4096]{1,0:T(8,128)(2,1)}, bf16[32,4096]{1,0:T(8,128)(2,1)S(1)}, u32[]{:S(2)}, u32[]{:S(2)}) %collective-permute-start.26) | collective-permute-done | bytes 262176 | tf_op jit(solution)/shard_map/ppermute | solution.py:278
  175.9 3.9 %collective-permute-done.33 = bf16[32,4096]{1,0:T(8,128)(2,1)S(1)} collective-permute-done((bf16[32,4096]{1,0:T(8,128)(2,1)}, bf16[32,4096]{1,0:T(8,128)(2,1)S(1)}, u32[]{:S(2)}, u32[]{:S(2)}) %collective-permute-start.33) | collective-permute-done | bytes 262176 | tf_op jit(solution)/shard_map/ppermute | solution.py:278
  179.9 1.1 pad_maximum_fusion.2.hid
  181.0 1.1 pad_maximum_fusion.4.hid
  182.1 1.2 pad_maximum_fusion.5.hid
  183.2 1.1 pad_maximum_fusion.6.hid
  184.3 4.0 %pad_maximum_fusion = bf16[2,2,2,2,2,256,256]{6,5,4,3,2,1,0:T(8,128)(2,1)} fusion(bf16[1,2,2,2,2,256,256]{6,5,4,3,2,1,0:T(8,128)(2,1)S(1)} %get-tuple-element.29, bf16[1,2,2,2,2,256,256]{6,5,4,3,2,1,0:T(8,128)(2,1)} %bitcast.46), kind=kLoop, calls=%fused_computation.5 | loop fusion | flops 2097152 | bytes 8388608 | tf_op jit(solution)/shard_map/stack | solution.py:338
  188.3 13.6 %shard_map.122 = f32[128,2048]{1,0:T(8,128)} custom-call(s32[65]{0:T(128)} %pad_add_fusion.2.scal, bf16[128,4096]{1,0:T(8,128)(2,1)} %pad_maximum_fusion.2.hid, bf16[4096,2048]{1,0:T(8,128)(2,1)} %w.7, bf16[32,256,256]{2,1,0:T(8,128)(2,1)} %bitcast.176, s32[128,1]{1,0:T(8,128)} %copy.68.slot), custom_call_target="tpu_custom_call" | custom-call | flops 2147483648 | bytes 16777216 | tf_op jit(solution)/shard_map/pallas_call | solution.py:225
  201.9 1.1 fusion.18
  203.0 3.7 %collective-permute-start.16 = (bf16[4,8,2048]{2,1,0:T(8,128)(2,1)S(1)}, bf16[4,8,2048]{2,1,0:T(8,128)(2,1)S(1)}, u32[]{:S(2)}, u32[]{:S(2)}) collective-permute-start(bf16[4,8,2048]{2,1,0:T(8,128)(2,1)S(1)} %get-tuple-element.31), channel_id=1, source_target_pairs={{0,3},{1,0},{2,1},{3,2},{4,7},{5,4},{6,5},{7,6},{8,11},{9,8},{10,9... | collective-permute-start | bytes 393224 | tf_op jit(solution)/shard_map/ppermute | solution.py:393
  207.4 13.6 %shard_map.125 = f32[128,2048]{1,0:T(8,128)} custom-call(s32[65]{0:T(128)} %pad_add_fusion.2.scal, bf16[128,4096]{1,0:T(8,128)(2,1)} %pad_maximum_fusion.4.hid, bf16[4096,2048]{1,0:T(8,128)(2,1)} %w.7, bf16[32,256,256]{2,1,0:T(8,128)(2,1)} %bitcast.177, s32[128,1]{1,0:T(8,128)} %copy.72.slot), custom_call_target="tpu_custom_call" | custom-call | flops 2147483648 | bytes 16777216 | tf_op jit(solution)/shard_map/pallas_call | solution.py:225
  221.0 1.1 fusion.20
  222.1 2.9 %collective-permute-start.23 = (bf16[4,8,2048]{2,1,0:T(8,128)(2,1)S(1)}, bf16[4,8,2048]{2,1,0:T(8,128)(2,1)S(1)}, u32[]{:S(2)}, u32[]{:S(2)}) collective-permute-start(bf16[4,8,2048]{2,1,0:T(8,128)(2,1)S(1)} %get-tuple-element.34), channel_id=1, source_target_pairs={{0,3},{1,0},{2,1},{3,2},{4,7},{5,4},{6,5},{7,6},{8,11},{9,8},{10,9... | collective-permute-start | bytes 393224 | tf_op jit(solution)/shard_map/ppermute | solution.py:393
  225.0 1.3 collective-permute-start.22
  226.3 13.8 %shard_map.128 = f32[128,2048]{1,0:T(8,128)} custom-call(s32[65]{0:T(128)} %pad_add_fusion.2.scal, bf16[128,4096]{1,0:T(8,128)(2,1)} %pad_maximum_fusion.5.hid, bf16[4096,2048]{1,0:T(8,128)(2,1)} %w.7, bf16[32,256,256]{2,1,0:T(8,128)(2,1)} %bitcast.178, s32[128,1]{1,0:T(8,128)} %copy.76.slot), custom_call_target="tpu_custom_call" | custom-call | flops 2147483648 | bytes 16777216 | tf_op jit(solution)/shard_map/pallas_call | solution.py:225
  240.1 1.1 fusion.22
  241.2 13.6 %shard_map.131 = f32[128,2048]{1,0:T(8,128)} custom-call(s32[65]{0:T(128)} %pad_add_fusion.2.scal, bf16[128,4096]{1,0:T(8,128)(2,1)} %pad_maximum_fusion.6.hid, bf16[4096,2048]{1,0:T(8,128)(2,1)} %w.7, bf16[32,256,256]{2,1,0:T(8,128)(2,1)} %bitcast.179, s32[128,1]{1,0:T(8,128)} %copy.80.slot), custom_call_target="tpu_custom_call" | custom-call | flops 2147483648 | bytes 16777216 | tf_op jit(solution)/shard_map/pallas_call | solution.py:225
  254.8 1.1 fusion.24
  256.1 3.8 %collective-permute-start.30 = (bf16[4,8,2048]{2,1,0:T(8,128)(2,1)S(1)}, bf16[4,8,2048]{2,1,0:T(8,128)(2,1)S(1)}, u32[]{:S(2)}, u32[]{:S(2)}) collective-permute-start(bf16[4,8,2048]{2,1,0:T(8,128)(2,1)S(1)} %get-tuple-element.37), channel_id=1, source_target_pairs={{0,3},{1,0},{2,1},{3,2},{4,7},{5,4},{6,5},{7,6},{8,11},{9,8},{10,9... | collective-permute-start | bytes 393224 | tf_op jit(solution)/shard_map/ppermute | solution.py:393
  259.9 1.0 fusion.13
  261.6 3.2 %collective-permute-start.37 = (bf16[4,8,2048]{2,1,0:T(8,128)(2,1)S(1)}, bf16[4,8,2048]{2,1,0:T(8,128)(2,1)S(1)}, u32[]{:S(2)}, u32[]{:S(2)}) collective-permute-start(bf16[4,8,2048]{2,1,0:T(8,128)(2,1)S(1)} %get-tuple-element.40), channel_id=1, source_target_pairs={{0,3},{1,0},{2,1},{3,2},{4,7},{5,4},{6,5},{7,6},{8,11},{9,8},{10,9... | collective-permute-start | bytes 393224 | tf_op jit(solution)/shard_map/ppermute | solution.py:393
  264.8 5.6 %collective-permute-start.36 = (bf16[4,8,2048]{2,1,0:T(8,128)(2,1)S(1)}, bf16[4,8,2048]{2,1,0:T(8,128)(2,1)S(1)}, u32[]{:S(2)}, u32[]{:S(2)}) collective-permute-start(bf16[4,8,2048]{2,1,0:T(8,128)(2,1)S(1)} %get-tuple-element.41), channel_id=1, source_target_pairs={{0,2},{1,3},{2,0},{3,1},{4,6},{5,7},{6,4},{7,5},{8,10},{9,11},{10,... | collective-permute-start | bytes 393224 | tf_op jit(solution)/shard_map/ppermute | solution.py:393
  271.5 1.2 collective-permute-start.35
  272.7 5.7 %collective-permute-done.29 = bf16[4,8,2048]{2,1,0:T(8,128)(2,1)S(1)} collective-permute-done((bf16[4,8,2048]{2,1,0:T(8,128)(2,1)S(1)}, bf16[4,8,2048]{2,1,0:T(8,128)(2,1)S(1)}, u32[]{:S(2)}, u32[]{:S(2)}) %collective-permute-start.29) | collective-permute-done | bytes 131104 | tf_op jit(solution)/shard_map/ppermute | solution.py:393
  278.4 1.2 fusion.7
  281.3 1.2 collective-permute-done.36
  282.5 1.0 fusion.4
  (184 shorter events, 31.1 us)
Async XLA Ops:
  0.0 6.6 %copy-start = (bf16[512,2048]{1,0:T(8,128)(2,1)S(1)}, bf16[512,2048]{1,0:T(8,128)(2,1)}, u32[]{:S(2)}) copy-start(bf16[512,2048]{1,0:T(8,128)(2,1)} %param.14) | copy-start | bytes 6291460
  0.9 30.1 %collective-permute-start.2 = (s32[4,6]{0,1:T(8,128)S(1)}, s32[4,6]{0,1:T(8,128)S(1)}, u32[]{:S(2)}, u32[]{:S(2)}) collective-permute-start(s32[4,6]{0,1:T(8,128)S(1)} %pad_add_fusion.1), channel_id=1, source_target_pairs={{0,4},{4,8},{8,12},{12,0},{1,5},{5,9},{9,13},{13,1},{2,6},{6,10},{... | collective-permute-start | bytes 296 | tf_op jit(solution)/shard_map/ppermute | solution.py:314
  1.4 29.7 %collective-permute-start.1 = (s32[4,6]{0,1:T(8,128)S(1)}, s32[4,6]{0,1:T(8,128)S(1)}, u32[]{:S(2)}, u32[]{:S(2)}) collective-permute-start(s32[4,6]{0,1:T(8,128)S(1)} %pad_add_fusion.1), channel_id=1, source_target_pairs={{0,8},{4,12},{8,0},{12,4},{1,9},{5,13},{9,1},{13,5},{2,10},{6,14},... | collective-permute-start | bytes 296 | tf_op jit(solution)/shard_map/ppermute | solution.py:314
  4.0 27.2 %collective-permute-start = (s32[4,6]{0,1:T(8,128)S(1)}, s32[4,6]{0,1:T(8,128)S(1)}, u32[]{:S(2)}, u32[]{:S(2)}) collective-permute-start(s32[4,6]{0,1:T(8,128)S(1)} %pad_add_fusion.1), channel_id=1, source_target_pairs={{0,12},{4,0},{8,4},{12,8},{1,13},{5,1},{9,5},{13,9},{2,14},{6,2},{... | collective-permute-start | bytes 296 | tf_op jit(solution)/shard_map/ppermute | solution.py:314
  6.6 23.5 %copy-start.18 = (s32[512]{0:T(512)}, s32[512]{0:T(512)S(1)}, u32[]{:S(2)}) copy-start(s32[512]{0:T(512)S(1)} %constant_dynamic-update-slice_fusion.5) | copy-start | bytes 6148
  11.8 2.0 copy-start.2
  13.8 14.5 %copy-start.14 = (bf16[4,2,256,256]{3,2,1,0:T(8,128)(2,1)S(1)}, bf16[4,2,256,256]{3,2,1,0:T(8,128)(2,1)}, u32[]{:S(2)}) copy-start(bf16[4,2,256,256]{3,2,1,0:T(8,128)(2,1)} %param.20) | copy-start | bytes 3145732
  13.8 15.1 %copy-start.19 = (s32[512]{0:T(512)S(1)}, s32[512]{0:T(512)}, u32[]{:S(2)}) copy-start(s32[512]{0:T(512)} %param.24) | copy-start | bytes 6148
  13.8 15.1 %copy-start.20 = (s32[16]{0:T(128)S(1)}, s32[16]{0:T(128)}, u32[]{:S(2)}) copy-start(s32[16]{0:T(128)} %param.25) | copy-start | bytes 196
  28.2 71.7 %collective-permute-start.3 = (f32[2,64,4096]{2,1,0:T(8,128)}, f32[2,64,4096]{2,1,0:T(8,128)}, u32[]{:S(2)}, u32[]{:S(2)}) collective-permute-start(f32[2,64,4096]{2,1,0:T(8,128)} %get-tuple-element.15), channel_id=1, source_target_pairs={{0,4},{4,0},{8,12},{12,8},{1,5},{5,1},{9,13},{13,9},{2,6},{6,2},{1... | collective-permute-start | bytes 6291464 | tf_op jit(solution)/shard_map/ppermute | solution.py:275
  28.3 66.5 %collective-permute-start.11 = (bf16[2,2,256,256]{3,2,1,0:T(8,128)(2,1)S(1)}, bf16[2,2,256,256]{3,2,1,0:T(8,128)(2,1)}, u32[]{:S(2)}, u32[]{:S(2)}) collective-permute-start(bf16[2,2,256,256]{3,2,1,0:T(8,128)(2,1)S(1)} %constant_dynamic-slice_fusion), channel_id=1, source_target_pairs={{0,8},{4,12},{8,0},{12,4},{1,9},{5,13},{9,1},{13,5},{2,10},{6,14},... | collective-permute-start | bytes 1572872 | tf_op jit(solution)/shard_map/ppermute | solution.py:278
  29.2 2.8 copy-start.15
  42.0 28.9 %collective-permute-start.5 = (bf16[2,128,1024]{2,1,0:T(8,128)(2,1)S(1)}, bf16[2,128,1024]{2,1,0:T(8,128)(2,1)S(1)}, u32[]{:S(2)}, u32[]{:S(2)}) collective-permute-start(bf16[2,128,1024]{2,1,0:T(8,128)(2,1)S(1)} %bitcast.189), channel_id=1, source_target_pairs={{0,4},{4,0},{8,12},{12,8},{1,5},{5,1},{9,13},{13,9},{2,6},{6,2},{1... | collective-permute-start | bytes 1572872 | tf_op jit(solution)/shard_map/ppermute | solution.py:275
  56.3 53.8 %collective-permute-start.17 = (f32[2,64,4096]{2,1,0:T(8,128)}, f32[2,64,4096]{2,1,0:T(8,128)}, u32[]{:S(2)}, u32[]{:S(2)}) collective-permute-start(f32[2,64,4096]{2,1,0:T(8,128)} %get-tuple-element.17), channel_id=1, source_target_pairs={{0,4},{4,0},{8,12},{12,8},{1,5},{5,1},{9,13},{13,9},{2,6},{6,2},{1... | collective-permute-start | bytes 6291464 | tf_op jit(solution)/shard_map/ppermute | solution.py:275
  70.7 44.4 %collective-permute-start.24 = (f32[2,64,4096]{2,1,0:T(8,128)}, f32[2,64,4096]{2,1,0:T(8,128)}, u32[]{:S(2)}, u32[]{:S(2)}) collective-permute-start(f32[2,64,4096]{2,1,0:T(8,128)} %get-tuple-element.19), channel_id=1, source_target_pairs={{0,4},{4,0},{8,12},{12,8},{1,5},{5,1},{9,13},{13,9},{2,6},{6,2},{1... | collective-permute-start | bytes 6291464 | tf_op jit(solution)/shard_map/ppermute | solution.py:275
  71.1 15.7 %collective-permute-start.6 = (bf16[128,1024]{1,0:T(8,128)(2,1)S(1)}, bf16[128,1024]{1,0:T(8,128)(2,1)S(1)}, u32[]{:S(2)}, u32[]{:S(2)}) collective-permute-start(bf16[128,1024]{1,0:T(8,128)(2,1)S(1)} %slice_bitcast_fusion.2), channel_id=1, source_target_pairs={{0,8},{4,12},{8,0},{12,4},{1,9},{5,13},{9,1},{13,5},{2,10},{6,14},... | collective-permute-start | bytes 786440 | tf_op jit(solution)/shard_map/ppermute | solution.py:278
  72.5 14.5 %copy-start.16 = (s32[512]{0:T(512)S(1)}, s32[512]{0:T(512)}, u32[]{:S(2)}) copy-start(s32[512]{0:T(512)} %copy-done.15) | copy-start | bytes 6148
  86.8 32.0 %collective-permute-start.31 = (f32[2,64,4096]{2,1,0:T(8,128)}, f32[2,64,4096]{2,1,0:T(8,128)}, u32[]{:S(2)}, u32[]{:S(2)}) collective-permute-start(f32[2,64,4096]{2,1,0:T(8,128)} %get-tuple-element.21), channel_id=1, source_target_pairs={{0,4},{4,0},{8,12},{12,8},{1,5},{5,1},{9,13},{13,9},{2,6},{6,2},{1... | collective-permute-start | bytes 6291464 | tf_op jit(solution)/shard_map/ppermute | solution.py:275
  87.8 7.5 %copy-start.17 = (s32[512]{0:T(512)S(1)}, s32[512]{0:T(512)}, u32[]{:S(2)}) copy-start(s32[512]{0:T(512)} %copy-done.15) | copy-start | bytes 6148
  94.8 2.8 collective-permute-start.7
  95.3 3.8 %copy-start.5 = (bf16[4,128,1024]{2,1,0:T(8,128)(2,1)S(1)}, bf16[4,128,1024]{2,1,0:T(8,128)(2,1)}, u32[]{:S(2)}) copy-start(bf16[4,128,1024]{2,1,0:T(8,128)(2,1)} %shard_map.120) | copy-start | bytes 3145732
  97.6 33.7 %collective-permute-start.12 = (bf16[2,2,2,256,256]{4,3,2,1,0:T(8,128)(2,1)}, bf16[2,2,2,256,256]{4,3,2,1,0:T(8,128)(2,1)}, u32[]{:S(2)}, u32[]{:S(2)}) collective-permute-start(bf16[2,2,2,256,256]{4,3,2,1,0:T(8,128)(2,1)} %get-tuple-element.43), channel_id=1, source_target_pairs={{0,16},{16,0},{1,17},{17,1},{2,18},{18,2},{3,19},{19,3},{4,20},{20... | collective-permute-start | bytes 3145736 | tf_op jit(solution)/shard_map/ppermute | solution.py:331
  99.1 7.7 %copy-start.12 = (bf16[2,128,1024]{2,1,0:T(8,128)(2,1)}, bf16[2,128,1024]{2,1,0:T(8,128)(2,1)S(1)}, u32[]{:S(2)}) copy-start(bf16[2,128,1024]{2,1,0:T(8,128)(2,1)S(1)} %slice_add_fusion) | copy-start | bytes 1572868
  99.9 23.0 %collective-permute-start.8 = (bf16[128,1024]{1,0:T(8,128)(2,1)}, bf16[128,1024]{1,0:T(8,128)(2,1)S(1)}, u32[]{:S(2)}, u32[]{:S(2)}) collective-permute-start(bf16[128,1024]{1,0:T(8,128)(2,1)} %slice_bitcast_fusion), channel_id=1, source_target_pairs={{0,8},{4,12},{8,0},{12,4},{1,9},{5,13},{9,1},{13,5},{2,10},{6,14},... | collective-permute-start | bytes 786440 | tf_op jit(solution)/shard_map/ppermute | solution.py:278
  110.1 15.5 %collective-permute-start.4 = (bf16[2,32,4096]{2,1,0:T(8,128)(2,1)}, bf16[2,32,4096]{2,1,0:T(8,128)(2,1)}, u32[]{:S(2)}, u32[]{:S(2)}) collective-permute-start(bf16[2,32,4096]{2,1,0:T(8,128)(2,1)} %slice.240), channel_id=1, source_target_pairs={{0,8},{4,12},{8,0},{12,4},{1,9},{5,13},{9,1},{13,5},{2,10},{6,14},... | collective-permute-start | bytes 1572872 | tf_op jit(solution)/shard_map/ppermute | solution.py:278
  111.6 4.4 %copy-start.10 = (f32[2,64,4096]{2,1,0:T(8,128)S(1)}, f32[2,64,4096]{2,1,0:T(8,128)}, u32[]{:S(2)}) copy-start(f32[2,64,4096]{2,1,0:T(8,128)} %get-tuple-element.18) | copy-start | bytes 6291460
  115.1 22.3 %collective-permute-start.18 = (bf16[2,32,4096]{2,1,0:T(8,128)(2,1)}, bf16[2,32,4096]{2,1,0:T(8,128)(2,1)}, u32[]{:S(2)}, u32[]{:S(2)}) collective-permute-start(bf16[2,32,4096]{2,1,0:T(8,128)(2,1)} %slice.239), channel_id=1, source_target_pairs={{0,8},{4,12},{8,0},{12,4},{1,9},{5,13},{9,1},{13,5},{2,10},{6,14},... | collective-permute-start | bytes 1572872 | tf_op jit(solution)/shard_map/ppermute | solution.py:278
  116.0 4.0 %copy-start.11 = (f32[2,64,4096]{2,1,0:T(8,128)S(1)}, f32[2,64,4096]{2,1,0:T(8,128)}, u32[]{:S(2)}) copy-start(f32[2,64,4096]{2,1,0:T(8,128)} %get-tuple-element.20) | copy-start | bytes 6291460
  118.8 28.9 %collective-permute-start.25 = (bf16[2,32,4096]{2,1,0:T(8,128)(2,1)}, bf16[2,32,4096]{2,1,0:T(8,128)(2,1)}, u32[]{:S(2)}, u32[]{:S(2)}) collective-permute-start(bf16[2,32,4096]{2,1,0:T(8,128)(2,1)} %slice.238), channel_id=1, source_target_pairs={{0,8},{4,12},{8,0},{12,4},{1,9},{5,13},{9,1},{13,5},{2,10},{6,14},... | collective-permute-start | bytes 1572872 | tf_op jit(solution)/shard_map/ppermute | solution.py:278
  120.0 3.8 %copy-start.13 = (bf16[2,128,1024]{2,1,0:T(8,128)(2,1)S(1)}, bf16[2,128,1024]{2,1,0:T(8,128)(2,1)}, u32[]{:S(2)}) copy-start(bf16[2,128,1024]{2,1,0:T(8,128)(2,1)} %copy-done.12) | copy-start | bytes 1572868
  121.9 3.6 %copy-start.3 = (f32[2,64,4096]{2,1,0:T(8,128)}, f32[2,64,4096]{2,1,0:T(8,128)S(1)}, u32[]{:S(2)}) copy-start(f32[2,64,4096]{2,1,0:T(8,128)S(1)} %add.572) | copy-start | bytes 6291460
  122.9 36.1 %collective-permute-start.32 = (bf16[2,32,4096]{2,1,0:T(8,128)(2,1)}, bf16[2,32,4096]{2,1,0:T(8,128)(2,1)}, u32[]{:S(2)}, u32[]{:S(2)}) collective-permute-start(bf16[2,32,4096]{2,1,0:T(8,128)(2,1)} %slice.237), channel_id=1, source_target_pairs={{0,8},{4,12},{8,0},{12,4},{1,9},{5,13},{9,1},{13,5},{2,10},{6,14},... | collective-permute-start | bytes 1572872 | tf_op jit(solution)/shard_map/ppermute | solution.py:278
  129.6 35.0 %collective-permute-start.9 = (bf16[32,4096]{1,0:T(8,128)(2,1)}, bf16[32,4096]{1,0:T(8,128)(2,1)S(1)}, u32[]{:S(2)}, u32[]{:S(2)}) collective-permute-start(bf16[32,4096]{1,0:T(8,128)(2,1)} %shard_map.121), channel_id=1, source_target_pairs={{0,8},{4,12},{8,0},{12,4},{1,9},{5,13},{9,1},{13,5},{2,10},{6,14},... | collective-permute-start | bytes 786440 | tf_op jit(solution)/shard_map/ppermute | solution.py:278
  134.1 2.2 copy-start.4
  134.1 50.2 %collective-permute-start.13 = (bf16[2,2,2,2,256,256]{5,4,3,2,1,0:T(8,128)(2,1)}, bf16[2,2,2,2,256,256]{5,4,3,2,1,0:T(8,128)(2,1)}, u32[]{:S(2)}, u32[]{:S(2)}) collective-permute-start(bf16[2,2,2,2,256,256]{5,4,3,2,1,0:T(8,128)(2,1)} %get-tuple-element.28), channel_id=1, source_target_pairs={{0,4},{4,0},{8,12},{12,8},{1,5},{5,1},{9,13},{13,9},{2,6},{6,2},{1... | collective-permute-start | bytes 6291464 | tf_op jit(solution)/shard_map/ppermute | solution.py:275
  141.4 23.2 %copy-start.6 = (bf16[32,4096]{1,0:T(8,128)(2,1)S(1)}, bf16[32,4096]{1,0:T(8,128)(2,1)}, u32[]{:S(2)}) copy-start(bf16[32,4096]{1,0:T(8,128)(2,1)} %shard_map.121) | copy-start | bytes 786436
  141.4 28.8 %collective-permute-start.19 = (bf16[32,4096]{1,0:T(8,128)(2,1)}, bf16[32,4096]{1,0:T(8,128)(2,1)S(1)}, u32[]{:S(2)}, u32[]{:S(2)}) collective-permute-start(bf16[32,4096]{1,0:T(8,128)(2,1)} %shard_map.124), channel_id=1, source_target_pairs={{0,8},{4,12},{8,0},{12,4},{1,9},{5,13},{9,1},{13,5},{2,10},{6,14},... | collective-permute-start | bytes 786440 | tf_op jit(solution)/shard_map/ppermute | solution.py:278
  147.8 22.4 %copy-start.7 = (bf16[32,4096]{1,0:T(8,128)(2,1)S(1)}, bf16[32,4096]{1,0:T(8,128)(2,1)}, u32[]{:S(2)}) copy-start(bf16[32,4096]{1,0:T(8,128)(2,1)} %shard_map.124) | copy-start | bytes 786436
  151.9 23.9 %copy-start.8 = (bf16[32,4096]{1,0:T(8,128)(2,1)S(1)}, bf16[32,4096]{1,0:T(8,128)(2,1)}, u32[]{:S(2)}) copy-start(bf16[32,4096]{1,0:T(8,128)(2,1)} %shard_map.127) | copy-start | bytes 786436
  151.9 23.9 %collective-permute-start.26 = (bf16[32,4096]{1,0:T(8,128)(2,1)}, bf16[32,4096]{1,0:T(8,128)(2,1)S(1)}, u32[]{:S(2)}, u32[]{:S(2)}) collective-permute-start(bf16[32,4096]{1,0:T(8,128)(2,1)} %shard_map.127), channel_id=1, source_target_pairs={{0,8},{4,12},{8,0},{12,4},{1,9},{5,13},{9,1},{13,5},{2,10},{6,14},... | collective-permute-start | bytes 786440 | tf_op jit(solution)/shard_map/ppermute | solution.py:278
  163.0 16.8 %copy-start.9 = (bf16[32,4096]{1,0:T(8,128)(2,1)S(1)}, bf16[32,4096]{1,0:T(8,128)(2,1)}, u32[]{:S(2)}) copy-start(bf16[32,4096]{1,0:T(8,128)(2,1)} %shard_map.130) | copy-start | bytes 786436
  163.0 16.8 %collective-permute-start.33 = (bf16[32,4096]{1,0:T(8,128)(2,1)}, bf16[32,4096]{1,0:T(8,128)(2,1)S(1)}, u32[]{:S(2)}, u32[]{:S(2)}) collective-permute-start(bf16[32,4096]{1,0:T(8,128)(2,1)} %shard_map.130), channel_id=1, source_target_pairs={{0,8},{4,12},{8,0},{12,4},{1,9},{5,13},{9,1},{13,5},{2,10},{6,14},... | collective-permute-start | bytes 786440 | tf_op jit(solution)/shard_map/ppermute | solution.py:278
  164.6 15.4 %collective-permute-start.10 = (bf16[64,4096]{1,0:T(8,128)(2,1)S(1)}, bf16[64,4096]{1,0:T(8,128)(2,1)S(1)}, u32[]{:S(2)}, u32[]{:S(2)}) collective-permute-start(bf16[64,4096]{1,0:T(8,128)(2,1)S(1)} %pad_maximum_fusion.7), channel_id=1, source_target_pairs={{0,4},{4,0},{8,12},{12,8},{1,5},{5,1},{9,13},{13,9},{2,6},{6,2},{1... | collective-permute-start | bytes 1572872 | tf_op jit(solution)/shard_map/ppermute | solution.py:275
  170.2 10.8 %collective-permute-start.20 = (bf16[64,4096]{1,0:T(8,128)(2,1)S(1)}, bf16[64,4096]{1,0:T(8,128)(2,1)S(1)}, u32[]{:S(2)}, u32[]{:S(2)}) collective-permute-start(bf16[64,4096]{1,0:T(8,128)(2,1)S(1)} %pad_maximum_fusion.8), channel_id=1, source_target_pairs={{0,4},{4,0},{8,12},{12,8},{1,5},{5,1},{9,13},{13,9},{2,6},{6,2},{1... | collective-permute-start | bytes 1572872 | tf_op jit(solution)/shard_map/ppermute | solution.py:275
  175.8 6.3 %collective-permute-start.27 = (bf16[64,4096]{1,0:T(8,128)(2,1)S(1)}, bf16[64,4096]{1,0:T(8,128)(2,1)S(1)}, u32[]{:S(2)}, u32[]{:S(2)}) collective-permute-start(bf16[64,4096]{1,0:T(8,128)(2,1)S(1)} %pad_maximum_fusion.9), channel_id=1, source_target_pairs={{0,4},{4,0},{8,12},{12,8},{1,5},{5,1},{9,13},{13,9},{2,6},{6,2},{1... | collective-permute-start | bytes 1572872 | tf_op jit(solution)/shard_map/ppermute | solution.py:275
  179.9 3.4 %collective-permute-start.34 = (bf16[64,4096]{1,0:T(8,128)(2,1)S(1)}, bf16[64,4096]{1,0:T(8,128)(2,1)S(1)}, u32[]{:S(2)}, u32[]{:S(2)}) collective-permute-start(bf16[64,4096]{1,0:T(8,128)(2,1)S(1)} %pad_maximum_fusion.10), channel_id=1, source_target_pairs={{0,4},{4,0},{8,12},{12,8},{1,5},{5,1},{9,13},{13,9},{2,6},{6,2},{1... | collective-permute-start | bytes 1572872 | tf_op jit(solution)/shard_map/ppermute | solution.py:275
  203.0 52.9 %collective-permute-start.16 = (bf16[4,8,2048]{2,1,0:T(8,128)(2,1)S(1)}, bf16[4,8,2048]{2,1,0:T(8,128)(2,1)S(1)}, u32[]{:S(2)}, u32[]{:S(2)}) collective-permute-start(bf16[4,8,2048]{2,1,0:T(8,128)(2,1)S(1)} %get-tuple-element.31), channel_id=1, source_target_pairs={{0,3},{1,0},{2,1},{3,2},{4,7},{5,4},{6,5},{7,6},{8,11},{9,8},{10,9... | collective-permute-start | bytes 393224 | tf_op jit(solution)/shard_map/ppermute | solution.py:393
  206.7 49.3 %collective-permute-start.15 = (bf16[4,8,2048]{2,1,0:T(8,128)(2,1)S(1)}, bf16[4,8,2048]{2,1,0:T(8,128)(2,1)S(1)}, u32[]{:S(2)}, u32[]{:S(2)}) collective-permute-start(bf16[4,8,2048]{2,1,0:T(8,128)(2,1)S(1)} %get-tuple-element.32), channel_id=1, source_target_pairs={{0,2},{1,3},{2,0},{3,1},{4,6},{5,7},{6,4},{7,5},{8,10},{9,11},{10,... | collective-permute-start | bytes 393224 | tf_op jit(solution)/shard_map/ppermute | solution.py:393
  206.7 53.2 %collective-permute-start.14 = (bf16[4,8,2048]{2,1,0:T(8,128)(2,1)S(1)}, bf16[4,8,2048]{2,1,0:T(8,128)(2,1)S(1)}, u32[]{:S(2)}, u32[]{:S(2)}) collective-permute-start(bf16[4,8,2048]{2,1,0:T(8,128)(2,1)S(1)} %get-tuple-element.30), channel_id=1, source_target_pairs={{0,1},{1,2},{2,3},{3,0},{4,5},{5,6},{6,7},{7,4},{8,9},{9,10},{10,1... | collective-permute-start | bytes 393224 | tf_op jit(solution)/shard_map/ppermute | solution.py:393
  222.1 38.8 %collective-permute-start.23 = (bf16[4,8,2048]{2,1,0:T(8,128)(2,1)S(1)}, bf16[4,8,2048]{2,1,0:T(8,128)(2,1)S(1)}, u32[]{:S(2)}, u32[]{:S(2)}) collective-permute-start(bf16[4,8,2048]{2,1,0:T(8,128)(2,1)S(1)} %get-tuple-element.34), channel_id=1, source_target_pairs={{0,3},{1,0},{2,1},{3,2},{4,7},{5,4},{6,5},{7,6},{8,11},{9,8},{10,9... | collective-permute-start | bytes 393224 | tf_op jit(solution)/shard_map/ppermute | solution.py:393
  225.0 36.6 %collective-permute-start.22 = (bf16[4,8,2048]{2,1,0:T(8,128)(2,1)S(1)}, bf16[4,8,2048]{2,1,0:T(8,128)(2,1)S(1)}, u32[]{:S(2)}, u32[]{:S(2)}) collective-permute-start(bf16[4,8,2048]{2,1,0:T(8,128)(2,1)S(1)} %get-tuple-element.35), channel_id=1, source_target_pairs={{0,2},{1,3},{2,0},{3,1},{4,6},{5,7},{6,4},{7,5},{8,10},{9,11},{10,... | collective-permute-start | bytes 393224 | tf_op jit(solution)/shard_map/ppermute | solution.py:393
  256.0 8.8 %collective-permute-start.21 = (bf16[4,8,2048]{2,1,0:T(8,128)(2,1)S(1)}, bf16[4,8,2048]{2,1,0:T(8,128)(2,1)S(1)}, u32[]{:S(2)}, u32[]{:S(2)}) collective-permute-start(bf16[4,8,2048]{2,1,0:T(8,128)(2,1)S(1)} %get-tuple-element.33), channel_id=1, source_target_pairs={{0,1},{1,2},{2,3},{3,0},{4,5},{5,6},{6,7},{7,4},{8,9},{9,10},{10,1... | collective-permute-start | bytes 393224 | tf_op jit(solution)/shard_map/ppermute | solution.py:393
  256.1 15.4 %collective-permute-start.30 = (bf16[4,8,2048]{2,1,0:T(8,128)(2,1)S(1)}, bf16[4,8,2048]{2,1,0:T(8,128)(2,1)S(1)}, u32[]{:S(2)}, u32[]{:S(2)}) collective-permute-start(bf16[4,8,2048]{2,1,0:T(8,128)(2,1)S(1)} %get-tuple-element.37), channel_id=1, source_target_pairs={{0,3},{1,0},{2,1},{3,2},{4,7},{5,4},{6,5},{7,6},{8,11},{9,8},{10,9... | collective-permute-start | bytes 393224 | tf_op jit(solution)/shard_map/ppermute | solution.py:393
  259.9 18.5 %collective-permute-start.29 = (bf16[4,8,2048]{2,1,0:T(8,128)(2,1)S(1)}, bf16[4,8,2048]{2,1,0:T(8,128)(2,1)S(1)}, u32[]{:S(2)}, u32[]{:S(2)}) collective-permute-start(bf16[4,8,2048]{2,1,0:T(8,128)(2,1)S(1)} %get-tuple-element.38), channel_id=1, source_target_pairs={{0,2},{1,3},{2,0},{3,1},{4,6},{5,7},{6,4},{7,5},{8,10},{9,11},{10,... | collective-permute-start | bytes 393224 | tf_op jit(solution)/shard_map/ppermute | solution.py:393
  260.9 17.5 %collective-permute-start.28 = (bf16[4,8,2048]{2,1,0:T(8,128)(2,1)S(1)}, bf16[4,8,2048]{2,1,0:T(8,128)(2,1)S(1)}, u32[]{:S(2)}, u32[]{:S(2)}) collective-permute-start(bf16[4,8,2048]{2,1,0:T(8,128)(2,1)S(1)} %get-tuple-element.36), channel_id=1, source_target_pairs={{0,1},{1,2},{2,3},{3,0},{4,5},{5,6},{6,7},{7,4},{8,9},{9,10},{10,1... | collective-permute-start | bytes 393224 | tf_op jit(solution)/shard_map/ppermute | solution.py:393
  261.6 19.7 %collective-permute-start.37 = (bf16[4,8,2048]{2,1,0:T(8,128)(2,1)S(1)}, bf16[4,8,2048]{2,1,0:T(8,128)(2,1)S(1)}, u32[]{:S(2)}, u32[]{:S(2)}) collective-permute-start(bf16[4,8,2048]{2,1,0:T(8,128)(2,1)S(1)} %get-tuple-element.40), channel_id=1, source_target_pairs={{0,3},{1,0},{2,1},{3,2},{4,7},{5,4},{6,5},{7,6},{8,11},{9,8},{10,9... | collective-permute-start | bytes 393224 | tf_op jit(solution)/shard_map/ppermute | solution.py:393
  264.8 17.7 %collective-permute-start.36 = (bf16[4,8,2048]{2,1,0:T(8,128)(2,1)S(1)}, bf16[4,8,2048]{2,1,0:T(8,128)(2,1)S(1)}, u32[]{:S(2)}, u32[]{:S(2)}) collective-permute-start(bf16[4,8,2048]{2,1,0:T(8,128)(2,1)S(1)} %get-tuple-element.41), channel_id=1, source_target_pairs={{0,2},{1,3},{2,0},{3,1},{4,6},{5,7},{6,4},{7,5},{8,10},{9,11},{10,... | collective-permute-start | bytes 393224 | tf_op jit(solution)/shard_map/ppermute | solution.py:393
  271.5 11.0 %collective-permute-start.35 = (bf16[4,8,2048]{2,1,0:T(8,128)(2,1)S(1)}, bf16[4,8,2048]{2,1,0:T(8,128)(2,1)S(1)}, u32[]{:S(2)}, u32[]{:S(2)}) collective-permute-start(bf16[4,8,2048]{2,1,0:T(8,128)(2,1)S(1)} %get-tuple-element.39), channel_id=1, source_target_pairs={{0,1},{1,2},{2,3},{3,0},{4,5},{5,6},{6,7},{7,4},{8,9},{9,10},{10,1... | collective-permute-start | bytes 393224 | tf_op jit(solution)/shard_map/ppermute | solution.py:393
  278.4 6.6 %copy-start.1 = (bf16[512,2048]{1,0:T(8,128)(2,1)S(1)}, bf16[512,2048]{1,0:T(8,128)(2,1)}, u32[]{:S(2)}) copy-start(bf16[512,2048]{1,0:T(8,128)(2,1)} %param.14) | copy-start | bytes 6291460

commit v2 on v1

v2 whole, which is shorter than its diff:
```python
import functools

import jax
import jax.numpy as jnp
from jax import lax
from jax.experimental import pallas as pl
from jax.experimental.pallas import tpu as pltpu
from jax.sharding import PartitionSpec as P

CAP = 128
CHUNKS = (1, 2, 1)
VMEM = 56 * 1024 * 1024
BF = jnp.bfloat16
F32 = jnp.float32


def cost(flops, moved):
    return pl.CostEstimate(flops=int(flops), bytes_accessed=int(moved), transcendentals=0)


def whole(shape):
    zeros = (0,) * len(shape)
    return pl.BlockSpec(shape, lambda *_: zeros)


def pack_body(owners, per_owner, kinds, capacity, scal, x, sl, ss, table, out, code):
    tile = 256
    rows, held = x.shape
    here = held // tile
    owner_l = sl[...] // per_owner
    first = lax.broadcasted_iota(jnp.int32, (rows, rows), 0)
    second = lax.broadcasted_iota(jnp.int32, (rows, rows), 1)
    ahead = ((ss[...] // per_owner) == owner_l) & (first < second)
    pos = jnp.sum(jnp.where(ahead, 1, 0), axis=0, keepdims=True)
    code[...] = sl[...] * capacity + pos
    target = pos
    for o in range(owners):
        target = target + jnp.where(owner_l == o, scal[1 + o] * capacity, 0)
    hot = lax.broadcasted_iota(jnp.int32, (owners * capacity, rows), 0) == target
    hot = jnp.where(hot, 1.0, 0.0).astype(BF)
    lanes = lax.broadcasted_iota(jnp.int32, (rows, table.shape[0]), 1)
    slot_hot = jnp.where(ss[...] == lanes, 1.0, 0.0).astype(BF)
    block = jnp.dot(slot_hot, table[...], preferred_element_type=F32)
    block = block - (scal[0] * here).astype(F32)
    for j in range(kinds):
        at = block[:, j : j + 1]
        picked = jnp.zeros((rows, tile), BF)
        for b in range(here):
            picked = jnp.where(at == float(b), x[:, b * tile : (b + 1) * tile], picked)
        out[:, j * tile : (j + 1) * tile] = jnp.dot(hot, picked, preferred_element_type=F32).astype(BF)


def pack(scal, x, sl, ss, table, owners, per_owner, kinds):
    rows = x.shape[0]
    width = kinds * 256
    return pl.pallas_call(
        functools.partial(pack_body, owners, per_owner, kinds, CAP),
        grid_spec=pltpu.PrefetchScalarGridSpec(
            num_scalar_prefetch=1,
            grid=(1,),
            in_specs=[whole(x.shape), whole((1, rows)), whole((rows, 1)), whole(table.shape)],
            out_specs=[whole((owners * CAP, width)), whole((1, rows))],
        ),
        out_shape=[
            jax.ShapeDtypeStruct((owners * CAP, width), BF),
            jax.ShapeDtypeStruct((1, rows), jnp.int32),
        ],
        compiler_params=pltpu.CompilerParams(vmem_limit_bytes=VMEM),
        cost_estimate=cost(4e9, 4e6),
    )(scal, x, sl, ss, table)


def product_body(owners, per_owner, per_slot, pieces, scal, x, gt, ut, code, out):
    tile = 256
    capacity = x.shape[0]
    rows = code.shape[1]
    slot_l = code[...] // capacity
    place = lax.broadcasted_iota(jnp.int32, (capacity, rows), 0) == code[...] % capacity
    mine = place & (slot_l // per_owner == scal[0])
    slot = jnp.sum(jnp.where(mine, slot_l % per_owner + 1, 0), axis=1, keepdims=True) - 1
    hot = jnp.where(mine, 1.0, 0.0).astype(BF)
    for kind, tiles in enumerate((gt, ut)):
        for j in range(per_slot):
            at = (kind * per_slot + j) * tile
            source = x[:, at : at + tile]
            total = jnp.zeros((capacity, tile), F32)
            for s in range(per_owner):
                picked = jnp.where(slot == s, source, jnp.zeros_like(source))
                total = total + jnp.dot(picked, tiles[s, j], preferred_element_type=F32)
            spread = lax.dot_general(
                hot, total.astype(BF), (((0,), (0,)), ((), ())), preferred_element_type=F32
            ).astype(BF)
            for home, offset, size, start in pieces:
                out[home, offset : offset + size, at : at + tile] = spread[start : start + size]


def product(scal, x, gt, ut, code, owners, per_owner, pieces):
    rows = code.shape[1]
    per_slot = gt.shape[1]
    shape = (owners, rows // owners, x.shape[1])
    return pl.pallas_call(
        functools.partial(product_body, owners, per_owner, per_slot, pieces),
        grid_spec=pltpu.PrefetchScalarGridSpec(
            num_scalar_prefetch=1,
            grid=(1,),
            in_specs=[whole(x.shape), whole(gt.shape), whole(ut.shape), whole((1, rows))],
            out_specs=whole(shape),
        ),
        out_shape=jax.ShapeDtypeStruct(shape, BF),
        compiler_params=pltpu.CompilerParams(vmem_limit_bytes=VMEM),
        cost_estimate=cost(4e9, 4e6),
    )(scal, x, gt, ut, code)


def gate_up_body(x, wg, wu, send, keep):
    half = send.shape[1]
    for i, w in enumerate((wg, wu)):
        total = jnp.dot(x[...], w[...], preferred_element_type=F32)
        send[i] = total[:half].astype(send.dtype)
        keep[i] = total[half:]


def gate_up(x, wg, wu):
    rows, depth = x.shape
    width = wg.shape[1]
    block = min(1024, width)
    outs = pl.BlockSpec((2, rows // 2, block), lambda i: (0, 0, i))
    weights = pl.BlockSpec((depth, block), lambda i: (0, i))
    return pl.pallas_call(
        gate_up_body,
        grid=(width // block,),
        in_specs=[whole(x.shape), weights, weights],
        out_specs=[outs, outs],
        out_shape=[jax.ShapeDtypeStruct((2, rows // 2, width), F32)] * 2,
        compiler_params=pltpu.CompilerParams(vmem_limit_bytes=VMEM),
        cost_estimate=cost(4 * rows * depth * width, 4 * depth * width),
    )(x, wg, wu)


def activate_body(per_slot, start, each, keep, core, got, delta, where, out):
    tile = 256
    step = pl.program_id(0)
    across = out.shape[1] // tile
    at = [where[start : start + each, k : k + 1] - step * across for k in range(2 * per_slot)]
    adds = [
        delta[start : start + each, k * tile : (k + 1) * tile].astype(F32) for k in range(2 * per_slot)
    ]
    for b in range(across):
        cols = slice(b * tile, (b + 1) * tile)
        sums = []
        for kind in range(2):
            total = keep[kind, :, cols] + core[kind, :, cols] + got[kind, :, cols].astype(F32)
            for k in range(kind * per_slot, (kind + 1) * per_slot):
                total = total + jnp.where(at[k] == b, adds[k], 0.0)
            sums.append(total)
        gate, up = sums
        out[:, cols] = (gate / (1.0 + jnp.exp(-gate)) * up).astype(BF)


def activate(keep, core, got, delta, where, per_slot, start):
    each, width = got.shape[1:]
    last = keep.shape[1] // each - 1
    block = min(1024, width)
    own = pl.BlockSpec((2, each, block), lambda i: (0, last, i))
    return pl.pallas_call(
        functools.partial(activate_body, per_slot, start, each),
        grid=(width // block,),
        in_specs=[
            own,
            own,
            pl.BlockSpec((2, each, block), lambda i: (0, 0, i)),
            whole(delta.shape),
            whole(where.shape),
        ],
        out_specs=pl.BlockSpec((each, block), lambda i: (0, i)),
        out_shape=jax.ShapeDtypeStruct((each, width), BF),
        compiler_params=pltpu.CompilerParams(vmem_limit_bytes=VMEM),
        cost_estimate=cost(20 * each * width, 24 * each * width),
    )(keep, core, got, delta, where)


def down_body(width_tiles, here, count, start, scal, far, near, w, tiles, slot, out, hid):
    tile = 256
    me = scal[0]
    across = out.shape[1] // tile
    step = pl.program_id(0)
    half = far.shape[0]

    @pl.when(step == 0)
    def _():
        hid[:half] = far[...]
        hid[half:] = near[...]

    out[...] = jnp.dot(hid[...], w[...], preferred_element_type=F32)

    def one(i, carry):
        place = scal[1 + count + i]
        block = place % width_tiles - me * here - step * across

        @pl.when((block >= 0) & (block < across))
        def _():
            source = hid[:, pl.ds(pl.multiple_of((place // width_tiles) * tile, tile), tile)]
            hit = slot[start : start + 2 * half] == scal[1 + i]
            picked = jnp.where(hit, source, jnp.zeros_like(source))
            add = jnp.dot(picked, tiles[i], preferred_element_type=F32)
            cols = pl.ds(pl.multiple_of(block * tile, tile), tile)
            out[:, cols] = out[:, cols] + add

        return carry

    lax.fori_loop(0, count, one, 0)


def down(scal, far, near, w, tiles, slot, width_tiles, start):
    rows, depth = 2 * far.shape[0], far.shape[1]
    width = w.shape[1]
    block = min(512, width)
    count = tiles.shape[0]
    return pl.pallas_call(
        functools.partial(down_body, width_tiles, width // 256, count, start),
        grid_spec=pltpu.PrefetchScalarGridSpec(
            num_scalar_prefetch=1,
            grid=(width // block,),
            in_specs=[
                whole(far.shape),
                whole(near.shape),
                pl.BlockSpec((depth, block), lambda i, s: (0, i)),
                whole(tiles.shape),
                whole(slot.shape),
            ],
            out_specs=pl.BlockSpec((rows, block), lambda i, s: (0, i)),
            scratch_shapes=[pltpu.VMEM((rows, depth), BF)],
        ),
        out_shape=jax.ShapeDtypeStruct((rows, width), F32),
        compiler_params=pltpu.CompilerParams(vmem_limit_bytes=VMEM),
        cost_estimate=cost(3 * rows * depth * width, 3 * depth * width),
    )(scal, far, near, w, tiles, slot)


def shards(
    tokens,
    gate_weight,
    up_weight,
    down_weight,
    gate_tiles,
    up_tiles,
    down_tiles,
    gate_pattern,
    up_pattern,
    down_pattern,
    row_variant,
    variant_slot,
):
    owners = lax.axis_size("delta")
    shift = lax.axis_size("tensor")
    groups = lax.axis_size("groups")
    me = lax.axis_index("delta")
    here_t = lax.axis_index("tensor")
    my_core, my_y = me % 2, me // 2
    ys = owners // 2
    per_owner, per_slot = gate_pattern.shape
    slots = owners * per_owner
    rows, shard_width = tokens.shape
    width = gate_weight.shape[1]
    col_tiles = width // 256
    width_tiles = shard_width * owners // 256
    unit = rows // sum(CHUNKS)
    sizes = [unit * c for c in CHUNKS]

    def core_swap(x):
        return lax.ppermute(x, "delta", [(i, i ^ 1) for i in range(owners)])

    def y_move(x, k):
        return lax.ppermute(x, "delta", [(i, (i + 2 * k) % owners) for i in range(owners)])

    order_y = [(my_y + k) % ys for k in range(1, ys)] + [my_y]
    homes = jnp.stack([y * 2 + c for c in (1 - my_core, my_core) for y in order_y]).astype(jnp.int32)

    def reduce_homes(x, axis):
        half = owners // 2
        kept = x[half:] + core_swap(x[:half])
        total = kept[ys - 1]
        for k in range(1, ys):
            total = total + y_move(kept[k - 1], k)
        return total

    row_ids = []
    offset = 0
    for size in sizes:
        each = size // (owners * shift)
        ids = (
            jnp.arange(shift, dtype=jnp.int32)[None, :, None] * (rows // shift)
            + offset
            + homes[:, None, None] * each
            + jnp.arange(each, dtype=jnp.int32)[None, None, :]
        )
        row_ids.append(ids.reshape(-1))
        offset += owners * each
    row_of = jnp.concatenate(row_ids)

    hit = row_variant[:, None] == jnp.arange(variant_slot.shape[0], dtype=jnp.int32)[None, :]
    slot_rows = jnp.sum(jnp.where(hit, variant_slot[None, :], 0), axis=1)

    own = jnp.concatenate([gate_pattern, up_pattern, down_pattern], axis=1)
    seen = jnp.stack([own] + [lax.ppermute(own, "delta", [(i, (i - k) % owners) for i in range(owners)]) for k in range(1, owners)])
    back = (jnp.arange(owners, dtype=jnp.int32) - me) % owners
    by_owner = jnp.sum(
        jnp.where(
            (back[:, None] == jnp.arange(owners, dtype=jnp.int32)[None, :])[:, :, None, None], seen[None], 0
        ),
        axis=1,
    ).reshape(slots, 3 * per_slot)
    kinds = 2 * per_slot
    at_home = jnp.stack(
        [((d // 2) - my_y - 1) % ys + ys * jnp.where(d % 2 == my_core, 1, 0) for d in range(owners)]
    ).astype(jnp.int32)
    scal = jnp.concatenate([me.astype(jnp.int32)[None], at_home])
    blocks_in = (by_owner[:, :kinds] // col_tiles).astype(BF)
    table = jnp.pad(blocks_in, ((0, -slots % 128), (0, -kinds % 128)))

    if groups == 2 and per_owner % 2 == 0:
        part = per_owner // 2
        mine_g = lax.axis_index("groups")
        piece = lax.dynamic_slice_in_dim(down_tiles, mine_g * part, part, 0)
        gathered = jnp.stack([y_move(piece, -k) for k in range(1, ys)] + [piece])
        other = lax.ppermute(gathered, "groups", [(0, 1), (1, 0)])
        both = jnp.stack([gathered, other])
        firsts = [mine_g * part, (1 - mine_g) * part]
    else:
        part = per_owner
        both = jnp.stack([y_move(down_tiles, -k) for k in range(1, ys)] + [down_tiles])[None]
        firsts = [0]
    all_tiles = jnp.stack([core_swap(both), both]).reshape(-1, 256, 256)
    tile_slots = jnp.stack(
        [
            (y * 2 + c) * per_owner + first + s
            for c in (1 - my_core, my_core)
            for first in firsts
            for y in order_y
            for s in range(part)
        ]
    ).astype(jnp.int32)
    picked = tile_slots[:, None] == jnp.arange(slots, dtype=jnp.int32)[None, :]
    places = jnp.sum(jnp.where(picked[:, :, None], by_owner[None, :, kinds:], 0), axis=1).reshape(-1)
    down_scal = jnp.concatenate([me.astype(jnp.int32)[None], jnp.repeat(tile_slots, per_slot), places])

    def after(x, *earlier):
        return lax.optimization_barrier((x, *earlier))[0]

    def transform(i, x):
        send, keep = gate_up(x, gate_weight, up_weight)
        return keep, core_swap(send)

    def exchange(keep, core):
        each = keep.shape[1] // ys
        return [
            y_move(
                (keep[:, (k - 1) * each : k * each] + core[:, (k - 1) * each : k * each]).astype(BF), k
            )
            for k in range(1, ys)
        ]

    starts = [sum(sizes[:i]) for i in range(len(sizes))]
    inners = [s // owners for s in starts]
    xs = [jnp.take(tokens, ids, axis=0) for ids in row_ids]
    kept = [None] * len(sizes)
    cores = [None] * len(sizes)
    gots = [None] * len(sizes)

    kept[0], cores[0] = transform(0, xs[0])
    packed, code = pack(
        scal, after(tokens, kept[0]), slot_rows[None, :], slot_rows[:, None], table, owners, per_owner, kinds
    )
    gots[0] = exchange(kept[0], cores[0])
    features = reduce_homes(packed.reshape(owners, CAP, -1), 0)
    code_q = jnp.sum(
        jnp.where(row_of[:, None] == jnp.arange(rows, dtype=jnp.int32)[None, :], code, 0), axis=1
    )
    slot_q = code_q // CAP
    pieces = tuple(
        (home, inner, size // owners, start + home * (size // owners))
        for size, start, inner in zip(sizes, starts, inners)
        for home in range(owners)
    )
    slot_home = jnp.concatenate([slot_q[s + size - size // owners : s + size] for s, size in zip(starts, sizes)])
    hot_home = slot_home[:, None] == jnp.arange(slots, dtype=jnp.int32)[None, :]
    where = jnp.sum(
        jnp.where(hot_home[:, :, None], (by_owner[:, :kinds] % col_tiles)[None], 0), axis=1
    )
    ss_q = slot_q[:, None]

    for i in range(1, len(sizes)):
        kept[i], cores[i] = transform(i, after(xs[i], kept[i - 1], packed))
        if i == 1:
            spread = product(
                scal, after(features, kept[1]), gate_tiles, up_tiles, code_q[None, :], owners, per_owner, pieces
            )
            home_delta = reduce_homes(spread, 0)
        gots[i] = exchange(kept[i], cores[i])

    result = []
    for i, size in enumerate(sizes):
        keep = kept[i]
        got = gots[i][0]
        if ys > 2:
            got = sum(g.astype(F32) for g in gots[i])
        hid = activate(keep, cores[i], got, home_delta, where, per_slot, inners[i])
        chip = jnp.concatenate([y_move(hid, -k) for k in range(1, ys)] + [hid])
        out = down(down_scal, core_swap(chip), chip, down_weight, all_tiles, ss_q, width_tiles, starts[i])
        blocks = out.reshape(owners, shift, size // (owners * shift), shard_width).transpose(1, 0, 2, 3)
        total = lax.dynamic_index_in_dim(blocks, here_t, 0, keepdims=False)
        for k in range(1, shift):
            gone = lax.dynamic_index_in_dim(blocks, (here_t + k) % shift, 0, keepdims=False).astype(BF)
            total = total + lax.ppermute(
                gone, "tensor", [(i, (i + k) % shift) for i in range(shift)]
            ).astype(F32)
        result.append(total.astype(BF))

    placed = [jnp.take(r, at_home, axis=0).reshape(-1, shard_width) for r in result]
    return jnp.concatenate(placed, axis=0)


def solution(mesh):
    return jax.shard_map(
        shards,
        mesh=mesh,
        in_specs=(
            P("groups", "delta"),
            P("delta", "tensor"),
            P("delta", "tensor"),
            P("tensor", "delta"),
            P("delta", "tensor", None, None),
            P("delta", "tensor", None, None),
            P("delta", "tensor", None, None),
            P("delta", "tensor"),
            P("delta", "tensor"),
            P("delta", "tensor"),
            P("groups"),
            P("groups"),
        ),
        out_specs=P(("groups", "tensor"), "delta"),
        check_vma=False,
    )
```

time: 286 us -> 262 us (0.916)
  waiting for transfers between devices: 33.8 us -> 69.4 us
  Pallas kernels: 141 us -> 112 us
  starting transfers between devices: 41.7 us -> 28 us
  local copies, waits for them, and re-layouts: 34.7 us -> 24.6 us
  other arithmetic: 33.1 us -> 25.7 us
    ppermute x12 -> x9, waiting for transfers between devices: 6.95 us -> 32 us  [shards(): lax.ppermute(gone, 'tensor', [(i, (i + k) % shift) for i in range(shift)])]
    ppermute x1, waiting for transfers between devices: 0.01 us -> 15.9 us  [shards(): other = lax.ppermute(gathered, 'groups', [(0, 1), (1, 0)])]
    slice x20 -> x2, local copies, waits for them, and re-layouts: 15.9 us -> 0.14 us  [shards(): slot_q[s + size - size // owners:s + size]]
    ppermute x12 -> x9, starting transfers between devices: 23.1 us -> 10 us  [shards(): lax.ppermute(gone, 'tensor', [(i, (i + k) % shift) for i in range(shift)])]
    pallas_call x4 -> x3, Pallas kernels: 54.6 us -> 42.9 us  [down(): pl.pallas_call(functools.partial(down_body, width_tiles, width // 256, co...]
    pallas_call x4 -> x3, Pallas kernels: 56.8 us -> 45.5 us  [gate_up(): pl.pallas_call(gate_up_body, grid=(width // block,), in_specs=[whole(x.sh...]
    add x4 -> x0, other arithmetic: 9.03 us -> none  [shards(): summed = keep + core_swap(send)]
    pallas_call x5 -> x4, Pallas kernels: 24.7 us -> 19.2 us  [the longest x3 12.2 us: activate(): pl.pallas_call(functools.partial(activate_body, per_slot, start, each), g...]
  transfers between devices with their start and end apart: 38 -> 31, of which waited for: 8 -> 9; matrix products, arithmetic and copies ran while one was open for 21% -> 16% of each run, Pallas kernels for 45% -> 37%
where the time goes in v2:
time: 262 us; the launch traced here: 261 us
  Pallas kernels  112 us (43%)
  waiting for transfers between devices  69.4 us (26%)
  starting transfers between devices  28 us (11%)
  other arithmetic  25.7 us (10%)
  local copies, waits for them, and re-layouts  24.6 us (9%)
    pallas_call x3, Pallas kernels, gate_up(): pl.pallas_call(gate_up_body, grid=(width // block,), in_specs=[whole(x.sh...  45.5 us
    pallas_call x3, Pallas kernels, down(): pl.pallas_call(functools.partial(down_body, width_tiles, width // 256, co...  42.9 us
    ppermute x9, waiting for transfers between devices, shards(): lax.ppermute(gone, 'tensor', [(i, (i + k) % shift) for i in range(shift)])  32 us
    ppermute x9, waiting for transfers between devices, y_move(): lax.ppermute(x, 'delta', [(i, (i + 2 * k) % owners) for i in range(owners)])  21.5 us
    ppermute x1, waiting for transfers between devices, shards(): other = lax.ppermute(gathered, 'groups', [(0, 1), (1, 0)])  15.9 us
    pallas_call x3, Pallas kernels, activate(): pl.pallas_call(functools.partial(activate_body, per_slot, start, each), g...  12.2 us
    ppermute x9, starting transfers between devices, y_move(): lax.ppermute(x, 'delta', [(i, (i + 2 * k) % owners) for i in range(owners)])  10.9 us
    ppermute x9, starting transfers between devices, shards(): lax.ppermute(gone, 'tensor', [(i, (i + k) % shift) for i in range(shift)])  10 us
  transfers between devices with their start and end apart: 31, of which 9 were waited for; matrix products, arithmetic and copies ran while one was open for 16% of the time, Pallas kernels for 37%

profile of v2, /device:TPU:0, one launch (start us, length us, event | category | flops | bytes accessed | tf_op | source)
XLA Modules:
  0.0 260.5 jit_solution(17986282987775491335)
XLA Ops:
  0.0 0.8 pad_add_fusion.1
  1.3 2.6 collective-permute-start.1
  3.9 1.4 collective-permute-start
  5.8 3.3 %gather_fusion.2 = bf16[128,2048]{1,0:T(8,128)(2,1)S(1)} fusion(bf16[512,2048]{1,0:T(8,128)(2,1)} %x.2, s32[1024]{0:T(1024)S(1)} %pad_clamp_fusion.4), kind=kCustom, calls=%fused_computation.clone | custom fusion | bytes 1049088 | tf_op jit(solution)/shard_map/jit(_take)/gather | solution.py:365
  9.2 0.9 broadcast_select_fusion.2.x
  10.1 14.2 %shard_map.118 = (f32[2,64,4096]{2,1,0:T(8,128)}, f32[2,64,4096]{2,1,0:T(8,128)}) custom-call(bf16[128,2048]{1,0:T(8,128)(2,1)} %broadcast_select_fusion.2.x, bf16[2048,4096]{1,0:T(8,128)(2,1)} %wg.5, bf16[2048,4096]{1,0:T(8,128)(2,1)} %wu.5), custom_call_target="tpu_custom_call" | custom-call | flops 4294967296 | bytes 33554432 | tf_op jit(solution)/shard_map/pallas_call | solution.py:129
  24.3 0.9 constant_dynamic-slice_fusion
  26.2 0.8 fusion.36
  28.2 0.9 copy.44.ss
  29.1 1.4 gather_fusion
  30.5 1.7 gather_fusion.4
  32.5 1.2 broadcast_select_fusion.x
  33.6 0.9 broadcast_select_fusion.1.x
  35.6 7.0 %shard_map.119 = (bf16[512,1024]{1,0:T(8,128)(2,1)}, s32[1,512]{1,0:T(1,128)}) custom-call(s32[5]{0:T(128)} %concatenate.59.scal, bf16[512,2048]{1,0:T(8,128)(2,1)} %x.2, s32[1,512]{1,0:T(1,128)} %bitcast.159, s32[512,1]{1,0:T(8,128)} %copy.44.ss, bf16[128,128]{1,0:T(8,128)(2,1)} %pad.4.table), custom_call_target="tpu_custom_call" | custom-call | flops 4000000000 | bytes 4000000 | tf_op jit(solution)/shard_map/pallas_call | solution.py:56
  42.5 1.3 fusion.34
  44.0 17.1 %shard_map.120 = (f32[2,128,4096]{2,1,0:T(8,128)}, f32[2,128,4096]{2,1,0:T(8,128)}) custom-call(bf16[256,2048]{1,0:T(8,128)(2,1)} %broadcast_select_fusion.x, bf16[2048,4096]{1,0:T(8,128)(2,1)} %wg.5, bf16[2048,4096]{1,0:T(8,128)(2,1)} %wu.5), custom_call_target="tpu_custom_call" | custom-call | flops 8589934592 | bytes 33554432 | tf_op jit(solution)/shard_map/pallas_call | solution.py:129
  61.2 14.2 %shard_map.126 = (f32[2,64,4096]{2,1,0:T(8,128)}, f32[2,64,4096]{2,1,0:T(8,128)}) custom-call(bf16[128,2048]{1,0:T(8,128)(2,1)} %broadcast_select_fusion.1.x, bf16[2048,4096]{1,0:T(8,128)(2,1)} %wg.5, bf16[2048,4096]{1,0:T(8,128)(2,1)} %wu.5), custom_call_target="tpu_custom_call" | custom-call | flops 4294967296 | bytes 33554432 | tf_op jit(solution)/shard_map/pallas_call | solution.py:129
  76.3 1.7 collective-permute-start.6
  78.3 6.5 %collective-permute-done.6 = bf16[128,1024]{1,0:T(8,128)(2,1)S(1)} collective-permute-done((bf16[128,1024]{1,0:T(8,128)(2,1)S(1)}, bf16[128,1024]{1,0:T(8,128)(2,1)S(1)}, u32[]{:S(2)}, u32[]{:S(2)}) %collective-permute-start.6) | collective-permute-done | bytes 262176 | tf_op jit(solution)/shard_map/ppermute | solution.py:274
  85.5 4.6 %shard_map.121 = bf16[4,128,1024]{2,1,0:T(8,128)(2,1)} custom-call(s32[5]{0:T(128)} %concatenate.59.scal, bf16[128,1024]{1,0:T(8,128)(2,1)} %fusion.11.x, bf16[4,2,256,256]{3,2,1,0:T(8,128)(2,1)} %gt.1, bf16[4,2,256,256]{3,2,1,0:T(8,128)(2,1)} %ut.1, s32[1,512]{1,0:T(1,128)} %bitcast.156), custom_call_target="tpu_custom_call" | custom-call | flops 4000000000 | bytes 4000000 | tf_op jit(solution)/shard_map/pallas_call | solution.py:101
  90.1 1.9 slice.103
  93.2 0.8 copy.47
  94.0 0.9 add_select_fusion.slot
  94.9 1.5 fusion.32
  96.4 1.7 collective-permute-start.12
  98.1 1.3 slice_add_fusion.3
  99.4 1.4 fusion.2
  100.8 1.6 collective-permute-start.4
  102.4 1.0 fusion.1
  103.9 1.6 collective-permute-start.8
  106.1 15.9 %collective-permute-done.12 = bf16[2,2,2,256,256]{4,3,2,1,0:T(8,128)(2,1)S(1)} collective-permute-done((bf16[2,2,2,256,256]{4,3,2,1,0:T(8,128)(2,1)S(1)}, bf16[2,2,2,256,256]{4,3,2,1,0:T(8,128)(2,1)S(1)}, u32[]{:S(2)}, u32[]{:S(2)}) %collective-permute-start.12) | collective-permute-done | bytes 1048608 | tf_op jit(solution)/shard_map/ppermute | solution.py:326
  122.0 1.6 pad_maximum_fusion.1
  123.6 8.1 %collective-permute-done.8 = bf16[128,1024]{1,0:T(8,128)(2,1)S(1)} collective-permute-done((bf16[128,1024]{1,0:T(8,128)(2,1)S(1)}, bf16[128,1024]{1,0:T(8,128)(2,1)S(1)}, u32[]{:S(2)}, u32[]{:S(2)}) %collective-permute-start.8) | collective-permute-done | bytes 262176 | tf_op jit(solution)/shard_map/ppermute | solution.py:274
  132.5 3.9 %shard_map.122 = bf16[32,4096]{1,0:T(8,128)(2,1)} custom-call(f32[2,64,4096]{2,1,0:T(8,128)} %get-tuple-element.19.keep, f32[2,64,4096]{2,1,0:T(8,128)} %collective-permute-done.3.core, bf16[2,32,4096]{2,1,0:T(8,128)(2,1)} %collective-permute-done.4.got, bf16[128,1024]{1,0:T(8,128)(2,1)} %fusion.10.delta, s32[128,4]{1,0:T(8,128)} %copy.46.where), custom_call_target="tpu_custom_call" | custom-call | flops 2621440 | bytes 3145728 | tf_op jit(solution)/shard_map/pallas_call | solution.py:165
  136.3 1.5 collective-permute-start.9
  137.9 3.8 %shard_map.127 = bf16[32,4096]{1,0:T(8,128)(2,1)} custom-call(f32[2,64,4096]{2,1,0:T(8,128)} %get-tuple-element.29.keep, f32[2,64,4096]{2,1,0:T(8,128)} %copy-done.6, bf16[2,32,4096]{2,1,0:T(8,128)(2,1)} %collective-permute-done.25.got, bf16[128,1024]{1,0:T(8,128)(2,1)} %fusion.10.delta, s32[128,4]{1,0:T(8,128)} %copy.46.where), custom_call_target="tpu_custom_call" | custom-call | flops 2621440 | bytes 3145728 | tf_op jit(solution)/shard_map/pallas_call | solution.py:165
  141.7 0.8 collective-permute-start.26
  142.5 2.8 %fusion = bf16[2,64,4096]{2,1,0:T(8,128)(2,1)} fusion(f32[2,128,4096]{2,1,0:T(8,128)} %collective-permute-done.17.core, f32[2,128,4096]{2,1,0:T(8,128)S(1)} %copy-done.3), kind=kLoop, calls=%fused_computation.8 | loop fusion | flops 1048576 | bytes 5242880 | tf_op jit(solution)/shard_map/convert_element_type | solution.py:358
  145.3 1.3 collective-permute-start.18
  146.7 4.5 %collective-permute-done.26 = bf16[32,4096]{1,0:T(8,128)(2,1)S(1)} collective-permute-done((bf16[32,4096]{1,0:T(8,128)(2,1)}, bf16[32,4096]{1,0:T(8,128)(2,1)S(1)}, u32[]{:S(2)}, u32[]{:S(2)}) %collective-permute-start.26) | collective-permute-done | bytes 262176 | tf_op jit(solution)/shard_map/ppermute | solution.py:274
  151.4 4.1 %pad_maximum_fusion = bf16[2,2,2,2,2,256,256]{6,5,4,3,2,1,0:T(8,128)(2,1)} fusion(bf16[1,2,2,2,2,256,256]{6,5,4,3,2,1,0:T(8,128)(2,1)S(1)} %get-tuple-element.41, bf16[1,2,2,2,2,256,256]{6,5,4,3,2,1,0:T(8,128)(2,1)} %bitcast.45), kind=kLoop, calls=%fused_computation.6 | loop fusion | flops 2097152 | bytes 8388608 | tf_op jit(solution)/shard_map/stack | solution.py:333
  155.5 0.8 copy-done.18
  156.3 13.5 %shard_map.123 = f32[128,2048]{1,0:T(8,128)} custom-call(s32[65]{0:T(128)} %pad_add_fusion.3.scal, bf16[64,4096]{1,0:T(8,128)(2,1)} %copy-done.18, bf16[64,4096]{1,0:T(8,128)(2,1)} %copy-done.11, bf16[4096,2048]{1,0:T(8,128)(2,1)} %w.5, bf16[32,256,256]{2,1,0:T(8,128)(2,1)} %bitcast.141, s32[512,1]{1,0:T(8,128)} %add_select_fusion.slot), custom_call_target="tpu_custom_call" | custom-call | flops 3221225472 | bytes 25165824 | tf_op jit(solution)/shard_map/pallas_call | solution.py:219
  169.8 2.4 collective-permute-done.18.got
  172.3 1.0 copy-done.14
  173.2 4.5 %shard_map.124 = bf16[64,4096]{1,0:T(8,128)(2,1)} custom-call(f32[2,128,4096]{2,1,0:T(8,128)} %get-tuple-element.24.keep, f32[2,128,4096]{2,1,0:T(8,128)} %collective-permute-done.17.core, bf16[2,64,4096]{2,1,0:T(8,128)(2,1)} %copy-done.14, bf16[128,1024]{1,0:T(8,128)(2,1)} %fusion.10.delta, s32[128,4]{1,0:T(8,128)} %copy.46.where), custom_call_target="tpu_custom_call" | custom-call | flops 5242880 | bytes 6291456 | tf_op jit(solution)/shard_map/pallas_call | solution.py:165
  177.8 1.5 collective-permute-start.19
  179.4 3.7 %collective-permute-start.16 = (bf16[4,8,2048]{2,1,0:T(8,128)(2,1)S(1)}, bf16[4,8,2048]{2,1,0:T(8,128)(2,1)S(1)}, u32[]{:S(2)}, u32[]{:S(2)}) collective-permute-start(bf16[4,8,2048]{2,1,0:T(8,128)(2,1)S(1)} %get-tuple-element.43), channel_id=1, source_target_pairs={{0,3},{1,0},{2,1},{3,2},{4,7},{5,4},{6,5},{7,6},{8,11},{9,8},{10,9... | collective-permute-start | bytes 393224 | tf_op jit(solution)/shard_map/ppermute | solution.py:414
  183.0 1.0 collective-permute-start.14
  184.0 0.8 copy-done.17
  184.8 13.5 %shard_map.128 = f32[128,2048]{1,0:T(8,128)} custom-call(s32[65]{0:T(128)} %pad_add_fusion.3.scal, bf16[64,4096]{1,0:T(8,128)(2,1)} %copy-done.17, bf16[64,4096]{1,0:T(8,128)(2,1)} %copy-done.10, bf16[4096,2048]{1,0:T(8,128)(2,1)} %w.5, bf16[32,256,256]{2,1,0:T(8,128)(2,1)} %bitcast.142, s32[512,1]{1,0:T(8,128)} %add_select_fusion.slot), custom_call_target="tpu_custom_call" | custom-call | flops 3221225472 | bytes 25165824 | tf_op jit(solution)/shard_map/pallas_call | solution.py:219
  198.5 1.4 copy-done.9
  200.7 2.2 collective-permute-start.30
  202.9 1.1 collective-permute-start.29
  204.7 2.5 collective-permute-done.30
  207.1 8.1 %collective-permute-done.29 = bf16[4,8,2048]{2,1,0:T(8,128)(2,1)} collective-permute-done((bf16[4,8,2048]{2,1,0:T(8,128)(2,1)}, bf16[4,8,2048]{2,1,0:T(8,128)(2,1)}, u32[]{:S(2)}, u32[]{:S(2)}) %collective-permute-start.29) | collective-permute-done | bytes 131104 | tf_op jit(solution)/shard_map/ppermute | solution.py:414
  215.2 1.0 fusion.14
  216.8 15.9 %shard_map.125 = f32[256,2048]{1,0:T(8,128)} custom-call(s32[65]{0:T(128)} %pad_add_fusion.3.scal, bf16[128,4096]{1,0:T(8,128)(2,1)} %collective-permute-done.20.far, bf16[128,4096]{1,0:T(8,128)(2,1)} %copy-done.7, bf16[4096,2048]{1,0:T(8,128)(2,1)} %w.5, bf16[32,256,256]{2,1,0:T(8,128)(2,1)} %bitcast.143, s32[512,1]{1,0:T(8,128)} %add_select_fusion.slot), custom_call_target="tpu_custom_call" | custom-call | flops 6442450944 | bytes 25165824 | tf_op jit(solution)/shard_map/pallas_call | solution.py:219
  232.8 1.5 fusion.8
  234.4 1.9 collective-permute-start.21
  236.4 4.7 %collective-permute-done.23 = bf16[4,16,2048]{2,1,0:T(8,128)(2,1)S(1)} collective-permute-done((bf16[4,16,2048]{2,1,0:T(8,128)(2,1)S(1)}, bf16[4,16,2048]{2,1,0:T(8,128)(2,1)S(1)}, u32[]{:S(2)}, u32[]{:S(2)}) %collective-permute-start.23) | collective-permute-done | bytes 262176 | tf_op jit(solution)/shard_map/ppermute | solution.py:414
  241.1 16.8 %collective-permute-done.22 = bf16[4,16,2048]{2,1,0:T(8,128)(2,1)S(1)} collective-permute-done((bf16[4,16,2048]{2,1,0:T(8,128)(2,1)S(1)}, bf16[4,16,2048]{2,1,0:T(8,128)(2,1)S(1)}, u32[]{:S(2)}, u32[]{:S(2)}) %collective-permute-start.22) | collective-permute-done | bytes 262176 | tf_op jit(solution)/shard_map/ppermute | solution.py:414
  257.9 1.2 fusion.5
  259.7 0.8 pad_maximum_fusion.6
  (158 shorter events, 13.0 us)
Async XLA Ops:
  0.0 24.3 %copy-start = (bf16[4,2,256,256]{3,2,1,0:T(8,128)(2,1)S(1)}, bf16[4,2,256,256]{3,2,1,0:T(8,128)(2,1)}, u32[]{:S(2)}) copy-start(bf16[4,2,256,256]{3,2,1,0:T(8,128)(2,1)} %param.22) | copy-start | bytes 3145732
  0.8 33.7 %collective-permute-start.2 = (s32[4,6]{0,1:T(8,128)S(1)}, s32[4,6]{0,1:T(8,128)S(1)}, u32[]{:S(2)}, u32[]{:S(2)}) collective-permute-start(s32[4,6]{0,1:T(8,128)S(1)} %pad_add_fusion.1), channel_id=1, source_target_pairs={{0,4},{4,8},{8,12},{12,0},{1,5},{5,9},{9,13},{13,1},{2,6},{6,10},{... | collective-permute-start | bytes 296 | tf_op jit(solution)/shard_map/ppermute | solution.py:305
  1.3 33.3 %collective-permute-start.1 = (s32[4,6]{0,1:T(8,128)S(1)}, s32[4,6]{0,1:T(8,128)S(1)}, u32[]{:S(2)}, u32[]{:S(2)}) collective-permute-start(s32[4,6]{0,1:T(8,128)S(1)} %pad_add_fusion.1), channel_id=1, source_target_pairs={{0,8},{4,12},{8,0},{12,4},{1,9},{5,13},{9,1},{13,5},{2,10},{6,14},... | collective-permute-start | bytes 296 | tf_op jit(solution)/shard_map/ppermute | solution.py:305
  3.9 30.8 %collective-permute-start = (s32[4,6]{0,1:T(8,128)S(1)}, s32[4,6]{0,1:T(8,128)S(1)}, u32[]{:S(2)}, u32[]{:S(2)}) collective-permute-start(s32[4,6]{0,1:T(8,128)S(1)} %pad_add_fusion.1), channel_id=1, source_target_pairs={{0,12},{4,0},{8,4},{12,8},{1,13},{5,1},{9,5},{13,9},{2,14},{6,2},{... | collective-permute-start | bytes 296 | tf_op jit(solution)/shard_map/ppermute | solution.py:305
  24.2 3.9 %copy-start.22 = (s32[512]{0:T(512)S(1)}, s32[512]{0:T(512)}, u32[]{:S(2)}) copy-start(s32[512]{0:T(512)} %param.26) | copy-start | bytes 6148
  24.2 3.9 %copy-start.23 = (s32[16]{0:T(128)S(1)}, s32[16]{0:T(128)}, u32[]{:S(2)}) copy-start(s32[16]{0:T(128)} %param.27) | copy-start | bytes 196
  24.2 4.9 %copy-start.2 = (bf16[512,2048]{1,0:T(8,128)(2,1)S(1)}, bf16[512,2048]{1,0:T(8,128)(2,1)}, u32[]{:S(2)}) copy-start(bf16[512,2048]{1,0:T(8,128)(2,1)} %x.2) | copy-start | bytes 6291460
  24.2 75.1 %collective-permute-start.3 = (f32[2,64,4096]{2,1,0:T(8,128)}, f32[2,64,4096]{2,1,0:T(8,128)}, u32[]{:S(2)}, u32[]{:S(2)}) collective-permute-start(f32[2,64,4096]{2,1,0:T(8,128)} %get-tuple-element.20), channel_id=1, source_target_pairs={{0,4},{4,0},{8,12},{12,8},{1,5},{5,1},{9,13},{13,9},{2,6},{6,2},{1... | collective-permute-start | bytes 6291464 | tf_op jit(solution)/shard_map/ppermute | solution.py:271
  25.2 69.6 %collective-permute-start.11 = (bf16[2,2,256,256]{3,2,1,0:T(8,128)(2,1)}, bf16[2,2,256,256]{3,2,1,0:T(8,128)(2,1)}, u32[]{:S(2)}, u32[]{:S(2)}) collective-permute-start(bf16[2,2,256,256]{3,2,1,0:T(8,128)(2,1)} %constant_dynamic-slice_fusion), channel_id=1, source_target_pairs={{0,8},{4,12},{8,0},{12,4},{1,9},{5,13},{9,1},{13,5},{2,10},{6,14},... | collective-permute-start | bytes 1572872 | tf_op jit(solution)/shard_map/ppermute | solution.py:274
  28.2 2.3 copy-start.20
  32.2 1.4 copy-start.12
  43.8 32.3 %collective-permute-start.5 = (bf16[2,128,1024]{2,1,0:T(8,128)(2,1)S(1)}, bf16[2,128,1024]{2,1,0:T(8,128)(2,1)S(1)}, u32[]{:S(2)}, u32[]{:S(2)}) collective-permute-start(bf16[2,128,1024]{2,1,0:T(8,128)(2,1)S(1)} %bitcast.152), channel_id=1, source_target_pairs={{0,4},{4,0},{8,12},{12,8},{1,5},{5,1},{9,13},{13,9},{2,6},{6,2},{1... | collective-permute-start | bytes 1572872 | tf_op jit(solution)/shard_map/ppermute | solution.py:271
  61.2 14.2 %copy-start.21 = (s32[1,512]{1,0:T(1,128)S(1)}, s32[1,512]{1,0:T(1,128)}, u32[]{:S(2)}) copy-start(s32[1,512]{1,0:T(1,128)} %get-tuple-element.26) | copy-start | bytes 6148
  75.6 9.9 %copy-start.19 = (s32[512]{0:T(512)}, s32[512]{0:T(512)S(1)}, u32[]{:S(2)}) copy-start(s32[512]{0:T(512)S(1)} %select_reduce_fusion) | copy-start | bytes 6148
  75.8 66.8 %collective-permute-start.17 = (f32[2,128,4096]{2,1,0:T(8,128)}, f32[2,128,4096]{2,1,0:T(8,128)}, u32[]{:S(2)}, u32[]{:S(2)}) collective-permute-start(f32[2,128,4096]{2,1,0:T(8,128)} %get-tuple-element.27), channel_id=1, source_target_pairs={{0,4},{4,0},{8,12},{12,8},{1,5},{5,1},{9,13},{13,9},{2,6},{6,2},{1... | collective-permute-start | bytes 12582920 | tf_op jit(solution)/shard_map/ppermute | solution.py:271
  76.3 8.4 %collective-permute-start.6 = (bf16[128,1024]{1,0:T(8,128)(2,1)S(1)}, bf16[128,1024]{1,0:T(8,128)(2,1)S(1)}, u32[]{:S(2)}, u32[]{:S(2)}) collective-permute-start(bf16[128,1024]{1,0:T(8,128)(2,1)S(1)} %slice_bitcast_fusion.2), channel_id=1, source_target_pairs={{0,8},{4,12},{8,0},{12,4},{1,9},{5,13},{9,1},{13,5},{2,10},{6,14},... | collective-permute-start | bytes 786440 | tf_op jit(solution)/shard_map/ppermute | solution.py:274
  78.3 24.0 %collective-permute-start.24 = (f32[2,64,4096]{2,1,0:T(8,128)}, f32[2,64,4096]{2,1,0:T(8,128)S(1)}, u32[]{:S(2)}, u32[]{:S(2)}) collective-permute-start(f32[2,64,4096]{2,1,0:T(8,128)} %get-tuple-element.30), channel_id=1, source_target_pairs={{0,4},{4,0},{8,12},{12,8},{1,5},{5,1},{9,13},{13,9},{2,6},{6,2},{1... | collective-permute-start | bytes 6291464 | tf_op jit(solution)/shard_map/ppermute | solution.py:271
  92.0 6.1 %collective-permute-start.7 = (bf16[2,128,1024]{2,1,0:T(8,128)(2,1)}, bf16[2,128,1024]{2,1,0:T(8,128)(2,1)}, u32[]{:S(2)}, u32[]{:S(2)}) collective-permute-start(bf16[2,128,1024]{2,1,0:T(8,128)(2,1)} %slice.103), channel_id=1, source_target_pairs={{0,4},{4,0},{8,12},{12,8},{1,5},{5,1},{9,13},{13,9},{2,6},{6,2},{1... | collective-permute-start | bytes 1572872 | tf_op jit(solution)/shard_map/ppermute | solution.py:271
  94.9 4.5 %copy-start.4 = (f32[2,64,4096]{2,1,0:T(8,128)S(1)}, f32[2,64,4096]{2,1,0:T(8,128)}, u32[]{:S(2)}) copy-start(f32[2,64,4096]{2,1,0:T(8,128)} %get-tuple-element.19.keep) | copy-start | bytes 6291460
  96.4 6.0 %copy-start.5 = (f32[2,64,4096]{2,1,0:T(8,128)S(1)}, f32[2,64,4096]{2,1,0:T(8,128)}, u32[]{:S(2)}) copy-start(f32[2,64,4096]{2,1,0:T(8,128)} %get-tuple-element.29.keep) | copy-start | bytes 6291460
  96.4 25.6 %collective-permute-start.12 = (bf16[2,2,2,256,256]{4,3,2,1,0:T(8,128)(2,1)S(1)}, bf16[2,2,2,256,256]{4,3,2,1,0:T(8,128)(2,1)S(1)}, u32[]{:S(2)}, u32[]{:S(2)}) collective-permute-start(bf16[2,2,2,256,256]{4,3,2,1,0:T(8,128)(2,1)S(1)} %get-tuple-element.49), channel_id=1, source_target_pairs={{0,16},{16,0},{1,17},{17,1},{2,18},{18,2},{3,19},{19,3},{4,20},{20... | collective-permute-start | bytes 3145736 | tf_op jit(solution)/shard_map/ppermute | solution.py:326
  100.8 31.7 %collective-permute-start.4 = (bf16[2,32,4096]{2,1,0:T(8,128)(2,1)S(1)}, bf16[2,32,4096]{2,1,0:T(8,128)(2,1)}, u32[]{:S(2)}, u32[]{:S(2)}) collective-permute-start(bf16[2,32,4096]{2,1,0:T(8,128)(2,1)S(1)} %fusion.2), channel_id=1, source_target_pairs={{0,8},{4,12},{8,0},{12,4},{1,9},{5,13},{9,1},{13,5},{2,10},{6,14},... | collective-permute-start | bytes 1572872 | tf_op jit(solution)/shard_map/ppermute | solution.py:274
  102.4 19.6 %copy-start.6 = (f32[2,64,4096]{2,1,0:T(8,128)}, f32[2,64,4096]{2,1,0:T(8,128)S(1)}, u32[]{:S(2)}) copy-start(f32[2,64,4096]{2,1,0:T(8,128)S(1)} %collective-permute-done.24.core) | copy-start | bytes 6291460
  103.4 34.5 %collective-permute-start.25 = (bf16[2,32,4096]{2,1,0:T(8,128)(2,1)}, bf16[2,32,4096]{2,1,0:T(8,128)(2,1)}, u32[]{:S(2)}, u32[]{:S(2)}) collective-permute-start(bf16[2,32,4096]{2,1,0:T(8,128)(2,1)} %fusion.1), channel_id=1, source_target_pairs={{0,8},{4,12},{8,0},{12,4},{1,9},{5,13},{9,1},{13,5},{2,10},{6,14},... | collective-permute-start | bytes 1572872 | tf_op jit(solution)/shard_map/ppermute | solution.py:274
  103.9 27.8 %collective-permute-start.8 = (bf16[128,1024]{1,0:T(8,128)(2,1)S(1)}, bf16[128,1024]{1,0:T(8,128)(2,1)S(1)}, u32[]{:S(2)}, u32[]{:S(2)}) collective-permute-start(bf16[128,1024]{1,0:T(8,128)(2,1)S(1)} %slice_bitcast_fusion), channel_id=1, source_target_pairs={{0,8},{4,12},{8,0},{12,4},{1,9},{5,13},{9,1},{13,5},{2,10},{6,14},... | collective-permute-start | bytes 786440 | tf_op jit(solution)/shard_map/ppermute | solution.py:274
  123.6 27.7 %collective-permute-start.13 = (bf16[2,2,2,2,256,256]{5,4,3,2,1,0:T(8,128)(2,1)}, bf16[2,2,2,2,256,256]{5,4,3,2,1,0:T(8,128)(2,1)}, u32[]{:S(2)}, u32[]{:S(2)}) collective-permute-start(bf16[2,2,2,2,256,256]{5,4,3,2,1,0:T(8,128)(2,1)} %get-tuple-element.40), channel_id=1, source_target_pairs={{0,4},{4,0},{8,12},{12,8},{1,5},{5,1},{9,13},{13,9},{2,6},{6,2},{1... | collective-permute-start | bytes 6291464 | tf_op jit(solution)/shard_map/ppermute | solution.py:271
  136.3 6.2 %copy-start.3 = (f32[2,128,4096]{2,1,0:T(8,128)S(1)}, f32[2,128,4096]{2,1,0:T(8,128)}, u32[]{:S(2)}) copy-start(f32[2,128,4096]{2,1,0:T(8,128)} %get-tuple-element.24.keep) | copy-start | bytes 12582916
  136.3 10.3 %collective-permute-start.9 = (bf16[32,4096]{1,0:T(8,128)(2,1)}, bf16[32,4096]{1,0:T(8,128)(2,1)S(1)}, u32[]{:S(2)}, u32[]{:S(2)}) collective-permute-start(bf16[32,4096]{1,0:T(8,128)(2,1)} %shard_map.122), channel_id=1, source_target_pairs={{0,8},{4,12},{8,0},{12,4},{1,9},{5,13},{9,1},{13,5},{2,10},{6,14},... | collective-permute-start | bytes 786440 | tf_op jit(solution)/shard_map/ppermute | solution.py:274
  141.7 4.9 %copy-start.15 = (bf16[32,4096]{1,0:T(8,128)(2,1)S(1)}, bf16[32,4096]{1,0:T(8,128)(2,1)}, u32[]{:S(2)}) copy-start(bf16[32,4096]{1,0:T(8,128)(2,1)} %shard_map.122) | copy-start | bytes 786436
  141.7 9.5 %copy-start.16 = (bf16[32,4096]{1,0:T(8,128)(2,1)S(1)}, bf16[32,4096]{1,0:T(8,128)(2,1)}, u32[]{:S(2)}) copy-start(bf16[32,4096]{1,0:T(8,128)(2,1)} %shard_map.127) | copy-start | bytes 786436
  141.7 9.5 %collective-permute-start.26 = (bf16[32,4096]{1,0:T(8,128)(2,1)}, bf16[32,4096]{1,0:T(8,128)(2,1)S(1)}, u32[]{:S(2)}, u32[]{:S(2)}) collective-permute-start(bf16[32,4096]{1,0:T(8,128)(2,1)} %shard_map.127), channel_id=1, source_target_pairs={{0,8},{4,12},{8,0},{12,4},{1,9},{5,13},{9,1},{13,5},{2,10},{6,14},... | collective-permute-start | bytes 786440 | tf_op jit(solution)/shard_map/ppermute | solution.py:274
  145.3 26.9 %collective-permute-start.18 = (bf16[2,64,4096]{2,1,0:T(8,128)(2,1)}, bf16[2,64,4096]{2,1,0:T(8,128)(2,1)S(1)}, u32[]{:S(2)}, u32[]{:S(2)}) collective-permute-start(bf16[2,64,4096]{2,1,0:T(8,128)(2,1)} %fusion), channel_id=1, source_target_pairs={{0,8},{4,12},{8,0},{12,4},{1,9},{5,13},{9,1},{13,5},{2,10},{6,14},... | collective-permute-start | bytes 3145736 | tf_op jit(solution)/shard_map/ppermute | solution.py:274
  146.6 8.9 %copy-start.11 = (bf16[64,4096]{1,0:T(8,128)(2,1)}, bf16[64,4096]{1,0:T(8,128)(2,1)S(1)}, u32[]{:S(2)}) copy-start(bf16[64,4096]{1,0:T(8,128)(2,1)S(1)} %pad_maximum_fusion.4.near) | copy-start | bytes 1572868
  146.7 8.9 %collective-permute-start.10 = (bf16[64,4096]{1,0:T(8,128)(2,1)S(1)}, bf16[64,4096]{1,0:T(8,128)(2,1)S(1)}, u32[]{:S(2)}, u32[]{:S(2)}) collective-permute-start(bf16[64,4096]{1,0:T(8,128)(2,1)S(1)} %pad_maximum_fusion.4.near), channel_id=1, source_target_pairs={{0,4},{4,0},{8,12},{12,8},{1,5},{5,1},{9,13},{13,9},{2,6},{6,2},{1... | collective-permute-start | bytes 1572872 | tf_op jit(solution)/shard_map/ppermute | solution.py:271
  151.3 4.2 %copy-start.10 = (bf16[64,4096]{1,0:T(8,128)(2,1)}, bf16[64,4096]{1,0:T(8,128)(2,1)S(1)}, u32[]{:S(2)}) copy-start(bf16[64,4096]{1,0:T(8,128)(2,1)S(1)} %pad_maximum_fusion.5.near) | copy-start | bytes 1572868
  151.3 32.7 %collective-permute-start.27 = (bf16[64,4096]{1,0:T(8,128)(2,1)S(1)}, bf16[64,4096]{1,0:T(8,128)(2,1)S(1)}, u32[]{:S(2)}, u32[]{:S(2)}) collective-permute-start(bf16[64,4096]{1,0:T(8,128)(2,1)S(1)} %pad_maximum_fusion.5.near), channel_id=1, source_target_pairs={{0,4},{4,0},{8,12},{12,8},{1,5},{5,1},{9,13},{13,9},{2,6},{6,2},{1... | collective-permute-start | bytes 1572872 | tf_op jit(solution)/shard_map/ppermute | solution.py:271
  155.5 0.8 copy-start.18
  169.8 9.5 %copy-start.8 = (f32[128,2048]{1,0:T(8,128)S(1)}, f32[128,2048]{1,0:T(8,128)}, u32[]{:S(2)}) copy-start(f32[128,2048]{1,0:T(8,128)} %shard_map.123) | copy-start | bytes 3145732
  172.3 1.0 copy-start.14
  177.8 20.6 %collective-permute-start.19 = (bf16[64,4096]{1,0:T(8,128)(2,1)}, bf16[64,4096]{1,0:T(8,128)(2,1)S(1)}, u32[]{:S(2)}, u32[]{:S(2)}) collective-permute-start(bf16[64,4096]{1,0:T(8,128)(2,1)} %shard_map.124), channel_id=1, source_target_pairs={{0,8},{4,12},{8,0},{12,4},{1,9},{5,13},{9,1},{13,5},{2,10},{6,14},... | collective-permute-start | bytes 1572872 | tf_op jit(solution)/shard_map/ppermute | solution.py:274
  179.4 23.5 %collective-permute-start.16 = (bf16[4,8,2048]{2,1,0:T(8,128)(2,1)S(1)}, bf16[4,8,2048]{2,1,0:T(8,128)(2,1)S(1)}, u32[]{:S(2)}, u32[]{:S(2)}) collective-permute-start(bf16[4,8,2048]{2,1,0:T(8,128)(2,1)S(1)} %get-tuple-element.43), channel_id=1, source_target_pairs={{0,3},{1,0},{2,1},{3,2},{4,7},{5,4},{6,5},{7,6},{8,11},{9,8},{10,9... | collective-permute-start | bytes 393224 | tf_op jit(solution)/shard_map/ppermute | solution.py:414
  183.0 21.0 %collective-permute-start.15 = (bf16[4,8,2048]{2,1,0:T(8,128)(2,1)S(1)}, bf16[4,8,2048]{2,1,0:T(8,128)(2,1)S(1)}, u32[]{:S(2)}, u32[]{:S(2)}) collective-permute-start(bf16[4,8,2048]{2,1,0:T(8,128)(2,1)S(1)} %get-tuple-element.44), channel_id=1, source_target_pairs={{0,2},{1,3},{2,0},{3,1},{4,6},{5,7},{6,4},{7,5},{8,10},{9,11},{10,... | collective-permute-start | bytes 393224 | tf_op jit(solution)/shard_map/ppermute | solution.py:414
  183.0 15.3 %copy-start.13 = (bf16[64,4096]{1,0:T(8,128)(2,1)S(1)}, bf16[64,4096]{1,0:T(8,128)(2,1)}, u32[]{:S(2)}) copy-start(bf16[64,4096]{1,0:T(8,128)(2,1)} %shard_map.124) | copy-start | bytes 1572868
  183.0 21.0 %collective-permute-start.14 = (bf16[4,8,2048]{2,1,0:T(8,128)(2,1)S(1)}, bf16[4,8,2048]{2,1,0:T(8,128)(2,1)S(1)}, u32[]{:S(2)}, u32[]{:S(2)}) collective-permute-start(bf16[4,8,2048]{2,1,0:T(8,128)(2,1)S(1)} %get-tuple-element.42), channel_id=1, source_target_pairs={{0,1},{1,2},{2,3},{3,0},{4,5},{5,6},{6,7},{7,4},{8,9},{9,10},{10,1... | collective-permute-start | bytes 393224 | tf_op jit(solution)/shard_map/ppermute | solution.py:414
  184.0 0.8 copy-start.17
  198.3 1.6 copy-start.9
  198.4 18.4 %copy-start.7 = (bf16[128,4096]{1,0:T(8,128)(2,1)}, bf16[128,4096]{1,0:T(8,128)(2,1)S(1)}, u32[]{:S(2)}) copy-start(bf16[128,4096]{1,0:T(8,128)(2,1)S(1)} %pad_maximum_fusion.3.near) | copy-start | bytes 3145732
  198.4 18.4 %collective-permute-start.20 = (bf16[128,4096]{1,0:T(8,128)(2,1)S(1)}, bf16[128,4096]{1,0:T(8,128)(2,1)}, u32[]{:S(2)}, u32[]{:S(2)}) collective-permute-start(bf16[128,4096]{1,0:T(8,128)(2,1)S(1)} %pad_maximum_fusion.3.near), channel_id=1, source_target_pairs={{0,4},{4,0},{8,12},{12,8},{1,5},{5,1},{9,13},{13,9},{2,6},{6,2},{1... | collective-permute-start | bytes 3145736 | tf_op jit(solution)/shard_map/ppermute | solution.py:271
  200.7 6.5 %collective-permute-start.30 = (bf16[4,8,2048]{2,1,0:T(8,128)(2,1)}, bf16[4,8,2048]{2,1,0:T(8,128)(2,1)S(1)}, u32[]{:S(2)}, u32[]{:S(2)}) collective-permute-start(bf16[4,8,2048]{2,1,0:T(8,128)(2,1)} %get-tuple-element.46), channel_id=1, source_target_pairs={{0,3},{1,0},{2,1},{3,2},{4,7},{5,4},{6,5},{7,6},{8,11},{9,8},{10,9... | collective-permute-start | bytes 393224 | tf_op jit(solution)/shard_map/ppermute | solution.py:414
  202.9 12.3 %collective-permute-start.29 = (bf16[4,8,2048]{2,1,0:T(8,128)(2,1)}, bf16[4,8,2048]{2,1,0:T(8,128)(2,1)}, u32[]{:S(2)}, u32[]{:S(2)}) collective-permute-start(bf16[4,8,2048]{2,1,0:T(8,128)(2,1)} %get-tuple-element.47), channel_id=1, source_target_pairs={{0,2},{1,3},{2,0},{3,1},{4,6},{5,7},{6,4},{7,5},{8,10},{9,11},{10,... | collective-permute-start | bytes 393224 | tf_op jit(solution)/shard_map/ppermute | solution.py:414
  204.0 11.2 %collective-permute-start.28 = (bf16[4,8,2048]{2,1,0:T(8,128)(2,1)}, bf16[4,8,2048]{2,1,0:T(8,128)(2,1)}, u32[]{:S(2)}, u32[]{:S(2)}) collective-permute-start(bf16[4,8,2048]{2,1,0:T(8,128)(2,1)} %get-tuple-element.45), channel_id=1, source_target_pairs={{0,1},{1,2},{2,3},{3,0},{4,5},{5,6},{6,7},{7,4},{8,9},{9,10},{10,1... | collective-permute-start | bytes 393224 | tf_op jit(solution)/shard_map/ppermute | solution.py:414
  234.2 6.9 %collective-permute-start.23 = (bf16[4,16,2048]{2,1,0:T(8,128)(2,1)S(1)}, bf16[4,16,2048]{2,1,0:T(8,128)(2,1)S(1)}, u32[]{:S(2)}, u32[]{:S(2)}) collective-permute-start(bf16[4,16,2048]{2,1,0:T(8,128)(2,1)S(1)} %get-tuple-element.38), channel_id=1, source_target_pairs={{0,3},{1,0},{2,1},{3,2},{4,7},{5,4},{6,5},{7,6},{8,11},{9,8},{10,9... | collective-permute-start | bytes 786440 | tf_op jit(solution)/shard_map/ppermute | solution.py:414
  234.3 23.6 %collective-permute-start.22 = (bf16[4,16,2048]{2,1,0:T(8,128)(2,1)S(1)}, bf16[4,16,2048]{2,1,0:T(8,128)(2,1)S(1)}, u32[]{:S(2)}, u32[]{:S(2)}) collective-permute-start(bf16[4,16,2048]{2,1,0:T(8,128)(2,1)S(1)} %get-tuple-element.39), channel_id=1, source_target_pairs={{0,2},{1,3},{2,0},{3,1},{4,6},{5,7},{6,4},{7,5},{8,10},{9,11},{10,... | collective-permute-start | bytes 786440 | tf_op jit(solution)/shard_map/ppermute | solution.py:414
  234.4 26.2 %copy-start.1 = (bf16[4,2,256,256]{3,2,1,0:T(8,128)(2,1)S(1)}, bf16[4,2,256,256]{3,2,1,0:T(8,128)(2,1)}, u32[]{:S(2)}) copy-start(bf16[4,2,256,256]{3,2,1,0:T(8,128)(2,1)} %param.22) | copy-start | bytes 3145732
  234.4 23.5 %collective-permute-start.21 = (bf16[4,16,2048]{2,1,0:T(8,128)(2,1)S(1)}, bf16[4,16,2048]{2,1,0:T(8,128)(2,1)S(1)}, u32[]{:S(2)}, u32[]{:S(2)}) collective-permute-start(bf16[4,16,2048]{2,1,0:T(8,128)(2,1)S(1)} %get-tuple-element.37), channel_id=1, source_target_pairs={{0,1},{1,2},{2,3},{3,0},{4,5},{5,6},{6,7},{7,4},{8,9},{9,10},{10,1... | collective-permute-start | bytes 786440 | tf_op jit(solution)/shard_map/ppermute | solution.py:414

commit v3 on v2

--- a/solution.py
+++ b/solution.py
@@ -9,6 +9,7 @@
 
 CAP = 128
 CHUNKS = (1, 2, 1)
+SHORT = 120e9
 VMEM = 56 * 1024 * 1024
 BF = jnp.bfloat16
 F32 = jnp.float32
@@ -66,7 +67,7 @@
             jax.ShapeDtypeStruct((1, rows), jnp.int32),
         ],
         compiler_params=pltpu.CompilerParams(vmem_limit_bytes=VMEM),
-        cost_estimate=cost(4e9, 4e6),
+        cost_estimate=cost(SHORT, 4e6),
     )(scal, x, sl, ss, table)
 
 
@@ -108,36 +109,56 @@
         ),
         out_shape=jax.ShapeDtypeStruct(shape, BF),
         compiler_params=pltpu.CompilerParams(vmem_limit_bytes=VMEM),
-        cost_estimate=cost(4e9, 4e6),
+        cost_estimate=cost(SHORT, 4e6),
     )(scal, x, gt, ut, code)
 
 
-def gate_up_body(x, wg, wu, send, keep):
+def gate_up_body(pieces, scal, *refs):
+    blocks, (wg, wu, send, keep, x) = refs[:pieces], refs[pieces:]
     half = send.shape[1]
+
+    @pl.when(pl.program_id(0) == 0)
+    def _():
+        each = x.shape[0] // pieces
+        for i, block in enumerate(blocks):
+            x[i * each : (i + 1) * each] = block[...].reshape(each, x.shape[1])
+
     for i, w in enumerate((wg, wu)):
         total = jnp.dot(x[...], w[...], preferred_element_type=F32)
         send[i] = total[:half].astype(send.dtype)
         keep[i] = total[half:]
 
 
-def gate_up(x, wg, wu):
-    rows, depth = x.shape
+def gate_up(scal, tokens, wg, wu, owners, shift, start, size):
+    rows, depth = tokens.shape
     width = wg.shape[1]
     block = min(1024, width)
-    outs = pl.BlockSpec((2, rows // 2, block), lambda i: (0, 0, i))
-    weights = pl.BlockSpec((depth, block), lambda i: (0, i))
+    each = size // (owners * shift)
+    first = start // (shift * each)
+    view = tokens.reshape(shift, rows // (shift * each), each, depth)
+    outs = pl.BlockSpec((2, size // 2, block), lambda i, s: (0, 0, i))
+    weights = pl.BlockSpec((depth, block), lambda i, s: (0, i))
+    piece = [
+        pl.BlockSpec((shift, 1, each, depth), functools.partial(lambda h, i, s: (0, first + s[h], 0, 0), h))
+        for h in range(owners)
+    ]
     return pl.pallas_call(
-        gate_up_body,
-        grid=(width // block,),
-        in_specs=[whole(x.shape), weights, weights],
-        out_specs=[outs, outs],
-        out_shape=[jax.ShapeDtypeStruct((2, rows // 2, width), F32)] * 2,
+        functools.partial(gate_up_body, owners),
+        grid_spec=pltpu.PrefetchScalarGridSpec(
+            num_scalar_prefetch=1,
+            grid=(width // block,),
+            in_specs=[*piece, weights, weights],
+            out_specs=[outs, outs],
+            scratch_shapes=[pltpu.VMEM((size, depth), BF)],
+        ),
+        out_shape=[jax.ShapeDtypeStruct((2, size // 2, width), F32)] * 2,
         compiler_params=pltpu.CompilerParams(vmem_limit_bytes=VMEM),
-        cost_estimate=cost(4 * rows * depth * width, 4 * depth * width),
-    )(x, wg, wu)
-
-
-def activate_body(per_slot, start, each, keep, core, got, delta, where, out):
+        cost_estimate=cost(4 * size * depth * width, 4 * depth * width),
+    )(scal, *[view] * owners, wg, wu)
+
+
+def activate_body(per_slot, start, each, parts, keep, core, *refs):
+    gots, (delta, where, out) = refs[:parts], refs[parts:]
     tile = 256
     step = pl.program_id(0)
     across = out.shape[1] // tile
@@ -149,7 +170,8 @@
         cols = slice(b * tile, (b + 1) * tile)
         sums = []
         for kind in range(2):
-            total = keep[kind, :, cols] + core[kind, :, cols] + got[kind, :, cols].astype(F32)
+            got = gots[0][kind, :, cols] if parts == 1 else gots[kind][0, :, cols]
+            total = keep[kind, :, cols] + core[kind, :, cols] + got.astype(F32)
             for k in range(kind * per_slot, (kind + 1) * per_slot):
                 total = total + jnp.where(at[k] == b, adds[k], 0.0)
             sums.append(total)
@@ -157,26 +179,21 @@
         out[:, cols] = (gate / (1.0 + jnp.exp(-gate)) * up).astype(BF)
 
 
-def activate(keep, core, got, delta, where, per_slot, start):
-    each, width = got.shape[1:]
+def activate(keep, core, gots, delta, where, per_slot, start):
+    each, width = gots[0].shape[1:]
     last = keep.shape[1] // each - 1
-    block = min(1024, width)
+    block = min(2048, width)
     own = pl.BlockSpec((2, each, block), lambda i: (0, last, i))
+    taken = [pl.BlockSpec((g.shape[0], each, block), lambda i: (0, 0, i)) for g in gots]
     return pl.pallas_call(
-        functools.partial(activate_body, per_slot, start, each),
+        functools.partial(activate_body, per_slot, start, each, len(gots)),
         grid=(width // block,),
-        in_specs=[
-            own,
-            own,
-            pl.BlockSpec((2, each, block), lambda i: (0, 0, i)),
-            whole(delta.shape),
-            whole(where.shape),
-        ],
+        in_specs=[own, own, *taken, whole(delta.shape), whole(where.shape)],
         out_specs=pl.BlockSpec((each, block), lambda i: (0, i)),
         out_shape=jax.ShapeDtypeStruct((each, width), BF),
         compiler_params=pltpu.CompilerParams(vmem_limit_bytes=VMEM),
-        cost_estimate=cost(20 * each * width, 24 * each * width),
-    )(keep, core, got, delta, where)
+        cost_estimate=cost(SHORT, 24 * each * width),
+    )(keep, core, *gots, delta, where)
 
 
 def down_body(width_tiles, here, count, start, scal, far, near, w, tiles, slot, out, hid):
@@ -276,14 +293,6 @@
     order_y = [(my_y + k) % ys for k in range(1, ys)] + [my_y]
     homes = jnp.stack([y * 2 + c for c in (1 - my_core, my_core) for y in order_y]).astype(jnp.int32)
 
-    def reduce_homes(x, axis):
-        half = owners // 2
-        kept = x[half:] + core_swap(x[:half])
-        total = kept[ys - 1]
-        for k in range(1, ys):
-            total = total + y_move(kept[k - 1], k)
-        return total
-
     row_ids = []
     offset = 0
     for size in sizes:
@@ -328,7 +337,9 @@
         firsts = [mine_g * part, (1 - mine_g) * part]
     else:
         part = per_owner
-        both = jnp.stack([y_move(down_tiles, -k) for k in range(1, ys)] + [down_tiles])[None]
+        gathered = jnp.stack([y_move(down_tiles, -k) for k in range(1, ys)] + [down_tiles])
+        other = gathered
+        both = gathered[None]
         firsts = [0]
     all_tiles = jnp.stack([core_swap(both), both]).reshape(-1, 256, 256)
     tile_slots = jnp.stack(
@@ -347,32 +358,48 @@
     def after(x, *earlier):
         return lax.optimization_barrier((x, *earlier))[0]
 
-    def transform(i, x):
-        send, keep = gate_up(x, gate_weight, up_weight)
-        return keep, core_swap(send)
-
-    def exchange(keep, core):
-        each = keep.shape[1] // ys
-        return [
-            y_move(
-                (keep[:, (k - 1) * each : k * each] + core[:, (k - 1) * each : k * each]).astype(BF), k
-            )
-            for k in range(1, ys)
-        ]
-
     starts = [sum(sizes[:i]) for i in range(len(sizes))]
     inners = [s // owners for s in starts]
-    xs = [jnp.take(tokens, ids, axis=0) for ids in row_ids]
-    kept = [None] * len(sizes)
-    cores = [None] * len(sizes)
-    gots = [None] * len(sizes)
-
-    kept[0], cores[0] = transform(0, xs[0])
+    count = len(sizes)
+    kept, cores, sends, gots = ([None] * count for _ in range(4))
+
+    def multiply(i, *earlier):
+        send, kept[i] = gate_up(
+            after(homes, *earlier), tokens, gate_weight, up_weight, owners, shift, starts[i], sizes[i]
+        )
+        cores[i] = core_swap(send)
+
+    def exchange(i):
+        each = sizes[i] // owners
+        parts = [slice(0, 2)] if CHUNKS[i] == 1 else [slice(0, 1), slice(1, 2)]
+        sends[i], gots[i] = [], []
+        for part in parts:
+            got = None
+            for k in range(1, ys):
+                rows_k = slice((k - 1) * each, k * each)
+                sends[i].append((kept[i][part, rows_k] + cores[i][part, rows_k]).astype(BF))
+                moved = y_move(sends[i][-1], k)
+                if ys > 2:
+                    moved = moved.astype(F32)
+                got = moved if got is None else got + moved
+            gots[i].append(got)
+
+    def halve(x):
+        half = owners // 2
+        return x[half:] + core_swap(x[:half])
+
+    def finish(x, *earlier):
+        total = after(x[ys - 1], *earlier)
+        for k in range(1, ys):
+            total = total + y_move(x[k - 1], k)
+        return total
+
+    multiply(0)
     packed, code = pack(
-        scal, after(tokens, kept[0]), slot_rows[None, :], slot_rows[:, None], table, owners, per_owner, kinds
+        after(scal, kept[0], gathered), tokens, slot_rows[None, :], slot_rows[:, None], table, owners, per_owner, kinds
     )
-    gots[0] = exchange(kept[0], cores[0])
-    features = reduce_homes(packed.reshape(owners, CAP, -1), 0)
+    exchange(0)
+    packed = halve(packed.reshape(owners, CAP, -1))
     code_q = jnp.sum(
         jnp.where(row_of[:, None] == jnp.arange(rows, dtype=jnp.int32)[None, :], code, 0), axis=1
     )
@@ -389,32 +416,52 @@
     )
     ss_q = slot_q[:, None]
 
-    for i in range(1, len(sizes)):
-        kept[i], cores[i] = transform(i, after(xs[i], kept[i - 1], packed))
+    for i in range(1, count):
         if i == 1:
+            multiply(1, *sends[0], packed)
+            features = finish(packed, kept[1])
             spread = product(
-                scal, after(features, kept[1]), gate_tiles, up_tiles, code_q[None, :], owners, per_owner, pieces
+                after(scal, kept[1], *gots[0], other), features, gate_tiles, up_tiles, code_q[None, :], owners, per_owner, pieces
             )
-            home_delta = reduce_homes(spread, 0)
-        gots[i] = exchange(kept[i], cores[i])
-
-    result = []
-    for i, size in enumerate(sizes):
-        keep = kept[i]
-        got = gots[i][0]
-        if ys > 2:
-            got = sum(g.astype(F32) for g in gots[i])
-        hid = activate(keep, cores[i], got, home_delta, where, per_slot, inners[i])
-        chip = jnp.concatenate([y_move(hid, -k) for k in range(1, ys)] + [hid])
-        out = down(down_scal, core_swap(chip), chip, down_weight, all_tiles, ss_q, width_tiles, starts[i])
-        blocks = out.reshape(owners, shift, size // (owners * shift), shard_width).transpose(1, 0, 2, 3)
+            exchange(1)
+            spread = halve(spread)
+            held = (spread,)
+        else:
+            multiply(i, *sends[i - 1], *gots[i - 2], *held)
+            held = ()
+            exchange(i)
+    home_delta = finish(spread, kept[2])
+
+    def finish_hidden(i, *earlier):
+        hid = activate(kept[i], cores[i], gots[i], home_delta, after(where, *earlier), per_slot, inners[i])
+        return hid, jnp.concatenate([y_move(hid, -k) for k in range(1, ys)] + [hid])
+
+    def finish_down(i, chip, *earlier):
+        out = down(
+            after(down_scal, *earlier), core_swap(chip), chip, down_weight, all_tiles, ss_q, width_tiles, starts[i]
+        )
+        blocks = out.reshape(owners, shift, sizes[i] // (owners * shift), shard_width).transpose(1, 0, 2, 3)
         total = lax.dynamic_index_in_dim(blocks, here_t, 0, keepdims=False)
+        gone = [
+            lax.dynamic_index_in_dim(blocks, (here_t + k) % shift, 0, keepdims=False).astype(BF)
+            for k in range(1, shift)
+        ]
         for k in range(1, shift):
-            gone = lax.dynamic_index_in_dim(blocks, (here_t + k) % shift, 0, keepdims=False).astype(BF)
             total = total + lax.ppermute(
-                gone, "tensor", [(i, (i + k) % shift) for i in range(shift)]
+                gone[k - 1], "tensor", [(i, (i + k) % shift) for i in range(shift)]
             ).astype(F32)
-        result.append(total.astype(BF))
+        return gone, total.astype(BF)
+
+    chips, result = [], []
+    hid, chip = finish_hidden(0, kept[count - 1], all_tiles, gots[1][0])
+    chips.append(chip)
+    for i in range(1, count):
+        hid, chip = finish_hidden(i, hid, *sends[count - 1])
+        chips.append(chip)
+    gone = ()
+    for i in range(count):
+        gone, total = finish_down(i, chips[i], *gone)
+        result.append(total)
 
     placed = [jnp.take(r, at_home, axis=0).reshape(-1, shard_width) for r in result]
     return jnp.concatenate(placed, axis=0)

time: 262 us -> 252 us (0.962)
  waiting for transfers between devices: 69.4 us -> 49.4 us
  starting transfers between devices: 28 us -> 41.9 us
    ppermute x9, waiting for transfers between devices: 32 us -> 16.4 us  [finish_down(): lax.ppermute(gone[k - 1], 'tensor', [(i, (i + k) % shift) for i in range(...]
    ppermute x9, starting transfers between devices: 10 us -> 24.5 us  [finish_down(): lax.ppermute(gone[k - 1], 'tensor', [(i, (i + k) % shift) for i in range(...]
    gather x3 -> x0, local copies, waits for them, and re-layouts: 6.39 us -> none  [shards(): xs = [jnp.take(tokens, ids, axis=0) for ids in row_ids]]
    ppermute x1, waiting for transfers between devices: 15.9 us -> 11 us  [shards(): other = lax.ppermute(gathered, 'groups', [(0, 1), (1, 0)])]
    select_n x5 -> x0, other arithmetic: 2.98 us -> none  [shards(): xs = [jnp.take(tokens, ids, axis=0) for ids in row_ids]]
    unnamed x48 -> x54, local copies, waits for them, and re-layouts: 4.05 us -> 6.07 us
    ppermute x9 -> x10, waiting for transfers between devices: 21.5 us -> 20.6 us  [y_move(): lax.ppermute(x, 'delta', [(i, (i + 2 * k) % owners) for i in range(owners)])]
    ppermute x9 -> x10, starting transfers between devices: 10.9 us -> 10.4 us  [y_move(): lax.ppermute(x, 'delta', [(i, (i + 2 * k) % owners) for i in range(owners)])]
  transfers between devices with their start and end apart: 31 -> 32, of which waited for: 9 -> 7; matrix products, arithmetic and copies ran while one was open for 16% -> 16% of each run, Pallas kernels for 37% -> 44%
where the time goes in v3:
time: 252 us; the launch traced here: 251 us
  Pallas kernels  110 us (44%)
  waiting for transfers between devices  49.4 us (20%)
  starting transfers between devices  41.9 us (17%)
  other arithmetic  27.1 us (11%)
  local copies, waits for them, and re-layouts  22.7 us (9%)
    pallas_call x3, Pallas kernels, gate_up(): pl.pallas_call(functools.partial(gate_up_body, owners), grid_spec=pltpu.P...  47.9 us
    pallas_call x3, Pallas kernels, down(): pl.pallas_call(functools.partial(down_body, width_tiles, width // 256, co...  41.1 us
    ppermute x9, starting transfers between devices, finish_down(): lax.ppermute(gone[k - 1], 'tensor', [(i, (i + k) % shift) for i in range(...  24.5 us
    ppermute x10, waiting for transfers between devices, y_move(): lax.ppermute(x, 'delta', [(i, (i + 2 * k) % owners) for i in range(owners)])  20.6 us
    ppermute x9, waiting for transfers between devices, finish_down(): lax.ppermute(gone[k - 1], 'tensor', [(i, (i + k) % shift) for i in range(...  16.4 us
    ppermute x1, waiting for transfers between devices, shards(): other = lax.ppermute(gathered, 'groups', [(0, 1), (1, 0)])  11 us
    ppermute x10, starting transfers between devices, y_move(): lax.ppermute(x, 'delta', [(i, (i + 2 * k) % owners) for i in range(owners)])  10.4 us
    pallas_call x3, Pallas kernels, activate(): pl.pallas_call(functools.partial(activate_body, per_slot, start, each, le...  9.28 us
  transfers between devices with their start and end apart: 32, of which 7 were waited for; matrix products, arithmetic and copies ran while one was open for 16% of the time, Pallas kernels for 44%

profile of v3, /device:TPU:0, one launch (start us, length us, event | category | flops | bytes accessed | tf_op | source)
XLA Modules:
  0.0 251.5 jit_solution(12501585752425967502)
XLA Ops:
  0.0 0.8 pad_add_fusion.1
  1.3 2.6 %collective-permute-start.1 = (s32[4,6]{0,1:T(8,128)S(1)}, s32[4,6]{0,1:T(8,128)S(1)}, u32[]{:S(2)}, u32[]{:S(2)}) collective-permute-start(s32[4,6]{0,1:T(8,128)S(1)} %pad_add_fusion.1), channel_id=1, source_target_pairs={{0,8},{4,12},{8,0},{12,4},{1,9},{5,13},{9,1},{13,5},{2,10},{6,14},... | collective-permute-start | bytes 296 | tf_op jit(solution)/shard_map/ppermute | solution.py:314
  3.9 1.4 collective-permute-start
  6.4 15.0 %shard_map.118 = (f32[2,64,4096]{2,1,0:T(8,128)}, f32[2,64,4096]{2,1,0:T(8,128)}) custom-call(s32[4]{0:T(128)} %get-tuple-element.35.scal, bf16[4,16,8,2048]{3,2,1,0:T(8,128)(2,1)} %bitcast.138, bf16[4,16,8,2048]{3,2,1,0:T(8,128)(2,1)} %bitcast.139, bf16[4,16,8,2048]{3,2,1,0:T(8,128)(2,1)} %bitcast.140, bf16[4,16,8,2048]{3,2,1,0:T(8,128)(2,1)} %bitcast.141, ...), custom_call_target="tpu_custom_call" | custom-call | flops 4294967296 | bytes 33554432 | tf_op jit(solution)/shard_map/pallas_call | solution.py:145
  25.5 0.9 copy.44.ss
  27.6 1.1 fusion.31
  28.7 1.7 collective-permute-start.7
  30.4 6.9 %shard_map.119 = (bf16[512,1024]{1,0:T(8,128)(2,1)}, s32[1,512]{1,0:T(1,128)}) custom-call(s32[5]{0:T(128)} %concatenate.59.scal, bf16[512,2048]{1,0:T(8,128)(2,1)} %x.3, s32[1,512]{1,0:T(1,128)} %bitcast.168, s32[512,1]{1,0:T(8,128)} %copy.44.ss, bf16[128,128]{1,0:T(8,128)(2,1)} %pad.4.table), custom_call_target="tpu_custom_call" | custom-call | flops 120000004096 | bytes 4000000 | tf_op jit(solution)/shard_map/pallas_call | solution.py:57
  37.3 2.1 fusion.33
  40.7 0.8 collective-permute-done.6
  41.7 1.6 collective-permute-start.8
  43.3 11.0 %collective-permute-done.7 = bf16[2,2,2,256,256]{4,3,2,1,0:T(8,128)(2,1)S(1)} collective-permute-done((bf16[2,2,2,256,256]{4,3,2,1,0:T(8,128)(2,1)}, bf16[2,2,2,256,256]{4,3,2,1,0:T(8,128)(2,1)S(1)}, u32[]{:S(2)}, u32[]{:S(2)}) %collective-permute-start.7) | collective-permute-done | bytes 1048608 | tf_op jit(solution)/shard_map/ppermute | solution.py:335
  54.3 1.0 copy-done.7
  55.3 3.0 %pad_maximum_fusion.1 = (bf16[2,2,2,2,256,256]{5,4,3,2,1,0:T(8,128)(2,1)}, bf16[1,2,2,2,2,256,256]{6,5,4,3,2,1,0:T(8,128)(2,1)S(1)}) fusion(bf16[1,2,2,2,256,256]{5,4,3,2,1,0:T(8,128)(2,1)} %bitcast.160, bf16[1,2,2,2,256,256]{5,4,3,2,1,0:T(8,128)(2,1)S(1)} %get-tuple-element.63), kind=kLoop, calls=%fused_computation.4 | loop fusion | flops 1048576 | bytes 6291456 | tf_op jit(solution)/shard_map/stack | solution.py:336
  58.3 1.3 fusion.3
  59.7 1.8 collective-permute-start.4
  61.4 17.9 %shard_map.120 = (f32[2,128,4096]{2,1,0:T(8,128)}, f32[2,128,4096]{2,1,0:T(8,128)}) custom-call(s32[4]{0:T(128)} %get-tuple-element.35.scal, bf16[4,8,16,2048]{3,2,1,0:T(8,128)(2,1)} %bitcast.142, bf16[4,8,16,2048]{3,2,1,0:T(8,128)(2,1)} %bitcast.143, bf16[4,8,16,2048]{3,2,1,0:T(8,128)(2,1)} %bitcast.144, bf16[4,8,16,2048]{3,2,1,0:T(8,128)(2,1)} %bitcast.145, ...), custom_call_target="tpu_custom_call" | custom-call | flops 8589934592 | bytes 33554432 | tf_op jit(solution)/shard_map/pallas_call | solution.py:145
  79.5 0.8 add.422.x
  80.3 0.8 copy-done.24
  81.1 4.7 %shard_map.121 = bf16[4,128,1024]{2,1,0:T(8,128)(2,1)} custom-call(s32[5]{0:T(128)} %concatenate.59.scal, bf16[128,1024]{1,0:T(8,128)(2,1)} %add.422.x, bf16[4,2,256,256]{3,2,1,0:T(8,128)(2,1)} %gt.1, bf16[4,2,256,256]{3,2,1,0:T(8,128)(2,1)} %ut.1, s32[1,512]{1,0:T(1,128)} %bitcast.165), custom_call_target="tpu_custom_call" | custom-call | flops 120000004096 | bytes 4000000 | tf_op jit(solution)/shard_map/pallas_call | solution.py:102
  85.8 1.1 slice.105
  87.4 0.9 copy.47
  89.0 1.3 slice_add_fusion.4
  90.7 2.4 fusion.1
  93.1 1.8 collective-permute-start.13
  94.9 4.0 %pad_maximum_fusion = bf16[2,2,2,2,2,256,256]{6,5,4,3,2,1,0:T(8,128)(2,1)} fusion(bf16[1,2,2,2,2,256,256]{6,5,4,3,2,1,0:T(8,128)(2,1)S(1)} %get-tuple-element.56, bf16[1,2,2,2,2,256,256]{6,5,4,3,2,1,0:T(8,128)(2,1)} %bitcast.46), kind=kLoop, calls=%fused_computation.3 | loop fusion | flops 2097152 | bytes 8388608 | tf_op jit(solution)/shard_map/stack | solution.py:344
  99.2 15.0 %shard_map.122 = (f32[2,64,4096]{2,1,0:T(8,128)}, f32[2,64,4096]{2,1,0:T(8,128)}) custom-call(s32[4]{0:T(128)} %get-tuple-element.35.scal, bf16[4,16,8,2048]{3,2,1,0:T(8,128)(2,1)} %bitcast.146, bf16[4,16,8,2048]{3,2,1,0:T(8,128)(2,1)} %bitcast.147, bf16[4,16,8,2048]{3,2,1,0:T(8,128)(2,1)} %bitcast.148, bf16[4,16,8,2048]{3,2,1,0:T(8,128)(2,1)} %bitcast.149, ...), custom_call_target="tpu_custom_call" | custom-call | flops 4294967296 | bytes 33554432 | tf_op jit(solution)/shard_map/pallas_call | solution.py:145
  114.2 0.8 add.448.refs_1_.refs_2_
  115.0 0.8 copy-done.25
  115.8 0.7 copy.46.refs_2_
  116.5 2.9 %shard_map.123 = bf16[32,4096]{1,0:T(8,128)(2,1)} custom-call(f32[2,64,4096]{2,1,0:T(8,128)} %get-tuple-element.25.keep, f32[2,64,4096]{2,1,0:T(8,128)} %collective-permute-done.3.core, bf16[2,32,4096]{2,1,0:T(8,128)(2,1)} %copy-done.24, bf16[128,1024]{1,0:T(8,128)(2,1)} %add.448.refs_1_.refs_2_, s32[128,4]{1,0:T(8,128)} %copy.46.refs_2_), custom_call_target="tpu_custom_call" | custom-call | flops 120000004096 | bytes 3145728 | tf_op jit(solution)/shard_map/pallas_call | solution.py:188
  119.4 1.6 collective-permute-start.14
  121.0 1.3 fusion
  122.4 0.7 copy.53.refs_3_
  123.1 0.8 copy-done.26
  123.9 3.7 %shard_map.125 = bf16[64,4096]{1,0:T(8,128)(2,1)} custom-call(f32[2,128,4096]{2,1,0:T(8,128)} %get-tuple-element.30.keep, f32[2,128,4096]{2,1,0:T(8,128)} %collective-permute-done.10.core, bf16[1,64,4096]{2,1,0:T(8,128)(2,1)} %copy-done.25, bf16[1,64,4096]{2,1,0:T(8,128)(2,1)} %copy-done.26, bf16[128,1024]{1,0:T(8,128)(2,1)} %add.448.refs_1_.refs_2_, ...), custom_call_target="tpu_custom_call" | custom-call | flops 120000004096 | bytes 6291456 | tf_op jit(solution)/shard_map/pallas_call | solution.py:188
  128.0 0.9 add_select_fusion.slot
  128.9 1.6 collective-permute-start.26
  130.7 0.7 copy.56.refs_2_
  131.4 11.2 %collective-permute-done.21 = bf16[64,4096]{1,0:T(8,128)(2,1)S(1)} collective-permute-done((bf16[64,4096]{1,0:T(8,128)(2,1)}, bf16[64,4096]{1,0:T(8,128)(2,1)S(1)}, u32[]{:S(2)}, u32[]{:S(2)}) %collective-permute-start.21) | collective-permute-done | bytes 524320 | tf_op jit(solution)/shard_map/ppermute | solution.py:291
  142.6 1.1 pad_maximum_fusion.3.near
  143.8 9.4 %collective-permute-done.26.refs_0_ = bf16[2,32,4096]{2,1,0:T(8,128)(2,1)} collective-permute-done((bf16[2,32,4096]{2,1,0:T(8,128)(2,1)S(1)}, bf16[2,32,4096]{2,1,0:T(8,128)(2,1)}, u32[]{:S(2)}, u32[]{:S(2)}) %collective-permute-start.26) | collective-permute-done | bytes 524320 | tf_op jit(solution)/shard_map/ppermute | solution.py:291
  153.2 2.7 %shard_map.127 = bf16[32,4096]{1,0:T(8,128)(2,1)} custom-call(f32[2,64,4096]{2,1,0:T(8,128)} %get-tuple-element.36.keep, f32[2,64,4096]{2,1,0:T(8,128)} %collective-permute-done.20.core, bf16[2,32,4096]{2,1,0:T(8,128)(2,1)} %collective-permute-done.26.refs_0_, bf16[128,1024]{1,0:T(8,128)(2,1)} %add.448.refs_1_.refs_2_, s32[128,4]{1,0:T(8,128)} %copy.56.refs_2_), custom_call_target="tpu_custom_call" | custom-call | flops 120000004096 | bytes 3145728 | tf_op jit(solution)/shard_map/pallas_call | solution.py:188
  156.4 0.8 copy-done.8
  157.2 12.9 %shard_map.124 = f32[128,2048]{1,0:T(8,128)} custom-call(s32[65]{0:T(128)} %pad_add_fusion.3.scal, bf16[64,4096]{1,0:T(8,128)(2,1)} %copy-done.8, bf16[64,4096]{1,0:T(8,128)(2,1)} %copy-done.3, bf16[4096,2048]{1,0:T(8,128)(2,1)} %w.5, bf16[32,256,256]{2,1,0:T(8,128)(2,1)} %bitcast.150, s32[512,1]{1,0:T(8,128)} %add_select_fusion.slot), custom_call_target="tpu_custom_call" | custom-call | flops 3221225472 | bytes 25165824 | tf_op jit(solution)/shard_map/pallas_call | solution.py:236
  170.1 1.1 fusion.18
  171.3 4.5 %collective-permute-start.18 = (bf16[4,8,2048]{2,1,0:T(8,128)(2,1)S(1)}, bf16[4,8,2048]{2,1,0:T(8,128)(2,1)S(1)}, u32[]{:S(2)}, u32[]{:S(2)}) collective-permute-start(bf16[4,8,2048]{2,1,0:T(8,128)(2,1)S(1)} %get-tuple-element.60), channel_id=1, source_target_pairs={{0,3},{1,0},{2,1},{3,2},{4,7},{5,4},{6,5},{7,6},{8,11},{9,8},{10,9... | collective-permute-start | bytes 393224 | tf_op jit(solution)/shard_map/ppermute | solution.py:450
  176.5 1.0 copy-done.5
  177.6 15.3 %shard_map.126 = f32[256,2048]{1,0:T(8,128)} custom-call(s32[65]{0:T(128)} %pad_add_fusion.3.scal, bf16[128,4096]{1,0:T(8,128)(2,1)} %copy-done.5, bf16[128,4096]{1,0:T(8,128)(2,1)} %copy-done.2, bf16[4096,2048]{1,0:T(8,128)(2,1)} %w.5, bf16[32,256,256]{2,1,0:T(8,128)(2,1)} %bitcast.151, s32[512,1]{1,0:T(8,128)} %add_select_fusion.slot), custom_call_target="tpu_custom_call" | custom-call | flops 6442450944 | bytes 25165824 | tf_op jit(solution)/shard_map/pallas_call | solution.py:236
  192.9 1.5 fusion.8
  194.4 0.8 copy-done.9
  195.2 12.9 %shard_map.128 = f32[128,2048]{1,0:T(8,128)} custom-call(s32[65]{0:T(128)} %pad_add_fusion.3.scal, bf16[64,4096]{1,0:T(8,128)(2,1)} %copy-done.9, bf16[64,4096]{1,0:T(8,128)(2,1)} %copy-done.4, bf16[4096,2048]{1,0:T(8,128)(2,1)} %w.5, bf16[32,256,256]{2,1,0:T(8,128)(2,1)} %bitcast.152, s32[512,1]{1,0:T(8,128)} %add_select_fusion.slot), custom_call_target="tpu_custom_call" | custom-call | flops 3221225472 | bytes 25165824 | tf_op jit(solution)/shard_map/pallas_call | solution.py:236
  208.0 1.2 fusion.22
  209.2 5.5 %collective-permute-start.29 = (bf16[4,8,2048]{2,1,0:T(8,128)(2,1)S(1)}, bf16[4,8,2048]{2,1,0:T(8,128)(2,1)S(1)}, u32[]{:S(2)}, u32[]{:S(2)}) collective-permute-start(bf16[4,8,2048]{2,1,0:T(8,128)(2,1)S(1)} %get-tuple-element.57), channel_id=1, source_target_pairs={{0,1},{1,2},{2,3},{3,0},{4,5},{5,6},{6,7},{7,4},{8,9},{9,10},{10,1... | collective-permute-start | bytes 393224 | tf_op jit(solution)/shard_map/ppermute | solution.py:450
  214.7 1.5 collective-permute-start.30
  216.2 1.0 fusion.16
  217.9 2.9 %collective-permute-start.25 = (bf16[4,16,2048]{2,1,0:T(8,128)(2,1)S(1)}, bf16[4,16,2048]{2,1,0:T(8,128)(2,1)S(1)}, u32[]{:S(2)}, u32[]{:S(2)}) collective-permute-start(bf16[4,16,2048]{2,1,0:T(8,128)(2,1)S(1)} %get-tuple-element.52), channel_id=1, source_target_pairs={{0,3},{1,0},{2,1},{3,2},{4,7},{5,4},{6,5},{7,6},{8,11},{9,8},{10,9... | collective-permute-start | bytes 786440 | tf_op jit(solution)/shard_map/ppermute | solution.py:450
  220.8 9.5 %collective-permute-start.24 = (bf16[4,16,2048]{2,1,0:T(8,128)(2,1)S(1)}, bf16[4,16,2048]{2,1,0:T(8,128)(2,1)S(1)}, u32[]{:S(2)}, u32[]{:S(2)}) collective-permute-start(bf16[4,16,2048]{2,1,0:T(8,128)(2,1)S(1)} %get-tuple-element.54), channel_id=1, source_target_pairs={{0,2},{1,3},{2,0},{3,1},{4,6},{5,7},{6,4},{7,5},{8,10},{9,11},{10,... | collective-permute-start | bytes 786440 | tf_op jit(solution)/shard_map/ppermute | solution.py:450
  230.3 1.0 fusion.13
  231.4 0.8 gather_fusion.2
  232.3 3.2 %collective-permute-done.23 = bf16[4,16,2048]{2,1,0:T(8,128)(2,1)S(1)} collective-permute-done((bf16[4,16,2048]{2,1,0:T(8,128)(2,1)S(1)}, bf16[4,16,2048]{2,1,0:T(8,128)(2,1)S(1)}, u32[]{:S(2)}, u32[]{:S(2)}) %collective-permute-start.23) | collective-permute-done | bytes 262176 | tf_op jit(solution)/shard_map/ppermute | solution.py:450
  235.5 13.2 %collective-permute-done.24 = bf16[4,16,2048]{2,1,0:T(8,128)(2,1)S(1)} collective-permute-done((bf16[4,16,2048]{2,1,0:T(8,128)(2,1)S(1)}, bf16[4,16,2048]{2,1,0:T(8,128)(2,1)S(1)}, u32[]{:S(2)}, u32[]{:S(2)}) %collective-permute-start.24) | collective-permute-done | bytes 262176 | tf_op jit(solution)/shard_map/ppermute | solution.py:450
  248.7 1.2 fusion.6
  250.6 0.8 pad_maximum_fusion.6
  (153 shorter events, 13.9 us)
Async XLA Ops:
  0.0 5.3 %copy-start = (bf16[4,2,256,256]{3,2,1,0:T(8,128)(2,1)S(1)}, bf16[4,2,256,256]{3,2,1,0:T(8,128)(2,1)}, u32[]{:S(2)}) copy-start(bf16[4,2,256,256]{3,2,1,0:T(8,128)(2,1)} %param.20) | copy-start | bytes 3145732
  0.8 25.6 %collective-permute-start.2 = (s32[4,6]{0,1:T(8,128)S(1)}, s32[4,6]{0,1:T(8,128)S(1)}, u32[]{:S(2)}, u32[]{:S(2)}) collective-permute-start(s32[4,6]{0,1:T(8,128)S(1)} %pad_add_fusion.1), channel_id=1, source_target_pairs={{0,4},{4,8},{8,12},{12,0},{1,5},{5,9},{9,13},{13,1},{2,6},{6,10},{... | collective-permute-start | bytes 296 | tf_op jit(solution)/shard_map/ppermute | solution.py:314
  1.3 25.2 %collective-permute-start.1 = (s32[4,6]{0,1:T(8,128)S(1)}, s32[4,6]{0,1:T(8,128)S(1)}, u32[]{:S(2)}, u32[]{:S(2)}) collective-permute-start(s32[4,6]{0,1:T(8,128)S(1)} %pad_add_fusion.1), channel_id=1, source_target_pairs={{0,8},{4,12},{8,0},{12,4},{1,9},{5,13},{9,1},{13,5},{2,10},{6,14},... | collective-permute-start | bytes 296 | tf_op jit(solution)/shard_map/ppermute | solution.py:314
  3.9 22.7 %collective-permute-start = (s32[4,6]{0,1:T(8,128)S(1)}, s32[4,6]{0,1:T(8,128)S(1)}, u32[]{:S(2)}, u32[]{:S(2)}) collective-permute-start(s32[4,6]{0,1:T(8,128)S(1)} %pad_add_fusion.1), channel_id=1, source_target_pairs={{0,12},{4,0},{8,4},{12,8},{1,13},{5,1},{9,5},{13,9},{2,14},{6,2},{... | collective-permute-start | bytes 296 | tf_op jit(solution)/shard_map/ppermute | solution.py:314
  5.3 22.3 %collective-permute-start.5 = (bf16[2,2,256,256]{3,2,1,0:T(8,128)(2,1)S(1)}, bf16[2,2,256,256]{3,2,1,0:T(8,128)(2,1)S(1)}, u32[]{:S(2)}, u32[]{:S(2)}) collective-permute-start(bf16[2,2,256,256]{3,2,1,0:T(8,128)(2,1)S(1)} %constant_dynamic-slice_fusion), channel_id=1, source_target_pairs={{0,8},{4,12},{8,0},{12,4},{1,9},{5,13},{9,1},{13,5},{2,10},{6,14},... | collective-permute-start | bytes 1572872 | tf_op jit(solution)/shard_map/ppermute | solution.py:291
  6.4 15.1 %copy-start.17 = (s32[4]{0:T(128)S(1)}, s32[4]{0:T(128)}, u32[]{:S(2)}) copy-start(s32[4]{0:T(128)} %get-tuple-element.35.scal) | copy-start | bytes 52
  6.4 19.0 %copy-start.21 = (s32[512]{0:T(512)S(1)}, s32[512]{0:T(512)}, u32[]{:S(2)}) copy-start(s32[512]{0:T(512)} %param.24) | copy-start | bytes 6148
  6.4 19.0 %copy-start.23 = (s32[16]{0:T(128)S(1)}, s32[16]{0:T(128)}, u32[]{:S(2)}) copy-start(s32[16]{0:T(128)} %param.25) | copy-start | bytes 196
  21.3 37.0 %collective-permute-start.3 = (f32[2,64,4096]{2,1,0:T(8,128)}, f32[2,64,4096]{2,1,0:T(8,128)}, u32[]{:S(2)}, u32[]{:S(2)}) collective-permute-start(f32[2,64,4096]{2,1,0:T(8,128)} %get-tuple-element.26), channel_id=1, source_target_pairs={{0,4},{4,0},{8,12},{12,8},{1,5},{5,1},{9,13},{13,9},{2,6},{6,2},{1... | collective-permute-start | bytes 6291464 | tf_op jit(solution)/shard_map/ppermute | solution.py:288
  21.8 1.4 copy-start.18
  25.5 4.9 %copy-start.16 = (s32[512]{0:T(512)}, s32[512]{0:T(512)S(1)}, u32[]{:S(2)}) copy-start(s32[512]{0:T(512)S(1)} %select_reduce_fusion.2) | copy-start | bytes 6148
  28.7 25.6 %collective-permute-start.7 = (bf16[2,2,2,256,256]{4,3,2,1,0:T(8,128)(2,1)}, bf16[2,2,2,256,256]{4,3,2,1,0:T(8,128)(2,1)S(1)}, u32[]{:S(2)}, u32[]{:S(2)}) collective-permute-start(bf16[2,2,2,256,256]{4,3,2,1,0:T(8,128)(2,1)} %get-tuple-element.64), channel_id=1, source_target_pairs={{0,16},{16,0},{1,17},{17,1},{2,18},{18,2},{3,19},{19,3},{4,20},{20... | collective-permute-start | bytes 3145736 | tf_op jit(solution)/shard_map/ppermute | solution.py:335
  37.3 3.1 %copy-start.20 = (s32[1,512]{1,0:T(1,128)S(1)}, s32[1,512]{1,0:T(1,128)}, u32[]{:S(2)}) copy-start(s32[1,512]{1,0:T(1,128)} %get-tuple-element.33) | copy-start | bytes 6148
  39.3 2.1 collective-permute-start.6
  40.6 17.7 %copy-start.14 = (s32[512]{0:T(512)}, s32[512]{0:T(512)S(1)}, u32[]{:S(2)}) copy-start(s32[512]{0:T(512)S(1)} %select_reduce_fusion) | copy-start | bytes 6148
  41.7 37.8 %collective-permute-start.8 = (bf16[128,1024]{1,0:T(8,128)(2,1)S(1)}, bf16[128,1024]{1,0:T(8,128)(2,1)S(1)}, u32[]{:S(2)}, u32[]{:S(2)}) collective-permute-start(bf16[128,1024]{1,0:T(8,128)(2,1)S(1)} %get-tuple-element.69), channel_id=1, source_target_pairs={{0,8},{4,12},{8,0},{12,4},{1,9},{5,13},{9,1},{13,5},{2,10},{6,14},... | collective-permute-start | bytes 786440 | tf_op jit(solution)/shard_map/ppermute | solution.py:291
  54.3 1.0 copy-start.7
  55.3 3.0 %copy-start.10 = (f32[2,64,4096]{2,1,0:T(8,128)S(1)}, f32[2,64,4096]{2,1,0:T(8,128)}, u32[]{:S(2)}) copy-start(f32[2,64,4096]{2,1,0:T(8,128)} %get-tuple-element.25.keep) | copy-start | bytes 6291460
  58.3 36.5 %collective-permute-start.12 = (bf16[2,2,2,2,256,256]{5,4,3,2,1,0:T(8,128)(2,1)}, bf16[2,2,2,2,256,256]{5,4,3,2,1,0:T(8,128)(2,1)}, u32[]{:S(2)}, u32[]{:S(2)}) collective-permute-start(bf16[2,2,2,2,256,256]{5,4,3,2,1,0:T(8,128)(2,1)} %get-tuple-element.55), channel_id=1, source_target_pairs={{0,4},{4,0},{8,12},{12,8},{1,5},{5,1},{9,13},{13,9},{2,6},{6,2},{1... | collective-permute-start | bytes 6291464 | tf_op jit(solution)/shard_map/ppermute | solution.py:288
  59.7 20.6 %collective-permute-start.4 = (bf16[2,32,4096]{2,1,0:T(8,128)(2,1)S(1)}, bf16[2,32,4096]{2,1,0:T(8,128)(2,1)S(1)}, u32[]{:S(2)}, u32[]{:S(2)}) collective-permute-start(bf16[2,32,4096]{2,1,0:T(8,128)(2,1)S(1)} %fusion.3), channel_id=1, source_target_pairs={{0,8},{4,12},{8,0},{12,4},{1,9},{5,13},{9,1},{13,5},{2,10},{6,14},... | collective-permute-start | bytes 1572872 | tf_op jit(solution)/shard_map/ppermute | solution.py:291
  79.3 11.4 %collective-permute-start.10 = (f32[2,128,4096]{2,1,0:T(8,128)}, f32[2,128,4096]{2,1,0:T(8,128)}, u32[]{:S(2)}, u32[]{:S(2)}) collective-permute-start(f32[2,128,4096]{2,1,0:T(8,128)} %get-tuple-element.34), channel_id=1, source_target_pairs={{0,4},{4,0},{8,12},{12,8},{1,5},{5,1},{9,13},{13,9},{2,6},{6,2},{1... | collective-permute-start | bytes 12582920 | tf_op jit(solution)/shard_map/ppermute | solution.py:288
  80.3 0.8 copy-start.24
  81.1 6.3 %copy-start.15 = (s32[512]{0:T(512)S(1)}, s32[512]{0:T(512)}, u32[]{:S(2)}) copy-start(s32[512]{0:T(512)} %copy-done.14) | copy-start | bytes 6148
  86.9 2.1 collective-permute-start.9
  90.3 23.9 %collective-permute-start.11 = (bf16[128,1024]{1,0:T(8,128)(2,1)S(1)}, bf16[128,1024]{1,0:T(8,128)(2,1)S(1)}, u32[]{:S(2)}, u32[]{:S(2)}) collective-permute-start(bf16[128,1024]{1,0:T(8,128)(2,1)S(1)} %get-tuple-element.67), channel_id=1, source_target_pairs={{0,8},{4,12},{8,0},{12,4},{1,9},{5,13},{9,1},{13,5},{2,10},{6,14},... | collective-permute-start | bytes 786440 | tf_op jit(solution)/shard_map/ppermute | solution.py:291
  93.1 21.9 %collective-permute-start.13 = (bf16[1,64,4096]{2,1,0:T(8,128)(2,1)S(1)}, bf16[1,64,4096]{2,1,0:T(8,128)(2,1)S(1)}, u32[]{:S(2)}, u32[]{:S(2)}) collective-permute-start(bf16[1,64,4096]{2,1,0:T(8,128)(2,1)S(1)} %get-tuple-element.51), channel_id=1, source_target_pairs={{0,8},{4,12},{8,0},{12,4},{1,9},{5,13},{9,1},{13,5},{2,10},{6,14},... | collective-permute-start | bytes 1572872 | tf_op jit(solution)/shard_map/ppermute | solution.py:291
  98.8 24.3 %collective-permute-start.19 = (bf16[1,64,4096]{2,1,0:T(8,128)(2,1)S(1)}, bf16[1,64,4096]{2,1,0:T(8,128)(2,1)S(1)}, u32[]{:S(2)}, u32[]{:S(2)}) collective-permute-start(bf16[1,64,4096]{2,1,0:T(8,128)(2,1)S(1)} %get-tuple-element.50), channel_id=1, source_target_pairs={{0,8},{4,12},{8,0},{12,4},{1,9},{5,13},{9,1},{13,5},{2,10},{6,14},... | collective-permute-start | bytes 1572872 | tf_op jit(solution)/shard_map/ppermute | solution.py:291
  114.2 6.8 %collective-permute-start.20 = (f32[2,64,4096]{2,1,0:T(8,128)}, f32[2,64,4096]{2,1,0:T(8,128)}, u32[]{:S(2)}, u32[]{:S(2)}) collective-permute-start(f32[2,64,4096]{2,1,0:T(8,128)} %get-tuple-element.40), channel_id=1, source_target_pairs={{0,4},{4,0},{8,12},{12,8},{1,5},{5,1},{9,13},{13,9},{2,6},{6,2},{1... | collective-permute-start | bytes 6291464 | tf_op jit(solution)/shard_map/ppermute | solution.py:288
  115.0 0.8 copy-start.25
  116.5 4.5 %copy-start.11 = (f32[2,64,4096]{2,1,0:T(8,128)S(1)}, f32[2,64,4096]{2,1,0:T(8,128)}, u32[]{:S(2)}) copy-start(f32[2,64,4096]{2,1,0:T(8,128)} %get-tuple-element.36.keep) | copy-start | bytes 6291460
  119.4 11.2 %collective-permute-start.14 = (bf16[32,4096]{1,0:T(8,128)(2,1)}, bf16[32,4096]{1,0:T(8,128)(2,1)S(1)}, u32[]{:S(2)}, u32[]{:S(2)}) collective-permute-start(bf16[32,4096]{1,0:T(8,128)(2,1)} %shard_map.123), channel_id=1, source_target_pairs={{0,8},{4,12},{8,0},{12,4},{1,9},{5,13},{9,1},{13,5},{2,10},{6,14},... | collective-permute-start | bytes 786440 | tf_op jit(solution)/shard_map/ppermute | solution.py:291
  123.1 4.9 %copy-start.6 = (s32[512,1]{1,0:T(8,128)S(1)}, s32[512,1]{1,0:T(8,128)}, u32[]{:S(2)}) copy-start(s32[512,1]{1,0:T(8,128)} %copy.47) | copy-start | bytes 6148
  123.1 7.5 %copy-start.12 = (bf16[32,4096]{1,0:T(8,128)(2,1)S(1)}, bf16[32,4096]{1,0:T(8,128)(2,1)}, u32[]{:S(2)}) copy-start(bf16[32,4096]{1,0:T(8,128)(2,1)} %shard_map.123) | copy-start | bytes 786436
  123.1 0.8 copy-start.26
  127.6 15.0 %collective-permute-start.21 = (bf16[64,4096]{1,0:T(8,128)(2,1)}, bf16[64,4096]{1,0:T(8,128)(2,1)S(1)}, u32[]{:S(2)}, u32[]{:S(2)}) collective-permute-start(bf16[64,4096]{1,0:T(8,128)(2,1)} %shard_map.125), channel_id=1, source_target_pairs={{0,8},{4,12},{8,0},{12,4},{1,9},{5,13},{9,1},{13,5},{2,10},{6,14},... | collective-permute-start | bytes 1572872 | tf_op jit(solution)/shard_map/ppermute | solution.py:291
  128.9 24.3 %collective-permute-start.26 = (bf16[2,32,4096]{2,1,0:T(8,128)(2,1)S(1)}, bf16[2,32,4096]{2,1,0:T(8,128)(2,1)}, u32[]{:S(2)}, u32[]{:S(2)}) collective-permute-start(bf16[2,32,4096]{2,1,0:T(8,128)(2,1)S(1)} %fusion), channel_id=1, source_target_pairs={{0,8},{4,12},{8,0},{12,4},{1,9},{5,13},{9,1},{13,5},{2,10},{6,14},... | collective-permute-start | bytes 1572872 | tf_op jit(solution)/shard_map/ppermute | solution.py:291
  130.6 25.3 %copy-start.3 = (bf16[64,4096]{1,0:T(8,128)(2,1)}, bf16[64,4096]{1,0:T(8,128)(2,1)S(1)}, u32[]{:S(2)}) copy-start(bf16[64,4096]{1,0:T(8,128)(2,1)S(1)} %pad_maximum_fusion.4.near) | copy-start | bytes 1572868
  130.6 25.8 %collective-permute-start.15 = (bf16[64,4096]{1,0:T(8,128)(2,1)S(1)}, bf16[64,4096]{1,0:T(8,128)(2,1)S(1)}, u32[]{:S(2)}, u32[]{:S(2)}) collective-permute-start(bf16[64,4096]{1,0:T(8,128)(2,1)S(1)} %pad_maximum_fusion.4.near), channel_id=1, source_target_pairs={{0,4},{4,0},{8,12},{12,8},{1,5},{5,1},{9,13},{13,9},{2,6},{6,2},{1... | collective-permute-start | bytes 1572872 | tf_op jit(solution)/shard_map/ppermute | solution.py:288
  143.8 12.2 %copy-start.2 = (bf16[128,4096]{1,0:T(8,128)(2,1)}, bf16[128,4096]{1,0:T(8,128)(2,1)S(1)}, u32[]{:S(2)}) copy-start(bf16[128,4096]{1,0:T(8,128)(2,1)S(1)} %pad_maximum_fusion.3.near) | copy-start | bytes 3145732
  143.8 32.8 %collective-permute-start.22 = (bf16[128,4096]{1,0:T(8,128)(2,1)S(1)}, bf16[128,4096]{1,0:T(8,128)(2,1)S(1)}, u32[]{:S(2)}, u32[]{:S(2)}) collective-permute-start(bf16[128,4096]{1,0:T(8,128)(2,1)S(1)} %pad_maximum_fusion.3.near), channel_id=1, source_target_pairs={{0,4},{4,0},{8,12},{12,8},{1,5},{5,1},{9,13},{13,9},{2,6},{6,2},{1... | collective-permute-start | bytes 3145736 | tf_op jit(solution)/shard_map/ppermute | solution.py:288
  155.9 20.5 %copy-start.13 = (bf16[32,4096]{1,0:T(8,128)(2,1)S(1)}, bf16[32,4096]{1,0:T(8,128)(2,1)}, u32[]{:S(2)}) copy-start(bf16[32,4096]{1,0:T(8,128)(2,1)} %shard_map.127) | copy-start | bytes 786436
  155.9 20.4 %collective-permute-start.27 = (bf16[32,4096]{1,0:T(8,128)(2,1)}, bf16[32,4096]{1,0:T(8,128)(2,1)S(1)}, u32[]{:S(2)}, u32[]{:S(2)}) collective-permute-start(bf16[32,4096]{1,0:T(8,128)(2,1)} %shard_map.127), channel_id=1, source_target_pairs={{0,8},{4,12},{8,0},{12,4},{1,9},{5,13},{9,1},{13,5},{2,10},{6,14},... | collective-permute-start | bytes 786440 | tf_op jit(solution)/shard_map/ppermute | solution.py:291
  156.4 0.8 copy-start.8
  171.3 43.4 %collective-permute-start.18 = (bf16[4,8,2048]{2,1,0:T(8,128)(2,1)S(1)}, bf16[4,8,2048]{2,1,0:T(8,128)(2,1)S(1)}, u32[]{:S(2)}, u32[]{:S(2)}) collective-permute-start(bf16[4,8,2048]{2,1,0:T(8,128)(2,1)S(1)} %get-tuple-element.60), channel_id=1, source_target_pairs={{0,3},{1,0},{2,1},{3,2},{4,7},{5,4},{6,5},{7,6},{8,11},{9,8},{10,9... | collective-permute-start | bytes 393224 | tf_op jit(solution)/shard_map/ppermute | solution.py:450
  175.8 40.5 %collective-permute-start.16 = (bf16[4,8,2048]{2,1,0:T(8,128)(2,1)S(1)}, bf16[4,8,2048]{2,1,0:T(8,128)(2,1)S(1)}, u32[]{:S(2)}, u32[]{:S(2)}) collective-permute-start(bf16[4,8,2048]{2,1,0:T(8,128)(2,1)S(1)} %get-tuple-element.61), channel_id=1, source_target_pairs={{0,1},{1,2},{2,3},{3,0},{4,5},{5,6},{6,7},{7,4},{8,9},{9,10},{10,1... | collective-permute-start | bytes 393224 | tf_op jit(solution)/shard_map/ppermute | solution.py:450
  175.8 40.5 %collective-permute-start.17 = (bf16[4,8,2048]{2,1,0:T(8,128)(2,1)S(1)}, bf16[4,8,2048]{2,1,0:T(8,128)(2,1)S(1)}, u32[]{:S(2)}, u32[]{:S(2)}) collective-permute-start(bf16[4,8,2048]{2,1,0:T(8,128)(2,1)S(1)} %get-tuple-element.62), channel_id=1, source_target_pairs={{0,2},{1,3},{2,0},{3,1},{4,6},{5,7},{6,4},{7,5},{8,10},{9,11},{10,... | collective-permute-start | bytes 393224 | tf_op jit(solution)/shard_map/ppermute | solution.py:450
  176.4 16.4 %copy-start.4 = (bf16[64,4096]{1,0:T(8,128)(2,1)}, bf16[64,4096]{1,0:T(8,128)(2,1)S(1)}, u32[]{:S(2)}) copy-start(bf16[64,4096]{1,0:T(8,128)(2,1)S(1)} %pad_maximum_fusion.5.near) | copy-start | bytes 1572868
  176.4 17.9 %collective-permute-start.28 = (bf16[64,4096]{1,0:T(8,128)(2,1)S(1)}, bf16[64,4096]{1,0:T(8,128)(2,1)S(1)}, u32[]{:S(2)}, u32[]{:S(2)}) collective-permute-start(bf16[64,4096]{1,0:T(8,128)(2,1)S(1)} %pad_maximum_fusion.5.near), channel_id=1, source_target_pairs={{0,4},{4,0},{8,12},{12,8},{1,5},{5,1},{9,13},{13,9},{2,6},{6,2},{1... | collective-permute-start | bytes 1572872 | tf_op jit(solution)/shard_map/ppermute | solution.py:288
  176.5 1.1 copy-start.5
  194.4 0.8 copy-start.9
  208.0 24.2 %copy-start.19 = (pred[4]{0:T(512)(128)(4,1)S(1)}, pred[4]{0:T(512)(128)(4,1)}, u32[]{:S(2)}) copy-start(pred[4]{0:T(512)(128)(4,1)} %copy-done.18) | copy-start | bytes 16
  209.2 11.7 %collective-permute-start.29 = (bf16[4,8,2048]{2,1,0:T(8,128)(2,1)S(1)}, bf16[4,8,2048]{2,1,0:T(8,128)(2,1)S(1)}, u32[]{:S(2)}, u32[]{:S(2)}) collective-permute-start(bf16[4,8,2048]{2,1,0:T(8,128)(2,1)S(1)} %get-tuple-element.57), channel_id=1, source_target_pairs={{0,1},{1,2},{2,3},{3,0},{4,5},{5,6},{6,7},{7,4},{8,9},{9,10},{10,1... | collective-permute-start | bytes 393224 | tf_op jit(solution)/shard_map/ppermute | solution.py:450
  214.7 15.7 %collective-permute-start.31 = (bf16[4,8,2048]{2,1,0:T(8,128)(2,1)S(1)}, bf16[4,8,2048]{2,1,0:T(8,128)(2,1)S(1)}, u32[]{:S(2)}, u32[]{:S(2)}) collective-permute-start(bf16[4,8,2048]{2,1,0:T(8,128)(2,1)S(1)} %get-tuple-element.58), channel_id=1, source_target_pairs={{0,3},{1,0},{2,1},{3,2},{4,7},{5,4},{6,5},{7,6},{8,11},{9,8},{10,9... | collective-permute-start | bytes 393224 | tf_op jit(solution)/shard_map/ppermute | solution.py:450
  214.7 15.7 %collective-permute-start.30 = (bf16[4,8,2048]{2,1,0:T(8,128)(2,1)S(1)}, bf16[4,8,2048]{2,1,0:T(8,128)(2,1)S(1)}, u32[]{:S(2)}, u32[]{:S(2)}) collective-permute-start(bf16[4,8,2048]{2,1,0:T(8,128)(2,1)S(1)} %get-tuple-element.59), channel_id=1, source_target_pairs={{0,2},{1,3},{2,0},{3,1},{4,6},{5,7},{6,4},{7,5},{8,10},{9,11},{10,... | collective-permute-start | bytes 393224 | tf_op jit(solution)/shard_map/ppermute | solution.py:450
  217.2 33.3 %copy-start.22 = (pred[64]{0:T(512)(128)(4,1)S(1)}, pred[64]{0:T(512)(128)(4,1)}, u32[]{:S(2)}) copy-start(pred[64]{0:T(512)(128)(4,1)} %broadcast_in_dim.172) | copy-start | bytes 196
  217.9 14.4 %collective-permute-start.25 = (bf16[4,16,2048]{2,1,0:T(8,128)(2,1)S(1)}, bf16[4,16,2048]{2,1,0:T(8,128)(2,1)S(1)}, u32[]{:S(2)}, u32[]{:S(2)}) collective-permute-start(bf16[4,16,2048]{2,1,0:T(8,128)(2,1)S(1)} %get-tuple-element.52), channel_id=1, source_target_pairs={{0,3},{1,0},{2,1},{3,2},{4,7},{5,4},{6,5},{7,6},{8,11},{9,8},{10,9... | collective-permute-start | bytes 786440 | tf_op jit(solution)/shard_map/ppermute | solution.py:450
  220.8 14.6 %collective-permute-start.23 = (bf16[4,16,2048]{2,1,0:T(8,128)(2,1)S(1)}, bf16[4,16,2048]{2,1,0:T(8,128)(2,1)S(1)}, u32[]{:S(2)}, u32[]{:S(2)}) collective-permute-start(bf16[4,16,2048]{2,1,0:T(8,128)(2,1)S(1)} %get-tuple-element.53), channel_id=1, source_target_pairs={{0,1},{1,2},{2,3},{3,0},{4,5},{5,6},{6,7},{7,4},{8,9},{9,10},{10,1... | collective-permute-start | bytes 786440 | tf_op jit(solution)/shard_map/ppermute | solution.py:450
  220.8 27.8 %collective-permute-start.24 = (bf16[4,16,2048]{2,1,0:T(8,128)(2,1)S(1)}, bf16[4,16,2048]{2,1,0:T(8,128)(2,1)S(1)}, u32[]{:S(2)}, u32[]{:S(2)}) collective-permute-start(bf16[4,16,2048]{2,1,0:T(8,128)(2,1)S(1)} %get-tuple-element.54), channel_id=1, source_target_pairs={{0,2},{1,3},{2,0},{3,1},{4,6},{5,7},{6,4},{7,5},{8,10},{9,11},{10,... | collective-permute-start | bytes 786440 | tf_op jit(solution)/shard_map/ppermute | solution.py:450
  231.4 20.1 %copy-start.1 = (bf16[4,2,256,256]{3,2,1,0:T(8,128)(2,1)S(1)}, bf16[4,2,256,256]{3,2,1,0:T(8,128)(2,1)}, u32[]{:S(2)}) copy-start(bf16[4,2,256,256]{3,2,1,0:T(8,128)(2,1)} %param.20) | copy-start | bytes 3145732

commit v4 on v3

--- a/solution.py
+++ b/solution.py
@@ -8,7 +8,7 @@
 from jax.sharding import PartitionSpec as P
 
 CAP = 128
-CHUNKS = (1, 2, 1)
+CHUNKS = (2, 1, 1)
 SHORT = 120e9
 VMEM = 56 * 1024 * 1024
 BF = jnp.bfloat16
@@ -24,10 +24,22 @@
     return pl.BlockSpec(shape, lambda *_: zeros)
 
 
-def pack_body(owners, per_owner, kinds, capacity, scal, x, sl, ss, table, out, code):
+def pack_body(owners, per_owner, kinds, stride, capacity, col_tiles, scal, x, sl, ss, out, code, table):
     tile = 256
     rows, held = x.shape
     here = held // tile
+    me = scal[0]
+    height = table.shape[0]
+    at_row = lax.broadcasted_iota(jnp.int32, (height, 128), 0)
+    at_lane = lax.broadcasted_iota(jnp.int32, (height, 128), 1)
+    known = jnp.zeros((height, 128), jnp.int32)
+    for s in range(owners * per_owner):
+        back = (s // per_owner - me + owners) % owners
+        for j in range(kinds):
+            place = scal[1 + owners + (back * per_owner + s % per_owner) * stride + j]
+            known = jnp.where((at_row == s) & (at_lane == j), place // col_tiles, known)
+            known = jnp.where((at_row == s) & (at_lane == 64 + j), place % col_tiles, known)
+    table[...] = known.astype(F32).astype(BF)
     owner_l = sl[...] // per_owner
     first = lax.broadcasted_iota(jnp.int32, (rows, rows), 0)
     second = lax.broadcasted_iota(jnp.int32, (rows, rows), 1)
@@ -39,10 +51,10 @@
         target = target + jnp.where(owner_l == o, scal[1 + o] * capacity, 0)
     hot = lax.broadcasted_iota(jnp.int32, (owners * capacity, rows), 0) == target
     hot = jnp.where(hot, 1.0, 0.0).astype(BF)
-    lanes = lax.broadcasted_iota(jnp.int32, (rows, table.shape[0]), 1)
+    lanes = lax.broadcasted_iota(jnp.int32, (rows, height), 1)
     slot_hot = jnp.where(ss[...] == lanes, 1.0, 0.0).astype(BF)
     block = jnp.dot(slot_hot, table[...], preferred_element_type=F32)
-    block = block - (scal[0] * here).astype(F32)
+    block = block - (me * here).astype(F32)
     for j in range(kinds):
         at = block[:, j : j + 1]
         picked = jnp.zeros((rows, tile), BF)
@@ -51,24 +63,26 @@
         out[:, j * tile : (j + 1) * tile] = jnp.dot(hot, picked, preferred_element_type=F32).astype(BF)
 
 
-def pack(scal, x, sl, ss, table, owners, per_owner, kinds):
+def pack(scal, x, sl, ss, owners, per_owner, kinds, stride, col_tiles):
     rows = x.shape[0]
     width = kinds * 256
+    height = -(-owners * per_owner // 128) * 128
     return pl.pallas_call(
-        functools.partial(pack_body, owners, per_owner, kinds, CAP),
+        functools.partial(pack_body, owners, per_owner, kinds, stride, CAP, col_tiles),
         grid_spec=pltpu.PrefetchScalarGridSpec(
             num_scalar_prefetch=1,
             grid=(1,),
-            in_specs=[whole(x.shape), whole((1, rows)), whole((rows, 1)), whole(table.shape)],
-            out_specs=[whole((owners * CAP, width)), whole((1, rows))],
+            in_specs=[whole(x.shape), whole((1, rows)), whole((rows, 1))],
+            out_specs=[whole((owners * CAP, width)), whole((1, rows)), whole((height, 128))],
         ),
         out_shape=[
             jax.ShapeDtypeStruct((owners * CAP, width), BF),
             jax.ShapeDtypeStruct((1, rows), jnp.int32),
+            jax.ShapeDtypeStruct((height, 128), BF),
         ],
         compiler_params=pltpu.CompilerParams(vmem_limit_bytes=VMEM),
         cost_estimate=cost(SHORT, 4e6),
-    )(scal, x, sl, ss, table)
+    )(scal, x, sl, ss)
 
 
 def product_body(owners, per_owner, per_slot, pieces, scal, x, gt, ut, code, out):
@@ -157,12 +171,15 @@
     )(scal, *[view] * owners, wg, wu)
 
 
-def activate_body(per_slot, start, each, parts, keep, core, *refs):
-    gots, (delta, where, out) = refs[:parts], refs[parts:]
+def activate_body(per_slot, start, each, row, parts, keep, core, *refs):
+    gots, (delta, slot, table, out) = refs[:parts], refs[parts:]
     tile = 256
     step = pl.program_id(0)
     across = out.shape[1] // tile
-    at = [where[start : start + each, k : k + 1] - step * across for k in range(2 * per_slot)]
+    lanes = lax.broadcasted_iota(jnp.int32, (each, table.shape[0]), 1)
+    hot = jnp.where(slot[row : row + each] == lanes, 1.0, 0.0).astype(BF)
+    where = jnp.dot(hot, table[...], preferred_element_type=F32) - (step * across).astype(F32)
+    at = [where[:, 64 + k : 65 + k] for k in range(2 * per_slot)]
     adds = [
         delta[start : start + each, k * tile : (k + 1) * tile].astype(F32) for k in range(2 * per_slot)
     ]
@@ -173,85 +190,115 @@
             got = gots[0][kind, :, cols] if parts == 1 else gots[kind][0, :, cols]
             total = keep[kind, :, cols] + core[kind, :, cols] + got.astype(F32)
             for k in range(kind * per_slot, (kind + 1) * per_slot):
-                total = total + jnp.where(at[k] == b, adds[k], 0.0)
+                total = total + jnp.where(at[k] == float(b), adds[k], 0.0)
             sums.append(total)
         gate, up = sums
         out[:, cols] = (gate / (1.0 + jnp.exp(-gate)) * up).astype(BF)
 
 
-def activate(keep, core, gots, delta, where, per_slot, start):
+def activate(keep, core, gots, delta, slot, table, per_slot, start, row, flops):
     each, width = gots[0].shape[1:]
     last = keep.shape[1] // each - 1
     block = min(2048, width)
     own = pl.BlockSpec((2, each, block), lambda i: (0, last, i))
     taken = [pl.BlockSpec((g.shape[0], each, block), lambda i: (0, 0, i)) for g in gots]
     return pl.pallas_call(
-        functools.partial(activate_body, per_slot, start, each, len(gots)),
+        functools.partial(activate_body, per_slot, start, each, row, len(gots)),
         grid=(width // block,),
-        in_specs=[own, own, *taken, whole(delta.shape), whole(where.shape)],
+        in_specs=[own, own, *taken, whole(delta.shape), whole(slot.shape), whole(table.shape)],
         out_specs=pl.BlockSpec((each, block), lambda i: (0, i)),
         out_shape=jax.ShapeDtypeStruct((each, width), BF),
         compiler_params=pltpu.CompilerParams(vmem_limit_bytes=VMEM),
-        cost_estimate=cost(SHORT, 24 * each * width),
-    )(keep, core, *gots, delta, where)
-
-
-def down_body(width_tiles, here, count, start, scal, far, near, w, tiles, slot, out, hid):
+        cost_estimate=cost(flops, 24 * each * width),
+    )(keep, core, *gots, delta, slot, table)
+
+
+def down_body(width_tiles, here, plan, owners, per_owner, per_slot, start, scal, far, near, w, *refs):
+    tiles, (slot, out, hid, listed, number) = refs[: len(plan)], refs[len(plan) :]
     tile = 256
-    me = scal[0]
     across = out.shape[1] // tile
     step = pl.program_id(0)
     half = far.shape[0]
+    stride = 3 * per_slot
+    patterns = scal.shape[0] - owners * per_owner * stride
 
     @pl.when(step == 0)
     def _():
         hid[:half] = far[...]
         hid[half:] = near[...]
+        me = scal[0]
+        for r, (base, run) in enumerate(plan):
+            for at in range(number.shape[1]):
+                number[r, at] = 0
+
+            def one(i, carry):
+                local = i // per_slot
+                which = scal[base + local // run] + local % run
+                back = (which // per_owner - me + owners) % owners
+                row = back * per_owner + which % per_owner
+                place = scal[patterns + row * stride + 2 * per_slot + i % per_slot]
+                block = place % width_tiles - me * here
+
+                @pl.when((block >= 0) & (block < here))
+                def _():
+                    at = block // across
+                    n = number[r, at]
+                    listed[r * number.shape[1] + at, 4 * n] = i
+                    listed[r * number.shape[1] + at, 4 * n + 1] = which
+                    listed[r * number.shape[1] + at, 4 * n + 2] = place // width_tiles
+                    listed[r * number.shape[1] + at, 4 * n + 3] = block % across
+                    number[r, at] = n + 1
+
+                return carry
+
+            lax.fori_loop(0, tiles[r].shape[0], one, 0)
 
     out[...] = jnp.dot(hid[...], w[...], preferred_element_type=F32)
-
-    def one(i, carry):
-        place = scal[1 + count + i]
-        block = place % width_tiles - me * here - step * across
-
-        @pl.when((block >= 0) & (block < across))
-        def _():
-            source = hid[:, pl.ds(pl.multiple_of((place // width_tiles) * tile, tile), tile)]
-            hit = slot[start : start + 2 * half] == scal[1 + i]
+    for r in range(len(plan)):
+        entry = r * number.shape[1] + step
+
+        def add(n, carry):
+            i = listed[entry, 4 * n]
+            col = pl.multiple_of(listed[entry, 4 * n + 2] * tile, tile)
+            source = hid[:, pl.ds(col, tile)]
+            hit = slot[start : start + 2 * half] == listed[entry, 4 * n + 1]
             picked = jnp.where(hit, source, jnp.zeros_like(source))
-            add = jnp.dot(picked, tiles[i], preferred_element_type=F32)
-            cols = pl.ds(pl.multiple_of(block * tile, tile), tile)
-            out[:, cols] = out[:, cols] + add
-
-        return carry
-
-    lax.fori_loop(0, count, one, 0)
-
-
-def down(scal, far, near, w, tiles, slot, width_tiles, start):
+            cols = pl.ds(pl.multiple_of(listed[entry, 4 * n + 3] * tile, tile), tile)
+            out[:, cols] = out[:, cols] + jnp.dot(picked, tiles[r][i], preferred_element_type=F32)
+            return carry
+
+        lax.fori_loop(0, number[r, step], add, 0)
+
+
+def down(scal, far, near, w, tiles, plan, slot, width_tiles, owners, per_owner, per_slot, start, flops):
     rows, depth = 2 * far.shape[0], far.shape[1]
     width = w.shape[1]
     block = min(512, width)
-    count = tiles.shape[0]
+    steps = width // block
+    most = max(t.shape[0] for t in tiles)
     return pl.pallas_call(
-        functools.partial(down_body, width_tiles, width // 256, count, start),
+        functools.partial(down_body, width_tiles, width // 256, plan, owners, per_owner, per_slot, start),
         grid_spec=pltpu.PrefetchScalarGridSpec(
             num_scalar_prefetch=1,
-            grid=(width // block,),
+            grid=(steps,),
             in_specs=[
                 whole(far.shape),
                 whole(near.shape),
                 pl.BlockSpec((depth, block), lambda i, s: (0, i)),
-                whole(tiles.shape),
+                *[whole(t.shape) for t in tiles],
                 whole(slot.shape),
             ],
             out_specs=pl.BlockSpec((rows, block), lambda i, s: (0, i)),
-            scratch_shapes=[pltpu.VMEM((rows, depth), BF)],
+            scratch_shapes=[
+                pltpu.VMEM((rows, depth), BF),
+                pltpu.SMEM((len(tiles) * steps, 4 * most), jnp.int32),
+                pltpu.SMEM((len(tiles), steps), jnp.int32),
+            ],
         ),
         out_shape=jax.ShapeDtypeStruct((rows, width), F32),
         compiler_params=pltpu.CompilerParams(vmem_limit_bytes=VMEM),
-        cost_estimate=cost(3 * rows * depth * width, 3 * depth * width),
-    )(scal, far, near, w, tiles, slot)
+        cost_estimate=cost(flops, 1e6),
+    )(scal, far, near, w, *tiles, slot)
 
 
 def shards(
@@ -310,53 +357,42 @@
     hit = row_variant[:, None] == jnp.arange(variant_slot.shape[0], dtype=jnp.int32)[None, :]
     slot_rows = jnp.sum(jnp.where(hit, variant_slot[None, :], 0), axis=1)
 
+    def after(x, *earlier):
+        return lax.optimization_barrier((x, *earlier))[0]
+
+    kinds = 2 * per_slot
     own = jnp.concatenate([gate_pattern, up_pattern, down_pattern], axis=1)
-    seen = jnp.stack([own] + [lax.ppermute(own, "delta", [(i, (i - k) % owners) for i in range(owners)]) for k in range(1, owners)])
-    back = (jnp.arange(owners, dtype=jnp.int32) - me) % owners
-    by_owner = jnp.sum(
-        jnp.where(
-            (back[:, None] == jnp.arange(owners, dtype=jnp.int32)[None, :])[:, :, None, None], seen[None], 0
-        ),
-        axis=1,
-    ).reshape(slots, 3 * per_slot)
-    kinds = 2 * per_slot
+    seen = [own] + [
+        lax.ppermute(own, "delta", [(i, (i - k) % owners) for i in range(owners)]) for k in range(1, owners)
+    ]
+    patterns = jnp.concatenate([s.reshape(-1) for s in seen])
     at_home = jnp.stack(
         [((d // 2) - my_y - 1) % ys + ys * jnp.where(d % 2 == my_core, 1, 0) for d in range(owners)]
     ).astype(jnp.int32)
-    scal = jnp.concatenate([me.astype(jnp.int32)[None], at_home])
-    blocks_in = (by_owner[:, :kinds] // col_tiles).astype(BF)
-    table = jnp.pad(blocks_in, ((0, -slots % 128), (0, -kinds % 128)))
-
+    scal = jnp.concatenate([me.astype(jnp.int32)[None], at_home, patterns])
+
+    flat_tiles = down_tiles.reshape(-1, 256, 256)
     if groups == 2 and per_owner % 2 == 0:
         part = per_owner // 2
         mine_g = lax.axis_index("groups")
-        piece = lax.dynamic_slice_in_dim(down_tiles, mine_g * part, part, 0)
-        gathered = jnp.stack([y_move(piece, -k) for k in range(1, ys)] + [piece])
-        other = lax.ppermute(gathered, "groups", [(0, 1), (1, 0)])
-        both = jnp.stack([gathered, other])
-        firsts = [mine_g * part, (1 - mine_g) * part]
+        piece = lax.dynamic_slice_in_dim(flat_tiles, mine_g * part * per_slot, part * per_slot, 0)
+        halves = [mine_g * part, (1 - mine_g) * part]
     else:
-        part = per_owner
-        gathered = jnp.stack([y_move(down_tiles, -k) for k in range(1, ys)] + [down_tiles])
-        other = gathered
-        both = gathered[None]
-        firsts = [0]
-    all_tiles = jnp.stack([core_swap(both), both]).reshape(-1, 256, 256)
-    tile_slots = jnp.stack(
-        [
-            (y * 2 + c) * per_owner + first + s
-            for c in (1 - my_core, my_core)
-            for first in firsts
-            for y in order_y
-            for s in range(part)
-        ]
-    ).astype(jnp.int32)
-    picked = tile_slots[:, None] == jnp.arange(slots, dtype=jnp.int32)[None, :]
-    places = jnp.sum(jnp.where(picked[:, :, None], by_owner[None, :, kinds:], 0), axis=1).reshape(-1)
-    down_scal = jnp.concatenate([me.astype(jnp.int32)[None], jnp.repeat(tile_slots, per_slot), places])
-
-    def after(x, *earlier):
-        return lax.optimization_barrier((x, *earlier))[0]
+        part, piece, halves = per_owner, flat_tiles, [0]
+    from_y = jnp.concatenate([y_move(piece, -k) for k in range(1, ys)])
+    tiles = [from_y]
+    if len(halves) == 2:
+        tiles.append(lax.ppermute(from_y, "groups", [(0, 1), (1, 0)]))
+    arrived = tuple(tiles)
+    firsts, plan = [], []
+    for core in (my_core, 1 - my_core):
+        for first in halves:
+            plan.append((1 + len(firsts), part))
+            firsts.extend((y * 2 + core) * per_owner + first for y in order_y[:-1])
+        plan.append((1 + len(firsts), per_owner))
+        firsts.append((my_y * 2 + core) * per_owner)
+    plan = tuple(plan)
+    down_scal = jnp.concatenate([jnp.stack([me] + firsts).astype(jnp.int32), patterns])
 
     starts = [sum(sizes[:i]) for i in range(len(sizes))]
     inners = [s // owners for s in starts]
@@ -371,7 +407,7 @@
 
     def exchange(i):
         each = sizes[i] // owners
-        parts = [slice(0, 2)] if CHUNKS[i] == 1 else [slice(0, 1), slice(1, 2)]
+        parts = [slice(0, 2)]
         sends[i], gots[i] = [], []
         for part in parts:
             got = None
@@ -395,8 +431,16 @@
         return total
 
     multiply(0)
-    packed, code = pack(
-        after(scal, kept[0], gathered), tokens, slot_rows[None, :], slot_rows[:, None], table, owners, per_owner, kinds
+    packed, code, table = pack(
+        after(scal, kept[0], from_y),
+        tokens,
+        slot_rows[None, :],
+        slot_rows[:, None],
+        owners,
+        per_owner,
+        kinds,
+        3 * per_slot,
+        col_tiles,
     )
     exchange(0)
     packed = halve(packed.reshape(owners, CAP, -1))
@@ -409,11 +453,6 @@
         for size, start, inner in zip(sizes, starts, inners)
         for home in range(owners)
     )
-    slot_home = jnp.concatenate([slot_q[s + size - size // owners : s + size] for s, size in zip(starts, sizes)])
-    hot_home = slot_home[:, None] == jnp.arange(slots, dtype=jnp.int32)[None, :]
-    where = jnp.sum(
-        jnp.where(hot_home[:, :, None], (by_owner[:, :kinds] % col_tiles)[None], 0), axis=1
-    )
     ss_q = slot_q[:, None]
 
     for i in range(1, count):
@@ -421,7 +460,7 @@
             multiply(1, *sends[0], packed)
             features = finish(packed, kept[1])
             spread = product(
-                after(scal, kept[1], *gots[0], other), features, gate_tiles, up_tiles, code_q[None, :], owners, per_owner, pieces
+                after(scal, kept[1], *gots[0], *arrived), features, gate_tiles, up_tiles, code_q[None, :], owners, per_owner, pieces
             )
             exchange(1)
             spread = halve(spread)
@@ -432,36 +471,66 @@
             exchange(i)
     home_delta = finish(spread, kept[2])
 
+    near_tiles = [*tiles, flat_tiles]
+    all_tiles = near_tiles + [core_swap(after(t, kept[1])) for t in near_tiles]
+
     def finish_hidden(i, *earlier):
-        hid = activate(kept[i], cores[i], gots[i], home_delta, after(where, *earlier), per_slot, inners[i])
-        return hid, jnp.concatenate([y_move(hid, -k) for k in range(1, ys)] + [hid])
-
-    def finish_down(i, chip, *earlier):
+        each = sizes[i] // owners
+        hid = activate(
+            kept[i],
+            cores[i],
+            gots[i],
+            home_delta,
+            ss_q,
+            after(table, *earlier),
+            per_slot,
+            inners[i],
+            starts[i] + sizes[i] - each,
+            SHORT if i == 0 else 1e9,
+        )
+        return hid, [y_move(hid, -k) for k in range(1, ys)]
+
+    def join(hid, moved, *earlier):
+        return jnp.concatenate([after(m, *earlier) for m in moved] + [hid])
+
+    def finish_down(i, chip, earlier, sent=()):
         out = down(
-            after(down_scal, *earlier), core_swap(chip), chip, down_weight, all_tiles, ss_q, width_tiles, starts[i]
+            after(down_scal, *earlier),
+            core_swap(chip),
+            chip,
+            down_weight,
+            all_tiles,
+            plan,
+            ss_q,
+            width_tiles,
+            owners,
+            per_owner,
+            per_slot,
+            starts[i],
+            SHORT if i == count - 2 else 1e9,
         )
         blocks = out.reshape(owners, shift, sizes[i] // (owners * shift), shard_width).transpose(1, 0, 2, 3)
-        total = lax.dynamic_index_in_dim(blocks, here_t, 0, keepdims=False)
-        gone = [
-            lax.dynamic_index_in_dim(blocks, (here_t + k) % shift, 0, keepdims=False).astype(BF)
-            for k in range(1, shift)
-        ]
-        for k in range(1, shift):
-            total = total + lax.ppermute(
-                gone[k - 1], "tensor", [(i, (i + k) % shift) for i in range(shift)]
-            ).astype(F32)
+        gone = blocks.astype(BF)
+        came = lax.all_to_all(after(gone, *sent), "tensor", 0, 0)
+        own = lax.dynamic_index_in_dim(blocks, here_t, 0, keepdims=False)
+        total = own
+        for t in range(shift):
+            total = total + jnp.where(t == here_t, 0.0, came[t].astype(F32))
         return gone, total.astype(BF)
 
-    chips, result = [], []
-    hid, chip = finish_hidden(0, kept[count - 1], all_tiles, gots[1][0])
-    chips.append(chip)
+    result = []
+    hid, moved = finish_hidden(0, kept[count - 1], gots[1][0])
+    chip, out = None, ()
     for i in range(1, count):
-        hid, chip = finish_hidden(i, hid, *sends[count - 1])
-        chips.append(chip)
-    gone = ()
-    for i in range(count):
-        gone, total = finish_down(i, chips[i], *gone)
+        later, moved_later = finish_hidden(i, hid, *sends[count - 1], *out)
+        if i == 1:
+            chip = join(hid, moved, later)
+        next_chip = join(later, moved_later)
+        gone, total = finish_down(i - 1, chip, (later, *result[:-1]), result[-1:])
+        hid, chip, out = later, next_chip, (gone, next_chip)
         result.append(total)
+    gone, total = finish_down(count - 1, chip, (gone, *result[:-1]), result[-1:])
+    result.append(total)
 
     placed = [jnp.take(r, at_home, axis=0).reshape(-1, shard_width) for r in result]
     return jnp.concatenate(placed, axis=0)

time: 252 us -> 232 us (0.921)
  starting transfers between devices: 41.9 us -> 28.6 us
  other arithmetic: 27.1 us -> 16.2 us
  Pallas kernels: 110 us -> 115 us
  local copies, waits for them, and re-layouts: 22.7 us -> 19.1 us
  waiting for transfers between devices: 49.4 us -> 52.4 us
    ppermute x10 -> x1, waiting for transfers between devices: 27.4 us -> 0.01 us  [shards(): tiles.append(lax.ppermute(from_y, 'groups', [(0, 1), (1, 0)]))]
    ppermute x10 -> x1, starting transfers between devices: 26.2 us -> 1.56 us  [shards(): tiles.append(lax.ppermute(from_y, 'groups', [(0, 1), (1, 0)]))]
    all_to_all x0 -> x3, waiting for transfers between devices: none -> 24.1 us  [finish_down(): came = lax.all_to_all(after(gone, *sent), 'tensor', 0, 0)]
    all_to_all x0 -> x3, starting transfers between devices: none -> 12.5 us  [finish_down(): came = lax.all_to_all(after(gone, *sent), 'tensor', 0, 0)]
    another operation x4 -> x0, other arithmetic: 8.09 us -> none  [the longest x2 4.11 us: shards(): both = jnp.stack([gathered, other])]
    reshape x2 -> x7, local copies, waits for them, and re-layouts: 0.18 us -> 7.29 us  [the longest x3 6.95 us: finish_down(): out.reshape(owners, shift, sizes[i] // (owners * shift), shard_width)]
    ppermute x10 -> x9, waiting for transfers between devices: 20.6 us -> 25.9 us  [y_move(): lax.ppermute(x, 'delta', [(i, (i + 2 * k) % owners) for i in range(owners)])]
    pallas_call x7, Pallas kernels: 57.3 us -> 62.4 us  [the longest x3 44 us: down(): pl.pallas_call(functools.partial(down_body, width_tiles, width // 256, pl...]
  transfers between devices with their start and end apart: 32 -> 27, of which waited for: 7 -> 8; matrix products, arithmetic and copies ran while one was open for 16% -> 12% of each run, Pallas kernels for 44% -> 50%
where the time goes in v4:
time: 232 us; the launch traced here: 231 us
  Pallas kernels  115 us (50%)
  waiting for transfers between devices  52.4 us (23%)
  starting transfers between devices  28.6 us (12%)
  local copies, waits for them, and re-layouts  19.1 us (8%)
  other arithmetic  16.2 us (7%)
    pallas_call x3, Pallas kernels, gate_up(): pl.pallas_call(functools.partial(gate_up_body, owners), grid_spec=pltpu.P...  47.6 us
    pallas_call x3, Pallas kernels, down(): pl.pallas_call(functools.partial(down_body, width_tiles, width // 256, pl...  44 us
    ppermute x9, waiting for transfers between devices, y_move(): lax.ppermute(x, 'delta', [(i, (i + 2 * k) % owners) for i in range(owners)])  25.9 us
    all_to_all x3, waiting for transfers between devices, finish_down(): came = lax.all_to_all(after(gone, *sent), 'tensor', 0, 0)  24.1 us
    all_to_all x3, starting transfers between devices, finish_down(): came = lax.all_to_all(after(gone, *sent), 'tensor', 0, 0)  12.5 us
    pallas_call x3, Pallas kernels, activate(): pl.pallas_call(functools.partial(activate_body, per_slot, start, each, ro...  10.7 us
    ppermute x9, starting transfers between devices, y_move(): lax.ppermute(x, 'delta', [(i, (i + 2 * k) % owners) for i in range(owners)])  9.48 us
    pallas_call x1, Pallas kernels, pack(): pl.pallas_call(functools.partial(pack_body, owners, per_owner, kinds, str...  7.78 us
  transfers between devices with their start and end apart: 27, of which 8 were waited for; matrix products, arithmetic and copies ran while one was open for 12% of the time, Pallas kernels for 50%

profile of v4, /device:TPU:0, one launch (start us, length us, event | category | flops | bytes accessed | tf_op | source)
XLA Modules:
  0.0 231.4 jit_solution(16764789374094875315)
XLA Ops:
  0.0 0.7 pad_add_fusion
  0.7 2.4 %collective-permute-start = (s32[4,6]{0,1:T(8,128)S(1)}, s32[4,6]{0,1:T(8,128)S(1)}, u32[]{:S(2)}, u32[]{:S(2)}) collective-permute-start(s32[4,6]{0,1:T(8,128)S(1)} %pad_add_fusion), channel_id=1, source_target_pairs={{0,12},{4,0},{8,4},{12,8},{1,13},{5,1},{9,5},{13,9},{2,14},{6,2},{... | collective-permute-start | bytes 296 | tf_op jit(solution)/shard_map/ppermute | solution.py:366
  3.2 0.6 collective-permute-start.1
  4.0 1.1 constant_dynamic-slice_fusion
  5.0 1.3 collective-permute-start.4
  6.3 0.7 broadcast_multiply_fusion.1
  7.0 17.9 %shard_map.118 = (f32[2,128,4096]{2,1,0:T(8,128)}, f32[2,128,4096]{2,1,0:T(8,128)}) custom-call(s32[4]{0:T(128)} %get-tuple-element.43.scal, bf16[4,8,16,2048]{3,2,1,0:T(8,128)(2,1)} %bitcast.111, bf16[4,8,16,2048]{3,2,1,0:T(8,128)(2,1)} %bitcast.112, bf16[4,8,16,2048]{3,2,1,0:T(8,128)(2,1)} %bitcast.113, bf16[4,8,16,2048]{3,2,1,0:T(8,128)(2,1)} %bitcast.114, ...), custom_call_target="tpu_custom_call" | custom-call | flops 8589934592 | bytes 33554432 | tf_op jit(solution)/shard_map/pallas_call | solution.py:159
  25.7 0.9 copy.62.ss
  27.6 0.6 concatenate.58.scal
  28.2 7.8 %shard_map.119 = (bf16[512,1024]{1,0:T(8,128)(2,1)}, s32[1,512]{1,0:T(1,128)}, bf16[128,128]{1,0:T(8,128)(2,1)}) custom-call(s32[101]{0:T(128)} %concatenate.58.scal, bf16[512,2048]{1,0:T(8,128)(2,1)} %x.1, s32[1,512]{1,0:T(1,128)} %bitcast.139, s32[512,1]{1,0:T(8,128)} %copy.62.ss), custom_call_target="tpu_custom_call" | custom-call | flops 120000004096 | bytes 4000000 | tf_op jit(solution)/shard_map/pallas_call | solution.py:70
  36.0 1.3 fusion.12
  37.4 1.8 fusion
  39.2 1.5 collective-permute-start.8
  40.8 1.6 collective-permute-start.9
  42.4 0.8 select_reduce_fusion
  43.5 0.7 collective-permute-start.10
  44.2 14.8 %shard_map.120 = (f32[2,64,4096]{2,1,0:T(8,128)}, f32[2,64,4096]{2,1,0:T(8,128)}) custom-call(s32[4]{0:T(128)} %get-tuple-element.43.scal, bf16[4,16,8,2048]{3,2,1,0:T(8,128)(2,1)} %bitcast.115, bf16[4,16,8,2048]{3,2,1,0:T(8,128)(2,1)} %bitcast.116, bf16[4,16,8,2048]{3,2,1,0:T(8,128)(2,1)} %bitcast.117, bf16[4,16,8,2048]{3,2,1,0:T(8,128)(2,1)} %bitcast.118, ...), custom_call_target="tpu_custom_call" | custom-call | flops 4294967296 | bytes 33554432 | tf_op jit(solution)/shard_map/pallas_call | solution.py:159
  59.0 11.4 %collective-permute-done.10 = bf16[128,1024]{1,0:T(8,128)(2,1)S(1)} collective-permute-done((bf16[128,1024]{1,0:T(8,128)(2,1)S(1)}, bf16[128,1024]{1,0:T(8,128)(2,1)S(1)}, u32[]{:S(2)}, u32[]{:S(2)}) %collective-permute-start.10) | collective-permute-done | bytes 262176 | tf_op jit(solution)/shard_map/ppermute | solution.py:338
  70.4 0.8 add.299.x
  71.2 4.7 %shard_map.121 = bf16[4,128,1024]{2,1,0:T(8,128)(2,1)} custom-call(s32[101]{0:T(128)} %concatenate.58.scal, bf16[128,1024]{1,0:T(8,128)(2,1)} %add.299.x, bf16[4,2,256,256]{3,2,1,0:T(8,128)(2,1)} %gt.1, bf16[4,2,256,256]{3,2,1,0:T(8,128)(2,1)} %ut.1, s32[1,512]{1,0:T(1,128)} %bitcast.136), custom_call_target="tpu_custom_call" | custom-call | flops 120000004096 | bytes 4000000 | tf_op jit(solution)/shard_map/pallas_call | solution.py:116
  75.9 2.0 slice.123
  78.1 0.9 add_select_fusion.refs_2_.refs_6_
  79.0 0.5 collective-permute-start.18
  79.5 0.7 collective-permute-done.11
  80.2 1.3 slice_add_fusion.3
  81.4 1.3 fusion.3
  82.8 1.5 collective-permute-start.7
  84.3 0.7 collective-permute-start.12
  85.0 14.8 %shard_map.122 = (f32[2,64,4096]{2,1,0:T(8,128)}, f32[2,64,4096]{2,1,0:T(8,128)}) custom-call(s32[4]{0:T(128)} %get-tuple-element.43.scal, bf16[4,16,8,2048]{3,2,1,0:T(8,128)(2,1)} %bitcast.119, bf16[4,16,8,2048]{3,2,1,0:T(8,128)(2,1)} %bitcast.120, bf16[4,16,8,2048]{3,2,1,0:T(8,128)(2,1)} %bitcast.121, bf16[4,16,8,2048]{3,2,1,0:T(8,128)(2,1)} %bitcast.122, ...), custom_call_target="tpu_custom_call" | custom-call | flops 4294967296 | bytes 33554432 | tf_op jit(solution)/shard_map/pallas_call | solution.py:159
  99.8 2.6 %collective-permute-done.12 = bf16[128,1024]{1,0:T(8,128)(2,1)S(1)} collective-permute-done((bf16[128,1024]{1,0:T(8,128)(2,1)S(1)}, bf16[128,1024]{1,0:T(8,128)(2,1)S(1)}, u32[]{:S(2)}, u32[]{:S(2)}) %collective-permute-start.12) | collective-permute-done | bytes 262176 | tf_op jit(solution)/shard_map/ppermute | solution.py:338
  102.4 0.8 add.323.refs_1_
  103.2 4.5 %shard_map.123 = bf16[64,4096]{1,0:T(8,128)(2,1)} custom-call(f32[2,128,4096]{2,1,0:T(8,128)} %get-tuple-element.33.keep, f32[2,128,4096]{2,1,0:T(8,128)} %collective-permute-done.3.core, bf16[2,64,4096]{2,1,0:T(8,128)(2,1)} %collective-permute-done.8.refs_0_, bf16[128,1024]{1,0:T(8,128)(2,1)} %add.323.refs_1_, s32[512,1]{1,0:T(8,128)} %add_select_fusion.refs_2_.refs_6_, ...), custom_call_target="tpu_custom_call" | custom-call | flops 120000004096 | bytes 6291456 | tf_op jit(solution)/shard_map/pallas_call | solution.py:205
  107.7 1.4 collective-permute-start.14
  109.1 1.0 fusion.2
  110.1 3.1 %shard_map.124 = bf16[32,4096]{1,0:T(8,128)(2,1)} custom-call(f32[2,64,4096]{2,1,0:T(8,128)} %get-tuple-element.38.keep, f32[2,64,4096]{2,1,0:T(8,128)} %collective-permute-done.6.core, bf16[2,32,4096]{2,1,0:T(8,128)(2,1)} %copy-done.17, bf16[128,1024]{1,0:T(8,128)(2,1)} %add.323.refs_1_, s32[512,1]{1,0:T(8,128)} %add_select_fusion.refs_2_.refs_6_, ...), custom_call_target="tpu_custom_call" | custom-call | flops 1000000000 | bytes 3145728 | tf_op jit(solution)/shard_map/pallas_call | solution.py:205
  113.3 0.7 collective-permute-start.20
  114.0 8.8 %collective-permute-done.14 = bf16[64,4096]{1,0:T(8,128)(2,1)S(1)} collective-permute-done((bf16[64,4096]{1,0:T(8,128)(2,1)}, bf16[64,4096]{1,0:T(8,128)(2,1)S(1)}, u32[]{:S(2)}, u32[]{:S(2)}) %collective-permute-start.14) | collective-permute-done | bytes 524320 | tf_op jit(solution)/shard_map/ppermute | solution.py:338
  123.6 3.1 %collective-permute-done.20 = bf16[32,4096]{1,0:T(8,128)(2,1)S(1)} collective-permute-done((bf16[32,4096]{1,0:T(8,128)(2,1)}, bf16[32,4096]{1,0:T(8,128)(2,1)S(1)}, u32[]{:S(2)}, u32[]{:S(2)}) %collective-permute-start.20) | collective-permute-done | bytes 262176 | tf_op jit(solution)/shard_map/ppermute | solution.py:338
  126.7 1.4 collective-permute-start.19
  128.1 0.8 pad_maximum_fusion.1.near
  128.9 0.8 copy-done.9
  129.8 0.7 concatenate.57.scal
  130.5 16.0 %shard_map.125 = f32[256,2048]{1,0:T(8,128)} custom-call(s32[103]{0:T(128)} %concatenate.57.scal, bf16[128,4096]{1,0:T(8,128)(2,1)} %collective-permute-done.15.far, bf16[128,4096]{1,0:T(8,128)(2,1)} %copy-done.4, bf16[4096,2048]{1,0:T(8,128)(2,1)} %w.5, bf16[4,256,256]{2,1,0:T(8,128)(2,1)} %copy-done.5, bf16[4,256,256]{2,1,0:T(8,128)(2,1)} %copy-done.7, ...), custom_call_target="tpu_custom_call" | custom-call | flops 1000000000 | bytes 1000000 | tf_op jit(solution)/shard_map/pallas_call | solution.py:279
  146.5 2.8 %copy.79 = bf16[4,4,16,2048]{3,2,0,1:T(8,128)(2,1)} copy(f32[4,4,16,2048]{3,2,1,0:T(8,128)} %bitcast.123) | data formatting | bytes 3145728 | tf_op jit(solution)/shard_map/reshape | solution.py:512
  149.2 0.8 copy-done.16
  150.1 3.1 %shard_map.126 = bf16[32,4096]{1,0:T(8,128)(2,1)} custom-call(f32[2,64,4096]{2,1,0:T(8,128)} %get-tuple-element.44.keep, f32[2,64,4096]{2,1,0:T(8,128)} %copy-done.2, bf16[2,32,4096]{2,1,0:T(8,128)(2,1)} %copy-done.16, bf16[128,1024]{1,0:T(8,128)(2,1)} %add.323.refs_1_, s32[512,1]{1,0:T(8,128)} %add_select_fusion.refs_2_.refs_6_, ...), custom_call_target="tpu_custom_call" | custom-call | flops 1000000000 | bytes 3145728 | tf_op jit(solution)/shard_map/pallas_call | solution.py:205
  153.5 4.5 %all-to-all-start = ((bf16[4,4,16,2048]{3,2,1,0:T(8,128)(2,1)}), bf16[4,4,16,2048]{3,2,1,0:T(8,128)(2,1)S(1)}, u32[]{:S(2)}, u32[]{:S(2)}) async-start(bf16[4,4,16,2048]{3,2,1,0:T(8,128)(2,1)} %bitcast.108), calls=%async_computation | async-start | bytes 2097152 | tf_op jit(solution)/shard_map/all_to_all | solution.py:514
  158.1 14.0 %shard_map.127 = f32[128,2048]{1,0:T(8,128)} custom-call(s32[103]{0:T(128)} %concatenate.57.scal, bf16[64,4096]{1,0:T(8,128)(2,1)} %collective-permute-done.21.far, bf16[64,4096]{1,0:T(8,128)(2,1)} %pad_maximum_fusion.1.near, bf16[4096,2048]{1,0:T(8,128)(2,1)} %w.5, bf16[4,256,256]{2,1,0:T(8,128)(2,1)} %copy-done.5, bf16[4,256,256]{2,1,0:T(8,128)(2,1)} %copy-done.7, ...), custom_call_target="tpu_custom_call" | custom-call | flops 120000004096 | bytes 1000000 | tf_op jit(solution)/shard_map/pallas_call | solution.py:279
  172.1 2.1 copy.80
  174.2 10.7 %all-to-all-done = bf16[4,4,16,2048]{3,2,1,0:T(8,128)(2,1)S(1)} async-done(((bf16[4,4,16,2048]{3,2,1,0:T(8,128)(2,1)}), bf16[4,4,16,2048]{3,2,1,0:T(8,128)(2,1)S(1)}, u32[]{:S(2)}, u32[]{:S(2)}) %all-to-all-start) | async-done | bytes 1048608 | tf_op jit(solution)/shard_map/all_to_all | solution.py:514
  184.9 1.3 fusion.6
  186.1 3.5 %all-to-all-start.1 = ((bf16[4,4,8,2048]{3,2,1,0:T(8,128)(2,1)}), bf16[4,4,8,2048]{3,2,1,0:T(8,128)(2,1)S(1)}, u32[]{:S(2)}, u32[]{:S(2)}) async-start(bf16[4,4,8,2048]{3,2,1,0:T(8,128)(2,1)} %bitcast.109), calls=%async_computation.1 | async-start | bytes 1048576 | tf_op jit(solution)/shard_map/all_to_all | solution.py:514
  190.0 1.6 collective-permute-done.23.far
  191.7 0.8 copy-done.14
  192.5 14.0 %shard_map.128 = f32[128,2048]{1,0:T(8,128)} custom-call(s32[103]{0:T(128)} %concatenate.57.scal, bf16[64,4096]{1,0:T(8,128)(2,1)} %copy-done.14, bf16[64,4096]{1,0:T(8,128)(2,1)} %copy-done.10, bf16[4096,2048]{1,0:T(8,128)(2,1)} %w.5, bf16[4,256,256]{2,1,0:T(8,128)(2,1)} %copy-done.5, bf16[4,256,256]{2,1,0:T(8,128)(2,1)} %copy-done.7, ...), custom_call_target="tpu_custom_call" | custom-call | flops 1000000000 | bytes 1000000 | tf_op jit(solution)/shard_map/pallas_call | solution.py:279
  206.4 2.1 copy.81
  208.5 1.1 fusion.9
  209.6 4.4 %all-to-all-start.2 = ((bf16[4,4,8,2048]{3,2,1,0:T(8,128)(2,1)}), bf16[4,4,8,2048]{3,2,1,0:T(8,128)(2,1)S(1)}, u32[]{:S(2)}, u32[]{:S(2)}) async-start(bf16[4,4,8,2048]{3,2,1,0:T(8,128)(2,1)} %bitcast.110), calls=%async_computation.2 | async-start | bytes 1048576 | tf_op jit(solution)/shard_map/all_to_all | solution.py:514
  214.1 0.6 gather_fusion
  214.8 0.6 gather_fusion.1
  215.4 13.4 %all-to-all-done.2 = bf16[4,4,8,2048]{3,2,1,0:T(8,128)(2,1)S(1)} async-done(((bf16[4,4,8,2048]{3,2,1,0:T(8,128)(2,1)}), bf16[4,4,8,2048]{3,2,1,0:T(8,128)(2,1)S(1)}, u32[]{:S(2)}, u32[]{:S(2)}) %all-to-all-start.2) | async-done | bytes 524320 | tf_op jit(solution)/shard_map/all_to_all | solution.py:514
  228.8 1.1 fusion.8
  229.9 0.6 gather_fusion.2
  230.5 0.8 pad_maximum_fusion.3
  (127 shorter events, 4.5 us)
Async XLA Ops:
  0.7 26.3 %collective-permute-start = (s32[4,6]{0,1:T(8,128)S(1)}, s32[4,6]{0,1:T(8,128)S(1)}, u32[]{:S(2)}, u32[]{:S(2)}) collective-permute-start(s32[4,6]{0,1:T(8,128)S(1)} %pad_add_fusion), channel_id=1, source_target_pairs={{0,12},{4,0},{8,4},{12,8},{1,13},{5,1},{9,5},{13,9},{2,14},{6,2},{... | collective-permute-start | bytes 296 | tf_op jit(solution)/shard_map/ppermute | solution.py:366
  3.2 24.0 %collective-permute-start.1 = (s32[4,6]{0,1:T(8,128)S(1)}, s32[4,6]{0,1:T(8,128)S(1)}, u32[]{:S(2)}, u32[]{:S(2)}) collective-permute-start(s32[4,6]{0,1:T(8,128)S(1)} %pad_add_fusion), channel_id=1, source_target_pairs={{0,8},{4,12},{8,0},{12,4},{1,9},{5,13},{9,1},{13,5},{2,10},{6,14},... | collective-permute-start | bytes 296 | tf_op jit(solution)/shard_map/ppermute | solution.py:366
  3.8 23.6 %collective-permute-start.2 = (s32[4,6]{0,1:T(8,128)S(1)}, s32[4,6]{0,1:T(8,128)S(1)}, u32[]{:S(2)}, u32[]{:S(2)}) collective-permute-start(s32[4,6]{0,1:T(8,128)S(1)} %pad_add_fusion), channel_id=1, source_target_pairs={{0,4},{4,8},{8,12},{12,0},{1,5},{5,9},{9,13},{13,1},{2,6},{6,10},{... | collective-permute-start | bytes 296 | tf_op jit(solution)/shard_map/ppermute | solution.py:366
  5.0 23.1 %collective-permute-start.4 = (bf16[4,256,256]{2,1,0:T(8,128)(2,1)S(1)}, bf16[4,256,256]{2,1,0:T(8,128)(2,1)S(1)}, u32[]{:S(2)}, u32[]{:S(2)}) collective-permute-start(bf16[4,256,256]{2,1,0:T(8,128)(2,1)S(1)} %constant_dynamic-slice_fusion), channel_id=1, source_target_pairs={{0,8},{4,12},{8,0},{12,4},{1,9},{5,13},{9,1},{13,5},{2,10},{6,14},... | collective-permute-start | bytes 1572872 | tf_op jit(solution)/shard_map/ppermute | solution.py:338
  7.0 18.5 %copy-start.20 = (s32[4]{0:T(128)S(1)}, s32[4]{0:T(128)}, u32[]{:S(2)}) copy-start(s32[4]{0:T(128)} %get-tuple-element.43.scal) | copy-start | bytes 52
  7.0 18.6 %copy-start.30 = (s32[512]{0:T(512)S(1)}, s32[512]{0:T(512)}, u32[]{:S(2)}) copy-start(s32[512]{0:T(512)} %param.24) | copy-start | bytes 6148
  7.0 18.6 %copy-start.31 = (s32[16]{0:T(128)S(1)}, s32[16]{0:T(128)}, u32[]{:S(2)}) copy-start(s32[16]{0:T(128)} %param.25) | copy-start | bytes 196
  24.9 12.4 %collective-permute-start.3 = (f32[2,128,4096]{2,1,0:T(8,128)}, f32[2,128,4096]{2,1,0:T(8,128)}, u32[]{:S(2)}, u32[]{:S(2)}) collective-permute-start(f32[2,128,4096]{2,1,0:T(8,128)} %get-tuple-element.34), channel_id=1, source_target_pairs={{0,4},{4,0},{8,12},{12,8},{1,5},{5,1},{9,13},{13,9},{2,6},{6,2},{1... | collective-permute-start | bytes 12582920 | tf_op jit(solution)/shard_map/ppermute | solution.py:335
  25.6 10.4 %copy-start.21 = (s32[24]{0:T(128)}, s32[24]{0:T(128)S(1)}, u32[]{:S(2)}) copy-start(s32[24]{0:T(128)S(1)} %reshape.520) | copy-start | bytes 292
  25.7 2.5 %copy-start.19 = (s32[512]{0:T(512)}, s32[512]{0:T(512)S(1)}, u32[]{:S(2)}) copy-start(s32[512]{0:T(512)S(1)} %select_reduce_fusion.1) | copy-start | bytes 6148
  27.2 8.8 %copy-start.23 = (s32[24]{0:T(128)}, s32[24]{0:T(128)S(1)}, u32[]{:S(2)}) copy-start(s32[24]{0:T(128)S(1)} %reshape.521) | copy-start | bytes 292
  27.4 8.6 %copy-start.25 = (s32[24]{0:T(128)}, s32[24]{0:T(128)S(1)}, u32[]{:S(2)}) copy-start(s32[24]{0:T(128)S(1)} %reshape.522) | copy-start | bytes 292
  27.6 8.4 %copy-start.27 = (s32[24]{0:T(128)}, s32[24]{0:T(128)S(1)}, u32[]{:S(2)}) copy-start(s32[24]{0:T(128)S(1)} %reshape.523) | copy-start | bytes 292
  28.2 12.7 %copy-start.5 = (bf16[4,256,256]{2,1,0:T(8,128)(2,1)}, bf16[4,256,256]{2,1,0:T(8,128)(2,1)S(1)}, u32[]{:S(2)}) copy-start(bf16[4,256,256]{2,1,0:T(8,128)(2,1)S(1)} %collective-permute-done.4.refs_0_) | copy-start | bytes 1572868
  28.2 9.2 %copy-start.11 = (f32[2,128,4096]{2,1,0:T(8,128)S(1)}, f32[2,128,4096]{2,1,0:T(8,128)}, u32[]{:S(2)}) copy-start(f32[2,128,4096]{2,1,0:T(8,128)} %get-tuple-element.33.keep) | copy-start | bytes 12582916
  37.3 5.1 %copy-start.29 = (s32[1,512]{1,0:T(1,128)S(1)}, s32[1,512]{1,0:T(1,128)}, u32[]{:S(2)}) copy-start(s32[1,512]{1,0:T(1,128)} %get-tuple-element.42) | copy-start | bytes 6148
  37.3 6.0 %collective-permute-start.5 = (bf16[2,128,1024]{2,1,0:T(8,128)(2,1)S(1)}, bf16[2,128,1024]{2,1,0:T(8,128)(2,1)S(1)}, u32[]{:S(2)}, u32[]{:S(2)}) collective-permute-start(bf16[2,128,1024]{2,1,0:T(8,128)(2,1)S(1)} %bitcast.135), channel_id=1, source_target_pairs={{0,4},{4,0},{8,12},{12,8},{1,5},{5,1},{9,13},{13,9},{2,6},{6,2},{1... | collective-permute-start | bytes 1572872 | tf_op jit(solution)/shard_map/ppermute | solution.py:335
  39.2 32.0 %collective-permute-start.8 = (bf16[2,64,4096]{2,1,0:T(8,128)(2,1)S(1)}, bf16[2,64,4096]{2,1,0:T(8,128)(2,1)}, u32[]{:S(2)}, u32[]{:S(2)}) collective-permute-start(bf16[2,64,4096]{2,1,0:T(8,128)(2,1)S(1)} %fusion), channel_id=1, source_target_pairs={{0,8},{4,12},{8,0},{12,4},{1,9},{5,13},{9,1},{13,5},{2,10},{6,14},... | collective-permute-start | bytes 3145736 | tf_op jit(solution)/shard_map/ppermute | solution.py:338
  40.8 30.3 %collective-permute-start.9 = (bf16[4,256,256]{2,1,0:T(8,128)(2,1)S(1)}, bf16[4,256,256]{2,1,0:T(8,128)(2,1)S(1)}, u32[]{:S(2)}, u32[]{:S(2)}) collective-permute-start(bf16[4,256,256]{2,1,0:T(8,128)(2,1)S(1)} %collective-permute-done.4.refs_0_), channel_id=1, source_target_pairs={{0,16},{16,0},{1,17},{17,1},{2,18},{18,2},{3,19},{19,3},{4,20},{20... | collective-permute-start | bytes 1572872 | tf_op jit(solution)/shard_map/ppermute | solution.py:385
  43.5 26.9 %collective-permute-start.10 = (bf16[128,1024]{1,0:T(8,128)(2,1)S(1)}, bf16[128,1024]{1,0:T(8,128)(2,1)S(1)}, u32[]{:S(2)}, u32[]{:S(2)}) collective-permute-start(bf16[128,1024]{1,0:T(8,128)(2,1)S(1)} %get-tuple-element.68), channel_id=1, source_target_pairs={{0,8},{4,12},{8,0},{12,4},{1,9},{5,13},{9,1},{13,5},{2,10},{6,14},... | collective-permute-start | bytes 786440 | tf_op jit(solution)/shard_map/ppermute | solution.py:338
  59.0 22.4 %collective-permute-start.6 = (f32[2,64,4096]{2,1,0:T(8,128)}, f32[2,64,4096]{2,1,0:T(8,128)}, u32[]{:S(2)}, u32[]{:S(2)}) collective-permute-start(f32[2,64,4096]{2,1,0:T(8,128)} %get-tuple-element.39), channel_id=1, source_target_pairs={{0,4},{4,0},{8,12},{12,8},{1,5},{5,1},{9,13},{13,9},{2,6},{6,2},{1... | collective-permute-start | bytes 6291464 | tf_op jit(solution)/shard_map/ppermute | solution.py:335
  71.2 4.7 %copy-start.7 = (bf16[4,256,256]{2,1,0:T(8,128)(2,1)}, bf16[4,256,256]{2,1,0:T(8,128)(2,1)S(1)}, u32[]{:S(2)}) copy-start(bf16[4,256,256]{2,1,0:T(8,128)(2,1)S(1)} %collective-permute-done.9.refs_1_) | copy-start | bytes 1572868
  71.2 6.7 %copy-start.18 = (s32[512]{0:T(512)S(1)}, s32[512]{0:T(512)}, u32[]{:S(2)}) copy-start(s32[512]{0:T(512)} %select_reduce_fusion) | copy-start | bytes 6148
  71.2 7.8 %copy-start = (bf16[4,2,256,256]{3,2,1,0:T(8,128)(2,1)S(1)}, bf16[4,2,256,256]{3,2,1,0:T(8,128)(2,1)}, u32[]{:S(2)}) copy-start(bf16[4,2,256,256]{3,2,1,0:T(8,128)(2,1)} %param.20) | copy-start | bytes 3145732
  75.9 5.5 %copy-start.3 = (f32[2,64,4096]{2,1,0:T(8,128)S(1)}, f32[2,64,4096]{2,1,0:T(8,128)}, u32[]{:S(2)}) copy-start(f32[2,64,4096]{2,1,0:T(8,128)} %get-tuple-element.38.keep) | copy-start | bytes 6291460
  77.9 2.3 collective-permute-start.11
  79.0 51.5 %collective-permute-start.18 = (bf16[8,256,256]{2,1,0:T(8,128)(2,1)S(1)}, bf16[8,256,256]{2,1,0:T(8,128)(2,1)}, u32[]{:S(2)}, u32[]{:S(2)}) collective-permute-start(bf16[8,256,256]{2,1,0:T(8,128)(2,1)S(1)} %bitcast.129), channel_id=1, source_target_pairs={{0,4},{4,0},{8,12},{12,8},{1,5},{5,1},{9,13},{13,9},{2,6},{6,2},{1... | collective-permute-start | bytes 3145736 | tf_op jit(solution)/shard_map/ppermute | solution.py:335
  82.8 20.4 %collective-permute-start.7 = (bf16[2,32,4096]{2,1,0:T(8,128)(2,1)S(1)}, bf16[2,32,4096]{2,1,0:T(8,128)(2,1)S(1)}, u32[]{:S(2)}, u32[]{:S(2)}) collective-permute-start(bf16[2,32,4096]{2,1,0:T(8,128)(2,1)S(1)} %fusion.3), channel_id=1, source_target_pairs={{0,8},{4,12},{8,0},{12,4},{1,9},{5,13},{9,1},{13,5},{2,10},{6,14},... | collective-permute-start | bytes 1572872 | tf_op jit(solution)/shard_map/ppermute | solution.py:338
  84.3 18.2 %collective-permute-start.12 = (bf16[128,1024]{1,0:T(8,128)(2,1)S(1)}, bf16[128,1024]{1,0:T(8,128)(2,1)S(1)}, u32[]{:S(2)}, u32[]{:S(2)}) collective-permute-start(bf16[128,1024]{1,0:T(8,128)(2,1)S(1)} %get-tuple-element.66), channel_id=1, source_target_pairs={{0,8},{4,12},{8,0},{12,4},{1,9},{5,13},{9,1},{13,5},{2,10},{6,14},... | collective-permute-start | bytes 786440 | tf_op jit(solution)/shard_map/ppermute | solution.py:338
  99.8 9.3 %collective-permute-start.13 = (f32[2,64,4096]{2,1,0:T(8,128)}, f32[2,64,4096]{2,1,0:T(8,128)S(1)}, u32[]{:S(2)}, u32[]{:S(2)}) collective-permute-start(f32[2,64,4096]{2,1,0:T(8,128)} %get-tuple-element.48), channel_id=1, source_target_pairs={{0,4},{4,0},{8,12},{12,8},{1,5},{5,1},{9,13},{13,9},{2,6},{6,2},{1... | collective-permute-start | bytes 6291464 | tf_op jit(solution)/shard_map/ppermute | solution.py:335
  103.2 4.5 %copy-start.17 = (bf16[2,32,4096]{2,1,0:T(8,128)(2,1)}, bf16[2,32,4096]{2,1,0:T(8,128)(2,1)S(1)}, u32[]{:S(2)}) copy-start(bf16[2,32,4096]{2,1,0:T(8,128)(2,1)S(1)} %collective-permute-done.7.refs_0_) | copy-start | bytes 1572868
  103.2 5.9 %copy-start.1 = (f32[2,64,4096]{2,1,0:T(8,128)S(1)}, f32[2,64,4096]{2,1,0:T(8,128)}, u32[]{:S(2)}) copy-start(f32[2,64,4096]{2,1,0:T(8,128)} %get-tuple-element.44.keep) | copy-start | bytes 6291460
  107.7 15.1 %collective-permute-start.14 = (bf16[64,4096]{1,0:T(8,128)(2,1)}, bf16[64,4096]{1,0:T(8,128)(2,1)S(1)}, u32[]{:S(2)}, u32[]{:S(2)}) collective-permute-start(bf16[64,4096]{1,0:T(8,128)(2,1)} %shard_map.123), channel_id=1, source_target_pairs={{0,8},{4,12},{8,0},{12,4},{1,9},{5,13},{9,1},{13,5},{2,10},{6,14},... | collective-permute-start | bytes 1572872 | tf_op jit(solution)/shard_map/ppermute | solution.py:338
  109.1 4.1 %copy-start.2 = (f32[2,64,4096]{2,1,0:T(8,128)}, f32[2,64,4096]{2,1,0:T(8,128)S(1)}, u32[]{:S(2)}) copy-start(f32[2,64,4096]{2,1,0:T(8,128)S(1)} %collective-permute-done.13.core) | copy-start | bytes 6291460
  110.1 12.7 %copy-start.15 = (bf16[64,4096]{1,0:T(8,128)(2,1)S(1)}, bf16[64,4096]{1,0:T(8,128)(2,1)}, u32[]{:S(2)}) copy-start(bf16[64,4096]{1,0:T(8,128)(2,1)} %shard_map.123) | copy-start | bytes 1572868
  113.3 9.7 %copy-start.8 = (bf16[4,256,256]{2,1,0:T(8,128)(2,1)S(1)}, bf16[4,256,256]{2,1,0:T(8,128)(2,1)}, u32[]{:S(2)}) copy-start(bf16[4,256,256]{2,1,0:T(8,128)(2,1)} %copy-done.7) | copy-start | bytes 1572868
  113.3 10.2 %copy-start.6 = (bf16[4,256,256]{2,1,0:T(8,128)(2,1)S(1)}, bf16[4,256,256]{2,1,0:T(8,128)(2,1)}, u32[]{:S(2)}) copy-start(bf16[4,256,256]{2,1,0:T(8,128)(2,1)} %copy-done.5) | copy-start | bytes 1572868
  113.3 14.8 %copy-start.13 = (bf16[32,4096]{1,0:T(8,128)(2,1)S(1)}, bf16[32,4096]{1,0:T(8,128)(2,1)}, u32[]{:S(2)}) copy-start(bf16[32,4096]{1,0:T(8,128)(2,1)} %shard_map.124) | copy-start | bytes 786436
  113.3 16.5 %copy-start.22 = (s32[24]{0:T(128)S(1)}, s32[24]{0:T(128)}, u32[]{:S(2)}) copy-start(s32[24]{0:T(128)} %copy-done.21) | copy-start | bytes 292
  113.3 16.5 %copy-start.24 = (s32[24]{0:T(128)S(1)}, s32[24]{0:T(128)}, u32[]{:S(2)}) copy-start(s32[24]{0:T(128)} %copy-done.23) | copy-start | bytes 292
  113.3 16.5 %copy-start.26 = (s32[24]{0:T(128)S(1)}, s32[24]{0:T(128)}, u32[]{:S(2)}) copy-start(s32[24]{0:T(128)} %copy-done.25) | copy-start | bytes 292
  113.3 16.5 %copy-start.28 = (s32[24]{0:T(128)S(1)}, s32[24]{0:T(128)}, u32[]{:S(2)}) copy-start(s32[24]{0:T(128)} %copy-done.27) | copy-start | bytes 292
  113.3 13.4 %collective-permute-start.20 = (bf16[32,4096]{1,0:T(8,128)(2,1)}, bf16[32,4096]{1,0:T(8,128)(2,1)S(1)}, u32[]{:S(2)}, u32[]{:S(2)}) collective-permute-start(bf16[32,4096]{1,0:T(8,128)(2,1)} %shard_map.124), channel_id=1, source_target_pairs={{0,8},{4,12},{8,0},{12,4},{1,9},{5,13},{9,1},{13,5},{2,10},{6,14},... | collective-permute-start | bytes 786440 | tf_op jit(solution)/shard_map/ppermute | solution.py:338
  122.9 7.6 %copy-start.4 = (bf16[128,4096]{1,0:T(8,128)(2,1)}, bf16[128,4096]{1,0:T(8,128)(2,1)S(1)}, u32[]{:S(2)}) copy-start(bf16[128,4096]{1,0:T(8,128)(2,1)S(1)} %pad_maximum_fusion.near) | copy-start | bytes 3145732
  122.9 7.6 %collective-permute-start.15 = (bf16[128,4096]{1,0:T(8,128)(2,1)S(1)}, bf16[128,4096]{1,0:T(8,128)(2,1)}, u32[]{:S(2)}, u32[]{:S(2)}) collective-permute-start(bf16[128,4096]{1,0:T(8,128)(2,1)S(1)} %pad_maximum_fusion.near), channel_id=1, source_target_pairs={{0,4},{4,0},{8,12},{12,8},{1,5},{5,1},{9,13},{13,9},{2,6},{6,2},{1... | collective-permute-start | bytes 3145736 | tf_op jit(solution)/shard_map/ppermute | solution.py:335
  123.0 5.9 %collective-permute-start.17 = (bf16[4,256,256]{2,1,0:T(8,128)(2,1)S(1)}, bf16[4,256,256]{2,1,0:T(8,128)(2,1)S(1)}, u32[]{:S(2)}, u32[]{:S(2)}) collective-permute-start(bf16[4,256,256]{2,1,0:T(8,128)(2,1)S(1)} %copy-done.8), channel_id=1, source_target_pairs={{0,4},{4,0},{8,12},{12,8},{1,5},{5,1},{9,13},{13,9},{2,6},{6,2},{1... | collective-permute-start | bytes 1572872 | tf_op jit(solution)/shard_map/ppermute | solution.py:335
  123.5 7.0 %collective-permute-start.16 = (bf16[4,256,256]{2,1,0:T(8,128)(2,1)S(1)}, bf16[4,256,256]{2,1,0:T(8,128)(2,1)}, u32[]{:S(2)}, u32[]{:S(2)}) collective-permute-start(bf16[4,256,256]{2,1,0:T(8,128)(2,1)S(1)} %copy-done.6), channel_id=1, source_target_pairs={{0,4},{4,0},{8,12},{12,8},{1,5},{5,1},{9,13},{13,9},{2,6},{6,2},{1... | collective-permute-start | bytes 1572872 | tf_op jit(solution)/shard_map/ppermute | solution.py:335
  126.7 22.5 %collective-permute-start.19 = (bf16[2,32,4096]{2,1,0:T(8,128)(2,1)}, bf16[2,32,4096]{2,1,0:T(8,128)(2,1)S(1)}, u32[]{:S(2)}, u32[]{:S(2)}) collective-permute-start(bf16[2,32,4096]{2,1,0:T(8,128)(2,1)} %fusion.2), channel_id=1, source_target_pairs={{0,8},{4,12},{8,0},{12,4},{1,9},{5,13},{9,1},{13,5},{2,10},{6,14},... | collective-permute-start | bytes 1572872 | tf_op jit(solution)/shard_map/ppermute | solution.py:338
  128.9 0.8 copy-start.9
  129.7 28.3 %collective-permute-start.21 = (bf16[64,4096]{1,0:T(8,128)(2,1)}, bf16[64,4096]{1,0:T(8,128)(2,1)}, u32[]{:S(2)}, u32[]{:S(2)}) collective-permute-start(bf16[64,4096]{1,0:T(8,128)(2,1)} %pad_maximum_fusion.1.near), channel_id=1, source_target_pairs={{0,4},{4,0},{8,12},{12,8},{1,5},{5,1},{9,13},{13,9},{2,6},{6,2},{1... | collective-permute-start | bytes 1572872 | tf_op jit(solution)/shard_map/ppermute | solution.py:335
  149.2 0.8 copy-start.16
  153.1 21.1 %collective-permute-start.22 = (bf16[32,4096]{1,0:T(8,128)(2,1)}, bf16[32,4096]{1,0:T(8,128)(2,1)S(1)}, u32[]{:S(2)}, u32[]{:S(2)}) collective-permute-start(bf16[32,4096]{1,0:T(8,128)(2,1)} %shard_map.126), channel_id=1, source_target_pairs={{0,8},{4,12},{8,0},{12,4},{1,9},{5,13},{9,1},{13,5},{2,10},{6,14},... | collective-permute-start | bytes 786440 | tf_op jit(solution)/shard_map/ppermute | solution.py:338
  153.5 31.4 %all-to-all-start = ((bf16[4,4,16,2048]{3,2,1,0:T(8,128)(2,1)}), bf16[4,4,16,2048]{3,2,1,0:T(8,128)(2,1)S(1)}, u32[]{:S(2)}, u32[]{:S(2)}) async-start(bf16[4,4,16,2048]{3,2,1,0:T(8,128)(2,1)} %bitcast.108), calls=%async_computation | async-start | bytes 2097152 | tf_op jit(solution)/shard_map/all_to_all | solution.py:514
  172.1 17.6 %copy-start.12 = (bf16[32,4096]{1,0:T(8,128)(2,1)S(1)}, bf16[32,4096]{1,0:T(8,128)(2,1)}, u32[]{:S(2)}) copy-start(bf16[32,4096]{1,0:T(8,128)(2,1)} %shard_map.126) | copy-start | bytes 786436
  186.1 22.4 %all-to-all-start.1 = ((bf16[4,4,8,2048]{3,2,1,0:T(8,128)(2,1)}), bf16[4,4,8,2048]{3,2,1,0:T(8,128)(2,1)S(1)}, u32[]{:S(2)}, u32[]{:S(2)}) async-start(bf16[4,4,8,2048]{3,2,1,0:T(8,128)(2,1)} %bitcast.109), calls=%async_computation.1 | async-start | bytes 1048576 | tf_op jit(solution)/shard_map/all_to_all | solution.py:514
  189.7 2.0 copy-start.10
  189.7 2.0 collective-permute-start.23
  191.7 0.8 copy-start.14
  209.6 19.2 %all-to-all-start.2 = ((bf16[4,4,8,2048]{3,2,1,0:T(8,128)(2,1)}), bf16[4,4,8,2048]{3,2,1,0:T(8,128)(2,1)S(1)}, u32[]{:S(2)}, u32[]{:S(2)}) async-start(bf16[4,4,8,2048]{3,2,1,0:T(8,128)(2,1)} %bitcast.110), calls=%async_computation.2 | async-start | bytes 1048576 | tf_op jit(solution)/shard_map/all_to_all | solution.py:514

commit v5 on v4

--- a/solution.py
+++ b/solution.py
@@ -8,7 +8,8 @@
 from jax.sharding import PartitionSpec as P
 
 CAP = 128
-CHUNKS = (2, 1, 1)
+CHUNKS = (2, 2)
+PARTS = 2
 SHORT = 120e9
 VMEM = 56 * 1024 * 1024
 BF = jnp.bfloat16
@@ -143,15 +144,16 @@
         keep[i] = total[half:]
 
 
-def gate_up(scal, tokens, wg, wu, owners, shift, start, size):
+def gate_up(scal, tokens, wg, wu, owners, shift, start, size, part):
     rows, depth = tokens.shape
-    width = wg.shape[1]
+    width = wg.shape[1] // PARTS
     block = min(1024, width)
+    skip = part * (width // block)
     each = size // (owners * shift)
     first = start // (shift * each)
     view = tokens.reshape(shift, rows // (shift * each), each, depth)
     outs = pl.BlockSpec((2, size // 2, block), lambda i, s: (0, 0, i))
-    weights = pl.BlockSpec((depth, block), lambda i, s: (0, i))
+    weights = pl.BlockSpec((depth, block), lambda i, s: (0, skip + i))
     piece = [
         pl.BlockSpec((shift, 1, each, depth), functools.partial(lambda h, i, s: (0, first + s[h], 0, 0), h))
         for h in range(owners)
@@ -171,14 +173,14 @@
     )(scal, *[view] * owners, wg, wu)
 
 
-def activate_body(per_slot, start, each, row, parts, keep, core, *refs):
+def activate_body(per_slot, start, each, row, parts, skip, keep, core, *refs):
     gots, (delta, slot, table, out) = refs[:parts], refs[parts:]
     tile = 256
     step = pl.program_id(0)
     across = out.shape[1] // tile
     lanes = lax.broadcasted_iota(jnp.int32, (each, table.shape[0]), 1)
     hot = jnp.where(slot[row : row + each] == lanes, 1.0, 0.0).astype(BF)
-    where = jnp.dot(hot, table[...], preferred_element_type=F32) - (step * across).astype(F32)
+    where = jnp.dot(hot, table[...], preferred_element_type=F32) - (skip + step * across).astype(F32)
     at = [where[:, 64 + k : 65 + k] for k in range(2 * per_slot)]
     adds = [
         delta[start : start + each, k * tile : (k + 1) * tile].astype(F32) for k in range(2 * per_slot)
@@ -196,14 +198,14 @@
         out[:, cols] = (gate / (1.0 + jnp.exp(-gate)) * up).astype(BF)
 
 
-def activate(keep, core, gots, delta, slot, table, per_slot, start, row, flops):
+def activate(keep, core, gots, delta, slot, table, per_slot, start, row, skip, flops):
     each, width = gots[0].shape[1:]
     last = keep.shape[1] // each - 1
     block = min(2048, width)
     own = pl.BlockSpec((2, each, block), lambda i: (0, last, i))
     taken = [pl.BlockSpec((g.shape[0], each, block), lambda i: (0, 0, i)) for g in gots]
     return pl.pallas_call(
-        functools.partial(activate_body, per_slot, start, each, row, len(gots)),
+        functools.partial(activate_body, per_slot, start, each, row, len(gots), skip),
         grid=(width // block,),
         in_specs=[own, own, *taken, whole(delta.shape), whole(slot.shape), whole(table.shape)],
         out_specs=pl.BlockSpec((each, block), lambda i: (0, i)),
@@ -213,19 +215,21 @@
     )(keep, core, *gots, delta, slot, table)
 
 
-def down_body(width_tiles, here, plan, owners, per_owner, per_slot, start, scal, far, near, w, *refs):
+def down_body(width_tiles, here, plan, owners, per_owner, per_slot, start, scal, *refs):
+    fars, nears, (w, *refs) = refs[:PARTS], refs[PARTS : 2 * PARTS], refs[2 * PARTS :]
     tiles, (slot, out, hid, listed, number) = refs[: len(plan)], refs[len(plan) :]
     tile = 256
     across = out.shape[1] // tile
     step = pl.program_id(0)
-    half = far.shape[0]
+    half, wide = fars[0].shape
     stride = 3 * per_slot
     patterns = scal.shape[0] - owners * per_owner * stride
 
     @pl.when(step == 0)
     def _():
-        hid[:half] = far[...]
-        hid[half:] = near[...]
+        for p in range(PARTS):
+            hid[:half, p * wide : (p + 1) * wide] = fars[p][...]
+            hid[half:, p * wide : (p + 1) * wide] = nears[p][...]
         me = scal[0]
         for r, (base, run) in enumerate(plan):
             for at in range(number.shape[1]):
@@ -270,8 +274,8 @@
         lax.fori_loop(0, number[r, step], add, 0)
 
 
-def down(scal, far, near, w, tiles, plan, slot, width_tiles, owners, per_owner, per_slot, start, flops):
-    rows, depth = 2 * far.shape[0], far.shape[1]
+def down(scal, fars, nears, w, tiles, plan, slot, width_tiles, owners, per_owner, per_slot, start, flops):
+    rows, depth = 2 * fars[0].shape[0], w.shape[0]
     width = w.shape[1]
     block = min(512, width)
     steps = width // block
@@ -282,8 +286,7 @@
             num_scalar_prefetch=1,
             grid=(steps,),
             in_specs=[
-                whole(far.shape),
-                whole(near.shape),
+                *[whole(f.shape) for f in (*fars, *nears)],
                 pl.BlockSpec((depth, block), lambda i, s: (0, i)),
                 *[whole(t.shape) for t in tiles],
                 whole(slot.shape),
@@ -298,7 +301,7 @@
         out_shape=jax.ShapeDtypeStruct((rows, width), F32),
         compiler_params=pltpu.CompilerParams(vmem_limit_bytes=VMEM),
         cost_estimate=cost(flops, 1e6),
-    )(scal, far, near, w, *tiles, slot)
+    )(scal, *fars, *nears, w, *tiles, slot)
 
 
 def shards(
@@ -396,29 +399,27 @@
 
     starts = [sum(sizes[:i]) for i in range(len(sizes))]
     inners = [s // owners for s in starts]
-    count = len(sizes)
-    kept, cores, sends, gots = ([None] * count for _ in range(4))
-
-    def multiply(i, *earlier):
-        send, kept[i] = gate_up(
-            after(homes, *earlier), tokens, gate_weight, up_weight, owners, shift, starts[i], sizes[i]
+    kept, cores, sends, gots = {}, {}, {}, {}
+
+    def multiply(u, *earlier):
+        i, part = u
+        send, kept[u] = gate_up(
+            after(homes, *earlier), tokens, gate_weight, up_weight, owners, shift, starts[i], sizes[i], part
         )
-        cores[i] = core_swap(send)
-
-    def exchange(i):
-        each = sizes[i] // owners
-        parts = [slice(0, 2)]
-        sends[i], gots[i] = [], []
-        for part in parts:
-            got = None
-            for k in range(1, ys):
-                rows_k = slice((k - 1) * each, k * each)
-                sends[i].append((kept[i][part, rows_k] + cores[i][part, rows_k]).astype(BF))
-                moved = y_move(sends[i][-1], k)
-                if ys > 2:
-                    moved = moved.astype(F32)
-                got = moved if got is None else got + moved
-            gots[i].append(got)
+        cores[u] = core_swap(send)
+
+    def exchange(u, *earlier):
+        each = sizes[u[0]] // owners
+        sends[u], got = [], None
+        own = after(kept[u], *earlier)
+        for k in range(1, ys):
+            rows_k = slice((k - 1) * each, k * each)
+            sends[u].append((own[:, rows_k] + cores[u][:, rows_k]).astype(BF))
+            moved = y_move(sends[u][-1], k)
+            if ys > 2:
+                moved = moved.astype(F32)
+            got = moved if got is None else got + moved
+        gots[u] = [got]
 
     def halve(x):
         half = owners // 2
@@ -430,9 +431,10 @@
             total = total + y_move(x[k - 1], k)
         return total
 
-    multiply(0)
+    ahead, second, third, fourth = (0, 0), (0, 1), (1, 0), (1, 1)
+    multiply(ahead)
     packed, code, table = pack(
-        after(scal, kept[0], from_y),
+        after(scal, kept[ahead], from_y),
         tokens,
         slot_rows[None, :],
         slot_rows[:, None],
@@ -442,7 +444,7 @@
         3 * per_slot,
         col_tiles,
     )
-    exchange(0)
+    exchange(ahead)
     packed = halve(packed.reshape(owners, CAP, -1))
     code_q = jnp.sum(
         jnp.where(row_of[:, None] == jnp.arange(rows, dtype=jnp.int32)[None, :], code, 0), axis=1
@@ -455,49 +457,52 @@
     )
     ss_q = slot_q[:, None]
 
-    for i in range(1, count):
-        if i == 1:
-            multiply(1, *sends[0], packed)
-            features = finish(packed, kept[1])
-            spread = product(
-                after(scal, kept[1], *gots[0], *arrived), features, gate_tiles, up_tiles, code_q[None, :], owners, per_owner, pieces
-            )
-            exchange(1)
-            spread = halve(spread)
-            held = (spread,)
-        else:
-            multiply(i, *sends[i - 1], *gots[i - 2], *held)
-            held = ()
-            exchange(i)
-    home_delta = finish(spread, kept[2])
+    multiply(second, *sends[ahead], packed)
+    features = finish(packed, kept[second])
+    spread = product(
+        after(scal, kept[second], *gots[ahead], *arrived),
+        features,
+        gate_tiles,
+        up_tiles,
+        code_q[None, :],
+        owners,
+        per_owner,
+        pieces,
+    )
+    exchange(second)
+    spread = halve(spread)
+    multiply(third, *sends[second], spread)
+    home_delta = finish(spread, kept[third])
 
     near_tiles = [*tiles, flat_tiles]
-    all_tiles = near_tiles + [core_swap(after(t, kept[1])) for t in near_tiles]
-
-    def finish_hidden(i, *earlier):
+    all_tiles = near_tiles + [core_swap(after(t, kept[second])) for t in near_tiles]
+
+    def finish_hidden(u, flops, *earlier):
+        i, part = u
         each = sizes[i] // owners
         hid = activate(
-            kept[i],
-            cores[i],
-            gots[i],
+            kept[u],
+            cores[u],
+            gots[u],
             home_delta,
             ss_q,
             after(table, *earlier),
             per_slot,
             inners[i],
             starts[i] + sizes[i] - each,
-            SHORT if i == 0 else 1e9,
+            part * (col_tiles // PARTS),
+            flops,
         )
         return hid, [y_move(hid, -k) for k in range(1, ys)]
 
     def join(hid, moved, *earlier):
         return jnp.concatenate([after(m, *earlier) for m in moved] + [hid])
 
-    def finish_down(i, chip, earlier, sent=()):
+    def finish_down(i, chips, earlier, sent=None):
         out = down(
             after(down_scal, *earlier),
-            core_swap(chip),
-            chip,
+            [core_swap(c) for c in chips],
+            chips,
             down_weight,
             all_tiles,
             plan,
@@ -507,29 +512,31 @@
             per_owner,
             per_slot,
             starts[i],
-            SHORT if i == count - 2 else 1e9,
+            1e9,
         )
         blocks = out.reshape(owners, shift, sizes[i] // (owners * shift), shard_width).transpose(1, 0, 2, 3)
-        gone = blocks.astype(BF)
-        came = lax.all_to_all(after(gone, *sent), "tensor", 0, 0)
-        own = lax.dynamic_index_in_dim(blocks, here_t, 0, keepdims=False)
-        total = own
-        for t in range(shift):
-            total = total + jnp.where(t == here_t, 0.0, came[t].astype(F32))
-        return gone, total.astype(BF)
-
-    result = []
-    hid, moved = finish_hidden(0, kept[count - 1], gots[1][0])
-    chip, out = None, ()
-    for i in range(1, count):
-        later, moved_later = finish_hidden(i, hid, *sends[count - 1], *out)
-        if i == 1:
-            chip = join(hid, moved, later)
-        next_chip = join(later, moved_later)
-        gone, total = finish_down(i - 1, chip, (later, *result[:-1]), result[-1:])
-        hid, chip, out = later, next_chip, (gone, next_chip)
-        result.append(total)
-    gone, total = finish_down(count - 1, chip, (gone, *result[:-1]), result[-1:])
+        total = lax.dynamic_index_in_dim(blocks, here_t, 0, keepdims=False)
+        came = []
+        for k in range(1, shift):
+            gone = lax.dynamic_index_in_dim(blocks, (here_t + k) % shift, 0, keepdims=False).astype(BF)
+            if sent is not None:
+                gone = after(gone, sent[k - 1])
+            came.append(lax.ppermute(gone, "tensor", [(j, (j + k) % shift) for j in range(shift)]))
+            total = total + came[-1].astype(F32)
+        return out, came, total.astype(BF)
+
+    hid_a, moved_a = finish_hidden(ahead, SHORT, kept[third], *gots[second])
+    exchange(third, hid_a)
+    multiply(fourth, *sends[third], hid_a)
+    hid_b, moved_b = finish_hidden(second, SHORT, kept[fourth], *gots[third], *moved_a)
+    exchange(fourth, hid_b)
+    hid_c, moved_c = finish_hidden(third, 1e9, hid_b, *sends[fourth])
+    hid_d, moved_d = finish_hidden(fourth, 1e9, hid_c)
+    first = [join(hid_a, moved_a, hid_b), join(hid_b, moved_b, hid_c)]
+    last = [join(hid_c, moved_c, hid_d), join(hid_d, moved_d)]
+    out, came, total = finish_down(0, first, (hid_d,))
+    result = [total]
+    out, came, total = finish_down(1, last, (out,), came)
     result.append(total)
 
     placed = [jnp.take(r, at_home, axis=0).reshape(-1, shard_width) for r in result]

time: 232 us -> 216 us (0.931); the launches traced: 231 us -> 212 us
  Pallas kernels: 115 us -> 98.7 us
  local copies, waits for them, and re-layouts: 19.1 us -> 15.6 us
  starting transfers between devices: 28.6 us -> 31.4 us
  waiting for transfers between devices: 52.4 us -> 49.9 us
    all_to_all x3 -> x0, waiting for transfers between devices: 24.1 us -> none  [finish_down(): came = lax.all_to_all(after(gone, *sent), 'tensor', 0, 0)]
    ppermute x0 -> x6, waiting for transfers between devices: none -> 13.8 us  [finish_down(): lax.ppermute(gone, 'tensor', [(j, (j + k) % shift) for j in range(shift)])]
    pallas_call x3 -> x2, Pallas kernels: 44 us -> 31.2 us  [down(): pl.pallas_call(functools.partial(down_body, width_tiles, width // 256, pl...]
    all_to_all x3 -> x0, starting transfers between devices: 12.5 us -> none  [finish_down(): came = lax.all_to_all(after(gone, *sent), 'tensor', 0, 0)]
    ppermute x0 -> x6, starting transfers between devices: none -> 12 us  [finish_down(): lax.ppermute(gone, 'tensor', [(j, (j + k) % shift) for j in range(shift)])]
    ppermute x9 -> x11, waiting for transfers between devices: 25.9 us -> 35.2 us  [y_move(): lax.ppermute(x, 'delta', [(i, (i + 2 * k) % owners) for i in range(owners)])]
    reshape x3 -> x0, local copies, waits for them, and re-layouts: 6.95 us -> none  [finish_down(): out.reshape(owners, shift, sizes[i] // (owners * shift), shard_width)]
    pallas_call x3 -> x4, Pallas kernels: 47.6 us -> 42.5 us  [gate_up(): pl.pallas_call(functools.partial(gate_up_body, owners), grid_spec=pltpu.P...]
  transfers between devices with their start and end apart: 27 -> 34, of which waited for: 8 -> 9; matrix products, arithmetic and copies ran while one was open for 12% -> 10% of each run, Pallas kernels for 50% -> 46%
where the time goes in v5:
time: 216 us; the launch traced here: 212 us
  Pallas kernels  98.7 us (46%)
  waiting for transfers between devices  49.9 us (23%)
  starting transfers between devices  31.4 us (15%)
  other arithmetic  16.2 us (8%)
  local copies, waits for them, and re-layouts  15.6 us (7%)
    pallas_call x4, Pallas kernels, gate_up(): pl.pallas_call(functools.partial(gate_up_body, owners), grid_spec=pltpu.P...  42.5 us
    ppermute x11, waiting for transfers between devices, y_move(): lax.ppermute(x, 'delta', [(i, (i + 2 * k) % owners) for i in range(owners)])  35.2 us
    pallas_call x2, Pallas kernels, down(): pl.pallas_call(functools.partial(down_body, width_tiles, width // 256, pl...  31.2 us
    ppermute x6, waiting for transfers between devices, finish_down(): lax.ppermute(gone, 'tensor', [(j, (j + k) % shift) for j in range(shift)])  13.8 us
    pallas_call x4, Pallas kernels, activate(): pl.pallas_call(functools.partial(activate_body, per_slot, start, each, ro...  13.2 us
    ppermute x11, starting transfers between devices, y_move(): lax.ppermute(x, 'delta', [(i, (i + 2 * k) % owners) for i in range(owners)])  12.9 us
    ppermute x6, starting transfers between devices, finish_down(): lax.ppermute(gone, 'tensor', [(j, (j + k) % shift) for j in range(shift)])  12 us
    pallas_call x1, Pallas kernels, pack(): pl.pallas_call(functools.partial(pack_body, owners, per_owner, kinds, str...  7.1 us
  transfers between devices with their start and end apart: 34, of which 9 were waited for; matrix products, arithmetic and copies ran while one was open for 10% of the time, Pallas kernels for 46%

profile of v5, /device:TPU:0, one launch (start us, length us, event | category | flops | bytes accessed | tf_op | source)
XLA Modules:
  0.0 212.2 jit_solution(15932880825558172292)
XLA Ops:
  0.0 0.7 pad_add_fusion
  0.7 2.4 %collective-permute-start = (s32[4,6]{0,1:T(8,128)S(1)}, s32[4,6]{0,1:T(8,128)S(1)}, u32[]{:S(2)}, u32[]{:S(2)}) collective-permute-start(s32[4,6]{0,1:T(8,128)S(1)} %pad_add_fusion), channel_id=1, source_target_pairs={{0,12},{4,0},{8,4},{12,8},{1,13},{5,1},{9,5},{13,9},{2,14},{6,2},{... | collective-permute-start | bytes 296 | tf_op jit(solution)/shard_map/ppermute | solution.py:369
  4.0 1.1 constant_dynamic-slice_fusion
  5.0 1.3 collective-permute-start.4
  6.9 10.6 %shard_map.118 = (f32[2,128,2048]{2,1,0:T(8,128)}, f32[2,128,2048]{2,1,0:T(8,128)}) custom-call(s32[4]{0:T(128)} %get-tuple-element.58.scal, bf16[4,8,16,2048]{3,2,1,0:T(8,128)(2,1)} %bitcast.80, bf16[4,8,16,2048]{3,2,1,0:T(8,128)(2,1)} %bitcast.81, bf16[4,8,16,2048]{3,2,1,0:T(8,128)(2,1)} %bitcast.82, bf16[4,8,16,2048]{3,2,1,0:T(8,128)(2,1)} %bitcast.83, ...), custom_call_target="tpu_custom_call" | custom-call | flops 4294967296 | bytes 16777216 | tf_op jit(solution)/shard_map/pallas_call | solution.py:161
  18.4 0.9 copy.38.ss
  20.4 7.1 %shard_map.119 = (bf16[512,1024]{1,0:T(8,128)(2,1)}, s32[1,512]{1,0:T(1,128)}, bf16[128,128]{1,0:T(8,128)(2,1)}) custom-call(s32[101]{0:T(128)} %concatenate.36.scal, bf16[512,2048]{1,0:T(8,128)(2,1)} %x.1, s32[1,512]{1,0:T(1,128)} %bitcast.111, s32[512,1]{1,0:T(8,128)} %copy.38.ss), custom_call_target="tpu_custom_call" | custom-call | flops 120000004096 | bytes 4000000 | tf_op jit(solution)/shard_map/pallas_call | solution.py:71
  27.5 1.3 fusion.18
  29.3 1.5 collective-permute-start.8
  30.8 0.8 select_reduce_fusion
  31.8 1.7 fusion.3
  33.5 1.5 collective-permute-start.7
  35.0 0.7 collective-permute-start.9
  35.7 10.6 %shard_map.120 = (f32[2,128,2048]{2,1,0:T(8,128)}, f32[2,128,2048]{2,1,0:T(8,128)}) custom-call(s32[4]{0:T(128)} %get-tuple-element.58.scal, bf16[4,8,16,2048]{3,2,1,0:T(8,128)(2,1)} %bitcast.84, bf16[4,8,16,2048]{3,2,1,0:T(8,128)(2,1)} %bitcast.85, bf16[4,8,16,2048]{3,2,1,0:T(8,128)(2,1)} %bitcast.86, bf16[4,8,16,2048]{3,2,1,0:T(8,128)(2,1)} %bitcast.87, ...), custom_call_target="tpu_custom_call" | custom-call | flops 4294967296 | bytes 16777216 | tf_op jit(solution)/shard_map/pallas_call | solution.py:161
  46.3 6.9 %collective-permute-done.9 = bf16[128,1024]{1,0:T(8,128)(2,1)S(1)} collective-permute-done((bf16[128,1024]{1,0:T(8,128)(2,1)S(1)}, bf16[128,1024]{1,0:T(8,128)(2,1)S(1)}, u32[]{:S(2)}, u32[]{:S(2)}) %collective-permute-start.9) | collective-permute-done | bytes 262176 | tf_op jit(solution)/shard_map/ppermute | solution.py:341
  53.2 0.8 add.259.x
  54.0 4.7 %shard_map.121 = bf16[4,128,1024]{2,1,0:T(8,128)(2,1)} custom-call(s32[101]{0:T(128)} %concatenate.36.scal, bf16[128,1024]{1,0:T(8,128)(2,1)} %add.259.x, bf16[4,2,256,256]{3,2,1,0:T(8,128)(2,1)} %gt.1, bf16[4,2,256,256]{3,2,1,0:T(8,128)(2,1)} %ut.1, s32[1,512]{1,0:T(1,128)} %bitcast.108), custom_call_target="tpu_custom_call" | custom-call | flops 120000004096 | bytes 4000000 | tf_op jit(solution)/shard_map/pallas_call | solution.py:117
  58.7 1.2 slice.83
  60.1 0.9 add_select_fusion.refs_2_.refs_11_
  61.0 0.9 collective-permute-done.10
  61.9 1.7 fusion.2
  63.6 1.5 collective-permute-start.12
  65.1 0.7 collective-permute-start.11
  65.8 10.7 %shard_map.122 = (f32[2,128,2048]{2,1,0:T(8,128)}, f32[2,128,2048]{2,1,0:T(8,128)}) custom-call(s32[4]{0:T(128)} %get-tuple-element.58.scal, bf16[4,8,16,2048]{3,2,1,0:T(8,128)(2,1)} %bitcast.88, bf16[4,8,16,2048]{3,2,1,0:T(8,128)(2,1)} %bitcast.89, bf16[4,8,16,2048]{3,2,1,0:T(8,128)(2,1)} %bitcast.90, bf16[4,8,16,2048]{3,2,1,0:T(8,128)(2,1)} %bitcast.91, ...), custom_call_target="tpu_custom_call" | custom-call | flops 4294967296 | bytes 16777216 | tf_op jit(solution)/shard_map/pallas_call | solution.py:161
  76.5 6.8 %collective-permute-done.11 = bf16[128,1024]{1,0:T(8,128)(2,1)S(1)} collective-permute-done((bf16[128,1024]{1,0:T(8,128)(2,1)S(1)}, bf16[128,1024]{1,0:T(8,128)(2,1)S(1)}, u32[]{:S(2)}, u32[]{:S(2)}) %collective-permute-start.11) | collective-permute-done | bytes 262176 | tf_op jit(solution)/shard_map/ppermute | solution.py:341
  83.2 0.8 add.275.refs_1_
  84.0 3.4 %shard_map.123 = bf16[64,2048]{1,0:T(8,128)(2,1)} custom-call(f32[2,128,2048]{2,1,0:T(8,128)} %get-tuple-element.41.keep, f32[2,128,2048]{2,1,0:T(8,128)} %collective-permute-done.3.core, bf16[2,64,2048]{2,1,0:T(8,128)(2,1)} %copy-done.34, bf16[128,1024]{1,0:T(8,128)(2,1)} %add.275.refs_1_, s32[512,1]{1,0:T(8,128)} %add_select_fusion.refs_2_.refs_11_, ...), custom_call_target="tpu_custom_call" | custom-call | flops 120000004096 | bytes 3145728 | tf_op jit(solution)/shard_map/pallas_call | solution.py:207
  87.6 1.5 collective-permute-start.15
  89.1 0.9 collective-permute-start.16
  89.9 10.6 %shard_map.124 = (f32[2,128,2048]{2,1,0:T(8,128)}, f32[2,128,2048]{2,1,0:T(8,128)}) custom-call(s32[4]{0:T(128)} %get-tuple-element.58.scal, bf16[4,8,16,2048]{3,2,1,0:T(8,128)(2,1)} %bitcast.92, bf16[4,8,16,2048]{3,2,1,0:T(8,128)(2,1)} %bitcast.93, bf16[4,8,16,2048]{3,2,1,0:T(8,128)(2,1)} %bitcast.94, bf16[4,8,16,2048]{3,2,1,0:T(8,128)(2,1)} %bitcast.95, ...), custom_call_target="tpu_custom_call" | custom-call | flops 4294967296 | bytes 16777216 | tf_op jit(solution)/shard_map/pallas_call | solution.py:161
  100.6 5.9 %collective-permute-done.16 = bf16[64,2048]{1,0:T(8,128)(2,1)S(1)} collective-permute-done((bf16[64,2048]{1,0:T(8,128)(2,1)S(1)}, bf16[64,2048]{1,0:T(8,128)(2,1)S(1)}, u32[]{:S(2)}, u32[]{:S(2)}) %collective-permute-start.16) | collective-permute-done | bytes 262176 | tf_op jit(solution)/shard_map/ppermute | solution.py:341
  106.4 0.7 copy-done.18
  107.1 0.8 copy-done.16
  107.9 3.3 %shard_map.125 = bf16[64,2048]{1,0:T(8,128)(2,1)} custom-call(f32[2,128,2048]{2,1,0:T(8,128)} %get-tuple-element.46.keep, f32[2,128,2048]{2,1,0:T(8,128)} %collective-permute-done.6.core, bf16[2,64,2048]{2,1,0:T(8,128)(2,1)} %copy-done.35, bf16[128,1024]{1,0:T(8,128)(2,1)} %add.275.refs_1_, s32[512,1]{1,0:T(8,128)} %add_select_fusion.refs_2_.refs_11_, ...), custom_call_target="tpu_custom_call" | custom-call | flops 120000004096 | bytes 3145728 | tf_op jit(solution)/shard_map/pallas_call | solution.py:207
  111.3 0.9 fusion
  112.9 1.4 collective-permute-start.17
  115.4 3.2 %shard_map.126 = bf16[64,2048]{1,0:T(8,128)(2,1)} custom-call(f32[2,128,2048]{2,1,0:T(8,128)} %get-tuple-element.56.keep, f32[2,128,2048]{2,1,0:T(8,128)} %copy-done.2, bf16[2,64,2048]{2,1,0:T(8,128)(2,1)} %copy-done.16, bf16[128,1024]{1,0:T(8,128)(2,1)} %add.275.refs_1_, s32[512,1]{1,0:T(8,128)} %add_select_fusion.refs_2_.refs_11_, ...), custom_call_target="tpu_custom_call" | custom-call | flops 1000000000 | bytes 3145728 | tf_op jit(solution)/shard_map/pallas_call | solution.py:207
  118.6 1.5 collective-permute-start.27
  120.1 8.0 %collective-permute-done.17.refs_0_ = bf16[2,64,2048]{2,1,0:T(8,128)(2,1)} collective-permute-done((bf16[2,64,2048]{2,1,0:T(8,128)(2,1)}, bf16[2,64,2048]{2,1,0:T(8,128)(2,1)}, u32[]{:S(2)}, u32[]{:S(2)}) %collective-permute-start.17) | collective-permute-done | bytes 524320 | tf_op jit(solution)/shard_map/ppermute | solution.py:341
  128.0 3.2 %shard_map.127 = bf16[64,2048]{1,0:T(8,128)(2,1)} custom-call(f32[2,128,2048]{2,1,0:T(8,128)} %get-tuple-element.62.keep, f32[2,128,2048]{2,1,0:T(8,128)} %copy-done.4, bf16[2,64,2048]{2,1,0:T(8,128)(2,1)} %collective-permute-done.17.refs_0_, bf16[128,1024]{1,0:T(8,128)(2,1)} %add.275.refs_1_, s32[512,1]{1,0:T(8,128)} %add_select_fusion.refs_2_.refs_11_, ...), custom_call_target="tpu_custom_call" | custom-call | flops 1000000000 | bytes 3145728 | tf_op jit(solution)/shard_map/pallas_call | solution.py:207
  131.3 1.5 collective-permute-start.29
  132.8 0.8 pad_maximum_fusion.refs_2_
  133.6 0.8 pad_maximum_fusion.1.refs_3_
  134.5 4.7 %collective-permute-done.27 = bf16[64,2048]{1,0:T(8,128)(2,1)S(1)} collective-permute-done((bf16[64,2048]{1,0:T(8,128)(2,1)}, bf16[64,2048]{1,0:T(8,128)(2,1)S(1)}, u32[]{:S(2)}, u32[]{:S(2)}) %collective-permute-start.27) | collective-permute-done | bytes 262176 | tf_op jit(solution)/shard_map/ppermute | solution.py:341
  139.2 3.0 %collective-permute-done.29 = bf16[64,2048]{1,0:T(8,128)(2,1)S(1)} collective-permute-done((bf16[64,2048]{1,0:T(8,128)(2,1)}, bf16[64,2048]{1,0:T(8,128)(2,1)S(1)}, u32[]{:S(2)}, u32[]{:S(2)}) %collective-permute-start.29) | collective-permute-done | bytes 262176 | tf_op jit(solution)/shard_map/ppermute | solution.py:341
  142.2 0.9 pad_maximum_fusion.2.refs_2_
  143.0 0.9 pad_maximum_fusion.3.refs_3_
  144.4 0.8 copy-done.11
  146.1 1.0 copy-done.5
  147.1 15.6 %shard_map.128 = f32[256,2048]{1,0:T(8,128)} custom-call(s32[103]{0:T(128)} %concatenate.35.scal, bf16[128,2048]{1,0:T(8,128)(2,1)} %collective-permute-done.18.refs_0_, bf16[128,2048]{1,0:T(8,128)(2,1)} %collective-permute-done.20.refs_1_, bf16[128,2048]{1,0:T(8,128)(2,1)} %pad_maximum_fusion.refs_2_, bf16[128,2048]{1,0:T(8,128)(2,1)} %pad_maximum_fusion.1.refs_3_, ...), custom_call_target="tpu_custom_call" | custom-call | flops 1000000000 | bytes 1000000 | tf_op jit(solution)/shard_map/pallas_call | solution.py:283
  162.7 1.5 fusion.13
  164.1 2.0 collective-permute-start.24
  166.2 2.3 %collective-permute-start.25 = (bf16[4,16,2048]{2,1,0:T(8,128)(2,1)S(1)}, bf16[4,16,2048]{2,1,0:T(8,128)(2,1)S(1)}, u32[]{:S(2)}, u32[]{:S(2)}) collective-permute-start(bf16[4,16,2048]{2,1,0:T(8,128)(2,1)S(1)} %get-tuple-element.82), channel_id=1, source_target_pairs={{0,2},{1,3},{2,0},{3,1},{4,6},{5,7},{6,4},{7,5},{8,10},{9,11},{10,... | collective-permute-start | bytes 786440 | tf_op jit(solution)/shard_map/ppermute | solution.py:524
  168.5 1.5 collective-permute-start.26
  170.0 0.8 copy-done.15
  170.8 15.6 %shard_map.129 = f32[256,2048]{1,0:T(8,128)} custom-call(s32[103]{0:T(128)} %concatenate.35.scal, bf16[128,2048]{1,0:T(8,128)(2,1)} %copy-done.15, bf16[128,2048]{1,0:T(8,128)(2,1)} %collective-permute-done.30.refs_1_, bf16[128,2048]{1,0:T(8,128)(2,1)} %pad_maximum_fusion.2.refs_2_, bf16[128,2048]{1,0:T(8,128)(2,1)} %pad_maximum_fusion.3.refs_3_, ...), custom_call_target="tpu_custom_call" | custom-call | flops 1000000000 | bytes 1000000 | tf_op jit(solution)/shard_map/pallas_call | solution.py:283
  186.3 1.5 fusion.15
  187.8 1.0 collective-permute-start.31
  189.2 4.8 %collective-permute-start.33 = (bf16[4,16,2048]{2,1,0:T(8,128)(2,1)S(1)}, bf16[4,16,2048]{2,1,0:T(8,128)(2,1)S(1)}, u32[]{:S(2)}, u32[]{:S(2)}) collective-permute-start(bf16[4,16,2048]{2,1,0:T(8,128)(2,1)S(1)} %get-tuple-element.75), channel_id=1, source_target_pairs={{0,3},{1,0},{2,1},{3,2},{4,7},{5,4},{6,5},{7,6},{8,11},{9,8},{10,9... | collective-permute-start | bytes 786440 | tf_op jit(solution)/shard_map/ppermute | solution.py:524
  194.0 1.2 fusion.9
  195.7 3.2 %collective-permute-done.31 = bf16[4,16,2048]{2,1,0:T(8,128)(2,1)S(1)} collective-permute-done((bf16[4,16,2048]{2,1,0:T(8,128)(2,1)S(1)}, bf16[4,16,2048]{2,1,0:T(8,128)(2,1)S(1)}, u32[]{:S(2)}, u32[]{:S(2)}) %collective-permute-start.31) | collective-permute-done | bytes 262176 | tf_op jit(solution)/shard_map/ppermute | solution.py:524
  199.0 10.6 %collective-permute-done.32 = bf16[4,16,2048]{2,1,0:T(8,128)(2,1)S(1)} collective-permute-done((bf16[4,16,2048]{2,1,0:T(8,128)(2,1)S(1)}, bf16[4,16,2048]{2,1,0:T(8,128)(2,1)S(1)}, u32[]{:S(2)}, u32[]{:S(2)}) %collective-permute-start.32) | collective-permute-done | bytes 262176 | tf_op jit(solution)/shard_map/ppermute | solution.py:524
  209.5 1.2 fusion.6
  211.4 0.8 pad_maximum_fusion.4
  (139 shorter events, 9.3 us)
Async XLA Ops:
  0.7 18.5 %collective-permute-start = (s32[4,6]{0,1:T(8,128)S(1)}, s32[4,6]{0,1:T(8,128)S(1)}, u32[]{:S(2)}, u32[]{:S(2)}) collective-permute-start(s32[4,6]{0,1:T(8,128)S(1)} %pad_add_fusion), channel_id=1, source_target_pairs={{0,12},{4,0},{8,4},{12,8},{1,13},{5,1},{9,5},{13,9},{2,14},{6,2},{... | collective-permute-start | bytes 296 | tf_op jit(solution)/shard_map/ppermute | solution.py:369
  3.2 16.2 %collective-permute-start.1 = (s32[4,6]{0,1:T(8,128)S(1)}, s32[4,6]{0,1:T(8,128)S(1)}, u32[]{:S(2)}, u32[]{:S(2)}) collective-permute-start(s32[4,6]{0,1:T(8,128)S(1)} %pad_add_fusion), channel_id=1, source_target_pairs={{0,8},{4,12},{8,0},{12,4},{1,9},{5,13},{9,1},{13,5},{2,10},{6,14},... | collective-permute-start | bytes 296 | tf_op jit(solution)/shard_map/ppermute | solution.py:369
  3.8 15.8 %collective-permute-start.2 = (s32[4,6]{0,1:T(8,128)S(1)}, s32[4,6]{0,1:T(8,128)S(1)}, u32[]{:S(2)}, u32[]{:S(2)}) collective-permute-start(s32[4,6]{0,1:T(8,128)S(1)} %pad_add_fusion), channel_id=1, source_target_pairs={{0,4},{4,8},{8,12},{12,0},{1,5},{5,9},{9,13},{13,1},{2,6},{6,10},{... | collective-permute-start | bytes 296 | tf_op jit(solution)/shard_map/ppermute | solution.py:369
  5.0 15.3 %collective-permute-start.4 = (bf16[4,256,256]{2,1,0:T(8,128)(2,1)S(1)}, bf16[4,256,256]{2,1,0:T(8,128)(2,1)S(1)}, u32[]{:S(2)}, u32[]{:S(2)}) collective-permute-start(bf16[4,256,256]{2,1,0:T(8,128)(2,1)S(1)} %constant_dynamic-slice_fusion), channel_id=1, source_target_pairs={{0,8},{4,12},{8,0},{12,4},{1,9},{5,13},{9,1},{13,5},{2,10},{6,14},... | collective-permute-start | bytes 1572872 | tf_op jit(solution)/shard_map/ppermute | solution.py:341
  6.9 11.3 %copy-start.32 = (s32[512]{0:T(512)S(1)}, s32[512]{0:T(512)}, u32[]{:S(2)}) copy-start(s32[512]{0:T(512)} %param.24) | copy-start | bytes 6148
  6.9 11.3 %copy-start.33 = (s32[16]{0:T(128)S(1)}, s32[16]{0:T(128)}, u32[]{:S(2)}) copy-start(s32[16]{0:T(128)} %param.25) | copy-start | bytes 196
  17.6 14.2 %collective-permute-start.3 = (f32[2,128,2048]{2,1,0:T(8,128)}, f32[2,128,2048]{2,1,0:T(8,128)}, u32[]{:S(2)}, u32[]{:S(2)}) collective-permute-start(f32[2,128,2048]{2,1,0:T(8,128)} %get-tuple-element.42), channel_id=1, source_target_pairs={{0,4},{4,0},{8,12},{12,8},{1,5},{5,1},{9,13},{13,9},{2,6},{6,2},{1... | collective-permute-start | bytes 6291464 | tf_op jit(solution)/shard_map/ppermute | solution.py:338
  18.2 9.2 %copy-start.23 = (s32[24]{0:T(128)}, s32[24]{0:T(128)S(1)}, u32[]{:S(2)}) copy-start(s32[24]{0:T(128)S(1)} %reshape.227) | copy-start | bytes 292
  18.4 2.0 copy-start.22
  19.4 8.1 %copy-start.25 = (s32[24]{0:T(128)}, s32[24]{0:T(128)S(1)}, u32[]{:S(2)}) copy-start(s32[24]{0:T(128)S(1)} %reshape.228) | copy-start | bytes 292
  19.6 7.9 %copy-start.27 = (s32[24]{0:T(128)}, s32[24]{0:T(128)S(1)}, u32[]{:S(2)}) copy-start(s32[24]{0:T(128)S(1)} %reshape.229) | copy-start | bytes 292
  19.8 7.7 %copy-start.29 = (s32[24]{0:T(128)}, s32[24]{0:T(128)S(1)}, u32[]{:S(2)}) copy-start(s32[24]{0:T(128)S(1)} %reshape.230) | copy-start | bytes 292
  20.4 8.9 %copy-start.6 = (bf16[4,256,256]{2,1,0:T(8,128)(2,1)}, bf16[4,256,256]{2,1,0:T(8,128)(2,1)S(1)}, u32[]{:S(2)}) copy-start(bf16[4,256,256]{2,1,0:T(8,128)(2,1)S(1)} %collective-permute-done.4.refs_5_) | copy-start | bytes 1572868
  27.5 3.3 %copy-start.31 = (s32[1,512]{1,0:T(1,128)S(1)}, s32[1,512]{1,0:T(1,128)}, u32[]{:S(2)}) copy-start(s32[1,512]{1,0:T(1,128)} %get-tuple-element.50) | copy-start | bytes 6148
  28.8 2.8 %collective-permute-start.5 = (bf16[2,128,1024]{2,1,0:T(8,128)(2,1)S(1)}, bf16[2,128,1024]{2,1,0:T(8,128)(2,1)S(1)}, u32[]{:S(2)}, u32[]{:S(2)}) collective-permute-start(bf16[2,128,1024]{2,1,0:T(8,128)(2,1)S(1)} %bitcast.107), channel_id=1, source_target_pairs={{0,4},{4,0},{8,12},{12,8},{1,5},{5,1},{9,13},{13,9},{2,6},{6,2},{1... | collective-permute-start | bytes 1572872 | tf_op jit(solution)/shard_map/ppermute | solution.py:338
  29.3 24.7 %collective-permute-start.8 = (bf16[4,256,256]{2,1,0:T(8,128)(2,1)S(1)}, bf16[4,256,256]{2,1,0:T(8,128)(2,1)S(1)}, u32[]{:S(2)}, u32[]{:S(2)}) collective-permute-start(bf16[4,256,256]{2,1,0:T(8,128)(2,1)S(1)} %collective-permute-done.4.refs_5_), channel_id=1, source_target_pairs={{0,16},{16,0},{1,17},{17,1},{2,18},{18,2},{3,19},{19,3},{4,20},{20... | collective-permute-start | bytes 1572872 | tf_op jit(solution)/shard_map/ppermute | solution.py:388
  33.5 20.5 %collective-permute-start.7 = (bf16[2,64,2048]{2,1,0:T(8,128)(2,1)S(1)}, bf16[2,64,2048]{2,1,0:T(8,128)(2,1)S(1)}, u32[]{:S(2)}, u32[]{:S(2)}) collective-permute-start(bf16[2,64,2048]{2,1,0:T(8,128)(2,1)S(1)} %fusion.3), channel_id=1, source_target_pairs={{0,8},{4,12},{8,0},{12,4},{1,9},{5,13},{9,1},{13,5},{2,10},{6,14},... | collective-permute-start | bytes 1572872 | tf_op jit(solution)/shard_map/ppermute | solution.py:341
  35.0 18.2 %collective-permute-start.9 = (bf16[128,1024]{1,0:T(8,128)(2,1)S(1)}, bf16[128,1024]{1,0:T(8,128)(2,1)S(1)}, u32[]{:S(2)}, u32[]{:S(2)}) collective-permute-start(bf16[128,1024]{1,0:T(8,128)(2,1)S(1)} %get-tuple-element.90), channel_id=1, source_target_pairs={{0,8},{4,12},{8,0},{12,4},{1,9},{5,13},{9,1},{13,5},{2,10},{6,14},... | collective-permute-start | bytes 786440 | tf_op jit(solution)/shard_map/ppermute | solution.py:341
  46.3 15.6 %collective-permute-start.6 = (f32[2,128,2048]{2,1,0:T(8,128)}, f32[2,128,2048]{2,1,0:T(8,128)}, u32[]{:S(2)}, u32[]{:S(2)}) collective-permute-start(f32[2,128,2048]{2,1,0:T(8,128)} %get-tuple-element.47), channel_id=1, source_target_pairs={{0,4},{4,0},{8,12},{12,8},{1,5},{5,1},{9,13},{13,9},{2,6},{6,2},{1... | collective-permute-start | bytes 6291464 | tf_op jit(solution)/shard_map/ppermute | solution.py:338
  54.0 4.7 %copy-start.8 = (bf16[4,256,256]{2,1,0:T(8,128)(2,1)}, bf16[4,256,256]{2,1,0:T(8,128)(2,1)S(1)}, u32[]{:S(2)}) copy-start(bf16[4,256,256]{2,1,0:T(8,128)(2,1)S(1)} %collective-permute-done.8.refs_6_) | copy-start | bytes 1572868
  54.0 4.7 %copy-start.34 = (bf16[2,64,2048]{2,1,0:T(8,128)(2,1)}, bf16[2,64,2048]{2,1,0:T(8,128)(2,1)S(1)}, u32[]{:S(2)}) copy-start(bf16[2,64,2048]{2,1,0:T(8,128)(2,1)S(1)} %collective-permute-done.7.refs_0_) | copy-start | bytes 1572868
  54.0 6.0 %copy-start.21 = (s32[512]{0:T(512)S(1)}, s32[512]{0:T(512)}, u32[]{:S(2)}) copy-start(s32[512]{0:T(512)} %select_reduce_fusion) | copy-start | bytes 6148
  58.7 3.2 %copy-start.12 = (bf16[4,128,1024]{2,1,0:T(8,128)(2,1)S(1)}, bf16[4,128,1024]{2,1,0:T(8,128)(2,1)}, u32[]{:S(2)}) copy-start(bf16[4,128,1024]{2,1,0:T(8,128)(2,1)} %shard_map.121) | copy-start | bytes 3145732
  59.9 2.0 collective-permute-start.10
  63.6 20.4 %collective-permute-start.12 = (bf16[2,64,2048]{2,1,0:T(8,128)(2,1)S(1)}, bf16[2,64,2048]{2,1,0:T(8,128)(2,1)S(1)}, u32[]{:S(2)}, u32[]{:S(2)}) collective-permute-start(bf16[2,64,2048]{2,1,0:T(8,128)(2,1)S(1)} %fusion.2), channel_id=1, source_target_pairs={{0,8},{4,12},{8,0},{12,4},{1,9},{5,13},{9,1},{13,5},{2,10},{6,14},... | collective-permute-start | bytes 1572872 | tf_op jit(solution)/shard_map/ppermute | solution.py:341
  65.1 18.1 %collective-permute-start.11 = (bf16[128,1024]{1,0:T(8,128)(2,1)S(1)}, bf16[128,1024]{1,0:T(8,128)(2,1)S(1)}, u32[]{:S(2)}, u32[]{:S(2)}) collective-permute-start(bf16[128,1024]{1,0:T(8,128)(2,1)S(1)} %get-tuple-element.88), channel_id=1, source_target_pairs={{0,8},{4,12},{8,0},{12,4},{1,9},{5,13},{9,1},{13,5},{2,10},{6,14},... | collective-permute-start | bytes 786440 | tf_op jit(solution)/shard_map/ppermute | solution.py:341
  76.5 11.0 %collective-permute-start.13 = (f32[2,128,2048]{2,1,0:T(8,128)}, f32[2,128,2048]{2,1,0:T(8,128)S(1)}, u32[]{:S(2)}, u32[]{:S(2)}) collective-permute-start(f32[2,128,2048]{2,1,0:T(8,128)} %get-tuple-element.57), channel_id=1, source_target_pairs={{0,4},{4,0},{8,12},{12,8},{1,5},{5,1},{9,13},{13,9},{2,6},{6,2},{1... | collective-permute-start | bytes 6291464 | tf_op jit(solution)/shard_map/ppermute | solution.py:338
  84.0 3.4 %copy-start.35 = (bf16[2,64,2048]{2,1,0:T(8,128)(2,1)}, bf16[2,64,2048]{2,1,0:T(8,128)(2,1)S(1)}, u32[]{:S(2)}) copy-start(bf16[2,64,2048]{2,1,0:T(8,128)(2,1)S(1)} %collective-permute-done.12.refs_0_) | copy-start | bytes 1572868
  84.0 3.4 %copy-start.1 = (f32[2,128,2048]{2,1,0:T(8,128)S(1)}, f32[2,128,2048]{2,1,0:T(8,128)}, u32[]{:S(2)}) copy-start(f32[2,128,2048]{2,1,0:T(8,128)} %get-tuple-element.56.keep) | copy-start | bytes 6291460
  87.5 1.6 copy-start.17
  87.5 13.0 %copy-start.2 = (f32[2,128,2048]{2,1,0:T(8,128)}, f32[2,128,2048]{2,1,0:T(8,128)S(1)}, u32[]{:S(2)}) copy-start(f32[2,128,2048]{2,1,0:T(8,128)S(1)} %collective-permute-done.13.core) | copy-start | bytes 6291460
  87.6 18.8 %collective-permute-start.15 = (bf16[2,64,2048]{2,1,0:T(8,128)(2,1)S(1)}, bf16[2,64,2048]{2,1,0:T(8,128)(2,1)S(1)}, u32[]{:S(2)}, u32[]{:S(2)}) collective-permute-start(bf16[2,64,2048]{2,1,0:T(8,128)(2,1)S(1)} %fusion.1), channel_id=1, source_target_pairs={{0,8},{4,12},{8,0},{12,4},{1,9},{5,13},{9,1},{13,5},{2,10},{6,14},... | collective-permute-start | bytes 1572872 | tf_op jit(solution)/shard_map/ppermute | solution.py:341
  89.1 17.4 %collective-permute-start.16 = (bf16[64,2048]{1,0:T(8,128)(2,1)S(1)}, bf16[64,2048]{1,0:T(8,128)(2,1)S(1)}, u32[]{:S(2)}, u32[]{:S(2)}) collective-permute-start(bf16[64,2048]{1,0:T(8,128)(2,1)S(1)} %copy-done.17), channel_id=1, source_target_pairs={{0,8},{4,12},{8,0},{12,4},{1,9},{5,13},{9,1},{13,5},{2,10},{6,14},... | collective-permute-start | bytes 786440 | tf_op jit(solution)/shard_map/ppermute | solution.py:341
  100.5 10.8 %collective-permute-start.14 = (f32[2,128,2048]{2,1,0:T(8,128)}, f32[2,128,2048]{2,1,0:T(8,128)S(1)}, u32[]{:S(2)}, u32[]{:S(2)}) collective-permute-start(f32[2,128,2048]{2,1,0:T(8,128)} %get-tuple-element.60), channel_id=1, source_target_pairs={{0,4},{4,0},{8,12},{12,8},{1,5},{5,1},{9,13},{13,9},{2,6},{6,2},{1... | collective-permute-start | bytes 6291464 | tf_op jit(solution)/shard_map/ppermute | solution.py:338
  107.9 3.4 %copy-start.3 = (f32[2,128,2048]{2,1,0:T(8,128)S(1)}, f32[2,128,2048]{2,1,0:T(8,128)}, u32[]{:S(2)}) copy-start(f32[2,128,2048]{2,1,0:T(8,128)} %get-tuple-element.62.keep) | copy-start | bytes 6291460
  111.3 3.0 %copy-start.9 = (bf16[4,256,256]{2,1,0:T(8,128)(2,1)S(1)}, bf16[4,256,256]{2,1,0:T(8,128)(2,1)}, u32[]{:S(2)}) copy-start(bf16[4,256,256]{2,1,0:T(8,128)(2,1)} %copy-done.8) | copy-start | bytes 1572868
  111.3 3.0 %copy-start = (bf16[4,2,256,256]{3,2,1,0:T(8,128)(2,1)S(1)}, bf16[4,2,256,256]{3,2,1,0:T(8,128)(2,1)}, u32[]{:S(2)}) copy-start(bf16[4,2,256,256]{3,2,1,0:T(8,128)(2,1)} %param.20) | copy-start | bytes 3145732
  112.9 15.2 %collective-permute-start.17 = (bf16[2,64,2048]{2,1,0:T(8,128)(2,1)}, bf16[2,64,2048]{2,1,0:T(8,128)(2,1)}, u32[]{:S(2)}, u32[]{:S(2)}) collective-permute-start(bf16[2,64,2048]{2,1,0:T(8,128)(2,1)} %fusion), channel_id=1, source_target_pairs={{0,8},{4,12},{8,0},{12,4},{1,9},{5,13},{9,1},{13,5},{2,10},{6,14},... | collective-permute-start | bytes 1572872 | tf_op jit(solution)/shard_map/ppermute | solution.py:341
  114.3 29.6 %collective-permute-start.22 = (bf16[4,256,256]{2,1,0:T(8,128)(2,1)S(1)}, bf16[4,256,256]{2,1,0:T(8,128)(2,1)S(1)}, u32[]{:S(2)}, u32[]{:S(2)}) collective-permute-start(bf16[4,256,256]{2,1,0:T(8,128)(2,1)S(1)} %copy-done.9), channel_id=1, source_target_pairs={{0,4},{4,0},{8,12},{12,8},{1,5},{5,1},{9,13},{13,9},{2,6},{6,2},{1... | collective-permute-start | bytes 1572872 | tf_op jit(solution)/shard_map/ppermute | solution.py:338
  114.3 31.8 %collective-permute-start.23 = (bf16[8,256,256]{2,1,0:T(8,128)(2,1)S(1)}, bf16[8,256,256]{2,1,0:T(8,128)(2,1)S(1)}, u32[]{:S(2)}, u32[]{:S(2)}) collective-permute-start(bf16[8,256,256]{2,1,0:T(8,128)(2,1)S(1)} %bitcast.99), channel_id=1, source_target_pairs={{0,4},{4,0},{8,12},{12,8},{1,5},{5,1},{9,13},{13,9},{2,6},{6,2},{1... | collective-permute-start | bytes 3145736 | tf_op jit(solution)/shard_map/ppermute | solution.py:338
  114.8 18.8 %collective-permute-start.19 = (bf16[64,2048]{1,0:T(8,128)(2,1)}, bf16[64,2048]{1,0:T(8,128)(2,1)S(1)}, u32[]{:S(2)}, u32[]{:S(2)}) collective-permute-start(bf16[64,2048]{1,0:T(8,128)(2,1)} %shard_map.125), channel_id=1, source_target_pairs={{0,8},{4,12},{8,0},{12,4},{1,9},{5,13},{9,1},{13,5},{2,10},{6,14},... | collective-permute-start | bytes 786440 | tf_op jit(solution)/shard_map/ppermute | solution.py:341
  118.6 14.2 %copy-start.19 = (bf16[64,2048]{1,0:T(8,128)(2,1)S(1)}, bf16[64,2048]{1,0:T(8,128)(2,1)}, u32[]{:S(2)}) copy-start(bf16[64,2048]{1,0:T(8,128)(2,1)} %copy-done.18) | copy-start | bytes 786436
  118.6 15.0 %copy-start.7 = (bf16[4,256,256]{2,1,0:T(8,128)(2,1)S(1)}, bf16[4,256,256]{2,1,0:T(8,128)(2,1)}, u32[]{:S(2)}) copy-start(bf16[4,256,256]{2,1,0:T(8,128)(2,1)} %copy-done.6) | copy-start | bytes 1572868
  118.6 15.0 %copy-start.20 = (bf16[64,2048]{1,0:T(8,128)(2,1)S(1)}, bf16[64,2048]{1,0:T(8,128)(2,1)}, u32[]{:S(2)}) copy-start(bf16[64,2048]{1,0:T(8,128)(2,1)} %shard_map.125) | copy-start | bytes 786436
  118.6 20.6 %collective-permute-start.27 = (bf16[64,2048]{1,0:T(8,128)(2,1)}, bf16[64,2048]{1,0:T(8,128)(2,1)S(1)}, u32[]{:S(2)}, u32[]{:S(2)}) collective-permute-start(bf16[64,2048]{1,0:T(8,128)(2,1)} %shard_map.126), channel_id=1, source_target_pairs={{0,8},{4,12},{8,0},{12,4},{1,9},{5,13},{9,1},{13,5},{2,10},{6,14},... | collective-permute-start | bytes 786440 | tf_op jit(solution)/shard_map/ppermute | solution.py:341
  131.3 10.9 %copy-start.13 = (bf16[64,2048]{1,0:T(8,128)(2,1)S(1)}, bf16[64,2048]{1,0:T(8,128)(2,1)}, u32[]{:S(2)}) copy-start(bf16[64,2048]{1,0:T(8,128)(2,1)} %shard_map.126) | copy-start | bytes 786436
  131.3 11.7 %copy-start.14 = (bf16[64,2048]{1,0:T(8,128)(2,1)S(1)}, bf16[64,2048]{1,0:T(8,128)(2,1)}, u32[]{:S(2)}) copy-start(bf16[64,2048]{1,0:T(8,128)(2,1)} %shard_map.127) | copy-start | bytes 786436
  131.3 14.1 %copy-start.24 = (s32[24]{0:T(128)S(1)}, s32[24]{0:T(128)}, u32[]{:S(2)}) copy-start(s32[24]{0:T(128)} %copy-done.23) | copy-start | bytes 292
  131.3 14.1 %copy-start.26 = (s32[24]{0:T(128)S(1)}, s32[24]{0:T(128)}, u32[]{:S(2)}) copy-start(s32[24]{0:T(128)} %copy-done.25) | copy-start | bytes 292
  131.3 14.1 %copy-start.28 = (s32[24]{0:T(128)S(1)}, s32[24]{0:T(128)}, u32[]{:S(2)}) copy-start(s32[24]{0:T(128)} %copy-done.27) | copy-start | bytes 292
  131.3 14.1 %copy-start.30 = (s32[24]{0:T(128)S(1)}, s32[24]{0:T(128)}, u32[]{:S(2)}) copy-start(s32[24]{0:T(128)} %copy-done.29) | copy-start | bytes 292
  131.3 10.8 %collective-permute-start.29 = (bf16[64,2048]{1,0:T(8,128)(2,1)}, bf16[64,2048]{1,0:T(8,128)(2,1)S(1)}, u32[]{:S(2)}, u32[]{:S(2)}) collective-permute-start(bf16[64,2048]{1,0:T(8,128)(2,1)} %shard_map.127), channel_id=1, source_target_pairs={{0,8},{4,12},{8,0},{12,4},{1,9},{5,13},{9,1},{13,5},{2,10},{6,14},... | collective-permute-start | bytes 786440 | tf_op jit(solution)/shard_map/ppermute | solution.py:341
  133.6 10.8 %collective-permute-start.21 = (bf16[4,256,256]{2,1,0:T(8,128)(2,1)S(1)}, bf16[4,256,256]{2,1,0:T(8,128)(2,1)S(1)}, u32[]{:S(2)}, u32[]{:S(2)}) collective-permute-start(bf16[4,256,256]{2,1,0:T(8,128)(2,1)S(1)} %copy-done.7), channel_id=1, source_target_pairs={{0,4},{4,0},{8,12},{12,8},{1,5},{5,1},{9,13},{13,9},{2,6},{6,2},{1... | collective-permute-start | bytes 1572872 | tf_op jit(solution)/shard_map/ppermute | solution.py:338
  139.2 6.9 %collective-permute-start.18 = (bf16[128,2048]{1,0:T(8,128)(2,1)}, bf16[128,2048]{1,0:T(8,128)(2,1)}, u32[]{:S(2)}, u32[]{:S(2)}) collective-permute-start(bf16[128,2048]{1,0:T(8,128)(2,1)} %pad_maximum_fusion.refs_2_), channel_id=1, source_target_pairs={{0,4},{4,0},{8,12},{12,8},{1,5},{5,1},{9,13},{13,9},{2,6},{6,2},{1... | collective-permute-start | bytes 1572872 | tf_op jit(solution)/shard_map/ppermute | solution.py:338
  142.2 3.9 %collective-permute-start.20 = (bf16[128,2048]{1,0:T(8,128)(2,1)}, bf16[128,2048]{1,0:T(8,128)(2,1)}, u32[]{:S(2)}, u32[]{:S(2)}) collective-permute-start(bf16[128,2048]{1,0:T(8,128)(2,1)} %pad_maximum_fusion.1.refs_3_), channel_id=1, source_target_pairs={{0,4},{4,0},{8,12},{12,8},{1,5},{5,1},{9,13},{13,9},{2,6},{6,2},{1... | collective-permute-start | bytes 1572872 | tf_op jit(solution)/shard_map/ppermute | solution.py:338
  143.9 2.2 %copy-start.10 = (bf16[4,256,256]{2,1,0:T(8,128)(2,1)}, bf16[4,256,256]{2,1,0:T(8,128)(2,1)S(1)}, u32[]{:S(2)}) copy-start(bf16[4,256,256]{2,1,0:T(8,128)(2,1)S(1)} %collective-permute-done.22.refs_9_) | copy-start | bytes 1572868
  143.9 26.1 %collective-permute-start.28 = (bf16[128,2048]{1,0:T(8,128)(2,1)}, bf16[128,2048]{1,0:T(8,128)(2,1)S(1)}, u32[]{:S(2)}, u32[]{:S(2)}) collective-permute-start(bf16[128,2048]{1,0:T(8,128)(2,1)} %pad_maximum_fusion.2.refs_2_), channel_id=1, source_target_pairs={{0,4},{4,0},{8,12},{12,8},{1,5},{5,1},{9,13},{13,9},{2,6},{6,2},{1... | collective-permute-start | bytes 1572872 | tf_op jit(solution)/shard_map/ppermute | solution.py:338
  145.2 24.8 %collective-permute-start.30 = (bf16[128,2048]{1,0:T(8,128)(2,1)}, bf16[128,2048]{1,0:T(8,128)(2,1)}, u32[]{:S(2)}, u32[]{:S(2)}) collective-permute-start(bf16[128,2048]{1,0:T(8,128)(2,1)} %pad_maximum_fusion.3.refs_3_), channel_id=1, source_target_pairs={{0,4},{4,0},{8,12},{12,8},{1,5},{5,1},{9,13},{13,9},{2,6},{6,2},{1... | collective-permute-start | bytes 1572872 | tf_op jit(solution)/shard_map/ppermute | solution.py:338
  164.1 23.7 %collective-permute-start.24 = (bf16[4,16,2048]{2,1,0:T(8,128)(2,1)S(1)}, bf16[4,16,2048]{2,1,0:T(8,128)(2,1)S(1)}, u32[]{:S(2)}, u32[]{:S(2)}) collective-permute-start(bf16[4,16,2048]{2,1,0:T(8,128)(2,1)S(1)} %get-tuple-element.80), channel_id=1, source_target_pairs={{0,1},{1,2},{2,3},{3,0},{4,5},{5,6},{6,7},{7,4},{8,9},{9,10},{10,1... | collective-permute-start | bytes 786440 | tf_op jit(solution)/shard_map/ppermute | solution.py:524
  166.2 22.7 %collective-permute-start.25 = (bf16[4,16,2048]{2,1,0:T(8,128)(2,1)S(1)}, bf16[4,16,2048]{2,1,0:T(8,128)(2,1)S(1)}, u32[]{:S(2)}, u32[]{:S(2)}) collective-permute-start(bf16[4,16,2048]{2,1,0:T(8,128)(2,1)S(1)} %get-tuple-element.82), channel_id=1, source_target_pairs={{0,2},{1,3},{2,0},{3,1},{4,6},{5,7},{6,4},{7,5},{8,10},{9,11},{10,... | collective-permute-start | bytes 786440 | tf_op jit(solution)/shard_map/ppermute | solution.py:524
  168.5 20.7 %collective-permute-start.26 = (bf16[4,16,2048]{2,1,0:T(8,128)(2,1)S(1)}, bf16[4,16,2048]{2,1,0:T(8,128)(2,1)S(1)}, u32[]{:S(2)}, u32[]{:S(2)}) collective-permute-start(bf16[4,16,2048]{2,1,0:T(8,128)(2,1)S(1)} %get-tuple-element.81), channel_id=1, source_target_pairs={{0,3},{1,0},{2,1},{3,2},{4,7},{5,4},{6,5},{7,6},{8,11},{9,8},{10,9... | collective-permute-start | bytes 786440 | tf_op jit(solution)/shard_map/ppermute | solution.py:524
  187.8 11.1 %collective-permute-start.31 = (bf16[4,16,2048]{2,1,0:T(8,128)(2,1)S(1)}, bf16[4,16,2048]{2,1,0:T(8,128)(2,1)S(1)}, u32[]{:S(2)}, u32[]{:S(2)}) collective-permute-start(bf16[4,16,2048]{2,1,0:T(8,128)(2,1)S(1)} %get-tuple-element.73), channel_id=1, source_target_pairs={{0,1},{1,2},{2,3},{3,0},{4,5},{5,6},{6,7},{7,4},{8,9},{9,10},{10,1... | collective-permute-start | bytes 786440 | tf_op jit(solution)/shard_map/ppermute | solution.py:524
  188.8 20.7 %collective-permute-start.32 = (bf16[4,16,2048]{2,1,0:T(8,128)(2,1)S(1)}, bf16[4,16,2048]{2,1,0:T(8,128)(2,1)S(1)}, u32[]{:S(2)}, u32[]{:S(2)}) collective-permute-start(bf16[4,16,2048]{2,1,0:T(8,128)(2,1)S(1)} %get-tuple-element.74), channel_id=1, source_target_pairs={{0,2},{1,3},{2,0},{3,1},{4,6},{5,7},{6,4},{7,5},{8,10},{9,11},{10,... | collective-permute-start | bytes 786440 | tf_op jit(solution)/shard_map/ppermute | solution.py:524
  189.2 20.4 %collective-permute-start.33 = (bf16[4,16,2048]{2,1,0:T(8,128)(2,1)S(1)}, bf16[4,16,2048]{2,1,0:T(8,128)(2,1)S(1)}, u32[]{:S(2)}, u32[]{:S(2)}) collective-permute-start(bf16[4,16,2048]{2,1,0:T(8,128)(2,1)S(1)} %get-tuple-element.75), channel_id=1, source_target_pairs={{0,3},{1,0},{2,1},{3,2},{4,7},{5,4},{6,5},{7,6},{8,11},{9,8},{10,9... | collective-permute-start | bytes 786440 | tf_op jit(solution)/shard_map/ppermute | solution.py:524
  (6 other events, 5.7 us)

commit v6 on v5

--- a/solution.py
+++ b/solution.py
@@ -173,6 +173,29 @@
     )(scal, *[view] * owners, wg, wu)
 
 
+def total_body(order, *refs):
+    total = refs[0][...]
+    for ref in refs[1:-1]:
+        total = total + ref[...]
+    refs[-1][...] = total
+
+
+def total_of(order, parts):
+    shape = parts[0].shape
+    return pl.pallas_call(
+        total_body,
+        grid_spec=pltpu.PrefetchScalarGridSpec(
+            num_scalar_prefetch=1,
+            grid=(1,),
+            in_specs=[whole(shape)] * len(parts),
+            out_specs=whole(shape),
+        ),
+        out_shape=jax.ShapeDtypeStruct(shape, parts[0].dtype),
+        compiler_params=pltpu.CompilerParams(vmem_limit_bytes=VMEM),
+        cost_estimate=cost(SHORT, 1e6),
+    )(order, *parts)
+
+
 def activate_body(per_slot, start, each, row, parts, skip, keep, core, *refs):
     gots, (delta, slot, table, out) = refs[:parts], refs[parts:]
     tile = 256
@@ -426,10 +449,7 @@
         return x[half:] + core_swap(x[:half])
 
     def finish(x, *earlier):
-        total = after(x[ys - 1], *earlier)
-        for k in range(1, ys):
-            total = total + y_move(x[k - 1], k)
-        return total
+        return total_of(after(homes, *earlier), [x[ys - 1]] + [y_move(x[k - 1], k) for k in range(1, ys)])
 
     ahead, second, third, fourth = (0, 0), (0, 1), (1, 0), (1, 1)
     multiply(ahead)
@@ -458,9 +478,10 @@
     ss_q = slot_q[:, None]
 
     multiply(second, *sends[ahead], packed)
-    features = finish(packed, kept[second])
+    features = finish(packed, kept[second], *gots[ahead])
+    exchange(second, features)
     spread = product(
-        after(scal, kept[second], *gots[ahead], *arrived),
+        after(scal, *sends[second], *arrived),
         features,
         gate_tiles,
         up_tiles,
@@ -469,10 +490,10 @@
         per_owner,
         pieces,
     )
-    exchange(second)
     spread = halve(spread)
     multiply(third, *sends[second], spread)
     home_delta = finish(spread, kept[third])
+    exchange(third, home_delta)
 
     near_tiles = [*tiles, flat_tiles]
     all_tiles = near_tiles + [core_swap(after(t, kept[second])) for t in near_tiles]
@@ -525,17 +546,16 @@
             total = total + came[-1].astype(F32)
         return out, came, total.astype(BF)
 
-    hid_a, moved_a = finish_hidden(ahead, SHORT, kept[third], *gots[second])
-    exchange(third, hid_a)
-    multiply(fourth, *sends[third], hid_a)
+    hid_a, moved_a = finish_hidden(ahead, 1e9, *sends[third])
+    multiply(fourth, *sends[third], hid_a, *gots[second])
     hid_b, moved_b = finish_hidden(second, SHORT, kept[fourth], *gots[third], *moved_a)
-    exchange(fourth, hid_b)
-    hid_c, moved_c = finish_hidden(third, 1e9, hid_b, *sends[fourth])
-    hid_d, moved_d = finish_hidden(fourth, 1e9, hid_c)
+    hid_c, moved_c = finish_hidden(third, 1e9, hid_b)
+    exchange(fourth, hid_c, *moved_b)
     first = [join(hid_a, moved_a, hid_b), join(hid_b, moved_b, hid_c)]
+    out, came, total = finish_down(0, first, sends[fourth])
+    result = [total]
+    hid_d, moved_d = finish_hidden(fourth, 1e9, out)
     last = [join(hid_c, moved_c, hid_d), join(hid_d, moved_d)]
-    out, came, total = finish_down(0, first, (hid_d,))
-    result = [total]
     out, came, total = finish_down(1, last, (out,), came)
     result.append(total)
 

time: 216 us -> 210 us (0.972)
  the two profiles are of different devices: /device:TPU:0 before, /device:TPU:5 now
where the time goes in v6:
time: 210 us; the launch traced here: 208 us
  Pallas kernels  104 us (50%)
  waiting for transfers between devices  41.6 us (20%)
  starting transfers between devices  31.3 us (15%)
  local copies, waits for them, and re-layouts  15.8 us (8%)
  other arithmetic  15.3 us (7%)
    pallas_call x4, Pallas kernels, gate_up(): pl.pallas_call(functools.partial(gate_up_body, owners), grid_spec=pltpu.P...  42.5 us
    pallas_call x2, Pallas kernels, down(): pl.pallas_call(functools.partial(down_body, width_tiles, width // 256, pl...  31.2 us
    ppermute x6, waiting for transfers between devices, finish_down(): lax.ppermute(gone, 'tensor', [(j, (j + k) % shift) for j in range(shift)])  21.7 us
    ppermute x11, waiting for transfers between devices, y_move(): lax.ppermute(x, 'delta', [(i, (i + 2 * k) % owners) for i in range(owners)])  18.9 us
    pallas_call x4, Pallas kernels, activate(): pl.pallas_call(functools.partial(activate_body, per_slot, start, each, ro...  13.1 us
    ppermute x6, starting transfers between devices, finish_down(): lax.ppermute(gone, 'tensor', [(j, (j + k) % shift) for j in range(shift)])  11.1 us
    ppermute x13, starting transfers between devices, core_swap(): return lax.ppermute(x, 'delta', [(i, i ^ 1) for i in range(owners)])  8.88 us
    ppermute x11, starting transfers between devices, y_move(): lax.ppermute(x, 'delta', [(i, (i + 2 * k) % owners) for i in range(owners)])  7.66 us
  transfers between devices with their start and end apart: 34, of which 9 were waited for; matrix products, arithmetic and copies ran while one was open for 11% of the time, Pallas kernels for 48%

profile of v6, /device:TPU:5, one launch (start us, length us, event | category | flops | bytes accessed | tf_op | source)
XLA Modules:
  0.0 208.1 jit_solution(1265659257416312082)
XLA Ops:
  0.0 0.7 pad_add_fusion
  0.7 0.7 collective-permute-start
  1.4 1.7 collective-permute-start.2
  3.1 1.1 constant_dynamic-slice_fusion
  4.2 1.2 collective-permute-start.4
  6.0 10.6 %shard_map.118 = (f32[2,128,2048]{2,1,0:T(8,128)}, f32[2,128,2048]{2,1,0:T(8,128)}) custom-call(s32[4]{0:T(128)} %get-tuple-element.60.scal.order, bf16[4,8,16,2048]{3,2,1,0:T(8,128)(2,1)} %bitcast.80, bf16[4,8,16,2048]{3,2,1,0:T(8,128)(2,1)} %bitcast.81, bf16[4,8,16,2048]{3,2,1,0:T(8,128)(2,1)} %bitcast.82, bf16[4,8,16,2048]{3,2,1,0:T(8,128)(2,1)} %bitcast.83, ...), custom_call_target="tpu_custom_call" | custom-call | flops 4294967296 | bytes 16777216 | tf_op jit(solution)/shard_map/pallas_call | solution.py:161
  17.0 0.9 copy.38.ss
  18.4 0.7 concatenate.36.scal
  19.1 7.1 %shard_map.119 = (bf16[512,1024]{1,0:T(8,128)(2,1)}, s32[1,512]{1,0:T(1,128)}, bf16[128,128]{1,0:T(8,128)(2,1)}) custom-call(s32[101]{0:T(128)} %concatenate.36.scal, bf16[512,2048]{1,0:T(8,128)(2,1)} %x.1, s32[1,512]{1,0:T(1,128)} %bitcast.110, s32[512,1]{1,0:T(8,128)} %copy.38.ss), custom_call_target="tpu_custom_call" | custom-call | flops 120000004096 | bytes 4000000 | tf_op jit(solution)/shard_map/pallas_call | solution.py:71
  26.2 2.2 %fusion.18 = (bf16[256,1024]{1,0:T(8,128)(2,1)}, bf16[256,1024]{1,0:T(8,128)(2,1)S(1)}) fusion(bf16[512,1024]{1,0:T(8,128)(2,1)} %get-tuple-element.45), kind=kLoop, calls=%fused_computation.67 | loop fusion | bytes 2097152 | tf_op jit(solution)/shard_map/slice | solution.py:449
  29.2 1.3 collective-permute-start.9
  30.5 0.8 select_reduce_fusion
  31.4 1.2 add.251
  32.6 1.3 fusion.3
  34.4 0.8 slice_bitcast_fusion.2
  35.1 1.1 collective-permute-start.7
  36.3 10.6 %shard_map.120 = (f32[2,128,2048]{2,1,0:T(8,128)}, f32[2,128,2048]{2,1,0:T(8,128)}) custom-call(s32[4]{0:T(128)} %get-tuple-element.60.scal.order, bf16[4,8,16,2048]{3,2,1,0:T(8,128)(2,1)} %bitcast.84, bf16[4,8,16,2048]{3,2,1,0:T(8,128)(2,1)} %bitcast.85, bf16[4,8,16,2048]{3,2,1,0:T(8,128)(2,1)} %bitcast.86, bf16[4,8,16,2048]{3,2,1,0:T(8,128)(2,1)} %bitcast.87, ...), custom_call_target="tpu_custom_call" | custom-call | flops 4294967296 | bytes 16777216 | tf_op jit(solution)/shard_map/pallas_call | solution.py:161
  46.8 0.9 collective-permute-start.8
  47.7 5.1 %collective-permute-done.7.refs_1_ = bf16[128,1024]{1,0:T(8,128)(2,1)S(1)} collective-permute-done((bf16[128,1024]{1,0:T(8,128)(2,1)S(1)}, bf16[128,1024]{1,0:T(8,128)(2,1)S(1)}, u32[]{:S(2)}, u32[]{:S(2)}) %collective-permute-start.7) | collective-permute-done | bytes 262176 | tf_op jit(solution)/shard_map/ppermute | solution.py:364
  52.8 0.7 copy-done.34
  53.5 2.6 %shard_map.121.x = bf16[128,1024]{1,0:T(8,128)(2,1)} custom-call(s32[4]{0:T(128)} %get-tuple-element.60.scal.order, bf16[128,1024]{1,0:T(8,128)(2,1)} %get-tuple-element.93.refs_0_, bf16[128,1024]{1,0:T(8,128)(2,1)} %copy-done.34), custom_call_target="tpu_custom_call" | custom-call | flops 120000004096 | bytes 1000000 | tf_op jit(solution)/shard_map/pallas_call | solution.py:185
  56.3 4.7 %shard_map.122 = bf16[4,128,1024]{2,1,0:T(8,128)(2,1)} custom-call(s32[101]{0:T(128)} %concatenate.36.scal, bf16[128,1024]{1,0:T(8,128)(2,1)} %shard_map.121.x, bf16[4,2,256,256]{3,2,1,0:T(8,128)(2,1)} %gt.1, bf16[4,2,256,256]{3,2,1,0:T(8,128)(2,1)} %ut.1, s32[1,512]{1,0:T(1,128)} %bitcast.107), custom_call_target="tpu_custom_call" | custom-call | flops 120000004096 | bytes 4000000 | tf_op jit(solution)/shard_map/pallas_call | solution.py:117
  60.9 1.1 slice.82
  62.0 1.2 collective-permute-start.10
  63.8 1.0 collective-permute-done.10
  64.8 1.1 slice_add_fusion.4
  65.9 0.7 slice_bitcast_fusion
  67.0 10.7 %shard_map.123 = (f32[2,128,2048]{2,1,0:T(8,128)}, f32[2,128,2048]{2,1,0:T(8,128)}) custom-call(s32[4]{0:T(128)} %get-tuple-element.60.scal.order, bf16[4,8,16,2048]{3,2,1,0:T(8,128)(2,1)} %bitcast.88, bf16[4,8,16,2048]{3,2,1,0:T(8,128)(2,1)} %bitcast.89, bf16[4,8,16,2048]{3,2,1,0:T(8,128)(2,1)} %bitcast.90, bf16[4,8,16,2048]{3,2,1,0:T(8,128)(2,1)} %bitcast.91, ...), custom_call_target="tpu_custom_call" | custom-call | flops 4294967296 | bytes 16777216 | tf_op jit(solution)/shard_map/pallas_call | solution.py:161
  78.4 4.2 %collective-permute-done.11.refs_1_ = bf16[128,1024]{1,0:T(8,128)(2,1)S(1)} collective-permute-done((bf16[128,1024]{1,0:T(8,128)(2,1)S(1)}, bf16[128,1024]{1,0:T(8,128)(2,1)S(1)}, u32[]{:S(2)}, u32[]{:S(2)}) %collective-permute-start.11) | collective-permute-done | bytes 262176 | tf_op jit(solution)/shard_map/ppermute | solution.py:364
  82.6 0.7 copy-done.35
  83.3 2.5 %shard_map.124.refs_1_ = bf16[128,1024]{1,0:T(8,128)(2,1)} custom-call(s32[4]{0:T(128)} %get-tuple-element.60.scal.order, bf16[128,1024]{1,0:T(8,128)(2,1)} %get-tuple-element.91.refs_0_, bf16[128,1024]{1,0:T(8,128)(2,1)} %copy-done.35), custom_call_target="tpu_custom_call" | custom-call | flops 120000004096 | bytes 1000000 | tf_op jit(solution)/shard_map/pallas_call | solution.py:185
  86.4 0.9 add_select_fusion.refs_2_.refs_11_
  87.3 1.1 collective-permute-start.21
  88.9 3.2 %shard_map.125 = bf16[64,2048]{1,0:T(8,128)(2,1)} custom-call(f32[2,128,2048]{2,1,0:T(8,128)} %get-tuple-element.42.keep, f32[2,128,2048]{2,1,0:T(8,128)} %collective-permute-done.3.core, bf16[2,64,2048]{2,1,0:T(8,128)(2,1)} %copy-done.18, bf16[128,1024]{1,0:T(8,128)(2,1)} %shard_map.124.refs_1_, s32[512,1]{1,0:T(8,128)} %add_select_fusion.refs_2_.refs_11_, ...), custom_call_target="tpu_custom_call" | custom-call | flops 1000000000 | bytes 3145728 | tf_op jit(solution)/shard_map/pallas_call | solution.py:230
  92.1 1.2 collective-permute-start.15
  93.2 10.5 %shard_map.126 = (f32[2,128,2048]{2,1,0:T(8,128)}, f32[2,128,2048]{2,1,0:T(8,128)}) custom-call(s32[4]{0:T(128)} %get-tuple-element.60.scal.order, bf16[4,8,16,2048]{3,2,1,0:T(8,128)(2,1)} %bitcast.92, bf16[4,8,16,2048]{3,2,1,0:T(8,128)(2,1)} %bitcast.93, bf16[4,8,16,2048]{3,2,1,0:T(8,128)(2,1)} %bitcast.94, bf16[4,8,16,2048]{3,2,1,0:T(8,128)(2,1)} %bitcast.95, ...), custom_call_target="tpu_custom_call" | custom-call | flops 4294967296 | bytes 16777216 | tf_op jit(solution)/shard_map/pallas_call | solution.py:161
  104.3 1.7 collective-permute-start.17
  106.0 3.4 %shard_map.127 = bf16[64,2048]{1,0:T(8,128)(2,1)} custom-call(f32[2,128,2048]{2,1,0:T(8,128)} %get-tuple-element.49.keep, f32[2,128,2048]{2,1,0:T(8,128)} %copy-done.17, bf16[2,64,2048]{2,1,0:T(8,128)(2,1)} %collective-permute-done.13.refs_0_, bf16[128,1024]{1,0:T(8,128)(2,1)} %shard_map.124.refs_1_, s32[512,1]{1,0:T(8,128)} %add_select_fusion.refs_2_.refs_11_, ...), custom_call_target="tpu_custom_call" | custom-call | flops 120000004096 | bytes 3145728 | tf_op jit(solution)/shard_map/pallas_call | solution.py:230
  109.8 3.3 %shard_map.128 = bf16[64,2048]{1,0:T(8,128)(2,1)} custom-call(f32[2,128,2048]{2,1,0:T(8,128)} %get-tuple-element.56.keep, f32[2,128,2048]{2,1,0:T(8,128)} %copy-done.6, bf16[2,64,2048]{2,1,0:T(8,128)(2,1)} %copy-done.19, bf16[128,1024]{1,0:T(8,128)(2,1)} %shard_map.124.refs_1_, s32[512,1]{1,0:T(8,128)} %add_select_fusion.refs_2_.refs_11_, ...), custom_call_target="tpu_custom_call" | custom-call | flops 1000000000 | bytes 3145728 | tf_op jit(solution)/shard_map/pallas_call | solution.py:230
  113.2 0.8 pad_maximum_fusion.refs_2_
  114.0 3.7 %collective-permute-done.16 = bf16[64,2048]{1,0:T(8,128)(2,1)} collective-permute-done((bf16[64,2048]{1,0:T(8,128)(2,1)}, bf16[64,2048]{1,0:T(8,128)(2,1)}, u32[]{:S(2)}, u32[]{:S(2)}) %collective-permute-start.16) | collective-permute-done | bytes 262176 | tf_op jit(solution)/shard_map/ppermute | solution.py:364
  117.7 0.8 collective-permute-start.18
  118.5 1.8 pad_maximum_fusion.1.refs_3_
  120.4 1.0 fusion
  122.7 0.8 copy-done.10
  123.5 0.7 collective-permute-start.26
  124.8 0.8 copy-done.15
  125.6 15.6 %shard_map.129 = f32[256,2048]{1,0:T(8,128)} custom-call(s32[103]{0:T(128)} %concatenate.35.scal, bf16[128,2048]{1,0:T(8,128)(2,1)} %copy-done.15, bf16[128,2048]{1,0:T(8,128)(2,1)} %collective-permute-done.19.refs_1_, bf16[128,2048]{1,0:T(8,128)(2,1)} %pad_maximum_fusion.refs_2_, bf16[128,2048]{1,0:T(8,128)(2,1)} %pad_maximum_fusion.1.refs_3_, ...), custom_call_target="tpu_custom_call" | custom-call | flops 1000000000 | bytes 1000000 | tf_op jit(solution)/shard_map/pallas_call | solution.py:306
  141.2 3.2 %shard_map.130 = bf16[64,2048]{1,0:T(8,128)(2,1)} custom-call(f32[2,128,2048]{2,1,0:T(8,128)} %get-tuple-element.64.keep, f32[2,128,2048]{2,1,0:T(8,128)} %copy-done.4, bf16[2,64,2048]{2,1,0:T(8,128)(2,1)} %collective-permute-done.27.refs_0_, bf16[128,1024]{1,0:T(8,128)(2,1)} %shard_map.124.refs_1_, s32[512,1]{1,0:T(8,128)} %add_select_fusion.refs_2_.refs_11_, ...), custom_call_target="tpu_custom_call" | custom-call | flops 1000000000 | bytes 3145728 | tf_op jit(solution)/shard_map/pallas_call | solution.py:230
  144.4 1.2 collective-permute-start.29
  145.6 1.0 pad_maximum_fusion.2.refs_2_
  146.7 5.2 %collective-permute-done.29 = bf16[64,2048]{1,0:T(8,128)(2,1)S(1)} collective-permute-done((bf16[64,2048]{1,0:T(8,128)(2,1)}, bf16[64,2048]{1,0:T(8,128)(2,1)S(1)}, u32[]{:S(2)}, u32[]{:S(2)}) %collective-permute-start.29) | collective-permute-done | bytes 262176 | tf_op jit(solution)/shard_map/ppermute | solution.py:364
  152.0 1.0 pad_maximum_fusion.3.refs_3_
  153.0 1.5 collective-permute-start.30
  154.6 1.2 collective-permute-start.23
  155.9 3.3 %collective-permute-start.24 = (bf16[4,16,2048]{2,1,0:T(8,128)(2,1)S(1)}, bf16[4,16,2048]{2,1,0:T(8,128)(2,1)S(1)}, u32[]{:S(2)}, u32[]{:S(2)}) collective-permute-start(bf16[4,16,2048]{2,1,0:T(8,128)(2,1)S(1)} %get-tuple-element.84), channel_id=1, source_target_pairs={{0,2},{1,3},{2,0},{3,1},{4,6},{5,7},{6,4},{7,5},{8,10},{9,11},{10,... | collective-permute-start | bytes 786440 | tf_op jit(solution)/shard_map/ppermute | solution.py:545
  159.6 15.6 %shard_map.131 = f32[256,2048]{1,0:T(8,128)} custom-call(s32[103]{0:T(128)} %concatenate.35.scal, bf16[128,2048]{1,0:T(8,128)(2,1)} %collective-permute-done.28.refs_0_, bf16[128,2048]{1,0:T(8,128)(2,1)} %collective-permute-done.30.refs_1_, bf16[128,2048]{1,0:T(8,128)(2,1)} %copy-done.11, bf16[128,2048]{1,0:T(8,128)(2,1)} %copy-done.12, ...), custom_call_target="tpu_custom_call" | custom-call | flops 1000000000 | bytes 1000000 | tf_op jit(solution)/shard_map/pallas_call | solution.py:306
  175.2 1.5 fusion.15
  177.5 5.3 %collective-permute-start.33 = (bf16[4,16,2048]{2,1,0:T(8,128)(2,1)S(1)}, bf16[4,16,2048]{2,1,0:T(8,128)(2,1)}, u32[]{:S(2)}, u32[]{:S(2)}) collective-permute-start(bf16[4,16,2048]{2,1,0:T(8,128)(2,1)S(1)} %get-tuple-element.77), channel_id=1, source_target_pairs={{0,3},{1,0},{2,1},{3,2},{4,7},{5,4},{6,5},{7,6},{8,11},{9,8},{10,9... | collective-permute-start | bytes 786440 | tf_op jit(solution)/shard_map/ppermute | solution.py:545
  183.5 2.1 collective-permute-done.31
  185.6 14.0 %collective-permute-done.32 = bf16[4,16,2048]{2,1,0:T(8,128)(2,1)} collective-permute-done((bf16[4,16,2048]{2,1,0:T(8,128)(2,1)S(1)}, bf16[4,16,2048]{2,1,0:T(8,128)(2,1)}, u32[]{:S(2)}, u32[]{:S(2)}) %collective-permute-start.32) | collective-permute-done | bytes 262176 | tf_op jit(solution)/shard_map/ppermute | solution.py:545
  199.6 5.6 %collective-permute-done.33 = bf16[4,16,2048]{2,1,0:T(8,128)(2,1)} collective-permute-done((bf16[4,16,2048]{2,1,0:T(8,128)(2,1)S(1)}, bf16[4,16,2048]{2,1,0:T(8,128)(2,1)}, u32[]{:S(2)}, u32[]{:S(2)}) %collective-permute-start.33) | collective-permute-done | bytes 262176 | tf_op jit(solution)/shard_map/ppermute | solution.py:545
  205.2 1.3 fusion.6
  207.2 0.8 pad_maximum_fusion.4
  (139 shorter events, 11.2 us)
Async XLA Ops:
  0.7 17.1 %collective-permute-start = (s32[4,6]{0,1:T(8,128)S(1)}, s32[4,6]{0,1:T(8,128)S(1)}, u32[]{:S(2)}, u32[]{:S(2)}) collective-permute-start(s32[4,6]{0,1:T(8,128)S(1)} %pad_add_fusion), channel_id=1, source_target_pairs={{0,12},{4,0},{8,4},{12,8},{1,13},{5,1},{9,5},{13,9},{2,14},{6,2},{... | collective-permute-start | bytes 296 | tf_op jit(solution)/shard_map/ppermute | solution.py:392
  1.4 16.6 %collective-permute-start.1 = (s32[4,6]{0,1:T(8,128)S(1)}, s32[4,6]{0,1:T(8,128)S(1)}, u32[]{:S(2)}, u32[]{:S(2)}) collective-permute-start(s32[4,6]{0,1:T(8,128)S(1)} %pad_add_fusion), channel_id=1, source_target_pairs={{0,8},{4,12},{8,0},{12,4},{1,9},{5,13},{9,1},{13,5},{2,10},{6,14},... | collective-permute-start | bytes 296 | tf_op jit(solution)/shard_map/ppermute | solution.py:392
  1.4 16.8 %collective-permute-start.2 = (s32[4,6]{0,1:T(8,128)S(1)}, s32[4,6]{0,1:T(8,128)S(1)}, u32[]{:S(2)}, u32[]{:S(2)}) collective-permute-start(s32[4,6]{0,1:T(8,128)S(1)} %pad_add_fusion), channel_id=1, source_target_pairs={{0,4},{4,8},{8,12},{12,0},{1,5},{5,9},{9,13},{13,1},{2,6},{6,10},{... | collective-permute-start | bytes 296 | tf_op jit(solution)/shard_map/ppermute | solution.py:392
  4.2 14.9 %collective-permute-start.4 = (bf16[4,256,256]{2,1,0:T(8,128)(2,1)S(1)}, bf16[4,256,256]{2,1,0:T(8,128)(2,1)S(1)}, u32[]{:S(2)}, u32[]{:S(2)}) collective-permute-start(bf16[4,256,256]{2,1,0:T(8,128)(2,1)S(1)} %constant_dynamic-slice_fusion), channel_id=1, source_target_pairs={{0,8},{4,12},{8,0},{12,4},{1,9},{5,13},{9,1},{13,5},{2,10},{6,14},... | collective-permute-start | bytes 1572872 | tf_op jit(solution)/shard_map/ppermute | solution.py:364
  6.0 10.9 %copy-start.32 = (s32[512]{0:T(512)S(1)}, s32[512]{0:T(512)}, u32[]{:S(2)}) copy-start(s32[512]{0:T(512)} %param.24) | copy-start | bytes 6148
  6.0 10.9 %copy-start.33 = (s32[16]{0:T(128)S(1)}, s32[16]{0:T(128)}, u32[]{:S(2)}) copy-start(s32[16]{0:T(128)} %param.25) | copy-start | bytes 196
  16.6 16.0 %collective-permute-start.3 = (f32[2,128,2048]{2,1,0:T(8,128)}, f32[2,128,2048]{2,1,0:T(8,128)}, u32[]{:S(2)}, u32[]{:S(2)}) collective-permute-start(f32[2,128,2048]{2,1,0:T(8,128)} %get-tuple-element.43), channel_id=1, source_target_pairs={{0,4},{4,0},{8,12},{12,8},{1,5},{5,1},{9,13},{13,9},{2,6},{6,2},{1... | collective-permute-start | bytes 6291464 | tf_op jit(solution)/shard_map/ppermute | solution.py:361
  16.8 2.2 %copy-start.23 = (s32[24]{0:T(128)}, s32[24]{0:T(128)S(1)}, u32[]{:S(2)}) copy-start(s32[24]{0:T(128)S(1)} %reshape.227) | copy-start | bytes 292
  17.0 2.1 %copy-start.22 = (s32[512]{0:T(512)}, s32[512]{0:T(512)S(1)}, u32[]{:S(2)}) copy-start(s32[512]{0:T(512)S(1)} %select_reduce_fusion.1) | copy-start | bytes 6148
  18.0 1.1 copy-start.25
  18.2 0.9 copy-start.27
  19.1 10.2 %copy-start.7 = (bf16[4,256,256]{2,1,0:T(8,128)(2,1)}, bf16[4,256,256]{2,1,0:T(8,128)(2,1)S(1)}, u32[]{:S(2)}) copy-start(bf16[4,256,256]{2,1,0:T(8,128)(2,1)S(1)} %collective-permute-done.4.refs_5_) | copy-start | bytes 1572868
  26.2 4.3 %copy-start.31 = (s32[1,512]{1,0:T(1,128)S(1)}, s32[1,512]{1,0:T(1,128)}, u32[]{:S(2)}) copy-start(s32[1,512]{1,0:T(1,128)} %get-tuple-element.52) | copy-start | bytes 6148
  26.2 6.4 %copy-start.2 = (f32[2,128,2048]{2,1,0:T(8,128)S(1)}, f32[2,128,2048]{2,1,0:T(8,128)}, u32[]{:S(2)}) copy-start(f32[2,128,2048]{2,1,0:T(8,128)} %get-tuple-element.42.keep) | copy-start | bytes 6291460
  28.4 2.9 %collective-permute-start.5 = (bf16[2,128,1024]{2,1,0:T(8,128)(2,1)}, bf16[2,128,1024]{2,1,0:T(8,128)(2,1)}, u32[]{:S(2)}, u32[]{:S(2)}) collective-permute-start(bf16[2,128,1024]{2,1,0:T(8,128)(2,1)} %bitcast.20), channel_id=1, source_target_pairs={{0,4},{4,0},{8,12},{12,8},{1,5},{5,1},{9,13},{13,9},{2,6},{6,2},{1... | collective-permute-start | bytes 1572872 | tf_op jit(solution)/shard_map/ppermute | solution.py:361
  29.2 27.0 %collective-permute-start.9 = (bf16[4,256,256]{2,1,0:T(8,128)(2,1)S(1)}, bf16[4,256,256]{2,1,0:T(8,128)(2,1)}, u32[]{:S(2)}, u32[]{:S(2)}) collective-permute-start(bf16[4,256,256]{2,1,0:T(8,128)(2,1)S(1)} %collective-permute-done.4.refs_5_), channel_id=1, source_target_pairs={{0,16},{16,0},{1,17},{17,1},{2,18},{18,2},{3,19},{19,3},{4,20},{20... | collective-permute-start | bytes 1572872 | tf_op jit(solution)/shard_map/ppermute | solution.py:411
  34.0 13.7 %collective-permute-start.6 = (bf16[2,64,2048]{2,1,0:T(8,128)(2,1)S(1)}, bf16[2,64,2048]{2,1,0:T(8,128)(2,1)S(1)}, u32[]{:S(2)}, u32[]{:S(2)}) collective-permute-start(bf16[2,64,2048]{2,1,0:T(8,128)(2,1)S(1)} %fusion.3), channel_id=1, source_target_pairs={{0,8},{4,12},{8,0},{12,4},{1,9},{5,13},{9,1},{13,5},{2,10},{6,14},... | collective-permute-start | bytes 1572872 | tf_op jit(solution)/shard_map/ppermute | solution.py:364
  35.1 17.7 %collective-permute-start.7 = (bf16[128,1024]{1,0:T(8,128)(2,1)S(1)}, bf16[128,1024]{1,0:T(8,128)(2,1)S(1)}, u32[]{:S(2)}, u32[]{:S(2)}) collective-permute-start(bf16[128,1024]{1,0:T(8,128)(2,1)S(1)} %get-tuple-element.92), channel_id=1, source_target_pairs={{0,8},{4,12},{8,0},{12,4},{1,9},{5,13},{9,1},{13,5},{2,10},{6,14},... | collective-permute-start | bytes 786440 | tf_op jit(solution)/shard_map/ppermute | solution.py:364
  46.8 9.3 %collective-permute-start.8 = (f32[2,128,2048]{2,1,0:T(8,128)}, f32[2,128,2048]{2,1,0:T(8,128)S(1)}, u32[]{:S(2)}, u32[]{:S(2)}) collective-permute-start(f32[2,128,2048]{2,1,0:T(8,128)} %get-tuple-element.50), channel_id=1, source_target_pairs={{0,4},{4,0},{8,12},{12,8},{1,5},{5,1},{9,13},{13,9},{2,6},{6,2},{1... | collective-permute-start | bytes 6291464 | tf_op jit(solution)/shard_map/ppermute | solution.py:361
  47.7 8.4 %copy-start.18 = (bf16[2,64,2048]{2,1,0:T(8,128)(2,1)}, bf16[2,64,2048]{2,1,0:T(8,128)(2,1)S(1)}, u32[]{:S(2)}) copy-start(bf16[2,64,2048]{2,1,0:T(8,128)(2,1)S(1)} %collective-permute-done.6.refs_0_) | copy-start | bytes 1572868
  53.5 2.6 %copy-start.16 = (f32[2,128,2048]{2,1,0:T(8,128)S(1)}, f32[2,128,2048]{2,1,0:T(8,128)}, u32[]{:S(2)}) copy-start(f32[2,128,2048]{2,1,0:T(8,128)} %get-tuple-element.49.keep) | copy-start | bytes 6291460
  56.1 4.8 %copy-start.17 = (f32[2,128,2048]{2,1,0:T(8,128)}, f32[2,128,2048]{2,1,0:T(8,128)S(1)}, u32[]{:S(2)}) copy-start(f32[2,128,2048]{2,1,0:T(8,128)S(1)} %collective-permute-done.8.core) | copy-start | bytes 6291460
  56.3 7.0 %copy-start.21 = (s32[512]{0:T(512)S(1)}, s32[512]{0:T(512)}, u32[]{:S(2)}) copy-start(s32[512]{0:T(512)} %select_reduce_fusion) | copy-start | bytes 6148
  62.0 2.8 %collective-permute-start.10 = (bf16[2,128,1024]{2,1,0:T(8,128)(2,1)S(1)}, bf16[2,128,1024]{2,1,0:T(8,128)(2,1)S(1)}, u32[]{:S(2)}, u32[]{:S(2)}) collective-permute-start(bf16[2,128,1024]{2,1,0:T(8,128)(2,1)S(1)} %slice.82), channel_id=1, source_target_pairs={{0,4},{4,0},{8,12},{12,8},{1,5},{5,1},{9,13},{13,9},{2,6},{6,2},{1... | collective-permute-start | bytes 1572872 | tf_op jit(solution)/shard_map/ppermute | solution.py:361
  63.4 28.7 %collective-permute-start.13 = (bf16[2,64,2048]{2,1,0:T(8,128)(2,1)S(1)}, bf16[2,64,2048]{2,1,0:T(8,128)(2,1)}, u32[]{:S(2)}, u32[]{:S(2)}) collective-permute-start(bf16[2,64,2048]{2,1,0:T(8,128)(2,1)S(1)} %fusion.2), channel_id=1, source_target_pairs={{0,8},{4,12},{8,0},{12,4},{1,9},{5,13},{9,1},{13,5},{2,10},{6,14},... | collective-permute-start | bytes 1572872 | tf_op jit(solution)/shard_map/ppermute | solution.py:364
  66.6 16.0 %collective-permute-start.11 = (bf16[128,1024]{1,0:T(8,128)(2,1)S(1)}, bf16[128,1024]{1,0:T(8,128)(2,1)S(1)}, u32[]{:S(2)}, u32[]{:S(2)}) collective-permute-start(bf16[128,1024]{1,0:T(8,128)(2,1)S(1)} %get-tuple-element.90), channel_id=1, source_target_pairs={{0,8},{4,12},{8,0},{12,4},{1,9},{5,13},{9,1},{13,5},{2,10},{6,14},... | collective-permute-start | bytes 786440 | tf_op jit(solution)/shard_map/ppermute | solution.py:364
  77.7 8.1 %collective-permute-start.12 = (f32[2,128,2048]{2,1,0:T(8,128)}, f32[2,128,2048]{2,1,0:T(8,128)S(1)}, u32[]{:S(2)}, u32[]{:S(2)}) collective-permute-start(f32[2,128,2048]{2,1,0:T(8,128)} %get-tuple-element.57), channel_id=1, source_target_pairs={{0,4},{4,0},{8,12},{12,8},{1,5},{5,1},{9,13},{13,9},{2,6},{6,2},{1... | collective-permute-start | bytes 6291464 | tf_op jit(solution)/shard_map/ppermute | solution.py:361
  83.3 2.6 %copy-start.5 = (f32[2,128,2048]{2,1,0:T(8,128)S(1)}, f32[2,128,2048]{2,1,0:T(8,128)}, u32[]{:S(2)}) copy-start(f32[2,128,2048]{2,1,0:T(8,128)} %get-tuple-element.56.keep) | copy-start | bytes 6291460
  85.9 2.5 %copy-start.8 = (bf16[4,256,256]{2,1,0:T(8,128)(2,1)S(1)}, bf16[4,256,256]{2,1,0:T(8,128)(2,1)}, u32[]{:S(2)}) copy-start(bf16[4,256,256]{2,1,0:T(8,128)(2,1)} %copy-done.7) | copy-start | bytes 1572868
  85.9 2.5 %copy-start = (bf16[4,2,256,256]{3,2,1,0:T(8,128)(2,1)S(1)}, bf16[4,2,256,256]{3,2,1,0:T(8,128)(2,1)}, u32[]{:S(2)}) copy-start(bf16[4,2,256,256]{3,2,1,0:T(8,128)(2,1)} %param.20) | copy-start | bytes 3145732
  85.9 6.2 %copy-start.6 = (f32[2,128,2048]{2,1,0:T(8,128)}, f32[2,128,2048]{2,1,0:T(8,128)S(1)}, u32[]{:S(2)}) copy-start(f32[2,128,2048]{2,1,0:T(8,128)S(1)} %collective-permute-done.12.core) | copy-start | bytes 6291460
  86.0 20.0 %collective-permute-start.14 = (bf16[2,64,2048]{2,1,0:T(8,128)(2,1)S(1)}, bf16[2,64,2048]{2,1,0:T(8,128)(2,1)S(1)}, u32[]{:S(2)}, u32[]{:S(2)}) collective-permute-start(bf16[2,64,2048]{2,1,0:T(8,128)(2,1)S(1)} %fusion.1), channel_id=1, source_target_pairs={{0,8},{4,12},{8,0},{12,4},{1,9},{5,13},{9,1},{13,5},{2,10},{6,14},... | collective-permute-start | bytes 1572872 | tf_op jit(solution)/shard_map/ppermute | solution.py:364
  87.3 34.6 %collective-permute-start.21 = (bf16[4,256,256]{2,1,0:T(8,128)(2,1)}, bf16[4,256,256]{2,1,0:T(8,128)(2,1)S(1)}, u32[]{:S(2)}, u32[]{:S(2)}) collective-permute-start(bf16[4,256,256]{2,1,0:T(8,128)(2,1)} %collective-permute-done.9.refs_6_), channel_id=1, source_target_pairs={{0,4},{4,0},{8,12},{12,8},{1,5},{5,1},{9,13},{13,9},{2,6},{6,2},{1... | collective-permute-start | bytes 1572872 | tf_op jit(solution)/shard_map/ppermute | solution.py:361
  88.4 33.9 %collective-permute-start.20 = (bf16[4,256,256]{2,1,0:T(8,128)(2,1)S(1)}, bf16[4,256,256]{2,1,0:T(8,128)(2,1)S(1)}, u32[]{:S(2)}, u32[]{:S(2)}) collective-permute-start(bf16[4,256,256]{2,1,0:T(8,128)(2,1)S(1)} %copy-done.8), channel_id=1, source_target_pairs={{0,4},{4,0},{8,12},{12,8},{1,5},{5,1},{9,13},{13,9},{2,6},{6,2},{1... | collective-permute-start | bytes 1572872 | tf_op jit(solution)/shard_map/ppermute | solution.py:361
  88.4 36.5 %collective-permute-start.22 = (bf16[8,256,256]{2,1,0:T(8,128)(2,1)S(1)}, bf16[8,256,256]{2,1,0:T(8,128)(2,1)}, u32[]{:S(2)}, u32[]{:S(2)}) collective-permute-start(bf16[8,256,256]{2,1,0:T(8,128)(2,1)S(1)} %bitcast.99), channel_id=1, source_target_pairs={{0,4},{4,0},{8,12},{12,8},{1,5},{5,1},{9,13},{13,9},{2,6},{6,2},{1... | collective-permute-start | bytes 3145736 | tf_op jit(solution)/shard_map/ppermute | solution.py:361
  92.1 12.3 %collective-permute-start.15 = (bf16[64,2048]{1,0:T(8,128)(2,1)}, bf16[64,2048]{1,0:T(8,128)(2,1)S(1)}, u32[]{:S(2)}, u32[]{:S(2)}) collective-permute-start(bf16[64,2048]{1,0:T(8,128)(2,1)} %shard_map.125), channel_id=1, source_target_pairs={{0,8},{4,12},{8,0},{12,4},{1,9},{5,13},{9,1},{13,5},{2,10},{6,14},... | collective-permute-start | bytes 786440 | tf_op jit(solution)/shard_map/ppermute | solution.py:364
  104.3 16.0 %collective-permute-start.17 = (f32[2,128,2048]{2,1,0:T(8,128)}, f32[2,128,2048]{2,1,0:T(8,128)S(1)}, u32[]{:S(2)}, u32[]{:S(2)}) collective-permute-start(f32[2,128,2048]{2,1,0:T(8,128)} %get-tuple-element.65), channel_id=1, source_target_pairs={{0,4},{4,0},{8,12},{12,8},{1,5},{5,1},{9,13},{13,9},{2,6},{6,2},{1... | collective-permute-start | bytes 6291464 | tf_op jit(solution)/shard_map/ppermute | solution.py:361
  106.0 3.4 %copy-start.19 = (bf16[2,64,2048]{2,1,0:T(8,128)(2,1)}, bf16[2,64,2048]{2,1,0:T(8,128)(2,1)S(1)}, u32[]{:S(2)}) copy-start(bf16[2,64,2048]{2,1,0:T(8,128)(2,1)S(1)} %collective-permute-done.14.refs_0_) | copy-start | bytes 1572868
  109.4 3.8 %copy-start.14 = (bf16[64,2048]{1,0:T(8,128)(2,1)S(1)}, bf16[64,2048]{1,0:T(8,128)(2,1)}, u32[]{:S(2)}) copy-start(bf16[64,2048]{1,0:T(8,128)(2,1)} %shard_map.125) | copy-start | bytes 786436
  109.4 9.1 %copy-start.20 = (bf16[64,2048]{1,0:T(8,128)(2,1)S(1)}, bf16[64,2048]{1,0:T(8,128)(2,1)}, u32[]{:S(2)}) copy-start(bf16[64,2048]{1,0:T(8,128)(2,1)} %shard_map.127) | copy-start | bytes 786436
  109.4 8.3 %collective-permute-start.16 = (bf16[64,2048]{1,0:T(8,128)(2,1)}, bf16[64,2048]{1,0:T(8,128)(2,1)}, u32[]{:S(2)}, u32[]{:S(2)}) collective-permute-start(bf16[64,2048]{1,0:T(8,128)(2,1)} %shard_map.127), channel_id=1, source_target_pairs={{0,8},{4,12},{8,0},{12,4},{1,9},{5,13},{9,1},{13,5},{2,10},{6,14},... | collective-permute-start | bytes 786440 | tf_op jit(solution)/shard_map/ppermute | solution.py:364
  109.8 10.5 %copy-start.3 = (f32[2,128,2048]{2,1,0:T(8,128)S(1)}, f32[2,128,2048]{2,1,0:T(8,128)}, u32[]{:S(2)}) copy-start(f32[2,128,2048]{2,1,0:T(8,128)} %get-tuple-element.64.keep) | copy-start | bytes 6291460
  113.2 10.3 %copy-start.13 = (bf16[64,2048]{1,0:T(8,128)(2,1)S(1)}, bf16[64,2048]{1,0:T(8,128)(2,1)}, u32[]{:S(2)}) copy-start(bf16[64,2048]{1,0:T(8,128)(2,1)} %shard_map.128) | copy-start | bytes 786436
  114.0 10.2 %copy-start.24 = (s32[24]{0:T(128)S(1)}, s32[24]{0:T(128)}, u32[]{:S(2)}) copy-start(s32[24]{0:T(128)} %copy-done.23) | copy-start | bytes 292
  114.0 10.2 %copy-start.26 = (s32[24]{0:T(128)S(1)}, s32[24]{0:T(128)}, u32[]{:S(2)}) copy-start(s32[24]{0:T(128)} %copy-done.25) | copy-start | bytes 292
  114.0 10.2 %copy-start.28 = (s32[24]{0:T(128)S(1)}, s32[24]{0:T(128)}, u32[]{:S(2)}) copy-start(s32[24]{0:T(128)} %copy-done.27) | copy-start | bytes 292
  114.0 10.2 %copy-start.30 = (s32[24]{0:T(128)S(1)}, s32[24]{0:T(128)}, u32[]{:S(2)}) copy-start(s32[24]{0:T(128)} %copy-done.29) | copy-start | bytes 292
  117.7 7.1 %collective-permute-start.18 = (bf16[128,2048]{1,0:T(8,128)(2,1)}, bf16[128,2048]{1,0:T(8,128)(2,1)S(1)}, u32[]{:S(2)}, u32[]{:S(2)}) collective-permute-start(bf16[128,2048]{1,0:T(8,128)(2,1)} %pad_maximum_fusion.refs_2_), channel_id=1, source_target_pairs={{0,4},{4,0},{8,12},{12,8},{1,5},{5,1},{9,13},{13,9},{2,6},{6,2},{1... | collective-permute-start | bytes 1572872 | tf_op jit(solution)/shard_map/ppermute | solution.py:361
  120.3 1.5 copy-start.4
  120.4 4.5 %collective-permute-start.19 = (bf16[128,2048]{1,0:T(8,128)(2,1)}, bf16[128,2048]{1,0:T(8,128)(2,1)}, u32[]{:S(2)}, u32[]{:S(2)}) collective-permute-start(bf16[128,2048]{1,0:T(8,128)(2,1)} %pad_maximum_fusion.1.refs_3_), channel_id=1, source_target_pairs={{0,4},{4,0},{8,12},{12,8},{1,5},{5,1},{9,13},{13,9},{2,6},{6,2},{1... | collective-permute-start | bytes 1572872 | tf_op jit(solution)/shard_map/ppermute | solution.py:361
  121.9 19.4 %collective-permute-start.27 = (bf16[2,64,2048]{2,1,0:T(8,128)(2,1)}, bf16[2,64,2048]{2,1,0:T(8,128)(2,1)}, u32[]{:S(2)}, u32[]{:S(2)}) collective-permute-start(bf16[2,64,2048]{2,1,0:T(8,128)(2,1)} %fusion), channel_id=1, source_target_pairs={{0,8},{4,12},{8,0},{12,4},{1,9},{5,13},{9,1},{13,5},{2,10},{6,14},... | collective-permute-start | bytes 1572872 | tf_op jit(solution)/shard_map/ppermute | solution.py:364
  123.5 22.1 %collective-permute-start.26 = (bf16[64,2048]{1,0:T(8,128)(2,1)S(1)}, bf16[64,2048]{1,0:T(8,128)(2,1)}, u32[]{:S(2)}, u32[]{:S(2)}) collective-permute-start(bf16[64,2048]{1,0:T(8,128)(2,1)S(1)} %copy-done.13), channel_id=1, source_target_pairs={{0,8},{4,12},{8,0},{12,4},{1,9},{5,13},{9,1},{13,5},{2,10},{6,14},... | collective-permute-start | bytes 786440 | tf_op jit(solution)/shard_map/ppermute | solution.py:364
  144.4 10.1 %copy-start.1 = (f32[256,2048]{1,0:T(8,128)S(1)}, f32[256,2048]{1,0:T(8,128)}, u32[]{:S(2)}) copy-start(f32[256,2048]{1,0:T(8,128)} %shard_map.129) | copy-start | bytes 6291460
  144.4 7.5 %collective-permute-start.29 = (bf16[64,2048]{1,0:T(8,128)(2,1)}, bf16[64,2048]{1,0:T(8,128)(2,1)S(1)}, u32[]{:S(2)}, u32[]{:S(2)}) collective-permute-start(bf16[64,2048]{1,0:T(8,128)(2,1)} %shard_map.130), channel_id=1, source_target_pairs={{0,8},{4,12},{8,0},{12,4},{1,9},{5,13},{9,1},{13,5},{2,10},{6,14},... | collective-permute-start | bytes 786440 | tf_op jit(solution)/shard_map/ppermute | solution.py:364
  146.6 12.9 %copy-start.11 = (bf16[128,2048]{1,0:T(8,128)(2,1)}, bf16[128,2048]{1,0:T(8,128)(2,1)S(1)}, u32[]{:S(2)}) copy-start(bf16[128,2048]{1,0:T(8,128)(2,1)S(1)} %pad_maximum_fusion.2.refs_2_) | copy-start | bytes 1572868
  146.6 12.9 %collective-permute-start.28 = (bf16[128,2048]{1,0:T(8,128)(2,1)S(1)}, bf16[128,2048]{1,0:T(8,128)(2,1)}, u32[]{:S(2)}, u32[]{:S(2)}) collective-permute-start(bf16[128,2048]{1,0:T(8,128)(2,1)S(1)} %pad_maximum_fusion.2.refs_2_), channel_id=1, source_target_pairs={{0,4},{4,0},{8,12},{12,8},{1,5},{5,1},{9,13},{13,9},{2,6},{6,2},{1... | collective-permute-start | bytes 1572872 | tf_op jit(solution)/shard_map/ppermute | solution.py:361
  152.9 6.6 %copy-start.12 = (bf16[128,2048]{1,0:T(8,128)(2,1)}, bf16[128,2048]{1,0:T(8,128)(2,1)S(1)}, u32[]{:S(2)}) copy-start(bf16[128,2048]{1,0:T(8,128)(2,1)S(1)} %pad_maximum_fusion.3.refs_3_) | copy-start | bytes 1572868
  153.0 6.6 %collective-permute-start.30 = (bf16[128,2048]{1,0:T(8,128)(2,1)S(1)}, bf16[128,2048]{1,0:T(8,128)(2,1)}, u32[]{:S(2)}, u32[]{:S(2)}) collective-permute-start(bf16[128,2048]{1,0:T(8,128)(2,1)S(1)} %pad_maximum_fusion.3.refs_3_), channel_id=1, source_target_pairs={{0,4},{4,0},{8,12},{12,8},{1,5},{5,1},{9,13},{13,9},{2,6},{6,2},{1... | collective-permute-start | bytes 1572872 | tf_op jit(solution)/shard_map/ppermute | solution.py:361
  154.6 22.0 %collective-permute-start.23 = (bf16[4,16,2048]{2,1,0:T(8,128)(2,1)S(1)}, bf16[4,16,2048]{2,1,0:T(8,128)(2,1)S(1)}, u32[]{:S(2)}, u32[]{:S(2)}) collective-permute-start(bf16[4,16,2048]{2,1,0:T(8,128)(2,1)S(1)} %get-tuple-element.82), channel_id=1, source_target_pairs={{0,1},{1,2},{2,3},{3,0},{4,5},{5,6},{6,7},{7,4},{8,9},{9,10},{10,1... | collective-permute-start | bytes 786440 | tf_op jit(solution)/shard_map/ppermute | solution.py:545
  155.9 21.4 %collective-permute-start.24 = (bf16[4,16,2048]{2,1,0:T(8,128)(2,1)S(1)}, bf16[4,16,2048]{2,1,0:T(8,128)(2,1)S(1)}, u32[]{:S(2)}, u32[]{:S(2)}) collective-permute-start(bf16[4,16,2048]{2,1,0:T(8,128)(2,1)S(1)} %get-tuple-element.84), channel_id=1, source_target_pairs={{0,2},{1,3},{2,0},{3,1},{4,6},{5,7},{6,4},{7,5},{8,10},{9,11},{10,... | collective-permute-start | bytes 786440 | tf_op jit(solution)/shard_map/ppermute | solution.py:545
  159.2 18.3 %collective-permute-start.25 = (bf16[4,16,2048]{2,1,0:T(8,128)(2,1)S(1)}, bf16[4,16,2048]{2,1,0:T(8,128)(2,1)S(1)}, u32[]{:S(2)}, u32[]{:S(2)}) collective-permute-start(bf16[4,16,2048]{2,1,0:T(8,128)(2,1)S(1)} %get-tuple-element.83), channel_id=1, source_target_pairs={{0,3},{1,0},{2,1},{3,2},{4,7},{5,4},{6,5},{7,6},{8,11},{9,8},{10,9... | collective-permute-start | bytes 786440 | tf_op jit(solution)/shard_map/ppermute | solution.py:545
  176.7 8.9 %collective-permute-start.31 = (bf16[4,16,2048]{2,1,0:T(8,128)(2,1)S(1)}, bf16[4,16,2048]{2,1,0:T(8,128)(2,1)S(1)}, u32[]{:S(2)}, u32[]{:S(2)}) collective-permute-start(bf16[4,16,2048]{2,1,0:T(8,128)(2,1)S(1)} %get-tuple-element.75), channel_id=1, source_target_pairs={{0,1},{1,2},{2,3},{3,0},{4,5},{5,6},{6,7},{7,4},{8,9},{9,10},{10,1... | collective-permute-start | bytes 786440 | tf_op jit(solution)/shard_map/ppermute | solution.py:545
  177.3 22.3 %collective-permute-start.32 = (bf16[4,16,2048]{2,1,0:T(8,128)(2,1)S(1)}, bf16[4,16,2048]{2,1,0:T(8,128)(2,1)}, u32[]{:S(2)}, u32[]{:S(2)}) collective-permute-start(bf16[4,16,2048]{2,1,0:T(8,128)(2,1)S(1)} %get-tuple-element.76), channel_id=1, source_target_pairs={{0,2},{1,3},{2,0},{3,1},{4,6},{5,7},{6,4},{7,5},{8,10},{9,11},{10,... | collective-permute-start | bytes 786440 | tf_op jit(solution)/shard_map/ppermute | solution.py:545
  177.5 27.7 %collective-permute-start.33 = (bf16[4,16,2048]{2,1,0:T(8,128)(2,1)S(1)}, bf16[4,16,2048]{2,1,0:T(8,128)(2,1)}, u32[]{:S(2)}, u32[]{:S(2)}) collective-permute-start(bf16[4,16,2048]{2,1,0:T(8,128)(2,1)S(1)} %get-tuple-element.77), channel_id=1, source_target_pairs={{0,3},{1,0},{2,1},{3,2},{4,7},{5,4},{6,5},{7,6},{8,11},{9,8},{10,9... | collective-permute-start | bytes 786440 | tf_op jit(solution)/shard_map/ppermute | solution.py:545
  (6 other events, 4.6 us)

commit v7 on v6

--- a/solution.py
+++ b/solution.py
@@ -8,7 +8,7 @@
 from jax.sharding import PartitionSpec as P
 
 CAP = 128
-CHUNKS = (2, 2)
+CHUNKS = (3, 1)
 PARTS = 2
 SHORT = 120e9
 VMEM = 56 * 1024 * 1024
@@ -25,7 +25,7 @@
     return pl.BlockSpec(shape, lambda *_: zeros)
 
 
-def pack_body(owners, per_owner, kinds, stride, capacity, col_tiles, scal, x, sl, ss, out, code, table):
+def pack_body(owners, per_owner, kinds, stride, capacity, col_tiles, scal, x, sl, ss, send, keep, code, table):
     tile = 256
     rows, held = x.shape
     here = held // tile
@@ -61,7 +61,9 @@
         picked = jnp.zeros((rows, tile), BF)
         for b in range(here):
             picked = jnp.where(at == float(b), x[:, b * tile : (b + 1) * tile], picked)
-        out[:, j * tile : (j + 1) * tile] = jnp.dot(hot, picked, preferred_element_type=F32).astype(BF)
+        found = jnp.dot(hot, picked, preferred_element_type=F32).astype(BF)
+        send[:, j * tile : (j + 1) * tile] = found[: send.shape[0]]
+        keep[:, j * tile : (j + 1) * tile] = found[send.shape[0] :]
 
 
 def pack(scal, x, sl, ss, owners, per_owner, kinds, stride, col_tiles):
@@ -74,10 +76,10 @@
             num_scalar_prefetch=1,
             grid=(1,),
             in_specs=[whole(x.shape), whole((1, rows)), whole((rows, 1))],
-            out_specs=[whole((owners * CAP, width)), whole((1, rows)), whole((height, 128))],
+            out_specs=[*[whole((owners // 2 * CAP, width))] * 2, whole((1, rows)), whole((height, 128))],
         ),
         out_shape=[
-            jax.ShapeDtypeStruct((owners * CAP, width), BF),
+            *[jax.ShapeDtypeStruct((owners // 2 * CAP, width), BF)] * 2,
             jax.ShapeDtypeStruct((1, rows), jnp.int32),
             jax.ShapeDtypeStruct((height, 128), BF),
         ],
@@ -86,7 +88,7 @@
     )(scal, x, sl, ss)
 
 
-def product_body(owners, per_owner, per_slot, pieces, scal, x, gt, ut, code, out):
+def product_body(owners, per_owner, per_slot, pieces, scal, x, gt, ut, code, send, keep):
     tile = 256
     capacity = x.shape[0]
     rows = code.shape[1]
@@ -107,22 +109,23 @@
                 hot, total.astype(BF), (((0,), (0,)), ((), ())), preferred_element_type=F32
             ).astype(BF)
             for home, offset, size, start in pieces:
-                out[home, offset : offset + size, at : at + tile] = spread[start : start + size]
+                out = send if home < owners // 2 else keep
+                out[home % (owners // 2), offset : offset + size, at : at + tile] = spread[start : start + size]
 
 
 def product(scal, x, gt, ut, code, owners, per_owner, pieces):
     rows = code.shape[1]
     per_slot = gt.shape[1]
-    shape = (owners, rows // owners, x.shape[1])
+    shape = (owners // 2, rows // owners, x.shape[1])
     return pl.pallas_call(
         functools.partial(product_body, owners, per_owner, per_slot, pieces),
         grid_spec=pltpu.PrefetchScalarGridSpec(
             num_scalar_prefetch=1,
             grid=(1,),
             in_specs=[whole(x.shape), whole(gt.shape), whole(ut.shape), whole((1, rows))],
-            out_specs=whole(shape),
+            out_specs=[whole(shape)] * 2,
         ),
-        out_shape=jax.ShapeDtypeStruct(shape, BF),
+        out_shape=[jax.ShapeDtypeStruct(shape, BF)] * 2,
         compiler_params=pltpu.CompilerParams(vmem_limit_bytes=VMEM),
         cost_estimate=cost(SHORT, 4e6),
     )(scal, x, gt, ut, code)
@@ -151,11 +154,12 @@
     skip = part * (width // block)
     each = size // (owners * shift)
     first = start // (shift * each)
-    view = tokens.reshape(shift, rows // (shift * each), each, depth)
+    unit = rows // (sum(CHUNKS) * owners * shift)
+    view = tokens.reshape(shift, rows // (shift * unit), unit, depth)
     outs = pl.BlockSpec((2, size // 2, block), lambda i, s: (0, 0, i))
     weights = pl.BlockSpec((depth, block), lambda i, s: (0, skip + i))
     piece = [
-        pl.BlockSpec((shift, 1, each, depth), functools.partial(lambda h, i, s: (0, first + s[h], 0, 0), h))
+        pl.BlockSpec((shift, each // unit, unit, depth), functools.partial(lambda h, i, s: (0, first + s[h], 0, 0), h))
         for h in range(owners)
     ]
     return pl.pallas_call(
@@ -173,27 +177,29 @@
     )(scal, *[view] * owners, wg, wu)
 
 
-def total_body(order, *refs):
-    total = refs[0][...]
-    for ref in refs[1:-1]:
+def total_body(order, keep, core, *refs):
+    total = keep[0] + core[0]
+    for ref in refs[:-1]:
         total = total + ref[...]
     refs[-1][...] = total
 
 
-def total_of(order, parts):
-    shape = parts[0].shape
+def total_of(order, keep, core, came):
+    shape = came[0].shape
+    last = keep.shape[0] - 1
+    own = pl.BlockSpec((1, *shape), lambda i, s: (last, 0, 0))
     return pl.pallas_call(
         total_body,
         grid_spec=pltpu.PrefetchScalarGridSpec(
             num_scalar_prefetch=1,
             grid=(1,),
-            in_specs=[whole(shape)] * len(parts),
+            in_specs=[own, own, *[whole(shape)] * len(came)],
             out_specs=whole(shape),
         ),
-        out_shape=jax.ShapeDtypeStruct(shape, parts[0].dtype),
+        out_shape=jax.ShapeDtypeStruct(shape, BF),
         compiler_params=pltpu.CompilerParams(vmem_limit_bytes=VMEM),
         cost_estimate=cost(SHORT, 1e6),
-    )(order, *parts)
+    )(order, keep, core, *came)
 
 
 def activate_body(per_slot, start, each, row, parts, skip, keep, core, *refs):
@@ -407,9 +413,6 @@
         part, piece, halves = per_owner, flat_tiles, [0]
     from_y = jnp.concatenate([y_move(piece, -k) for k in range(1, ys)])
     tiles = [from_y]
-    if len(halves) == 2:
-        tiles.append(lax.ppermute(from_y, "groups", [(0, 1), (1, 0)]))
-    arrived = tuple(tiles)
     firsts, plan = [], []
     for core in (my_core, 1 - my_core):
         for first in halves:
@@ -444,16 +447,14 @@
             got = moved if got is None else got + moved
         gots[u] = [got]
 
-    def halve(x):
-        half = owners // 2
-        return x[half:] + core_swap(x[:half])
-
-    def finish(x, *earlier):
-        return total_of(after(homes, *earlier), [x[ys - 1]] + [y_move(x[k - 1], k) for k in range(1, ys)])
+    def finish(keep, core, pieces, *earlier):
+        return total_of(
+            after(homes, *earlier), keep, core, [y_move(pieces[k - 1], k) for k in range(1, ys)]
+        )
 
     ahead, second, third, fourth = (0, 0), (0, 1), (1, 0), (1, 1)
     multiply(ahead)
-    packed, code, table = pack(
+    send, keep, code, table = pack(
         after(scal, kept[ahead], from_y),
         tokens,
         slot_rows[None, :],
@@ -465,7 +466,13 @@
         col_tiles,
     )
     exchange(ahead)
-    packed = halve(packed.reshape(owners, CAP, -1))
+    packed = keep.reshape(ys, CAP, -1)
+    packed_core = core_swap(send.reshape(ys, CAP, -1))
+    packed_sends = [packed[k - 1] + packed_core[k - 1] for k in range(1, ys)]
+    multiply(second, *sends[ahead], *packed_sends)
+    code = after(code, kept[second])
+    if len(halves) == 2:
+        tiles.append(lax.ppermute(after(from_y, kept[second]), "groups", [(0, 1), (1, 0)]))
     code_q = jnp.sum(
         jnp.where(row_of[:, None] == jnp.arange(rows, dtype=jnp.int32)[None, :], code, 0), axis=1
     )
@@ -477,11 +484,10 @@
     )
     ss_q = slot_q[:, None]
 
-    multiply(second, *sends[ahead], packed)
-    features = finish(packed, kept[second], *gots[ahead])
+    features = finish(packed, packed_core, packed_sends, kept[second], *gots[ahead])
     exchange(second, features)
-    spread = product(
-        after(scal, *sends[second], *arrived),
+    send, spread = product(
+        after(scal, *sends[second]),
         features,
         gate_tiles,
         up_tiles,
@@ -490,13 +496,11 @@
         per_owner,
         pieces,
     )
-    spread = halve(spread)
-    multiply(third, *sends[second], spread)
-    home_delta = finish(spread, kept[third])
+    spread_core = core_swap(send)
+    spread_sends = [spread[k - 1] + spread_core[k - 1] for k in range(1, ys)]
+    multiply(third, *sends[second], *spread_sends)
+    home_delta = finish(spread, spread_core, spread_sends, kept[third])
     exchange(third, home_delta)
-
-    near_tiles = [*tiles, flat_tiles]
-    all_tiles = near_tiles + [core_swap(after(t, kept[second])) for t in near_tiles]
 
     def finish_hidden(u, flops, *earlier):
         i, part = u
@@ -547,8 +551,10 @@
         return out, came, total.astype(BF)
 
     hid_a, moved_a = finish_hidden(ahead, 1e9, *sends[third])
+    near_tiles = [*tiles, flat_tiles]
+    all_tiles = near_tiles + [core_swap(after(t, hid_a)) for t in near_tiles]
     multiply(fourth, *sends[third], hid_a, *gots[second])
-    hid_b, moved_b = finish_hidden(second, SHORT, kept[fourth], *gots[third], *moved_a)
+    hid_b, moved_b = finish_hidden(second, SHORT, kept[fourth], *gots[third], *moved_a, *tiles[1:])
     hid_c, moved_c = finish_hidden(third, 1e9, hid_b)
     exchange(fourth, hid_c, *moved_b)
     first = [join(hid_a, moved_a, hid_b), join(hid_b, moved_b, hid_c)]

time: 210 us -> 213 us (1.014)
  the two profiles are of different devices: /device:TPU:5 before, /device:TPU:0 now
where the time goes in v7:
time: 213 us; the launch traced here: 212 us
  Pallas kernels  107 us (50%)
  starting transfers between devices  48.8 us (23%)
  waiting for transfers between devices  31.8 us (15%)
  local copies, waits for them, and re-layouts  12.8 us (6%)
  other arithmetic  11.2 us (5%)
    pallas_call x4, Pallas kernels, gate_up(): pl.pallas_call(functools.partial(gate_up_body, owners), grid_spec=pltpu.P...  45.6 us
    pallas_call x2, Pallas kernels, down(): pl.pallas_call(functools.partial(down_body, width_tiles, width // 256, pl...  30.7 us
    ppermute x6, starting transfers between devices, finish_down(): lax.ppermute(gone, 'tensor', [(j, (j + k) % shift) for j in range(shift)])  28 us
    ppermute x11, waiting for transfers between devices, y_move(): lax.ppermute(x, 'delta', [(i, (i + 2 * k) % owners) for i in range(owners)])  24.4 us
    ppermute x11, starting transfers between devices, y_move(): lax.ppermute(x, 'delta', [(i, (i + 2 * k) % owners) for i in range(owners)])  14 us
    pallas_call x4, Pallas kernels, activate(): pl.pallas_call(functools.partial(activate_body, per_slot, start, each, ro...  13.1 us
    pallas_call x1, Pallas kernels, pack(): pl.pallas_call(functools.partial(pack_body, owners, per_owner, kinds, str...  7.3 us
    pallas_call x2, Pallas kernels, total_of(): pl.pallas_call(total_body, grid_spec=pltpu.PrefetchScalarGridSpec(num_sca...  5.3 us
  transfers between devices with their start and end apart: 34, of which 11 were waited for; matrix products, arithmetic and copies ran while one was open for 7% of the time, Pallas kernels for 48%

profile of v7, /device:TPU:0, one launch (start us, length us, event | category | flops | bytes accessed | tf_op | source)
XLA Modules:
  0.0 211.9 jit_solution(8464297546356124137)
XLA Ops:
  0.0 0.7 pad_add_fusion
  0.7 2.4 %collective-permute-start = (s32[4,6]{0,1:T(8,128)S(1)}, s32[4,6]{0,1:T(8,128)S(1)}, u32[]{:S(2)}, u32[]{:S(2)}) collective-permute-start(s32[4,6]{0,1:T(8,128)S(1)} %pad_add_fusion), channel_id=1, source_target_pairs={{0,12},{4,0},{8,4},{12,8},{1,13},{5,1},{9,5},{13,9},{2,14},{6,2},{... | collective-permute-start | bytes 296 | tf_op jit(solution)/shard_map/ppermute | solution.py:398
  4.0 1.9 constant_dynamic-slice_fusion
  5.8 1.2 collective-permute-start.4
  7.1 0.7 broadcast_multiply_fusion.1
  7.7 13.4 %shard_map.118 = (f32[2,192,2048]{2,1,0:T(8,128)}, f32[2,192,2048]{2,1,0:T(8,128)}) custom-call(s32[4]{0:T(128)} %get-tuple-element.68.scal.order, bf16[4,16,8,2048]{3,2,1,0:T(8,128)(2,1)} %bitcast.86, bf16[4,16,8,2048]{3,2,1,0:T(8,128)(2,1)} %bitcast.87, bf16[4,16,8,2048]{3,2,1,0:T(8,128)(2,1)} %bitcast.88, bf16[4,16,8,2048]{3,2,1,0:T(8,128)(2,1)} %bitcast.89, ...), custom_call_target="tpu_custom_call" | custom-call | flops 6442450944 | bytes 16777216 | tf_op jit(solution)/shard_map/pallas_call | solution.py:165
  21.8 0.9 copy.38.ss
  23.8 0.7 concatenate.61.scal
  24.5 7.3 %shard_map.119 = (bf16[256,1024]{1,0:T(8,128)(2,1)}, bf16[256,1024]{1,0:T(8,128)(2,1)}, s32[1,512]{1,0:T(1,128)}, bf16[128,128]{1,0:T(8,128)(2,1)}) custom-call(s32[101]{0:T(128)} %concatenate.61.scal, bf16[512,2048]{1,0:T(8,128)(2,1)} %x.1, s32[1,512]{1,0:T(1,128)} %bitcast.114, s32[512,1]{1,0:T(8,128)} %copy.38.ss), custom_call_target="tpu_custom_call" | custom-call | flops 120000004096 | bytes 4000000 | tf_op jit(solution)/shard_map/pallas_call | solution.py:73
  31.9 1.1 fusion.1
  33.0 1.4 collective-permute-start.6
  34.4 1.1 collective-permute-start.7
  35.5 13.2 %shard_map.120 = (f32[2,192,2048]{2,1,0:T(8,128)}, f32[2,192,2048]{2,1,0:T(8,128)}) custom-call(s32[4]{0:T(128)} %get-tuple-element.68.scal.order, bf16[4,16,8,2048]{3,2,1,0:T(8,128)(2,1)} %bitcast.90, bf16[4,16,8,2048]{3,2,1,0:T(8,128)(2,1)} %bitcast.91, bf16[4,16,8,2048]{3,2,1,0:T(8,128)(2,1)} %bitcast.92, bf16[4,16,8,2048]{3,2,1,0:T(8,128)(2,1)} %bitcast.93, ...), custom_call_target="tpu_custom_call" | custom-call | flops 6442450944 | bytes 16777216 | tf_op jit(solution)/shard_map/pallas_call | solution.py:165
  48.8 0.8 select_reduce_fusion
  49.6 3.9 %collective-permute-done.6.refs_0_ = bf16[2,96,2048]{2,1,0:T(8,128)(2,1)S(1)} collective-permute-done((bf16[2,96,2048]{2,1,0:T(8,128)(2,1)}, bf16[2,96,2048]{2,1,0:T(8,128)(2,1)S(1)}, u32[]{:S(2)}, u32[]{:S(2)}) %collective-permute-start.6) | collective-permute-done | bytes 786464 | tf_op jit(solution)/shard_map/ppermute | solution.py:370
  53.5 5.4 %collective-permute-done.7.refs_0_ = bf16[128,1024]{1,0:T(8,128)(2,1)S(1)} collective-permute-done((bf16[128,1024]{1,0:T(8,128)(2,1)S(1)}, bf16[128,1024]{1,0:T(8,128)(2,1)S(1)}, u32[]{:S(2)}, u32[]{:S(2)}) %collective-permute-start.7) | collective-permute-done | bytes 262176 | tf_op jit(solution)/shard_map/ppermute | solution.py:370
  58.9 0.7 copy-done.41
  59.6 2.8 %shard_map.121.x = bf16[128,1024]{1,0:T(8,128)(2,1)} custom-call(s32[4]{0:T(128)} %get-tuple-element.68.scal.order, bf16[2,128,1024]{2,1,0:T(8,128)(2,1)} %bitcast.110, bf16[2,128,1024]{2,1,0:T(8,128)(2,1)} %copy-done.21, bf16[128,1024]{1,0:T(8,128)(2,1)} %copy-done.41), custom_call_target="tpu_custom_call" | custom-call | flops 120000004096 | bytes 1000000 | tf_op jit(solution)/shard_map/pallas_call | solution.py:191
  62.6 4.8 %shard_map.122 = (bf16[2,128,1024]{2,1,0:T(8,128)(2,1)}, bf16[2,128,1024]{2,1,0:T(8,128)(2,1)}) custom-call(s32[101]{0:T(128)} %concatenate.61.scal, bf16[128,1024]{1,0:T(8,128)(2,1)} %shard_map.121.x, bf16[4,2,256,256]{3,2,1,0:T(8,128)(2,1)} %gt.1, bf16[4,2,256,256]{3,2,1,0:T(8,128)(2,1)} %ut.1, s32[1,512]{1,0:T(1,128)} %bitcast.111), custom_call_target="tpu_custom_call" | custom-call | flops 120000004096 | bytes 4000000 | tf_op jit(solution)/shard_map/pallas_call | solution.py:120
  67.5 2.0 collective-permute-done.9.core
  69.5 1.1 fusion.11
  70.6 1.5 collective-permute-start.10
  72.1 0.9 add_select_fusion.refs_2_.refs_11_
  72.9 1.5 collective-permute-start.15
  75.0 9.6 %shard_map.123 = (f32[2,64,2048]{2,1,0:T(8,128)}, f32[2,64,2048]{2,1,0:T(8,128)}) custom-call(s32[4]{0:T(128)} %get-tuple-element.68.scal.order, bf16[4,16,8,2048]{3,2,1,0:T(8,128)(2,1)} %bitcast.94, bf16[4,16,8,2048]{3,2,1,0:T(8,128)(2,1)} %bitcast.95, bf16[4,16,8,2048]{3,2,1,0:T(8,128)(2,1)} %bitcast.96, bf16[4,16,8,2048]{3,2,1,0:T(8,128)(2,1)} %bitcast.97, ...), custom_call_target="tpu_custom_call" | custom-call | flops 2147483648 | bytes 16777216 | tf_op jit(solution)/shard_map/pallas_call | solution.py:165
  84.7 0.7 copy-done.40
  85.5 2.5 %shard_map.124.refs_1_ = bf16[128,1024]{1,0:T(8,128)(2,1)} custom-call(s32[4]{0:T(128)} %get-tuple-element.68.scal.order, bf16[2,128,1024]{2,1,0:T(8,128)(2,1)} %get-tuple-element.59.keep, bf16[2,128,1024]{2,1,0:T(8,128)(2,1)} %copy-done.22, bf16[128,1024]{1,0:T(8,128)(2,1)} %copy-done.40), custom_call_target="tpu_custom_call" | custom-call | flops 120000004096 | bytes 1000000 | tf_op jit(solution)/shard_map/pallas_call | solution.py:191
  88.1 0.9 copy-done.19
  89.0 3.9 %shard_map.125 = bf16[96,2048]{1,0:T(8,128)(2,1)} custom-call(f32[2,192,2048]{2,1,0:T(8,128)} %get-tuple-element.46.keep, f32[2,192,2048]{2,1,0:T(8,128)} %copy-done.2, bf16[2,96,2048]{2,1,0:T(8,128)(2,1)} %copy-done.12, bf16[128,1024]{1,0:T(8,128)(2,1)} %shard_map.124.refs_1_, s32[512,1]{1,0:T(8,128)} %add_select_fusion.refs_2_.refs_11_, ...), custom_call_target="tpu_custom_call" | custom-call | flops 1000000000 | bytes 4718592 | tf_op jit(solution)/shard_map/pallas_call | solution.py:236
  92.8 1.4 collective-permute-start.14
  94.9 1.0 collective-permute-done.12.refs_0_
  95.9 9.5 %shard_map.126 = (f32[2,64,2048]{2,1,0:T(8,128)}, f32[2,64,2048]{2,1,0:T(8,128)}) custom-call(s32[4]{0:T(128)} %get-tuple-element.68.scal.order, bf16[4,16,8,2048]{3,2,1,0:T(8,128)(2,1)} %bitcast.98, bf16[4,16,8,2048]{3,2,1,0:T(8,128)(2,1)} %bitcast.99, bf16[4,16,8,2048]{3,2,1,0:T(8,128)(2,1)} %bitcast.100, bf16[4,16,8,2048]{3,2,1,0:T(8,128)(2,1)} %bitcast.101, ...), custom_call_target="tpu_custom_call" | custom-call | flops 2147483648 | bytes 16777216 | tf_op jit(solution)/shard_map/pallas_call | solution.py:165
  105.4 4.7 %collective-permute-done.13.refs_0_ = bf16[2,32,2048]{2,1,0:T(8,128)(2,1)S(1)} collective-permute-done((bf16[2,32,2048]{2,1,0:T(8,128)(2,1)S(1)}, bf16[2,32,2048]{2,1,0:T(8,128)(2,1)S(1)}, u32[]{:S(2)}, u32[]{:S(2)}) %collective-permute-start.13) | collective-permute-done | bytes 262176 | tf_op jit(solution)/shard_map/ppermute | solution.py:370
  110.2 4.0 %shard_map.127 = bf16[96,2048]{1,0:T(8,128)(2,1)} custom-call(f32[2,192,2048]{2,1,0:T(8,128)} %get-tuple-element.54.keep, f32[2,192,2048]{2,1,0:T(8,128)} %copy-done.11, bf16[2,96,2048]{2,1,0:T(8,128)(2,1)} %copy-done.38, bf16[128,1024]{1,0:T(8,128)(2,1)} %shard_map.124.refs_1_, s32[512,1]{1,0:T(8,128)} %add_select_fusion.refs_2_.refs_11_, ...), custom_call_target="tpu_custom_call" | custom-call | flops 120000004096 | bytes 4718592 | tf_op jit(solution)/shard_map/pallas_call | solution.py:236
  114.2 1.4 collective-permute-start.16
  116.3 2.5 %shard_map.128 = bf16[32,2048]{1,0:T(8,128)(2,1)} custom-call(f32[2,64,2048]{2,1,0:T(8,128)} %get-tuple-element.64.keep, f32[2,64,2048]{2,1,0:T(8,128)} %copy-done.19, bf16[2,32,2048]{2,1,0:T(8,128)(2,1)} %copy-done.39, bf16[128,1024]{1,0:T(8,128)(2,1)} %shard_map.124.refs_1_, s32[512,1]{1,0:T(8,128)} %add_select_fusion.refs_2_.refs_11_, ...), custom_call_target="tpu_custom_call" | custom-call | flops 1000000000 | bytes 1572864 | tf_op jit(solution)/shard_map/pallas_call | solution.py:236
  118.8 6.3 %collective-permute-done.16 = bf16[96,2048]{1,0:T(8,128)(2,1)S(1)} collective-permute-done((bf16[96,2048]{1,0:T(8,128)(2,1)}, bf16[96,2048]{1,0:T(8,128)(2,1)S(1)}, u32[]{:S(2)}, u32[]{:S(2)}) %collective-permute-start.16) | collective-permute-done | bytes 393248 | tf_op jit(solution)/shard_map/ppermute | solution.py:370
  125.2 1.0 pad_maximum_fusion.1.refs_3_
  126.7 0.9 fusion.5
  127.7 2.1 collective-permute-done.21.refs_9_
  129.8 1.4 collective-permute-start.27
  131.7 0.7 concatenate.60.scal
  132.4 0.6 collective-permute-start.26
  133.0 1.0 copy-done.4
  134.0 17.6 %shard_map.129 = f32[384,2048]{1,0:T(8,128)} custom-call(s32[103]{0:T(128)} %concatenate.60.scal, bf16[192,2048]{1,0:T(8,128)(2,1)} %collective-permute-done.18.refs_0_, bf16[192,2048]{1,0:T(8,128)(2,1)} %collective-permute-done.19.refs_1_, bf16[192,2048]{1,0:T(8,128)(2,1)} %copy-done.5, bf16[192,2048]{1,0:T(8,128)(2,1)} %pad_maximum_fusion.1.refs_3_, ...), custom_call_target="tpu_custom_call" | custom-call | flops 1000000000 | bytes 1000000 | tf_op jit(solution)/shard_map/pallas_call | solution.py:312
  151.7 2.7 %shard_map.130 = bf16[32,2048]{1,0:T(8,128)(2,1)} custom-call(f32[2,64,2048]{2,1,0:T(8,128)} %get-tuple-element.73.keep, f32[2,64,2048]{2,1,0:T(8,128)} %copy-done.17, bf16[2,32,2048]{2,1,0:T(8,128)(2,1)} %collective-permute-done.27.refs_0_, bf16[128,1024]{1,0:T(8,128)(2,1)} %shard_map.124.refs_1_, s32[512,1]{1,0:T(8,128)} %add_select_fusion.refs_2_.refs_11_, ...), custom_call_target="tpu_custom_call" | custom-call | flops 1000000000 | bytes 1572864 | tf_op jit(solution)/shard_map/pallas_call | solution.py:236
  154.4 2.7 %collective-permute-start.29 = (bf16[32,2048]{1,0:T(8,128)(2,1)}, bf16[32,2048]{1,0:T(8,128)(2,1)S(1)}, u32[]{:S(2)}, u32[]{:S(2)}) collective-permute-start(bf16[32,2048]{1,0:T(8,128)(2,1)} %shard_map.130), channel_id=1, source_target_pairs={{0,8},{4,12},{8,0},{12,4},{1,9},{5,13},{9,1},{13,5},{2,10},{6,14},... | collective-permute-start | bytes 393224 | tf_op jit(solution)/shard_map/ppermute | solution.py:370
  157.2 3.0 %collective-permute-done.29 = bf16[32,2048]{1,0:T(8,128)(2,1)S(1)} collective-permute-done((bf16[32,2048]{1,0:T(8,128)(2,1)}, bf16[32,2048]{1,0:T(8,128)(2,1)S(1)}, u32[]{:S(2)}, u32[]{:S(2)}) %collective-permute-start.29) | collective-permute-done | bytes 131104 | tf_op jit(solution)/shard_map/ppermute | solution.py:370
  160.2 0.9 pad_maximum_fusion.4.refs_3_
  161.4 1.7 collective-permute-start.23
  163.1 3.0 %collective-permute-start.24 = (bf16[4,24,2048]{2,1,0:T(8,128)(2,1)S(1)}, bf16[4,24,2048]{2,1,0:T(8,128)(2,1)S(1)}, u32[]{:S(2)}, u32[]{:S(2)}) collective-permute-start(bf16[4,24,2048]{2,1,0:T(8,128)(2,1)S(1)} %get-tuple-element.91), channel_id=1, source_target_pairs={{0,2},{1,3},{2,0},{3,1},{4,6},{5,7},{6,4},{7,5},{8,10},{9,11},{10,... | collective-permute-start | bytes 1179656 | tf_op jit(solution)/shard_map/ppermute | solution.py:549
  166.1 1.7 collective-permute-start.25
  167.9 0.7 copy-done.14
  168.5 0.7 copy-done.15
  169.3 13.1 %shard_map.131 = f32[128,2048]{1,0:T(8,128)} custom-call(s32[103]{0:T(128)} %concatenate.60.scal, bf16[64,2048]{1,0:T(8,128)(2,1)} %copy-done.14, bf16[64,2048]{1,0:T(8,128)(2,1)} %copy-done.15, bf16[64,2048]{1,0:T(8,128)(2,1)} %copy-done.8, bf16[64,2048]{1,0:T(8,128)(2,1)} %copy-done.9, bf16[4096,2048]{1,0:T(8,128)(2,1)} %refs_4_.11, ...), custom_call_target="tpu_custom_call" | custom-call | flops 1000000000 | bytes 1000000 | tf_op jit(solution)/shard_map/pallas_call | solution.py:312
  182.4 1.1 fusion.18
  183.5 8.2 %collective-permute-start.31 = (bf16[4,8,2048]{2,1,0:T(8,128)(2,1)S(1)}, bf16[4,8,2048]{2,1,0:T(8,128)(2,1)S(1)}, u32[]{:S(2)}, u32[]{:S(2)}) collective-permute-start(bf16[4,8,2048]{2,1,0:T(8,128)(2,1)S(1)} %get-tuple-element.84), channel_id=1, source_target_pairs={{0,1},{1,2},{2,3},{3,0},{4,5},{5,6},{6,7},{7,4},{8,9},{9,10},{10,1... | collective-permute-start | bytes 393224 | tf_op jit(solution)/shard_map/ppermute | solution.py:549
  191.8 0.7 collective-permute-done.24
  192.5 1.2 collective-permute-start.32
  193.7 12.2 %collective-permute-start.33 = (bf16[4,8,2048]{2,1,0:T(8,128)(2,1)S(1)}, bf16[4,8,2048]{2,1,0:T(8,128)(2,1)S(1)}, u32[]{:S(2)}, u32[]{:S(2)}) collective-permute-start(bf16[4,8,2048]{2,1,0:T(8,128)(2,1)S(1)} %get-tuple-element.86), channel_id=1, source_target_pairs={{0,3},{1,0},{2,1},{3,2},{4,7},{5,4},{6,5},{7,6},{8,11},{9,8},{10,9... | collective-permute-start | bytes 393224 | tf_op jit(solution)/shard_map/ppermute | solution.py:549
  206.8 1.2 collective-permute-done.32
  208.0 1.4 collective-permute-done.33
  209.4 1.0 fusion.15
  211.0 0.8 pad_maximum_fusion.2
  (155 shorter events, 8.3 us)
Async XLA Ops:
  0.7 22.5 %collective-permute-start = (s32[4,6]{0,1:T(8,128)S(1)}, s32[4,6]{0,1:T(8,128)S(1)}, u32[]{:S(2)}, u32[]{:S(2)}) collective-permute-start(s32[4,6]{0,1:T(8,128)S(1)} %pad_add_fusion), channel_id=1, source_target_pairs={{0,12},{4,0},{8,4},{12,8},{1,13},{5,1},{9,5},{13,9},{2,14},{6,2},{... | collective-permute-start | bytes 296 | tf_op jit(solution)/shard_map/ppermute | solution.py:398
  3.2 20.3 %collective-permute-start.1 = (s32[4,6]{0,1:T(8,128)S(1)}, s32[4,6]{0,1:T(8,128)S(1)}, u32[]{:S(2)}, u32[]{:S(2)}) collective-permute-start(s32[4,6]{0,1:T(8,128)S(1)} %pad_add_fusion), channel_id=1, source_target_pairs={{0,8},{4,12},{8,0},{12,4},{1,9},{5,13},{9,1},{13,5},{2,10},{6,14},... | collective-permute-start | bytes 296 | tf_op jit(solution)/shard_map/ppermute | solution.py:398
  3.8 19.8 %collective-permute-start.2 = (s32[4,6]{0,1:T(8,128)S(1)}, s32[4,6]{0,1:T(8,128)S(1)}, u32[]{:S(2)}, u32[]{:S(2)}) collective-permute-start(s32[4,6]{0,1:T(8,128)S(1)} %pad_add_fusion), channel_id=1, source_target_pairs={{0,4},{4,8},{8,12},{12,0},{1,5},{5,9},{9,13},{13,1},{2,6},{6,10},{... | collective-permute-start | bytes 296 | tf_op jit(solution)/shard_map/ppermute | solution.py:398
  5.8 18.6 %collective-permute-start.4 = (bf16[4,256,256]{2,1,0:T(8,128)(2,1)}, bf16[4,256,256]{2,1,0:T(8,128)(2,1)}, u32[]{:S(2)}, u32[]{:S(2)}) collective-permute-start(bf16[4,256,256]{2,1,0:T(8,128)(2,1)} %constant_dynamic-slice_fusion), channel_id=1, source_target_pairs={{0,8},{4,12},{8,0},{12,4},{1,9},{5,13},{9,1},{13,5},{2,10},{6,14},... | collective-permute-start | bytes 1572872 | tf_op jit(solution)/shard_map/ppermute | solution.py:370
  7.7 13.9 %copy-start.24 = (s32[4]{0:T(128)S(1)}, s32[4]{0:T(128)}, u32[]{:S(2)}) copy-start(s32[4]{0:T(128)} %get-tuple-element.68.scal.order) | copy-start | bytes 52
  7.7 14.0 %copy-start.36 = (s32[512]{0:T(512)S(1)}, s32[512]{0:T(512)}, u32[]{:S(2)}) copy-start(s32[512]{0:T(512)} %param.22) | copy-start | bytes 6148
  7.7 14.0 %copy-start.37 = (s32[16]{0:T(128)S(1)}, s32[16]{0:T(128)}, u32[]{:S(2)}) copy-start(s32[16]{0:T(128)} %param.23) | copy-start | bytes 196
  21.1 10.8 %collective-permute-start.3 = (f32[2,192,2048]{2,1,0:T(8,128)}, f32[2,192,2048]{2,1,0:T(8,128)S(1)}, u32[]{:S(2)}, u32[]{:S(2)}) collective-permute-start(f32[2,192,2048]{2,1,0:T(8,128)} %get-tuple-element.47), channel_id=1, source_target_pairs={{0,4},{4,0},{8,12},{12,8},{1,5},{5,1},{9,13},{13,9},{2,6},{6,2},{1... | collective-permute-start | bytes 9437192 | tf_op jit(solution)/shard_map/ppermute | solution.py:367
  21.8 10.0 %copy-start.27 = (s32[24]{0:T(128)}, s32[24]{0:T(128)S(1)}, u32[]{:S(2)}) copy-start(s32[24]{0:T(128)S(1)} %reshape.445) | copy-start | bytes 292
  23.4 8.4 %copy-start.29 = (s32[24]{0:T(128)}, s32[24]{0:T(128)S(1)}, u32[]{:S(2)}) copy-start(s32[24]{0:T(128)S(1)} %reshape.446) | copy-start | bytes 292
  23.6 8.2 %copy-start.31 = (s32[24]{0:T(128)}, s32[24]{0:T(128)S(1)}, u32[]{:S(2)}) copy-start(s32[24]{0:T(128)S(1)} %reshape.447) | copy-start | bytes 292
  23.8 8.0 %copy-start.33 = (s32[24]{0:T(128)}, s32[24]{0:T(128)S(1)}, u32[]{:S(2)}) copy-start(s32[24]{0:T(128)S(1)} %reshape.448) | copy-start | bytes 292
  24.5 7.5 %copy-start.1 = (f32[2,192,2048]{2,1,0:T(8,128)S(1)}, f32[2,192,2048]{2,1,0:T(8,128)}, u32[]{:S(2)}) copy-start(f32[2,192,2048]{2,1,0:T(8,128)} %get-tuple-element.46.keep) | copy-start | bytes 9437188
  31.8 2.6 %collective-permute-start.5 = (bf16[2,128,1024]{2,1,0:T(8,128)(2,1)}, bf16[2,128,1024]{2,1,0:T(8,128)(2,1)S(1)}, u32[]{:S(2)}, u32[]{:S(2)}) collective-permute-start(bf16[2,128,1024]{2,1,0:T(8,128)(2,1)} %bitcast.116), channel_id=1, source_target_pairs={{0,4},{4,0},{8,12},{12,8},{1,5},{5,1},{9,13},{13,9},{2,6},{6,2},{1... | collective-permute-start | bytes 1572872 | tf_op jit(solution)/shard_map/ppermute | solution.py:367
  31.9 16.7 %copy-start.2 = (f32[2,192,2048]{2,1,0:T(8,128)}, f32[2,192,2048]{2,1,0:T(8,128)S(1)}, u32[]{:S(2)}) copy-start(f32[2,192,2048]{2,1,0:T(8,128)S(1)} %collective-permute-done.3.core) | copy-start | bytes 9437188
  33.0 20.5 %collective-permute-start.6 = (bf16[2,96,2048]{2,1,0:T(8,128)(2,1)}, bf16[2,96,2048]{2,1,0:T(8,128)(2,1)S(1)}, u32[]{:S(2)}, u32[]{:S(2)}) collective-permute-start(bf16[2,96,2048]{2,1,0:T(8,128)(2,1)} %fusion.1), channel_id=1, source_target_pairs={{0,8},{4,12},{8,0},{12,4},{1,9},{5,13},{9,1},{13,5},{2,10},{6,14},... | collective-permute-start | bytes 2359304 | tf_op jit(solution)/shard_map/ppermute | solution.py:370
  34.4 14.3 %copy-start.21 = (bf16[2,128,1024]{2,1,0:T(8,128)(2,1)}, bf16[2,128,1024]{2,1,0:T(8,128)(2,1)S(1)}, u32[]{:S(2)}) copy-start(bf16[2,128,1024]{2,1,0:T(8,128)(2,1)S(1)} %collective-permute-done.5.core) | copy-start | bytes 1572868
  34.4 14.3 %copy-start.35 = (s32[1,512]{1,0:T(1,128)S(1)}, s32[1,512]{1,0:T(1,128)}, u32[]{:S(2)}) copy-start(s32[1,512]{1,0:T(1,128)} %get-tuple-element.58) | copy-start | bytes 6148
  34.4 24.5 %collective-permute-start.7 = (bf16[128,1024]{1,0:T(8,128)(2,1)S(1)}, bf16[128,1024]{1,0:T(8,128)(2,1)S(1)}, u32[]{:S(2)}, u32[]{:S(2)}) collective-permute-start(bf16[128,1024]{1,0:T(8,128)(2,1)S(1)} %fusion.12), channel_id=1, source_target_pairs={{0,8},{4,12},{8,0},{12,4},{1,9},{5,13},{9,1},{13,5},{2,10},{6,14},... | collective-permute-start | bytes 786440 | tf_op jit(solution)/shard_map/ppermute | solution.py:370
  48.7 13.7 %collective-permute-start.8 = (f32[2,192,2048]{2,1,0:T(8,128)}, f32[2,192,2048]{2,1,0:T(8,128)S(1)}, u32[]{:S(2)}, u32[]{:S(2)}) collective-permute-start(f32[2,192,2048]{2,1,0:T(8,128)} %get-tuple-element.55), channel_id=1, source_target_pairs={{0,4},{4,0},{8,12},{12,8},{1,5},{5,1},{9,13},{13,9},{2,6},{6,2},{1... | collective-permute-start | bytes 9437192 | tf_op jit(solution)/shard_map/ppermute | solution.py:367
  53.5 5.4 %copy-start.12 = (bf16[2,96,2048]{2,1,0:T(8,128)(2,1)}, bf16[2,96,2048]{2,1,0:T(8,128)(2,1)S(1)}, u32[]{:S(2)}) copy-start(bf16[2,96,2048]{2,1,0:T(8,128)(2,1)S(1)} %collective-permute-done.6.refs_0_) | copy-start | bytes 2359300
  62.4 5.0 %copy-start.11 = (f32[2,192,2048]{2,1,0:T(8,128)}, f32[2,192,2048]{2,1,0:T(8,128)S(1)}, u32[]{:S(2)}) copy-start(f32[2,192,2048]{2,1,0:T(8,128)S(1)} %collective-permute-done.8.core) | copy-start | bytes 9437188
  62.6 4.8 %copy-start.25 = (s32[512]{0:T(512)S(1)}, s32[512]{0:T(512)}, u32[]{:S(2)}) copy-start(s32[512]{0:T(512)} %select_reduce_fusion) | copy-start | bytes 6148
  67.3 2.1 %collective-permute-start.9 = (bf16[2,128,1024]{2,1,0:T(8,128)(2,1)}, bf16[2,128,1024]{2,1,0:T(8,128)(2,1)S(1)}, u32[]{:S(2)}, u32[]{:S(2)}) collective-permute-start(bf16[2,128,1024]{2,1,0:T(8,128)(2,1)} %get-tuple-element.60), channel_id=1, source_target_pairs={{0,4},{4,0},{8,12},{12,8},{1,5},{5,1},{9,13},{13,9},{2,6},{6,2},{1... | collective-permute-start | bytes 1572872 | tf_op jit(solution)/shard_map/ppermute | solution.py:367
  69.5 15.2 %copy-start.22 = (bf16[2,128,1024]{2,1,0:T(8,128)(2,1)}, bf16[2,128,1024]{2,1,0:T(8,128)(2,1)S(1)}, u32[]{:S(2)}) copy-start(bf16[2,128,1024]{2,1,0:T(8,128)(2,1)S(1)} %collective-permute-done.9.core) | copy-start | bytes 1572868
  70.6 14.1 %collective-permute-start.10 = (bf16[128,1024]{1,0:T(8,128)(2,1)S(1)}, bf16[128,1024]{1,0:T(8,128)(2,1)S(1)}, u32[]{:S(2)}, u32[]{:S(2)}) collective-permute-start(bf16[128,1024]{1,0:T(8,128)(2,1)S(1)} %fusion.11), channel_id=1, source_target_pairs={{0,8},{4,12},{8,0},{12,4},{1,9},{5,13},{9,1},{13,5},{2,10},{6,14},... | collective-permute-start | bytes 786440 | tf_op jit(solution)/shard_map/ppermute | solution.py:370
  72.9 32.5 %collective-permute-start.15 = (bf16[4,256,256]{2,1,0:T(8,128)(2,1)}, bf16[4,256,256]{2,1,0:T(8,128)(2,1)}, u32[]{:S(2)}, u32[]{:S(2)}) collective-permute-start(bf16[4,256,256]{2,1,0:T(8,128)(2,1)} %collective-permute-done.4.refs_5_), channel_id=1, source_target_pairs={{0,16},{16,0},{1,17},{17,1},{2,18},{18,2},{3,19},{19,3},{4,20},{20... | collective-permute-start | bytes 1572872 | tf_op jit(solution)/shard_map/ppermute | solution.py:475
  74.4 21.5 %collective-permute-start.12 = (bf16[2,96,2048]{2,1,0:T(8,128)(2,1)S(1)}, bf16[2,96,2048]{2,1,0:T(8,128)(2,1)S(1)}, u32[]{:S(2)}, u32[]{:S(2)}) collective-permute-start(bf16[2,96,2048]{2,1,0:T(8,128)(2,1)S(1)} %fusion), channel_id=1, source_target_pairs={{0,8},{4,12},{8,0},{12,4},{1,9},{5,13},{9,1},{13,5},{2,10},{6,14},... | collective-permute-start | bytes 2359304 | tf_op jit(solution)/shard_map/ppermute | solution.py:370
  84.6 3.3 %collective-permute-start.11 = (f32[2,64,2048]{2,1,0:T(8,128)}, f32[2,64,2048]{2,1,0:T(8,128)S(1)}, u32[]{:S(2)}, u32[]{:S(2)}) collective-permute-start(f32[2,64,2048]{2,1,0:T(8,128)} %get-tuple-element.65), channel_id=1, source_target_pairs={{0,4},{4,0},{8,12},{12,8},{1,5},{5,1},{9,13},{13,9},{2,6},{6,2},{1... | collective-permute-start | bytes 3145736 | tf_op jit(solution)/shard_map/ppermute | solution.py:367
  92.8 17.3 %collective-permute-start.14 = (bf16[96,2048]{1,0:T(8,128)(2,1)}, bf16[96,2048]{1,0:T(8,128)(2,1)S(1)}, u32[]{:S(2)}, u32[]{:S(2)}) collective-permute-start(bf16[96,2048]{1,0:T(8,128)(2,1)} %shard_map.125), channel_id=1, source_target_pairs={{0,8},{4,12},{8,0},{12,4},{1,9},{5,13},{9,1},{13,5},{2,10},{6,14},... | collective-permute-start | bytes 1179656 | tf_op jit(solution)/shard_map/ppermute | solution.py:370
  94.2 16.0 %collective-permute-start.13 = (bf16[2,32,2048]{2,1,0:T(8,128)(2,1)S(1)}, bf16[2,32,2048]{2,1,0:T(8,128)(2,1)S(1)}, u32[]{:S(2)}, u32[]{:S(2)}) collective-permute-start(bf16[2,32,2048]{2,1,0:T(8,128)(2,1)S(1)} %fusion.6), channel_id=1, source_target_pairs={{0,8},{4,12},{8,0},{12,4},{1,9},{5,13},{9,1},{13,5},{2,10},{6,14},... | collective-permute-start | bytes 786440 | tf_op jit(solution)/shard_map/ppermute | solution.py:370
  95.9 9.5 %copy-start.38 = (bf16[2,96,2048]{2,1,0:T(8,128)(2,1)}, bf16[2,96,2048]{2,1,0:T(8,128)(2,1)S(1)}, u32[]{:S(2)}) copy-start(bf16[2,96,2048]{2,1,0:T(8,128)(2,1)S(1)} %collective-permute-done.12.refs_0_) | copy-start | bytes 2359300
  105.4 21.3 %collective-permute-start.17 = (f32[2,64,2048]{2,1,0:T(8,128)}, f32[2,64,2048]{2,1,0:T(8,128)S(1)}, u32[]{:S(2)}, u32[]{:S(2)}) collective-permute-start(f32[2,64,2048]{2,1,0:T(8,128)} %get-tuple-element.74), channel_id=1, source_target_pairs={{0,4},{4,0},{8,12},{12,8},{1,5},{5,1},{9,13},{13,9},{2,6},{6,2},{1... | collective-permute-start | bytes 3145736 | tf_op jit(solution)/shard_map/ppermute | solution.py:367
  110.2 4.0 %copy-start.39 = (bf16[2,32,2048]{2,1,0:T(8,128)(2,1)}, bf16[2,32,2048]{2,1,0:T(8,128)(2,1)S(1)}, u32[]{:S(2)}) copy-start(bf16[2,32,2048]{2,1,0:T(8,128)(2,1)S(1)} %collective-permute-done.13.refs_0_) | copy-start | bytes 786436
  110.2 5.4 %copy-start.3 = (bf16[4,2,256,256]{3,2,1,0:T(8,128)(2,1)S(1)}, bf16[4,2,256,256]{3,2,1,0:T(8,128)(2,1)}, u32[]{:S(2)}) copy-start(bf16[4,2,256,256]{3,2,1,0:T(8,128)(2,1)} %param.18) | copy-start | bytes 3145732
  110.2 5.4 %copy-start.7 = (bf16[96,2048]{1,0:T(8,128)(2,1)S(1)}, bf16[96,2048]{1,0:T(8,128)(2,1)}, u32[]{:S(2)}) copy-start(bf16[96,2048]{1,0:T(8,128)(2,1)} %shard_map.125) | copy-start | bytes 1179652
  114.2 11.0 %copy-start.13 = (bf16[96,2048]{1,0:T(8,128)(2,1)S(1)}, bf16[96,2048]{1,0:T(8,128)(2,1)}, u32[]{:S(2)}) copy-start(bf16[96,2048]{1,0:T(8,128)(2,1)} %shard_map.127) | copy-start | bytes 1179652
  114.2 12.6 %copy-start.16 = (f32[2,64,2048]{2,1,0:T(8,128)S(1)}, f32[2,64,2048]{2,1,0:T(8,128)}, u32[]{:S(2)}) copy-start(f32[2,64,2048]{2,1,0:T(8,128)} %get-tuple-element.73.keep) | copy-start | bytes 3145732
  114.2 11.0 %collective-permute-start.16 = (bf16[96,2048]{1,0:T(8,128)(2,1)}, bf16[96,2048]{1,0:T(8,128)(2,1)S(1)}, u32[]{:S(2)}, u32[]{:S(2)}) collective-permute-start(bf16[96,2048]{1,0:T(8,128)(2,1)} %shard_map.127), channel_id=1, source_target_pairs={{0,8},{4,12},{8,0},{12,4},{1,9},{5,13},{9,1},{13,5},{2,10},{6,14},... | collective-permute-start | bytes 1179656 | tf_op jit(solution)/shard_map/ppermute | solution.py:370
  115.6 17.4 %collective-permute-start.22 = (bf16[8,256,256]{2,1,0:T(8,128)(2,1)S(1)}, bf16[8,256,256]{2,1,0:T(8,128)(2,1)S(1)}, u32[]{:S(2)}, u32[]{:S(2)}) collective-permute-start(bf16[8,256,256]{2,1,0:T(8,128)(2,1)S(1)} %bitcast.107), channel_id=1, source_target_pairs={{0,4},{4,0},{8,12},{12,8},{1,5},{5,1},{9,13},{13,9},{2,6},{6,2},{1... | collective-permute-start | bytes 3145736 | tf_op jit(solution)/shard_map/ppermute | solution.py:367
  115.7 12.0 %copy-start.5 = (bf16[192,2048]{1,0:T(8,128)(2,1)}, bf16[192,2048]{1,0:T(8,128)(2,1)S(1)}, u32[]{:S(2)}) copy-start(bf16[192,2048]{1,0:T(8,128)(2,1)S(1)} %pad_maximum_fusion.refs_2_) | copy-start | bytes 2359300
  115.7 16.0 %copy-start.28 = (s32[24]{0:T(128)S(1)}, s32[24]{0:T(128)}, u32[]{:S(2)}) copy-start(s32[24]{0:T(128)} %copy-done.27) | copy-start | bytes 292
  115.7 16.0 %copy-start.30 = (s32[24]{0:T(128)S(1)}, s32[24]{0:T(128)}, u32[]{:S(2)}) copy-start(s32[24]{0:T(128)} %copy-done.29) | copy-start | bytes 292
  115.7 15.9 %copy-start.32 = (s32[24]{0:T(128)S(1)}, s32[24]{0:T(128)}, u32[]{:S(2)}) copy-start(s32[24]{0:T(128)} %copy-done.31) | copy-start | bytes 292
  115.7 15.9 %copy-start.34 = (s32[24]{0:T(128)S(1)}, s32[24]{0:T(128)}, u32[]{:S(2)}) copy-start(s32[24]{0:T(128)} %copy-done.33) | copy-start | bytes 292
  115.7 17.3 %collective-permute-start.18 = (bf16[192,2048]{1,0:T(8,128)(2,1)S(1)}, bf16[192,2048]{1,0:T(8,128)(2,1)}, u32[]{:S(2)}, u32[]{:S(2)}) collective-permute-start(bf16[192,2048]{1,0:T(8,128)(2,1)S(1)} %pad_maximum_fusion.refs_2_), channel_id=1, source_target_pairs={{0,4},{4,0},{8,12},{12,8},{1,5},{5,1},{9,13},{13,9},{2,6},{6,2},{1... | collective-permute-start | bytes 2359304 | tf_op jit(solution)/shard_map/ppermute | solution.py:367
  126.1 6.9 %collective-permute-start.19 = (bf16[192,2048]{1,0:T(8,128)(2,1)}, bf16[192,2048]{1,0:T(8,128)(2,1)}, u32[]{:S(2)}, u32[]{:S(2)}) collective-permute-start(bf16[192,2048]{1,0:T(8,128)(2,1)} %pad_maximum_fusion.1.refs_3_), channel_id=1, source_target_pairs={{0,4},{4,0},{8,12},{12,8},{1,5},{5,1},{9,13},{13,9},{2,6},{6,2},{1... | collective-permute-start | bytes 2359304 | tf_op jit(solution)/shard_map/ppermute | solution.py:367
  126.1 3.6 %collective-permute-start.21 = (bf16[4,256,256]{2,1,0:T(8,128)(2,1)}, bf16[4,256,256]{2,1,0:T(8,128)(2,1)S(1)}, u32[]{:S(2)}, u32[]{:S(2)}) collective-permute-start(bf16[4,256,256]{2,1,0:T(8,128)(2,1)} %collective-permute-done.15.refs_6_), channel_id=1, source_target_pairs={{0,4},{4,0},{8,12},{12,8},{1,5},{5,1},{9,13},{13,9},{2,6},{6,2},{1... | collective-permute-start | bytes 1572872 | tf_op jit(solution)/shard_map/ppermute | solution.py:367
  126.7 5.7 %collective-permute-start.20 = (bf16[4,256,256]{2,1,0:T(8,128)(2,1)}, bf16[4,256,256]{2,1,0:T(8,128)(2,1)}, u32[]{:S(2)}, u32[]{:S(2)}) collective-permute-start(bf16[4,256,256]{2,1,0:T(8,128)(2,1)} %collective-permute-done.4.refs_5_), channel_id=1, source_target_pairs={{0,4},{4,0},{8,12},{12,8},{1,5},{5,1},{9,13},{13,9},{2,6},{6,2},{1... | collective-permute-start | bytes 1572872 | tf_op jit(solution)/shard_map/ppermute | solution.py:367
  129.8 21.9 %collective-permute-start.27 = (bf16[2,32,2048]{2,1,0:T(8,128)(2,1)}, bf16[2,32,2048]{2,1,0:T(8,128)(2,1)}, u32[]{:S(2)}, u32[]{:S(2)}) collective-permute-start(bf16[2,32,2048]{2,1,0:T(8,128)(2,1)} %fusion.5), channel_id=1, source_target_pairs={{0,8},{4,12},{8,0},{12,4},{1,9},{5,13},{9,1},{13,5},{2,10},{6,14},... | collective-permute-start | bytes 786440 | tf_op jit(solution)/shard_map/ppermute | solution.py:370
  132.4 24.7 %collective-permute-start.26 = (bf16[32,2048]{1,0:T(8,128)(2,1)}, bf16[32,2048]{1,0:T(8,128)(2,1)S(1)}, u32[]{:S(2)}, u32[]{:S(2)}) collective-permute-start(bf16[32,2048]{1,0:T(8,128)(2,1)} %shard_map.128), channel_id=1, source_target_pairs={{0,8},{4,12},{8,0},{12,4},{1,9},{5,13},{9,1},{13,5},{2,10},{6,14},... | collective-permute-start | bytes 393224 | tf_op jit(solution)/shard_map/ppermute | solution.py:370
  151.6 5.4 %copy-start.23 = (bf16[32,2048]{1,0:T(8,128)(2,1)S(1)}, bf16[32,2048]{1,0:T(8,128)(2,1)}, u32[]{:S(2)}) copy-start(bf16[32,2048]{1,0:T(8,128)(2,1)} %shard_map.128) | copy-start | bytes 393220
  151.6 9.6 %copy-start = (f32[384,2048]{1,0:T(8,128)S(1)}, f32[384,2048]{1,0:T(8,128)}, u32[]{:S(2)}) copy-start(f32[384,2048]{1,0:T(8,128)} %shard_map.129) | copy-start | bytes 9437188
  154.4 5.9 %collective-permute-start.29 = (bf16[32,2048]{1,0:T(8,128)(2,1)}, bf16[32,2048]{1,0:T(8,128)(2,1)S(1)}, u32[]{:S(2)}, u32[]{:S(2)}) collective-permute-start(bf16[32,2048]{1,0:T(8,128)(2,1)} %shard_map.130), channel_id=1, source_target_pairs={{0,8},{4,12},{8,0},{12,4},{1,9},{5,13},{9,1},{13,5},{2,10},{6,14},... | collective-permute-start | bytes 393224 | tf_op jit(solution)/shard_map/ppermute | solution.py:370
  157.1 10.8 %copy-start.8 = (bf16[64,2048]{1,0:T(8,128)(2,1)}, bf16[64,2048]{1,0:T(8,128)(2,1)S(1)}, u32[]{:S(2)}) copy-start(bf16[64,2048]{1,0:T(8,128)(2,1)S(1)} %pad_maximum_fusion.3.refs_2_) | copy-start | bytes 786436
  157.1 10.7 %collective-permute-start.28 = (bf16[64,2048]{1,0:T(8,128)(2,1)S(1)}, bf16[64,2048]{1,0:T(8,128)(2,1)S(1)}, u32[]{:S(2)}, u32[]{:S(2)}) collective-permute-start(bf16[64,2048]{1,0:T(8,128)(2,1)S(1)} %pad_maximum_fusion.3.refs_2_), channel_id=1, source_target_pairs={{0,4},{4,0},{8,12},{12,8},{1,5},{5,1},{9,13},{13,9},{2,6},{6,2},{1... | collective-permute-start | bytes 786440 | tf_op jit(solution)/shard_map/ppermute | solution.py:367
  161.1 6.7 %copy-start.9 = (bf16[64,2048]{1,0:T(8,128)(2,1)}, bf16[64,2048]{1,0:T(8,128)(2,1)S(1)}, u32[]{:S(2)}) copy-start(bf16[64,2048]{1,0:T(8,128)(2,1)S(1)} %pad_maximum_fusion.4.refs_3_) | copy-start | bytes 786436
  161.1 6.7 %collective-permute-start.30 = (bf16[64,2048]{1,0:T(8,128)(2,1)S(1)}, bf16[64,2048]{1,0:T(8,128)(2,1)S(1)}, u32[]{:S(2)}, u32[]{:S(2)}) collective-permute-start(bf16[64,2048]{1,0:T(8,128)(2,1)S(1)} %pad_maximum_fusion.4.refs_3_), channel_id=1, source_target_pairs={{0,4},{4,0},{8,12},{12,8},{1,5},{5,1},{9,13},{13,9},{2,6},{6,2},{1... | collective-permute-start | bytes 786440 | tf_op jit(solution)/shard_map/ppermute | solution.py:367
  161.4 22.1 %collective-permute-start.23 = (bf16[4,24,2048]{2,1,0:T(8,128)(2,1)S(1)}, bf16[4,24,2048]{2,1,0:T(8,128)(2,1)S(1)}, u32[]{:S(2)}, u32[]{:S(2)}) collective-permute-start(bf16[4,24,2048]{2,1,0:T(8,128)(2,1)S(1)} %get-tuple-element.89), channel_id=1, source_target_pairs={{0,1},{1,2},{2,3},{3,0},{4,5},{5,6},{6,7},{7,4},{8,9},{9,10},{10,1... | collective-permute-start | bytes 1179656 | tf_op jit(solution)/shard_map/ppermute | solution.py:549
  163.1 29.3 %collective-permute-start.24 = (bf16[4,24,2048]{2,1,0:T(8,128)(2,1)S(1)}, bf16[4,24,2048]{2,1,0:T(8,128)(2,1)S(1)}, u32[]{:S(2)}, u32[]{:S(2)}) collective-permute-start(bf16[4,24,2048]{2,1,0:T(8,128)(2,1)S(1)} %get-tuple-element.91), channel_id=1, source_target_pairs={{0,2},{1,3},{2,0},{3,1},{4,6},{5,7},{6,4},{7,5},{8,10},{9,11},{10,... | collective-permute-start | bytes 1179656 | tf_op jit(solution)/shard_map/ppermute | solution.py:549
  166.1 27.6 %collective-permute-start.25 = (bf16[4,24,2048]{2,1,0:T(8,128)(2,1)S(1)}, bf16[4,24,2048]{2,1,0:T(8,128)(2,1)S(1)}, u32[]{:S(2)}, u32[]{:S(2)}) collective-permute-start(bf16[4,24,2048]{2,1,0:T(8,128)(2,1)S(1)} %get-tuple-element.90), channel_id=1, source_target_pairs={{0,3},{1,0},{2,1},{3,2},{4,7},{5,4},{6,5},{7,6},{8,11},{9,8},{10,9... | collective-permute-start | bytes 1179656 | tf_op jit(solution)/shard_map/ppermute | solution.py:549
  183.5 23.2 %collective-permute-start.31 = (bf16[4,8,2048]{2,1,0:T(8,128)(2,1)S(1)}, bf16[4,8,2048]{2,1,0:T(8,128)(2,1)S(1)}, u32[]{:S(2)}, u32[]{:S(2)}) collective-permute-start(bf16[4,8,2048]{2,1,0:T(8,128)(2,1)S(1)} %get-tuple-element.84), channel_id=1, source_target_pairs={{0,1},{1,2},{2,3},{3,0},{4,5},{5,6},{6,7},{7,4},{8,9},{9,10},{10,1... | collective-permute-start | bytes 393224 | tf_op jit(solution)/shard_map/ppermute | solution.py:549
  192.5 15.5 %collective-permute-start.32 = (bf16[4,8,2048]{2,1,0:T(8,128)(2,1)S(1)}, bf16[4,8,2048]{2,1,0:T(8,128)(2,1)S(1)}, u32[]{:S(2)}, u32[]{:S(2)}) collective-permute-start(bf16[4,8,2048]{2,1,0:T(8,128)(2,1)S(1)} %get-tuple-element.85), channel_id=1, source_target_pairs={{0,2},{1,3},{2,0},{3,1},{4,6},{5,7},{6,4},{7,5},{8,10},{9,11},{10,... | collective-permute-start | bytes 393224 | tf_op jit(solution)/shard_map/ppermute | solution.py:549
  193.7 15.7 %collective-permute-start.33 = (bf16[4,8,2048]{2,1,0:T(8,128)(2,1)S(1)}, bf16[4,8,2048]{2,1,0:T(8,128)(2,1)S(1)}, u32[]{:S(2)}, u32[]{:S(2)}) collective-permute-start(bf16[4,8,2048]{2,1,0:T(8,128)(2,1)S(1)} %get-tuple-element.86), channel_id=1, source_target_pairs={{0,3},{1,0},{2,1},{3,2},{4,7},{5,4},{6,5},{7,6},{8,11},{9,8},{10,9... | collective-permute-start | bytes 393224 | tf_op jit(solution)/shard_map/ppermute | solution.py:549
  (12 other events, 22.6 us)

commit v8 on v7

--- a/solution.py
+++ b/solution.py
@@ -8,7 +8,7 @@
 from jax.sharding import PartitionSpec as P
 
 CAP = 128
-CHUNKS = (3, 1)
+CHUNKS = (2, 2)
 PARTS = 2
 SHORT = 120e9
 VMEM = 56 * 1024 * 1024

time: 213 us -> 206 us (0.967)
  the two profiles are of different devices: /device:TPU:0 before, /device:TPU:5 now
where the time goes in v8:
time: 206 us; the launch traced here: 204 us
  Pallas kernels  104 us (50%)
  waiting for transfers between devices  36.9 us (18%)
  starting transfers between devices  35.1 us (17%)
  other arithmetic  15.5 us (8%)
  local copies, waits for them, and re-layouts  12.6 us (6%)
    pallas_call x4, Pallas kernels, gate_up(): pl.pallas_call(functools.partial(gate_up_body, owners), grid_spec=pltpu.P...  42.7 us
    pallas_call x2, Pallas kernels, down(): pl.pallas_call(functools.partial(down_body, width_tiles, width // 256, pl...  31 us
    ppermute x6, waiting for transfers between devices, finish_down(): lax.ppermute(gone, 'tensor', [(j, (j + k) % shift) for j in range(shift)])  20.9 us
    ppermute x11, waiting for transfers between devices, y_move(): lax.ppermute(x, 'delta', [(i, (i + 2 * k) % owners) for i in range(owners)])  14.6 us
    pallas_call x4, Pallas kernels, activate(): pl.pallas_call(functools.partial(activate_body, per_slot, start, each, ro...  13.1 us
    ppermute x13, starting transfers between devices, core_swap(): return lax.ppermute(x, 'delta', [(i, i ^ 1) for i in range(owners)])  12.6 us
    ppermute x6, starting transfers between devices, finish_down(): lax.ppermute(gone, 'tensor', [(j, (j + k) % shift) for j in range(shift)])  11 us
    ppermute x11, starting transfers between devices, y_move(): lax.ppermute(x, 'delta', [(i, (i + 2 * k) % owners) for i in range(owners)])  7.81 us
  transfers between devices with their start and end apart: 34, of which 8 were waited for; matrix products, arithmetic and copies ran while one was open for 9% of the time, Pallas kernels for 49%

profile of v8, /device:TPU:5, one launch (start us, length us, event | category | flops | bytes accessed | tf_op | source)
XLA Modules:
  0.0 204.3 jit_solution(2491270747665794789)
XLA Ops:
  0.0 0.7 pad_add_fusion
  0.7 0.7 collective-permute-start
  1.4 1.7 collective-permute-start.2
  3.1 1.1 constant_dynamic-slice_fusion
  4.2 1.2 collective-permute-start.4
  6.1 10.8 %shard_map.118 = (f32[2,128,2048]{2,1,0:T(8,128)}, f32[2,128,2048]{2,1,0:T(8,128)}) custom-call(s32[4]{0:T(128)} %get-tuple-element.69.scal.order, bf16[4,16,8,2048]{3,2,1,0:T(8,128)(2,1)} %bitcast.78, bf16[4,16,8,2048]{3,2,1,0:T(8,128)(2,1)} %bitcast.79, bf16[4,16,8,2048]{3,2,1,0:T(8,128)(2,1)} %bitcast.80, bf16[4,16,8,2048]{3,2,1,0:T(8,128)(2,1)} %bitcast.81, ...), custom_call_target="tpu_custom_call" | custom-call | flops 4294967296 | bytes 16777216 | tf_op jit(solution)/shard_map/pallas_call | solution.py:165
  17.2 0.8 copy.38.ss
  19.3 0.8 copy-done.7
  20.1 7.1 %shard_map.119 = (bf16[256,1024]{1,0:T(8,128)(2,1)}, bf16[256,1024]{1,0:T(8,128)(2,1)}, s32[1,512]{1,0:T(1,128)}, bf16[128,128]{1,0:T(8,128)(2,1)}) custom-call(s32[101]{0:T(128)} %concatenate.36.scal, bf16[512,2048]{1,0:T(8,128)(2,1)} %x.1, s32[1,512]{1,0:T(1,128)} %bitcast.108, s32[512,1]{1,0:T(8,128)} %copy.38.ss), custom_call_target="tpu_custom_call" | custom-call | flops 120000004096 | bytes 4000000 | tf_op jit(solution)/shard_map/pallas_call | solution.py:73
  28.0 1.4 collective-permute-done.5.core
  29.4 1.1 fusion.18
  31.0 1.3 fusion.3
  32.4 1.2 collective-permute-start.6
  33.5 10.6 %shard_map.120 = (f32[2,128,2048]{2,1,0:T(8,128)}, f32[2,128,2048]{2,1,0:T(8,128)}) custom-call(s32[4]{0:T(128)} %get-tuple-element.69.scal.order, bf16[4,16,8,2048]{3,2,1,0:T(8,128)(2,1)} %bitcast.82, bf16[4,16,8,2048]{3,2,1,0:T(8,128)(2,1)} %bitcast.83, bf16[4,16,8,2048]{3,2,1,0:T(8,128)(2,1)} %bitcast.84, bf16[4,16,8,2048]{3,2,1,0:T(8,128)(2,1)} %bitcast.85, ...), custom_call_target="tpu_custom_call" | custom-call | flops 4294967296 | bytes 16777216 | tf_op jit(solution)/shard_map/pallas_call | solution.py:165
  44.2 1.0 collective-permute-start.8
  45.2 0.8 select_reduce_fusion
  45.9 3.5 %collective-permute-done.6.refs_0_ = bf16[2,64,2048]{2,1,0:T(8,128)(2,1)S(1)} collective-permute-done((bf16[2,64,2048]{2,1,0:T(8,128)(2,1)S(1)}, bf16[2,64,2048]{2,1,0:T(8,128)(2,1)S(1)}, u32[]{:S(2)}, u32[]{:S(2)}) %collective-permute-start.6) | collective-permute-done | bytes 524320 | tf_op jit(solution)/shard_map/ppermute | solution.py:370
  49.4 0.8 copy-done.20
  50.2 0.7 copy-done.37
  50.9 2.7 %shard_map.121.x = bf16[128,1024]{1,0:T(8,128)(2,1)} custom-call(s32[4]{0:T(128)} %get-tuple-element.69.scal.order, bf16[2,128,1024]{2,1,0:T(8,128)(2,1)} %bitcast.104, bf16[2,128,1024]{2,1,0:T(8,128)(2,1)} %copy-done.22, bf16[128,1024]{1,0:T(8,128)(2,1)} %copy-done.37), custom_call_target="tpu_custom_call" | custom-call | flops 120000004096 | bytes 1000000 | tf_op jit(solution)/shard_map/pallas_call | solution.py:191
  53.7 4.7 %shard_map.122 = (bf16[2,128,1024]{2,1,0:T(8,128)(2,1)}, bf16[2,128,1024]{2,1,0:T(8,128)(2,1)}) custom-call(s32[101]{0:T(128)} %concatenate.36.scal, bf16[128,1024]{1,0:T(8,128)(2,1)} %shard_map.121.x, bf16[4,2,256,256]{3,2,1,0:T(8,128)(2,1)} %gt.1, bf16[4,2,256,256]{3,2,1,0:T(8,128)(2,1)} %ut.1, s32[1,512]{1,0:T(1,128)} %bitcast.105), custom_call_target="tpu_custom_call" | custom-call | flops 120000004096 | bytes 4000000 | tf_op jit(solution)/shard_map/pallas_call | solution.py:120
  58.5 1.2 collective-permute-start.9
  59.8 1.3 collective-permute-start.15
  61.5 1.1 fusion.17
  62.6 1.2 collective-permute-start.10
  63.8 10.6 %shard_map.123 = (f32[2,128,2048]{2,1,0:T(8,128)}, f32[2,128,2048]{2,1,0:T(8,128)}) custom-call(s32[4]{0:T(128)} %get-tuple-element.69.scal.order, bf16[4,16,8,2048]{3,2,1,0:T(8,128)(2,1)} %bitcast.86, bf16[4,16,8,2048]{3,2,1,0:T(8,128)(2,1)} %bitcast.87, bf16[4,16,8,2048]{3,2,1,0:T(8,128)(2,1)} %bitcast.88, bf16[4,16,8,2048]{3,2,1,0:T(8,128)(2,1)} %bitcast.89, ...), custom_call_target="tpu_custom_call" | custom-call | flops 4294967296 | bytes 16777216 | tf_op jit(solution)/shard_map/pallas_call | solution.py:165
  74.4 0.9 collective-permute-start.11
  75.3 4.6 %collective-permute-done.10.refs_0_ = bf16[128,1024]{1,0:T(8,128)(2,1)S(1)} collective-permute-done((bf16[128,1024]{1,0:T(8,128)(2,1)S(1)}, bf16[128,1024]{1,0:T(8,128)(2,1)S(1)}, u32[]{:S(2)}, u32[]{:S(2)}) %collective-permute-start.10) | collective-permute-done | bytes 262176 | tf_op jit(solution)/shard_map/ppermute | solution.py:370
  79.9 0.7 copy-done.38
  80.7 2.5 %shard_map.124.refs_1_ = bf16[128,1024]{1,0:T(8,128)(2,1)} custom-call(s32[4]{0:T(128)} %get-tuple-element.69.scal.order, bf16[2,128,1024]{2,1,0:T(8,128)(2,1)} %get-tuple-element.60.keep, bf16[2,128,1024]{2,1,0:T(8,128)(2,1)} %copy-done.23, bf16[128,1024]{1,0:T(8,128)(2,1)} %copy-done.38), custom_call_target="tpu_custom_call" | custom-call | flops 120000004096 | bytes 1000000 | tf_op jit(solution)/shard_map/pallas_call | solution.py:191
  83.7 1.0 add_select_fusion.refs_2_.refs_11_
  84.7 3.2 %shard_map.125 = bf16[64,2048]{1,0:T(8,128)(2,1)} custom-call(f32[2,128,2048]{2,1,0:T(8,128)} %get-tuple-element.47.keep, f32[2,128,2048]{2,1,0:T(8,128)} %collective-permute-done.3.core, bf16[2,64,2048]{2,1,0:T(8,128)(2,1)} %copy-done.20, bf16[128,1024]{1,0:T(8,128)(2,1)} %shard_map.124.refs_1_, s32[512,1]{1,0:T(8,128)} %add_select_fusion.refs_2_.refs_11_, ...), custom_call_target="tpu_custom_call" | custom-call | flops 1000000000 | bytes 3145728 | tf_op jit(solution)/shard_map/pallas_call | solution.py:236
  87.9 1.1 collective-permute-start.14
  89.0 1.7 collective-permute-start.21
  90.6 10.6 %shard_map.126 = (f32[2,128,2048]{2,1,0:T(8,128)}, f32[2,128,2048]{2,1,0:T(8,128)}) custom-call(s32[4]{0:T(128)} %get-tuple-element.69.scal.order, bf16[4,16,8,2048]{3,2,1,0:T(8,128)(2,1)} %bitcast.90, bf16[4,16,8,2048]{3,2,1,0:T(8,128)(2,1)} %bitcast.91, bf16[4,16,8,2048]{3,2,1,0:T(8,128)(2,1)} %bitcast.92, bf16[4,16,8,2048]{3,2,1,0:T(8,128)(2,1)} %bitcast.93, ...), custom_call_target="tpu_custom_call" | custom-call | flops 4294967296 | bytes 16777216 | tf_op jit(solution)/shard_map/pallas_call | solution.py:165
  101.8 1.5 collective-permute-start.22
  103.3 3.4 %shard_map.127 = bf16[64,2048]{1,0:T(8,128)(2,1)} custom-call(f32[2,128,2048]{2,1,0:T(8,128)} %get-tuple-element.55.keep, f32[2,128,2048]{2,1,0:T(8,128)} %copy-done.19, bf16[2,64,2048]{2,1,0:T(8,128)(2,1)} %collective-permute-done.12.refs_0_, bf16[128,1024]{1,0:T(8,128)(2,1)} %shard_map.124.refs_1_, s32[512,1]{1,0:T(8,128)} %add_select_fusion.refs_2_.refs_11_, ...), custom_call_target="tpu_custom_call" | custom-call | flops 120000004096 | bytes 3145728 | tf_op jit(solution)/shard_map/pallas_call | solution.py:236
  107.1 3.3 %shard_map.128 = bf16[64,2048]{1,0:T(8,128)(2,1)} custom-call(f32[2,128,2048]{2,1,0:T(8,128)} %get-tuple-element.65.keep, f32[2,128,2048]{2,1,0:T(8,128)} %copy-done.6, bf16[2,64,2048]{2,1,0:T(8,128)(2,1)} %copy-done.21, bf16[128,1024]{1,0:T(8,128)(2,1)} %shard_map.124.refs_1_, s32[512,1]{1,0:T(8,128)} %add_select_fusion.refs_2_.refs_11_, ...), custom_call_target="tpu_custom_call" | custom-call | flops 1000000000 | bytes 3145728 | tf_op jit(solution)/shard_map/pallas_call | solution.py:236
  110.4 0.8 pad_maximum_fusion.refs_2_
  111.3 3.7 %collective-permute-done.16 = bf16[64,2048]{1,0:T(8,128)(2,1)} collective-permute-done((bf16[64,2048]{1,0:T(8,128)(2,1)}, bf16[64,2048]{1,0:T(8,128)(2,1)}, u32[]{:S(2)}, u32[]{:S(2)}) %collective-permute-start.16) | collective-permute-done | bytes 262176 | tf_op jit(solution)/shard_map/ppermute | solution.py:370
  114.9 0.8 collective-permute-start.18
  115.7 1.9 pad_maximum_fusion.1.refs_3_
  117.7 1.1 fusion
  120.0 0.8 copy-done.12
  122.2 0.8 copy-done.17
  123.0 15.5 %shard_map.129 = f32[256,2048]{1,0:T(8,128)} custom-call(s32[103]{0:T(128)} %concatenate.35.scal, bf16[128,2048]{1,0:T(8,128)(2,1)} %copy-done.17, bf16[128,2048]{1,0:T(8,128)(2,1)} %collective-permute-done.19.refs_1_, bf16[128,2048]{1,0:T(8,128)(2,1)} %pad_maximum_fusion.refs_2_, bf16[128,2048]{1,0:T(8,128)(2,1)} %pad_maximum_fusion.1.refs_3_, ...), custom_call_target="tpu_custom_call" | custom-call | flops 1000000000 | bytes 1000000 | tf_op jit(solution)/shard_map/pallas_call | solution.py:312
  138.5 3.2 %shard_map.130 = bf16[64,2048]{1,0:T(8,128)(2,1)} custom-call(f32[2,128,2048]{2,1,0:T(8,128)} %get-tuple-element.74.keep, f32[2,128,2048]{2,1,0:T(8,128)} %copy-done.4, bf16[2,64,2048]{2,1,0:T(8,128)(2,1)} %collective-permute-done.27.refs_0_, bf16[128,1024]{1,0:T(8,128)(2,1)} %shard_map.124.refs_1_, s32[512,1]{1,0:T(8,128)} %add_select_fusion.refs_2_.refs_11_, ...), custom_call_target="tpu_custom_call" | custom-call | flops 1000000000 | bytes 3145728 | tf_op jit(solution)/shard_map/pallas_call | solution.py:236
  142.3 1.0 pad_maximum_fusion.2.refs_2_
  143.3 2.5 %collective-permute-start.28 = (bf16[128,2048]{1,0:T(8,128)(2,1)S(1)}, bf16[128,2048]{1,0:T(8,128)(2,1)}, u32[]{:S(2)}, u32[]{:S(2)}) collective-permute-start(bf16[128,2048]{1,0:T(8,128)(2,1)S(1)} %pad_maximum_fusion.2.refs_2_), channel_id=1, source_target_pairs={{0,4},{4,0},{8,12},{12,8},{1,5},{5,1},{9,13},{13,9},{2,6},{6,2},{1... | collective-permute-start | bytes 1572872 | tf_op jit(solution)/shard_map/ppermute | solution.py:367
  145.8 2.9 %collective-permute-done.29 = bf16[64,2048]{1,0:T(8,128)(2,1)S(1)} collective-permute-done((bf16[64,2048]{1,0:T(8,128)(2,1)}, bf16[64,2048]{1,0:T(8,128)(2,1)S(1)}, u32[]{:S(2)}, u32[]{:S(2)}) %collective-permute-start.29) | collective-permute-done | bytes 262176 | tf_op jit(solution)/shard_map/ppermute | solution.py:370
  148.6 1.0 pad_maximum_fusion.3.refs_3_
  149.6 2.0 collective-permute-start.30
  151.9 1.8 collective-permute-start.23
  153.7 1.6 collective-permute-start.24
  155.3 1.3 collective-permute-start.25
  156.6 15.5 %shard_map.131 = f32[256,2048]{1,0:T(8,128)} custom-call(s32[103]{0:T(128)} %concatenate.35.scal, bf16[128,2048]{1,0:T(8,128)(2,1)} %collective-permute-done.28.refs_0_, bf16[128,2048]{1,0:T(8,128)(2,1)} %collective-permute-done.30.refs_1_, bf16[128,2048]{1,0:T(8,128)(2,1)} %copy-done.13, bf16[128,2048]{1,0:T(8,128)(2,1)} %copy-done.14, ...), custom_call_target="tpu_custom_call" | custom-call | flops 1000000000 | bytes 1000000 | tf_op jit(solution)/shard_map/pallas_call | solution.py:312
  172.1 1.5 fusion.15
  173.6 0.8 collective-permute-start.31
  174.4 5.5 %collective-permute-start.33 = (bf16[4,16,2048]{2,1,0:T(8,128)(2,1)S(1)}, bf16[4,16,2048]{2,1,0:T(8,128)(2,1)}, u32[]{:S(2)}, u32[]{:S(2)}) collective-permute-start(bf16[4,16,2048]{2,1,0:T(8,128)(2,1)S(1)} %get-tuple-element.87), channel_id=1, source_target_pairs={{0,3},{1,0},{2,1},{3,2},{4,7},{5,4},{6,5},{7,6},{8,11},{9,8},{10,9... | collective-permute-start | bytes 786440 | tf_op jit(solution)/shard_map/ppermute | solution.py:549
  180.6 2.4 %collective-permute-done.31 = bf16[4,16,2048]{2,1,0:T(8,128)(2,1)S(1)} collective-permute-done((bf16[4,16,2048]{2,1,0:T(8,128)(2,1)S(1)}, bf16[4,16,2048]{2,1,0:T(8,128)(2,1)S(1)}, u32[]{:S(2)}, u32[]{:S(2)}) %collective-permute-start.31) | collective-permute-done | bytes 262176 | tf_op jit(solution)/shard_map/ppermute | solution.py:549
  183.0 12.9 %collective-permute-done.32 = bf16[4,16,2048]{2,1,0:T(8,128)(2,1)} collective-permute-done((bf16[4,16,2048]{2,1,0:T(8,128)(2,1)S(1)}, bf16[4,16,2048]{2,1,0:T(8,128)(2,1)}, u32[]{:S(2)}, u32[]{:S(2)}) %collective-permute-start.32) | collective-permute-done | bytes 262176 | tf_op jit(solution)/shard_map/ppermute | solution.py:549
  195.9 5.6 %collective-permute-done.33 = bf16[4,16,2048]{2,1,0:T(8,128)(2,1)} collective-permute-done((bf16[4,16,2048]{2,1,0:T(8,128)(2,1)S(1)}, bf16[4,16,2048]{2,1,0:T(8,128)(2,1)}, u32[]{:S(2)}, u32[]{:S(2)}) %collective-permute-start.33) | collective-permute-done | bytes 262176 | tf_op jit(solution)/shard_map/ppermute | solution.py:549
  201.5 1.3 fusion.6
  203.5 0.8 pad_maximum_fusion.4
  (141 shorter events, 10.4 us)
Async XLA Ops:
  0.7 17.3 %collective-permute-start = (s32[4,6]{0,1:T(8,128)S(1)}, s32[4,6]{0,1:T(8,128)S(1)}, u32[]{:S(2)}, u32[]{:S(2)}) collective-permute-start(s32[4,6]{0,1:T(8,128)S(1)} %pad_add_fusion), channel_id=1, source_target_pairs={{0,12},{4,0},{8,4},{12,8},{1,13},{5,1},{9,5},{13,9},{2,14},{6,2},{... | collective-permute-start | bytes 296 | tf_op jit(solution)/shard_map/ppermute | solution.py:398
  1.4 16.8 %collective-permute-start.1 = (s32[4,6]{0,1:T(8,128)S(1)}, s32[4,6]{0,1:T(8,128)S(1)}, u32[]{:S(2)}, u32[]{:S(2)}) collective-permute-start(s32[4,6]{0,1:T(8,128)S(1)} %pad_add_fusion), channel_id=1, source_target_pairs={{0,8},{4,12},{8,0},{12,4},{1,9},{5,13},{9,1},{13,5},{2,10},{6,14},... | collective-permute-start | bytes 296 | tf_op jit(solution)/shard_map/ppermute | solution.py:398
  1.4 17.0 %collective-permute-start.2 = (s32[4,6]{0,1:T(8,128)S(1)}, s32[4,6]{0,1:T(8,128)S(1)}, u32[]{:S(2)}, u32[]{:S(2)}) collective-permute-start(s32[4,6]{0,1:T(8,128)S(1)} %pad_add_fusion), channel_id=1, source_target_pairs={{0,4},{4,8},{8,12},{12,0},{1,5},{5,9},{9,13},{13,1},{2,6},{6,10},{... | collective-permute-start | bytes 296 | tf_op jit(solution)/shard_map/ppermute | solution.py:398
  4.2 15.1 %collective-permute-start.4 = (bf16[4,256,256]{2,1,0:T(8,128)(2,1)S(1)}, bf16[4,256,256]{2,1,0:T(8,128)(2,1)S(1)}, u32[]{:S(2)}, u32[]{:S(2)}) collective-permute-start(bf16[4,256,256]{2,1,0:T(8,128)(2,1)S(1)} %constant_dynamic-slice_fusion), channel_id=1, source_target_pairs={{0,8},{4,12},{8,0},{12,4},{1,9},{5,13},{9,1},{13,5},{2,10},{6,14},... | collective-permute-start | bytes 1572872 | tf_op jit(solution)/shard_map/ppermute | solution.py:370
  6.1 11.0 %copy-start.35 = (s32[512]{0:T(512)S(1)}, s32[512]{0:T(512)}, u32[]{:S(2)}) copy-start(s32[512]{0:T(512)} %param.24) | copy-start | bytes 6148
  6.1 11.0 %copy-start.36 = (s32[16]{0:T(128)S(1)}, s32[16]{0:T(128)}, u32[]{:S(2)}) copy-start(s32[16]{0:T(128)} %param.25) | copy-start | bytes 196
  16.8 14.2 %collective-permute-start.3 = (f32[2,128,2048]{2,1,0:T(8,128)}, f32[2,128,2048]{2,1,0:T(8,128)}, u32[]{:S(2)}, u32[]{:S(2)}) collective-permute-start(f32[2,128,2048]{2,1,0:T(8,128)} %get-tuple-element.48), channel_id=1, source_target_pairs={{0,4},{4,0},{8,12},{12,8},{1,5},{5,1},{9,13},{13,9},{2,6},{6,2},{1... | collective-permute-start | bytes 6291464 | tf_op jit(solution)/shard_map/ppermute | solution.py:367
  17.1 2.2 %copy-start.26 = (s32[24]{0:T(128)}, s32[24]{0:T(128)S(1)}, u32[]{:S(2)}) copy-start(s32[24]{0:T(128)S(1)} %reshape.233) | copy-start | bytes 292
  17.2 2.9 %copy-start.25 = (s32[512]{0:T(512)}, s32[512]{0:T(512)S(1)}, u32[]{:S(2)}) copy-start(s32[512]{0:T(512)S(1)} %select_reduce_fusion.1) | copy-start | bytes 6148
  18.2 1.1 copy-start.28
  20.1 10.9 %copy-start.2 = (f32[2,128,2048]{2,1,0:T(8,128)S(1)}, f32[2,128,2048]{2,1,0:T(8,128)}, u32[]{:S(2)}) copy-start(f32[2,128,2048]{2,1,0:T(8,128)} %get-tuple-element.47.keep) | copy-start | bytes 6291460
  27.2 2.2 %collective-permute-start.5 = (bf16[2,128,1024]{2,1,0:T(8,128)(2,1)}, bf16[2,128,1024]{2,1,0:T(8,128)(2,1)S(1)}, u32[]{:S(2)}, u32[]{:S(2)}) collective-permute-start(bf16[2,128,1024]{2,1,0:T(8,128)(2,1)} %bitcast.110), channel_id=1, source_target_pairs={{0,4},{4,0},{8,12},{12,8},{1,5},{5,1},{9,13},{13,9},{2,6},{6,2},{1... | collective-permute-start | bytes 1572872 | tf_op jit(solution)/shard_map/ppermute | solution.py:367
  29.4 14.7 %copy-start.22 = (bf16[2,128,1024]{2,1,0:T(8,128)(2,1)}, bf16[2,128,1024]{2,1,0:T(8,128)(2,1)S(1)}, u32[]{:S(2)}) copy-start(bf16[2,128,1024]{2,1,0:T(8,128)(2,1)S(1)} %collective-permute-done.5.core) | copy-start | bytes 1572868
  30.6 18.8 %collective-permute-start.7 = (bf16[128,1024]{1,0:T(8,128)(2,1)S(1)}, bf16[128,1024]{1,0:T(8,128)(2,1)S(1)}, u32[]{:S(2)}, u32[]{:S(2)}) collective-permute-start(bf16[128,1024]{1,0:T(8,128)(2,1)S(1)} %fusion.18), channel_id=1, source_target_pairs={{0,8},{4,12},{8,0},{12,4},{1,9},{5,13},{9,1},{13,5},{2,10},{6,14},... | collective-permute-start | bytes 786440 | tf_op jit(solution)/shard_map/ppermute | solution.py:370
  32.3 12.8 %copy-start.34 = (s32[1,512]{1,0:T(1,128)S(1)}, s32[1,512]{1,0:T(1,128)}, u32[]{:S(2)}) copy-start(s32[1,512]{1,0:T(1,128)} %get-tuple-element.59) | copy-start | bytes 6148
  32.4 17.1 %collective-permute-start.6 = (bf16[2,64,2048]{2,1,0:T(8,128)(2,1)S(1)}, bf16[2,64,2048]{2,1,0:T(8,128)(2,1)S(1)}, u32[]{:S(2)}, u32[]{:S(2)}) collective-permute-start(bf16[2,64,2048]{2,1,0:T(8,128)(2,1)S(1)} %fusion.3), channel_id=1, source_target_pairs={{0,8},{4,12},{8,0},{12,4},{1,9},{5,13},{9,1},{13,5},{2,10},{6,14},... | collective-permute-start | bytes 1572872 | tf_op jit(solution)/shard_map/ppermute | solution.py:370
  44.2 9.4 %collective-permute-start.8 = (f32[2,128,2048]{2,1,0:T(8,128)}, f32[2,128,2048]{2,1,0:T(8,128)S(1)}, u32[]{:S(2)}, u32[]{:S(2)}) collective-permute-start(f32[2,128,2048]{2,1,0:T(8,128)} %get-tuple-element.56), channel_id=1, source_target_pairs={{0,4},{4,0},{8,12},{12,8},{1,5},{5,1},{9,13},{13,9},{2,6},{6,2},{1... | collective-permute-start | bytes 6291464 | tf_op jit(solution)/shard_map/ppermute | solution.py:367
  50.9 2.7 %copy-start.18 = (f32[2,128,2048]{2,1,0:T(8,128)S(1)}, f32[2,128,2048]{2,1,0:T(8,128)}, u32[]{:S(2)}) copy-start(f32[2,128,2048]{2,1,0:T(8,128)} %get-tuple-element.55.keep) | copy-start | bytes 6291460
  53.6 4.8 %copy-start.19 = (f32[2,128,2048]{2,1,0:T(8,128)}, f32[2,128,2048]{2,1,0:T(8,128)S(1)}, u32[]{:S(2)}) copy-start(f32[2,128,2048]{2,1,0:T(8,128)S(1)} %collective-permute-done.8.core) | copy-start | bytes 6291460
  53.7 5.9 %copy-start.24 = (s32[512]{0:T(512)S(1)}, s32[512]{0:T(512)}, u32[]{:S(2)}) copy-start(s32[512]{0:T(512)} %select_reduce_fusion) | copy-start | bytes 6148
  53.7 6.1 %copy-start.8 = (bf16[4,256,256]{2,1,0:T(8,128)(2,1)S(1)}, bf16[4,256,256]{2,1,0:T(8,128)(2,1)}, u32[]{:S(2)}) copy-start(bf16[4,256,256]{2,1,0:T(8,128)(2,1)} %copy-done.7) | copy-start | bytes 1572868
  58.5 3.0 %collective-permute-start.9 = (bf16[2,128,1024]{2,1,0:T(8,128)(2,1)}, bf16[2,128,1024]{2,1,0:T(8,128)(2,1)S(1)}, u32[]{:S(2)}, u32[]{:S(2)}) collective-permute-start(bf16[2,128,1024]{2,1,0:T(8,128)(2,1)} %get-tuple-element.61), channel_id=1, source_target_pairs={{0,4},{4,0},{8,12},{12,8},{1,5},{5,1},{9,13},{13,9},{2,6},{6,2},{1... | collective-permute-start | bytes 1572872 | tf_op jit(solution)/shard_map/ppermute | solution.py:367
  59.8 29.1 %collective-permute-start.15 = (bf16[4,256,256]{2,1,0:T(8,128)(2,1)S(1)}, bf16[4,256,256]{2,1,0:T(8,128)(2,1)S(1)}, u32[]{:S(2)}, u32[]{:S(2)}) collective-permute-start(bf16[4,256,256]{2,1,0:T(8,128)(2,1)S(1)} %copy-done.8), channel_id=1, source_target_pairs={{0,16},{16,0},{1,17},{17,1},{2,18},{18,2},{3,19},{19,3},{4,20},{20... | collective-permute-start | bytes 1572872 | tf_op jit(solution)/shard_map/ppermute | solution.py:475
  61.1 29.5 %collective-permute-start.12 = (bf16[2,64,2048]{2,1,0:T(8,128)(2,1)S(1)}, bf16[2,64,2048]{2,1,0:T(8,128)(2,1)}, u32[]{:S(2)}, u32[]{:S(2)}) collective-permute-start(bf16[2,64,2048]{2,1,0:T(8,128)(2,1)S(1)} %fusion.2), channel_id=1, source_target_pairs={{0,8},{4,12},{8,0},{12,4},{1,9},{5,13},{9,1},{13,5},{2,10},{6,14},... | collective-permute-start | bytes 1572872 | tf_op jit(solution)/shard_map/ppermute | solution.py:370
  61.5 13.0 %copy-start.23 = (bf16[2,128,1024]{2,1,0:T(8,128)(2,1)}, bf16[2,128,1024]{2,1,0:T(8,128)(2,1)S(1)}, u32[]{:S(2)}) copy-start(bf16[2,128,1024]{2,1,0:T(8,128)(2,1)S(1)} %collective-permute-done.9.core) | copy-start | bytes 1572868
  62.6 17.3 %collective-permute-start.10 = (bf16[128,1024]{1,0:T(8,128)(2,1)S(1)}, bf16[128,1024]{1,0:T(8,128)(2,1)S(1)}, u32[]{:S(2)}, u32[]{:S(2)}) collective-permute-start(bf16[128,1024]{1,0:T(8,128)(2,1)S(1)} %fusion.17), channel_id=1, source_target_pairs={{0,8},{4,12},{8,0},{12,4},{1,9},{5,13},{9,1},{13,5},{2,10},{6,14},... | collective-permute-start | bytes 786440 | tf_op jit(solution)/shard_map/ppermute | solution.py:370
  74.4 8.8 %copy-start.5 = (f32[2,128,2048]{2,1,0:T(8,128)S(1)}, f32[2,128,2048]{2,1,0:T(8,128)}, u32[]{:S(2)}) copy-start(f32[2,128,2048]{2,1,0:T(8,128)} %get-tuple-element.65.keep) | copy-start | bytes 6291460
  74.4 8.7 %collective-permute-start.11 = (f32[2,128,2048]{2,1,0:T(8,128)}, f32[2,128,2048]{2,1,0:T(8,128)S(1)}, u32[]{:S(2)}, u32[]{:S(2)}) collective-permute-start(f32[2,128,2048]{2,1,0:T(8,128)} %get-tuple-element.66), channel_id=1, source_target_pairs={{0,4},{4,0},{8,12},{12,8},{1,5},{5,1},{9,13},{13,9},{2,6},{6,2},{1... | collective-permute-start | bytes 6291464 | tf_op jit(solution)/shard_map/ppermute | solution.py:367
  83.2 4.7 %copy-start.6 = (f32[2,128,2048]{2,1,0:T(8,128)}, f32[2,128,2048]{2,1,0:T(8,128)S(1)}, u32[]{:S(2)}) copy-start(f32[2,128,2048]{2,1,0:T(8,128)S(1)} %collective-permute-done.11.core) | copy-start | bytes 6291460
  83.3 20.0 %collective-permute-start.13 = (bf16[2,64,2048]{2,1,0:T(8,128)(2,1)S(1)}, bf16[2,64,2048]{2,1,0:T(8,128)(2,1)S(1)}, u32[]{:S(2)}, u32[]{:S(2)}) collective-permute-start(bf16[2,64,2048]{2,1,0:T(8,128)(2,1)S(1)} %fusion.1), channel_id=1, source_target_pairs={{0,8},{4,12},{8,0},{12,4},{1,9},{5,13},{9,1},{13,5},{2,10},{6,14},... | collective-permute-start | bytes 1572872 | tf_op jit(solution)/shard_map/ppermute | solution.py:370
  87.9 13.5 %copy-start.9 = (bf16[4,256,256]{2,1,0:T(8,128)(2,1)S(1)}, bf16[4,256,256]{2,1,0:T(8,128)(2,1)}, u32[]{:S(2)}) copy-start(bf16[4,256,256]{2,1,0:T(8,128)(2,1)} %copy-done.7) | copy-start | bytes 1572868
  87.9 14.0 %copy-start = (bf16[4,2,256,256]{3,2,1,0:T(8,128)(2,1)S(1)}, bf16[4,2,256,256]{3,2,1,0:T(8,128)(2,1)}, u32[]{:S(2)}) copy-start(bf16[4,2,256,256]{3,2,1,0:T(8,128)(2,1)} %param.20) | copy-start | bytes 3145732
  87.9 14.0 %collective-permute-start.14 = (bf16[64,2048]{1,0:T(8,128)(2,1)}, bf16[64,2048]{1,0:T(8,128)(2,1)S(1)}, u32[]{:S(2)}, u32[]{:S(2)}) collective-permute-start(bf16[64,2048]{1,0:T(8,128)(2,1)} %shard_map.125), channel_id=1, source_target_pairs={{0,8},{4,12},{8,0},{12,4},{1,9},{5,13},{9,1},{13,5},{2,10},{6,14},... | collective-permute-start | bytes 786440 | tf_op jit(solution)/shard_map/ppermute | solution.py:370
  89.0 12.3 %copy-start.10 = (bf16[4,256,256]{2,1,0:T(8,128)(2,1)}, bf16[4,256,256]{2,1,0:T(8,128)(2,1)S(1)}, u32[]{:S(2)}) copy-start(bf16[4,256,256]{2,1,0:T(8,128)(2,1)S(1)} %collective-permute-done.15.refs_6_) | copy-start | bytes 1572868
  89.0 30.2 %collective-permute-start.21 = (bf16[4,256,256]{2,1,0:T(8,128)(2,1)S(1)}, bf16[4,256,256]{2,1,0:T(8,128)(2,1)S(1)}, u32[]{:S(2)}, u32[]{:S(2)}) collective-permute-start(bf16[4,256,256]{2,1,0:T(8,128)(2,1)S(1)} %collective-permute-done.15.refs_6_), channel_id=1, source_target_pairs={{0,4},{4,0},{8,12},{12,8},{1,5},{5,1},{9,13},{13,9},{2,6},{6,2},{1... | collective-permute-start | bytes 1572872 | tf_op jit(solution)/shard_map/ppermute | solution.py:367
  101.3 16.4 %collective-permute-start.17 = (f32[2,128,2048]{2,1,0:T(8,128)}, f32[2,128,2048]{2,1,0:T(8,128)S(1)}, u32[]{:S(2)}, u32[]{:S(2)}) collective-permute-start(f32[2,128,2048]{2,1,0:T(8,128)} %get-tuple-element.75), channel_id=1, source_target_pairs={{0,4},{4,0},{8,12},{12,8},{1,5},{5,1},{9,13},{13,9},{2,6},{6,2},{1... | collective-permute-start | bytes 6291464 | tf_op jit(solution)/shard_map/ppermute | solution.py:367
  101.3 18.2 %collective-permute-start.20 = (bf16[4,256,256]{2,1,0:T(8,128)(2,1)S(1)}, bf16[4,256,256]{2,1,0:T(8,128)(2,1)S(1)}, u32[]{:S(2)}, u32[]{:S(2)}) collective-permute-start(bf16[4,256,256]{2,1,0:T(8,128)(2,1)S(1)} %copy-done.9), channel_id=1, source_target_pairs={{0,4},{4,0},{8,12},{12,8},{1,5},{5,1},{9,13},{13,9},{2,6},{6,2},{1... | collective-permute-start | bytes 1572872 | tf_op jit(solution)/shard_map/ppermute | solution.py:367
  101.8 20.3 %collective-permute-start.22 = (bf16[8,256,256]{2,1,0:T(8,128)(2,1)S(1)}, bf16[8,256,256]{2,1,0:T(8,128)(2,1)}, u32[]{:S(2)}, u32[]{:S(2)}) collective-permute-start(bf16[8,256,256]{2,1,0:T(8,128)(2,1)S(1)} %bitcast.97), channel_id=1, source_target_pairs={{0,4},{4,0},{8,12},{12,8},{1,5},{5,1},{9,13},{13,9},{2,6},{6,2},{1... | collective-permute-start | bytes 3145736 | tf_op jit(solution)/shard_map/ppermute | solution.py:367
  103.3 3.4 %copy-start.21 = (bf16[2,64,2048]{2,1,0:T(8,128)(2,1)}, bf16[2,64,2048]{2,1,0:T(8,128)(2,1)S(1)}, u32[]{:S(2)}) copy-start(bf16[2,64,2048]{2,1,0:T(8,128)(2,1)S(1)} %collective-permute-done.13.refs_0_) | copy-start | bytes 1572868
  106.7 3.7 %copy-start.16 = (bf16[64,2048]{1,0:T(8,128)(2,1)S(1)}, bf16[64,2048]{1,0:T(8,128)(2,1)}, u32[]{:S(2)}) copy-start(bf16[64,2048]{1,0:T(8,128)(2,1)} %shard_map.125) | copy-start | bytes 786436
  106.7 8.2 %collective-permute-start.16 = (bf16[64,2048]{1,0:T(8,128)(2,1)}, bf16[64,2048]{1,0:T(8,128)(2,1)}, u32[]{:S(2)}, u32[]{:S(2)}) collective-permute-start(bf16[64,2048]{1,0:T(8,128)(2,1)} %shard_map.127), channel_id=1, source_target_pairs={{0,8},{4,12},{8,0},{12,4},{1,9},{5,13},{9,1},{13,5},{2,10},{6,14},... | collective-permute-start | bytes 786440 | tf_op jit(solution)/shard_map/ppermute | solution.py:370
  107.1 10.6 %copy-start.3 = (f32[2,128,2048]{2,1,0:T(8,128)S(1)}, f32[2,128,2048]{2,1,0:T(8,128)}, u32[]{:S(2)}) copy-start(f32[2,128,2048]{2,1,0:T(8,128)} %get-tuple-element.74.keep) | copy-start | bytes 6291460
  110.4 10.4 %copy-start.15 = (bf16[64,2048]{1,0:T(8,128)(2,1)S(1)}, bf16[64,2048]{1,0:T(8,128)(2,1)}, u32[]{:S(2)}) copy-start(bf16[64,2048]{1,0:T(8,128)(2,1)} %shard_map.128) | copy-start | bytes 786436
  111.2 10.2 %copy-start.27 = (s32[24]{0:T(128)S(1)}, s32[24]{0:T(128)}, u32[]{:S(2)}) copy-start(s32[24]{0:T(128)} %copy-done.26) | copy-start | bytes 292
  111.2 10.2 %copy-start.29 = (s32[24]{0:T(128)S(1)}, s32[24]{0:T(128)}, u32[]{:S(2)}) copy-start(s32[24]{0:T(128)} %copy-done.28) | copy-start | bytes 292
  111.2 10.2 %copy-start.31 = (s32[24]{0:T(128)S(1)}, s32[24]{0:T(128)}, u32[]{:S(2)}) copy-start(s32[24]{0:T(128)} %copy-done.30) | copy-start | bytes 292
  111.2 10.2 %copy-start.33 = (s32[24]{0:T(128)S(1)}, s32[24]{0:T(128)}, u32[]{:S(2)}) copy-start(s32[24]{0:T(128)} %copy-done.32) | copy-start | bytes 292
  114.9 7.2 %collective-permute-start.18 = (bf16[128,2048]{1,0:T(8,128)(2,1)}, bf16[128,2048]{1,0:T(8,128)(2,1)S(1)}, u32[]{:S(2)}, u32[]{:S(2)}) collective-permute-start(bf16[128,2048]{1,0:T(8,128)(2,1)} %pad_maximum_fusion.refs_2_), channel_id=1, source_target_pairs={{0,4},{4,0},{8,12},{12,8},{1,5},{5,1},{9,13},{13,9},{2,6},{6,2},{1... | collective-permute-start | bytes 1572872 | tf_op jit(solution)/shard_map/ppermute | solution.py:367
  117.6 1.5 copy-start.4
  117.6 4.5 %collective-permute-start.19 = (bf16[128,2048]{1,0:T(8,128)(2,1)}, bf16[128,2048]{1,0:T(8,128)(2,1)}, u32[]{:S(2)}, u32[]{:S(2)}) collective-permute-start(bf16[128,2048]{1,0:T(8,128)(2,1)} %pad_maximum_fusion.1.refs_3_), channel_id=1, source_target_pairs={{0,4},{4,0},{8,12},{12,8},{1,5},{5,1},{9,13},{13,9},{2,6},{6,2},{1... | collective-permute-start | bytes 1572872 | tf_op jit(solution)/shard_map/ppermute | solution.py:367
  119.2 19.3 %collective-permute-start.27 = (bf16[2,64,2048]{2,1,0:T(8,128)(2,1)}, bf16[2,64,2048]{2,1,0:T(8,128)(2,1)}, u32[]{:S(2)}, u32[]{:S(2)}) collective-permute-start(bf16[2,64,2048]{2,1,0:T(8,128)(2,1)} %fusion), channel_id=1, source_target_pairs={{0,8},{4,12},{8,0},{12,4},{1,9},{5,13},{9,1},{13,5},{2,10},{6,14},... | collective-permute-start | bytes 1572872 | tf_op jit(solution)/shard_map/ppermute | solution.py:370
  120.8 21.5 %collective-permute-start.26 = (bf16[64,2048]{1,0:T(8,128)(2,1)S(1)}, bf16[64,2048]{1,0:T(8,128)(2,1)}, u32[]{:S(2)}, u32[]{:S(2)}) collective-permute-start(bf16[64,2048]{1,0:T(8,128)(2,1)S(1)} %copy-done.15), channel_id=1, source_target_pairs={{0,8},{4,12},{8,0},{12,4},{1,9},{5,13},{9,1},{13,5},{2,10},{6,14},... | collective-permute-start | bytes 786440 | tf_op jit(solution)/shard_map/ppermute | solution.py:370
  141.7 10.1 %copy-start.1 = (f32[256,2048]{1,0:T(8,128)S(1)}, f32[256,2048]{1,0:T(8,128)}, u32[]{:S(2)}) copy-start(f32[256,2048]{1,0:T(8,128)} %shard_map.129) | copy-start | bytes 6291460
  141.7 7.0 %collective-permute-start.29 = (bf16[64,2048]{1,0:T(8,128)(2,1)}, bf16[64,2048]{1,0:T(8,128)(2,1)S(1)}, u32[]{:S(2)}, u32[]{:S(2)}) collective-permute-start(bf16[64,2048]{1,0:T(8,128)(2,1)} %shard_map.130), channel_id=1, source_target_pairs={{0,8},{4,12},{8,0},{12,4},{1,9},{5,13},{9,1},{13,5},{2,10},{6,14},... | collective-permute-start | bytes 786440 | tf_op jit(solution)/shard_map/ppermute | solution.py:370
  143.3 13.3 %copy-start.13 = (bf16[128,2048]{1,0:T(8,128)(2,1)}, bf16[128,2048]{1,0:T(8,128)(2,1)S(1)}, u32[]{:S(2)}) copy-start(bf16[128,2048]{1,0:T(8,128)(2,1)S(1)} %pad_maximum_fusion.2.refs_2_) | copy-start | bytes 1572868
  143.3 13.3 %collective-permute-start.28 = (bf16[128,2048]{1,0:T(8,128)(2,1)S(1)}, bf16[128,2048]{1,0:T(8,128)(2,1)}, u32[]{:S(2)}, u32[]{:S(2)}) collective-permute-start(bf16[128,2048]{1,0:T(8,128)(2,1)S(1)} %pad_maximum_fusion.2.refs_2_), channel_id=1, source_target_pairs={{0,4},{4,0},{8,12},{12,8},{1,5},{5,1},{9,13},{13,9},{2,6},{6,2},{1... | collective-permute-start | bytes 1572872 | tf_op jit(solution)/shard_map/ppermute | solution.py:367
  149.6 7.0 %copy-start.14 = (bf16[128,2048]{1,0:T(8,128)(2,1)}, bf16[128,2048]{1,0:T(8,128)(2,1)S(1)}, u32[]{:S(2)}) copy-start(bf16[128,2048]{1,0:T(8,128)(2,1)S(1)} %pad_maximum_fusion.3.refs_3_) | copy-start | bytes 1572868
  149.6 7.0 %collective-permute-start.30 = (bf16[128,2048]{1,0:T(8,128)(2,1)S(1)}, bf16[128,2048]{1,0:T(8,128)(2,1)}, u32[]{:S(2)}, u32[]{:S(2)}) collective-permute-start(bf16[128,2048]{1,0:T(8,128)(2,1)S(1)} %pad_maximum_fusion.3.refs_3_), channel_id=1, source_target_pairs={{0,4},{4,0},{8,12},{12,8},{1,5},{5,1},{9,13},{13,9},{2,6},{6,2},{1... | collective-permute-start | bytes 1572872 | tf_op jit(solution)/shard_map/ppermute | solution.py:367
  151.9 21.7 %collective-permute-start.23 = (bf16[4,16,2048]{2,1,0:T(8,128)(2,1)S(1)}, bf16[4,16,2048]{2,1,0:T(8,128)(2,1)S(1)}, u32[]{:S(2)}, u32[]{:S(2)}) collective-permute-start(bf16[4,16,2048]{2,1,0:T(8,128)(2,1)S(1)} %get-tuple-element.92), channel_id=1, source_target_pairs={{0,1},{1,2},{2,3},{3,0},{4,5},{5,6},{6,7},{7,4},{8,9},{9,10},{10,1... | collective-permute-start | bytes 786440 | tf_op jit(solution)/shard_map/ppermute | solution.py:549
  153.7 20.7 %collective-permute-start.24 = (bf16[4,16,2048]{2,1,0:T(8,128)(2,1)S(1)}, bf16[4,16,2048]{2,1,0:T(8,128)(2,1)S(1)}, u32[]{:S(2)}, u32[]{:S(2)}) collective-permute-start(bf16[4,16,2048]{2,1,0:T(8,128)(2,1)S(1)} %get-tuple-element.94), channel_id=1, source_target_pairs={{0,2},{1,3},{2,0},{3,1},{4,6},{5,7},{6,4},{7,5},{8,10},{9,11},{10,... | collective-permute-start | bytes 786440 | tf_op jit(solution)/shard_map/ppermute | solution.py:549
  155.3 19.1 %collective-permute-start.25 = (bf16[4,16,2048]{2,1,0:T(8,128)(2,1)S(1)}, bf16[4,16,2048]{2,1,0:T(8,128)(2,1)S(1)}, u32[]{:S(2)}, u32[]{:S(2)}) collective-permute-start(bf16[4,16,2048]{2,1,0:T(8,128)(2,1)S(1)} %get-tuple-element.93), channel_id=1, source_target_pairs={{0,3},{1,0},{2,1},{3,2},{4,7},{5,4},{6,5},{7,6},{8,11},{9,8},{10,9... | collective-permute-start | bytes 786440 | tf_op jit(solution)/shard_map/ppermute | solution.py:549
  173.6 9.3 %collective-permute-start.31 = (bf16[4,16,2048]{2,1,0:T(8,128)(2,1)S(1)}, bf16[4,16,2048]{2,1,0:T(8,128)(2,1)S(1)}, u32[]{:S(2)}, u32[]{:S(2)}) collective-permute-start(bf16[4,16,2048]{2,1,0:T(8,128)(2,1)S(1)} %get-tuple-element.85), channel_id=1, source_target_pairs={{0,1},{1,2},{2,3},{3,0},{4,5},{5,6},{6,7},{7,4},{8,9},{9,10},{10,1... | collective-permute-start | bytes 786440 | tf_op jit(solution)/shard_map/ppermute | solution.py:549
  174.4 21.5 %collective-permute-start.32 = (bf16[4,16,2048]{2,1,0:T(8,128)(2,1)S(1)}, bf16[4,16,2048]{2,1,0:T(8,128)(2,1)}, u32[]{:S(2)}, u32[]{:S(2)}) collective-permute-start(bf16[4,16,2048]{2,1,0:T(8,128)(2,1)S(1)} %get-tuple-element.86), channel_id=1, source_target_pairs={{0,2},{1,3},{2,0},{3,1},{4,6},{5,7},{6,4},{7,5},{8,10},{9,11},{10,... | collective-permute-start | bytes 786440 | tf_op jit(solution)/shard_map/ppermute | solution.py:549
  174.4 27.0 %collective-permute-start.33 = (bf16[4,16,2048]{2,1,0:T(8,128)(2,1)S(1)}, bf16[4,16,2048]{2,1,0:T(8,128)(2,1)}, u32[]{:S(2)}, u32[]{:S(2)}) collective-permute-start(bf16[4,16,2048]{2,1,0:T(8,128)(2,1)S(1)} %get-tuple-element.87), channel_id=1, source_target_pairs={{0,3},{1,0},{2,1},{3,2},{4,7},{5,4},{6,5},{7,6},{8,11},{9,8},{10,9... | collective-permute-start | bytes 786440 | tf_op jit(solution)/shard_map/ppermute | solution.py:549
  (9 other events, 7.1 us)

commit v9 on v8

--- a/solution.py
+++ b/solution.py
@@ -244,51 +244,80 @@
     )(keep, core, *gots, delta, slot, table)
 
 
-def down_body(width_tiles, here, plan, owners, per_owner, per_slot, start, scal, *refs):
+def hits_body(width_tiles, here, across, plan, counts, owners, per_owner, per_slot, scal, listed):
+    stride = 3 * per_slot
+    patterns = scal.shape[0] - owners * per_owner * stride
+    last = listed.shape[1] - 1
+    steps = here // across
+    me = scal[0]
+    for r, (base, run) in enumerate(plan):
+        for at in range(steps):
+            listed[r * steps + at, last] = 0
+
+        def one(i, carry):
+            local = i // per_slot
+            which = scal[base + local // run] + local % run
+            back = (which // per_owner - me + owners) % owners
+            row = back * per_owner + which % per_owner
+            place = scal[patterns + row * stride + 2 * per_slot + i % per_slot]
+            block = place % width_tiles - me * here
+
+            @pl.when((block >= 0) & (block < here))
+            def _():
+                entry = r * steps + block // across
+                n = listed[entry, last]
+                listed[entry, 4 * n] = i
+                listed[entry, 4 * n + 1] = which
+                listed[entry, 4 * n + 2] = place // width_tiles
+                listed[entry, 4 * n + 3] = block % across
+                listed[entry, last] = n + 1
+
+            return carry
+
+        lax.fori_loop(0, counts[r], one, 0)
+
+
+def hits(scal, width, width_tiles, plan, counts, owners, per_owner, per_slot):
+    block = min(512, width)
+    shape = (len(plan) * (width // block), 4 * max(counts) + 1)
+    return pl.pallas_call(
+        functools.partial(
+            hits_body, width_tiles, width // 256, block // 256, plan, counts, owners, per_owner, per_slot
+        ),
+        in_specs=[pl.BlockSpec(memory_space=pltpu.SMEM)],
+        out_specs=pl.BlockSpec(memory_space=pltpu.SMEM),
+        out_shape=jax.ShapeDtypeStruct(shape, jnp.int32),
+        cost_estimate=cost(1e6, 1e4),
+    )(scal)
+
+
+def down_body(arrays, steps, skip, start, listed, *refs):
     fars, nears, (w, *refs) = refs[:PARTS], refs[PARTS : 2 * PARTS], refs[2 * PARTS :]
-    tiles, (slot, out, hid, listed, number) = refs[: len(plan)], refs[len(plan) :]
+    sources, (slot, out, hid, *refs) = refs[:arrays], refs[arrays:]
+    tiles, arrived = refs[:arrays], refs[arrays]
     tile = 256
-    across = out.shape[1] // tile
     step = pl.program_id(0)
     half, wide = fars[0].shape
-    stride = 3 * per_slot
-    patterns = scal.shape[0] - owners * per_owner * stride
+    last = listed.shape[1] - 1
+    copies = [pltpu.make_async_copy(sources[r], tiles[r], arrived.at[r]) for r in range(arrays)]
 
     @pl.when(step == 0)
     def _():
+        for copy in copies:
+            copy.start()
         for p in range(PARTS):
             hid[:half, p * wide : (p + 1) * wide] = fars[p][...]
             hid[half:, p * wide : (p + 1) * wide] = nears[p][...]
-        me = scal[0]
-        for r, (base, run) in enumerate(plan):
-            for at in range(number.shape[1]):
-                number[r, at] = 0
-
-            def one(i, carry):
-                local = i // per_slot
-                which = scal[base + local // run] + local % run
-                back = (which // per_owner - me + owners) % owners
-                row = back * per_owner + which % per_owner
-                place = scal[patterns + row * stride + 2 * per_slot + i % per_slot]
-                block = place % width_tiles - me * here
-
-                @pl.when((block >= 0) & (block < here))
-                def _():
-                    at = block // across
-                    n = number[r, at]
-                    listed[r * number.shape[1] + at, 4 * n] = i
-                    listed[r * number.shape[1] + at, 4 * n + 1] = which
-                    listed[r * number.shape[1] + at, 4 * n + 2] = place // width_tiles
-                    listed[r * number.shape[1] + at, 4 * n + 3] = block % across
-                    number[r, at] = n + 1
-
-                return carry
-
-            lax.fori_loop(0, tiles[r].shape[0], one, 0)
 
     out[...] = jnp.dot(hid[...], w[...], preferred_element_type=F32)
-    for r in range(len(plan)):
-        entry = r * number.shape[1] + step
+
+    @pl.when(step == 0)
+    def _():
+        for copy in copies:
+            copy.wait()
+
+    for r in range(arrays):
+        entry = r * steps + skip + step
 
         def add(n, carry):
             i = listed[entry, 4 * n]
@@ -300,37 +329,37 @@
             out[:, cols] = out[:, cols] + jnp.dot(picked, tiles[r][i], preferred_element_type=F32)
             return carry
 
-        lax.fori_loop(0, number[r, step], add, 0)
-
-
-def down(scal, fars, nears, w, tiles, plan, slot, width_tiles, owners, per_owner, per_slot, start, flops):
+        lax.fori_loop(0, listed[entry, last], add, 0)
+
+
+def down(listed, fars, nears, w, tiles, slot, start, parts, part):
     rows, depth = 2 * fars[0].shape[0], w.shape[0]
-    width = w.shape[1]
-    block = min(512, width)
-    steps = width // block
-    most = max(t.shape[0] for t in tiles)
+    block = min(512, w.shape[1])
+    steps = w.shape[1] // block
+    here = steps // parts
+    skip = part * here
     return pl.pallas_call(
-        functools.partial(down_body, width_tiles, width // 256, plan, owners, per_owner, per_slot, start),
+        functools.partial(down_body, len(tiles), steps, skip, start),
         grid_spec=pltpu.PrefetchScalarGridSpec(
             num_scalar_prefetch=1,
-            grid=(steps,),
+            grid=(here,),
             in_specs=[
                 *[whole(f.shape) for f in (*fars, *nears)],
-                pl.BlockSpec((depth, block), lambda i, s: (0, i)),
-                *[whole(t.shape) for t in tiles],
+                pl.BlockSpec((depth, block), lambda i, s: (0, skip + i)),
+                *[pl.BlockSpec(memory_space=pl.ANY)] * len(tiles),
                 whole(slot.shape),
             ],
             out_specs=pl.BlockSpec((rows, block), lambda i, s: (0, i)),
             scratch_shapes=[
                 pltpu.VMEM((rows, depth), BF),
-                pltpu.SMEM((len(tiles) * steps, 4 * most), jnp.int32),
-                pltpu.SMEM((len(tiles), steps), jnp.int32),
+                *[pltpu.VMEM(t.shape, BF) for t in tiles],
+                pltpu.SemaphoreType.DMA((len(tiles),)),
             ],
         ),
-        out_shape=jax.ShapeDtypeStruct((rows, width), F32),
+        out_shape=jax.ShapeDtypeStruct((rows, here * block), F32),
         compiler_params=pltpu.CompilerParams(vmem_limit_bytes=VMEM),
-        cost_estimate=cost(flops, 1e6),
-    )(scal, *fars, *nears, w, *tiles, slot)
+        cost_estimate=cost(1e9, 1e6),
+    )(listed, *fars, *nears, w, *tiles, slot)
 
 
 def shards(
@@ -523,22 +552,13 @@
     def join(hid, moved, *earlier):
         return jnp.concatenate([after(m, *earlier) for m in moved] + [hid])
 
-    def finish_down(i, chips, earlier, sent=None):
-        out = down(
-            after(down_scal, *earlier),
-            [core_swap(c) for c in chips],
-            chips,
-            down_weight,
-            all_tiles,
-            plan,
-            ss_q,
-            width_tiles,
-            owners,
-            per_owner,
-            per_slot,
-            starts[i],
-            1e9,
+    def multiply_down(i, chips, fars, parts, part, *earlier):
+        return down(
+            after(listed, *earlier), fars, chips, down_weight, all_tiles, ss_q, starts[i], parts, part
         )
+
+    def finish_down(i, outs, sent=None):
+        out = outs[0] if len(outs) == 1 else jnp.concatenate(outs, axis=1)
         blocks = out.reshape(owners, shift, sizes[i] // (owners * shift), shard_width).transpose(1, 0, 2, 3)
         total = lax.dynamic_index_in_dim(blocks, here_t, 0, keepdims=False)
         came = []
@@ -548,21 +568,37 @@
                 gone = after(gone, sent[k - 1])
             came.append(lax.ppermute(gone, "tensor", [(j, (j + k) % shift) for j in range(shift)]))
             total = total + came[-1].astype(F32)
-        return out, came, total.astype(BF)
+        return came, total.astype(BF)
 
     hid_a, moved_a = finish_hidden(ahead, 1e9, *sends[third])
     near_tiles = [*tiles, flat_tiles]
     all_tiles = near_tiles + [core_swap(after(t, hid_a)) for t in near_tiles]
+    listed = hits(
+        after(down_scal, kept[second]),
+        shard_width,
+        width_tiles,
+        plan,
+        [t.shape[0] for t in all_tiles],
+        owners,
+        per_owner,
+        per_slot,
+    )
     multiply(fourth, *sends[third], hid_a, *gots[second])
     hid_b, moved_b = finish_hidden(second, SHORT, kept[fourth], *gots[third], *moved_a, *tiles[1:])
     hid_c, moved_c = finish_hidden(third, 1e9, hid_b)
     exchange(fourth, hid_c, *moved_b)
     first = [join(hid_a, moved_a, hid_b), join(hid_b, moved_b, hid_c)]
-    out, came, total = finish_down(0, first, sends[fourth])
+    fars = [core_swap(c) for c in first]
+    split = 2 if shard_width >= 1024 else 1
+    outs = [multiply_down(0, first, fars, split, 0, *sends[fourth])]
+    hid_d, moved_d = finish_hidden(fourth, 1e9, outs[0])
+    if split == 2:
+        outs.append(multiply_down(0, first, fars, split, 1, hid_d))
+    came, total = finish_down(0, outs)
     result = [total]
-    hid_d, moved_d = finish_hidden(fourth, 1e9, out)
-    last = [join(hid_c, moved_c, hid_d), join(hid_d, moved_d)]
-    out, came, total = finish_down(1, last, (out,), came)
+    last = [join(hid_c, moved_c, hid_d), join(hid_d, moved_d, *outs[1:])]
+    outs = [multiply_down(1, last, [core_swap(c) for c in last], 1, 0, *outs)]
+    came, total = finish_down(1, outs, came)
     result.append(total)
 
     placed = [jnp.take(r, at_home, axis=0).reshape(-1, shard_width) for r in result]

time: 206 us -> 207 us (level)
  the two profiles are of different devices: /device:TPU:5 before, /device:TPU:0 now
where the time goes in v9:
time: 207 us
  Pallas kernels  109 us (53%)
  waiting for transfers between devices  36.7 us (18%)
  starting transfers between devices  32.7 us (16%)
  other arithmetic  14.6 us (7%)
  local copies, waits for them, and re-layouts  12.6 us (6%)
    pallas_call x4, Pallas kernels, gate_up(): pl.pallas_call(functools.partial(gate_up_body, owners), grid_spec=pltpu.P...  42.5 us
    pallas_call x3, Pallas kernels, down(): pl.pallas_call(functools.partial(down_body, len(tiles), steps, skip, star...  33.4 us
    ppermute x6, waiting for transfers between devices, finish_down(): lax.ppermute(gone, 'tensor', [(j, (j + k) % shift) for j in range(shift)])  19.6 us
    ppermute x11, waiting for transfers between devices, y_move(): lax.ppermute(x, 'delta', [(i, (i + 2 * k) % owners) for i in range(owners)])  15.3 us
    ppermute x11, starting transfers between devices, y_move(): lax.ppermute(x, 'delta', [(i, (i + 2 * k) % owners) for i in range(owners)])  13.5 us
    pallas_call x4, Pallas kernels, activate(): pl.pallas_call(functools.partial(activate_body, per_slot, start, each, ro...  13.1 us
    ppermute x6, starting transfers between devices, finish_down(): lax.ppermute(gone, 'tensor', [(j, (j + k) % shift) for j in range(shift)])  12.5 us
    pallas_call x1, Pallas kernels, pack(): pl.pallas_call(functools.partial(pack_body, owners, per_owner, kinds, str...  7.13 us
  transfers between devices with their start and end apart: 34, of which 8 were waited for; matrix products, arithmetic and copies ran while one was open for 9% of the time, Pallas kernels for 51%

profile of v9, /device:TPU:0, one launch (start us, length us, event | category | flops | bytes accessed | tf_op | source)
XLA Modules:
  0.0 206.7 jit_solution(6139526865119130959)
XLA Ops:
  0.0 0.7 pad_add_fusion
  0.7 2.4 %collective-permute-start = (s32[4,6]{0,1:T(8,128)S(1)}, s32[4,6]{0,1:T(8,128)S(1)}, u32[]{:S(2)}, u32[]{:S(2)}) collective-permute-start(s32[4,6]{0,1:T(8,128)S(1)} %pad_add_fusion), channel_id=1, source_target_pairs={{0,12},{4,0},{8,4},{12,8},{1,13},{5,1},{9,5},{13,9},{2,14},{6,2},{... | collective-permute-start | bytes 296 | tf_op jit(solution)/shard_map/ppermute | solution.py:427
  4.0 1.1 constant_dynamic-slice_fusion
  5.0 1.3 collective-permute-start.4
  6.9 10.7 %shard_map.118 = (f32[2,128,2048]{2,1,0:T(8,128)}, f32[2,128,2048]{2,1,0:T(8,128)}) custom-call(s32[4]{0:T(128)} %get-tuple-element.73.scal.order, bf16[4,16,8,2048]{3,2,1,0:T(8,128)(2,1)} %bitcast.78, bf16[4,16,8,2048]{3,2,1,0:T(8,128)(2,1)} %bitcast.79, bf16[4,16,8,2048]{3,2,1,0:T(8,128)(2,1)} %bitcast.80, bf16[4,16,8,2048]{3,2,1,0:T(8,128)(2,1)} %bitcast.81, ...), custom_call_target="tpu_custom_call" | custom-call | flops 4294967296 | bytes 16777216 | tf_op jit(solution)/shard_map/pallas_call | solution.py:165
  18.3 0.9 copy.38.ss
  19.7 0.7 concatenate.39.scal
  20.5 7.1 %shard_map.119 = (bf16[256,1024]{1,0:T(8,128)(2,1)}, bf16[256,1024]{1,0:T(8,128)(2,1)}, s32[1,512]{1,0:T(1,128)}, bf16[128,128]{1,0:T(8,128)(2,1)}) custom-call(s32[101]{0:T(128)} %concatenate.39.scal, bf16[512,2048]{1,0:T(8,128)(2,1)} %x.1, s32[1,512]{1,0:T(1,128)} %bitcast.109, s32[512,1]{1,0:T(8,128)} %copy.38.ss), custom_call_target="tpu_custom_call" | custom-call | flops 120000004096 | bytes 4000000 | tf_op jit(solution)/shard_map/pallas_call | solution.py:73
  28.0 1.7 collective-permute-done.5.core
  29.7 1.1 fusion.18
  30.9 1.5 collective-permute-start.7
  32.3 1.3 fusion.3
  33.7 0.7 collective-permute-start.6
  34.4 10.6 %shard_map.120 = (f32[2,128,2048]{2,1,0:T(8,128)}, f32[2,128,2048]{2,1,0:T(8,128)}) custom-call(s32[4]{0:T(128)} %get-tuple-element.73.scal.order, bf16[4,16,8,2048]{3,2,1,0:T(8,128)(2,1)} %bitcast.82, bf16[4,16,8,2048]{3,2,1,0:T(8,128)(2,1)} %bitcast.83, bf16[4,16,8,2048]{3,2,1,0:T(8,128)(2,1)} %bitcast.84, bf16[4,16,8,2048]{3,2,1,0:T(8,128)(2,1)} %bitcast.85, ...), custom_call_target="tpu_custom_call" | custom-call | flops 4294967296 | bytes 16777216 | tf_op jit(solution)/shard_map/pallas_call | solution.py:165
  45.1 0.8 select_reduce_fusion
  45.9 4.6 %collective-permute-done.6.refs_0_ = bf16[2,64,2048]{2,1,0:T(8,128)(2,1)S(1)} collective-permute-done((bf16[2,64,2048]{2,1,0:T(8,128)(2,1)S(1)}, bf16[2,64,2048]{2,1,0:T(8,128)(2,1)S(1)}, u32[]{:S(2)}, u32[]{:S(2)}) %collective-permute-start.6) | collective-permute-done | bytes 524320 | tf_op jit(solution)/shard_map/ppermute | solution.py:399
  50.5 0.8 copy-done.19
  51.3 0.7 copy-done.38
  52.0 2.7 %shard_map.122.x = bf16[128,1024]{1,0:T(8,128)(2,1)} custom-call(s32[4]{0:T(128)} %get-tuple-element.73.scal.order, bf16[2,128,1024]{2,1,0:T(8,128)(2,1)} %bitcast.105, bf16[2,128,1024]{2,1,0:T(8,128)(2,1)} %copy-done.22, bf16[128,1024]{1,0:T(8,128)(2,1)} %copy-done.38), custom_call_target="tpu_custom_call" | custom-call | flops 120000004096 | bytes 1000000 | tf_op jit(solution)/shard_map/pallas_call | solution.py:191
  54.8 4.7 %shard_map.123 = (bf16[2,128,1024]{2,1,0:T(8,128)(2,1)}, bf16[2,128,1024]{2,1,0:T(8,128)(2,1)}) custom-call(s32[101]{0:T(128)} %concatenate.39.scal, bf16[128,1024]{1,0:T(8,128)(2,1)} %shard_map.122.x, bf16[4,2,256,256]{3,2,1,0:T(8,128)(2,1)} %gt.1, bf16[4,2,256,256]{3,2,1,0:T(8,128)(2,1)} %ut.1, s32[1,512]{1,0:T(1,128)} %bitcast.106), custom_call_target="tpu_custom_call" | custom-call | flops 120000004096 | bytes 4000000 | tf_op jit(solution)/shard_map/pallas_call | solution.py:120
  59.7 1.6 collective-permute-start.15
  61.2 1.4 collective-permute-start.12
  62.6 1.1 fusion.17
  63.8 0.7 collective-permute-start.10
  64.5 10.6 %shard_map.124 = (f32[2,128,2048]{2,1,0:T(8,128)}, f32[2,128,2048]{2,1,0:T(8,128)}) custom-call(s32[4]{0:T(128)} %get-tuple-element.73.scal.order, bf16[4,16,8,2048]{3,2,1,0:T(8,128)(2,1)} %bitcast.86, bf16[4,16,8,2048]{3,2,1,0:T(8,128)(2,1)} %bitcast.87, bf16[4,16,8,2048]{3,2,1,0:T(8,128)(2,1)} %bitcast.88, bf16[4,16,8,2048]{3,2,1,0:T(8,128)(2,1)} %bitcast.89, ...), custom_call_target="tpu_custom_call" | custom-call | flops 4294967296 | bytes 16777216 | tf_op jit(solution)/shard_map/pallas_call | solution.py:165
  75.1 5.8 %collective-permute-done.10.refs_0_ = bf16[128,1024]{1,0:T(8,128)(2,1)S(1)} collective-permute-done((bf16[128,1024]{1,0:T(8,128)(2,1)S(1)}, bf16[128,1024]{1,0:T(8,128)(2,1)S(1)}, u32[]{:S(2)}, u32[]{:S(2)}) %collective-permute-start.10) | collective-permute-done | bytes 262176 | tf_op jit(solution)/shard_map/ppermute | solution.py:399
  80.9 0.7 copy-done.39
  81.6 2.5 %shard_map.125.refs_1_ = bf16[128,1024]{1,0:T(8,128)(2,1)} custom-call(s32[4]{0:T(128)} %get-tuple-element.73.scal.order, bf16[2,128,1024]{2,1,0:T(8,128)(2,1)} %get-tuple-element.64.keep, bf16[2,128,1024]{2,1,0:T(8,128)(2,1)} %copy-done.23, bf16[128,1024]{1,0:T(8,128)(2,1)} %copy-done.39), custom_call_target="tpu_custom_call" | custom-call | flops 120000004096 | bytes 1000000 | tf_op jit(solution)/shard_map/pallas_call | solution.py:191
  84.3 1.5 collective-permute-start.13
  85.7 0.9 add_select_fusion.refs_2_.refs_11_
  86.6 3.2 %shard_map.126 = bf16[64,2048]{1,0:T(8,128)(2,1)} custom-call(f32[2,128,2048]{2,1,0:T(8,128)} %get-tuple-element.50.keep, f32[2,128,2048]{2,1,0:T(8,128)} %collective-permute-done.3.core, bf16[2,64,2048]{2,1,0:T(8,128)(2,1)} %copy-done.19, bf16[128,1024]{1,0:T(8,128)(2,1)} %shard_map.125.refs_1_, s32[512,1]{1,0:T(8,128)} %add_select_fusion.refs_2_.refs_11_, ...), custom_call_target="tpu_custom_call" | custom-call | flops 1000000000 | bytes 3145728 | tf_op jit(solution)/shard_map/pallas_call | solution.py:236
  90.4 10.6 %shard_map.127 = (f32[2,128,2048]{2,1,0:T(8,128)}, f32[2,128,2048]{2,1,0:T(8,128)}) custom-call(s32[4]{0:T(128)} %get-tuple-element.73.scal.order, bf16[4,16,8,2048]{3,2,1,0:T(8,128)(2,1)} %bitcast.90, bf16[4,16,8,2048]{3,2,1,0:T(8,128)(2,1)} %bitcast.91, bf16[4,16,8,2048]{3,2,1,0:T(8,128)(2,1)} %bitcast.92, bf16[4,16,8,2048]{3,2,1,0:T(8,128)(2,1)} %bitcast.93, ...), custom_call_target="tpu_custom_call" | custom-call | flops 4294967296 | bytes 16777216 | tf_op jit(solution)/shard_map/pallas_call | solution.py:165
  101.7 1.5 collective-permute-done.14
  103.2 3.4 %shard_map.128 = bf16[64,2048]{1,0:T(8,128)(2,1)} custom-call(f32[2,128,2048]{2,1,0:T(8,128)} %get-tuple-element.59.keep, f32[2,128,2048]{2,1,0:T(8,128)} %copy-done.18, bf16[2,64,2048]{2,1,0:T(8,128)(2,1)} %copy-done.37, bf16[128,1024]{1,0:T(8,128)(2,1)} %shard_map.125.refs_1_, s32[512,1]{1,0:T(8,128)} %add_select_fusion.refs_2_.refs_11_, ...), custom_call_target="tpu_custom_call" | custom-call | flops 120000004096 | bytes 3145728 | tf_op jit(solution)/shard_map/pallas_call | solution.py:236
  106.6 1.5 collective-permute-start.16
  108.0 3.4 %shard_map.129 = bf16[64,2048]{1,0:T(8,128)(2,1)} custom-call(f32[2,128,2048]{2,1,0:T(8,128)} %get-tuple-element.69.keep, f32[2,128,2048]{2,1,0:T(8,128)} %copy-done.8, bf16[2,64,2048]{2,1,0:T(8,128)(2,1)} %copy-done.20, bf16[128,1024]{1,0:T(8,128)(2,1)} %shard_map.125.refs_1_, s32[512,1]{1,0:T(8,128)} %add_select_fusion.refs_2_.refs_11_, ...), custom_call_target="tpu_custom_call" | custom-call | flops 1000000000 | bytes 3145728 | tf_op jit(solution)/shard_map/pallas_call | solution.py:236
  111.4 0.8 pad_maximum_fusion.1.refs_2_
  112.3 3.4 %collective-permute-done.16 = bf16[64,2048]{1,0:T(8,128)(2,1)} collective-permute-done((bf16[64,2048]{1,0:T(8,128)(2,1)}, bf16[64,2048]{1,0:T(8,128)(2,1)}, u32[]{:S(2)}, u32[]{:S(2)}) %collective-permute-start.16) | collective-permute-done | bytes 262176 | tf_op jit(solution)/shard_map/ppermute | solution.py:399
  115.7 1.8 pad_maximum_fusion.2.refs_3_
  118.1 0.7 copy-done.6
  118.9 1.4 collective-permute-start.23
  121.0 0.7 concatenate.38.scal
  121.7 3.5 %shard_map.121.listed = s32[24,33]{1,0:T(8,128)} custom-call(s32[103]{0:T(128)} %concatenate.38.scal), custom_call_target="tpu_custom_call" | custom-call | flops 1000000 | bytes 10000 | tf_op jit(solution)/shard_map/pallas_call | solution.py:283
  125.2 1.0 copy-done.1
  126.2 9.1 %shard_map.130 = f32[256,1024]{1,0:T(8,128)} custom-call(s32[24,33]{1,0:T(8,128)} %shard_map.121.listed, bf16[128,2048]{1,0:T(8,128)(2,1)} %collective-permute-done.18.refs_0_, bf16[128,2048]{1,0:T(8,128)(2,1)} %collective-permute-done.19.refs_1_, bf16[128,2048]{1,0:T(8,128)(2,1)} %pad_maximum_fusion.1.refs_2_, bf16[128,2048]{1,0:T(8,128)(2,1)} %pad_maximum_fusion.2.refs_3_, ...), custom_call_target="tpu_custom_call" | custom-call | flops 1000000000 | bytes 1000000 | tf_op jit(solution)/shard_map/pallas_call | solution.py:341
  135.2 3.2 %shard_map.131 = bf16[64,2048]{1,0:T(8,128)(2,1)} custom-call(f32[2,128,2048]{2,1,0:T(8,128)} %get-tuple-element.78.keep, f32[2,128,2048]{2,1,0:T(8,128)} %copy-done.6, bf16[2,64,2048]{2,1,0:T(8,128)(2,1)} %collective-permute-done.23.refs_0_, bf16[128,1024]{1,0:T(8,128)(2,1)} %shard_map.125.refs_1_, s32[512,1]{1,0:T(8,128)} %add_select_fusion.refs_2_.refs_11_, ...), custom_call_target="tpu_custom_call" | custom-call | flops 1000000000 | bytes 3145728 | tf_op jit(solution)/shard_map/pallas_call | solution.py:236
  138.4 2.4 %collective-permute-start.29 = (bf16[64,2048]{1,0:T(8,128)(2,1)}, bf16[64,2048]{1,0:T(8,128)(2,1)S(1)}, u32[]{:S(2)}, u32[]{:S(2)}) collective-permute-start(bf16[64,2048]{1,0:T(8,128)(2,1)} %shard_map.131), channel_id=1, source_target_pairs={{0,8},{4,12},{8,0},{12,4},{1,9},{5,13},{9,1},{13,5},{2,10},{6,14},... | collective-permute-start | bytes 786440 | tf_op jit(solution)/shard_map/ppermute | solution.py:399
  140.8 1.0 pad_maximum_fusion.3.refs_2_
  141.9 10.2 %shard_map.132 = f32[256,1024]{1,0:T(8,128)} custom-call(s32[24,33]{1,0:T(8,128)} %shard_map.121.listed, bf16[128,2048]{1,0:T(8,128)(2,1)} %collective-permute-done.18.refs_0_, bf16[128,2048]{1,0:T(8,128)(2,1)} %collective-permute-done.19.refs_1_, bf16[128,2048]{1,0:T(8,128)(2,1)} %pad_maximum_fusion.1.refs_2_, bf16[128,2048]{1,0:T(8,128)(2,1)} %pad_maximum_fusion.2.refs_3_, ...), custom_call_target="tpu_custom_call" | custom-call | flops 1000000000 | bytes 1000000 | tf_op jit(solution)/shard_map/pallas_call | solution.py:341
  152.3 1.4 pad_maximum_fusion
  153.9 0.9 collective-permute-start.24
  154.8 3.5 %collective-permute-start.25 = (bf16[4,16,2048]{2,1,0:T(8,128)(2,1)S(1)}, bf16[4,16,2048]{2,1,0:T(8,128)(2,1)S(1)}, u32[]{:S(2)}, u32[]{:S(2)}) collective-permute-start(bf16[4,16,2048]{2,1,0:T(8,128)(2,1)S(1)} %get-tuple-element.100), channel_id=1, source_target_pairs={{0,2},{1,3},{2,0},{3,1},{4,6},{5,7},{6,4},{7,5},{8,10},{9,11},{10,... | collective-permute-start | bytes 786440 | tf_op jit(solution)/shard_map/ppermute | solution.py:569
  158.4 1.3 collective-permute-start.26
  159.7 0.8 copy-done.15
  160.5 0.8 copy-done.16
  161.3 14.2 %shard_map.133 = f32[256,2048]{1,0:T(8,128)} custom-call(s32[24,33]{1,0:T(8,128)} %shard_map.121.listed, bf16[128,2048]{1,0:T(8,128)(2,1)} %copy-done.15, bf16[128,2048]{1,0:T(8,128)(2,1)} %copy-done.16, bf16[128,2048]{1,0:T(8,128)(2,1)} %copy-done.10, bf16[128,2048]{1,0:T(8,128)(2,1)} %copy-done.11, bf16[4096,2048]{1,0:T(8,128)(2,1)} %refs_4_.13, ...), custom_call_target="tpu_custom_call" | custom-call | flops 1000000000 | bytes 1000000 | tf_op jit(solution)/shard_map/pallas_call | solution.py:341
  175.4 1.5 fusion.15
  177.0 0.9 collective-permute-start.32
  177.9 5.8 %collective-permute-start.33 = (bf16[4,16,2048]{2,1,0:T(8,128)(2,1)S(1)}, bf16[4,16,2048]{2,1,0:T(8,128)(2,1)S(1)}, u32[]{:S(2)}, u32[]{:S(2)}) collective-permute-start(bf16[4,16,2048]{2,1,0:T(8,128)(2,1)S(1)} %get-tuple-element.93), channel_id=1, source_target_pairs={{0,3},{1,0},{2,1},{3,2},{4,7},{5,4},{6,5},{7,6},{8,11},{9,8},{10,9... | collective-permute-start | bytes 786440 | tf_op jit(solution)/shard_map/ppermute | solution.py:569
  184.4 3.7 %collective-permute-done.31 = bf16[4,16,2048]{2,1,0:T(8,128)(2,1)S(1)} collective-permute-done((bf16[4,16,2048]{2,1,0:T(8,128)(2,1)S(1)}, bf16[4,16,2048]{2,1,0:T(8,128)(2,1)S(1)}, u32[]{:S(2)}, u32[]{:S(2)}) %collective-permute-start.31) | collective-permute-done | bytes 262176 | tf_op jit(solution)/shard_map/ppermute | solution.py:569
  188.1 10.5 %collective-permute-done.32 = bf16[4,16,2048]{2,1,0:T(8,128)(2,1)S(1)} collective-permute-done((bf16[4,16,2048]{2,1,0:T(8,128)(2,1)S(1)}, bf16[4,16,2048]{2,1,0:T(8,128)(2,1)S(1)}, u32[]{:S(2)}, u32[]{:S(2)}) %collective-permute-start.32) | collective-permute-done | bytes 262176 | tf_op jit(solution)/shard_map/ppermute | solution.py:569
  198.5 5.5 %collective-permute-done.33 = bf16[4,16,2048]{2,1,0:T(8,128)(2,1)S(1)} collective-permute-done((bf16[4,16,2048]{2,1,0:T(8,128)(2,1)S(1)}, bf16[4,16,2048]{2,1,0:T(8,128)(2,1)S(1)}, u32[]{:S(2)}, u32[]{:S(2)}) %collective-permute-start.33) | collective-permute-done | bytes 262176 | tf_op jit(solution)/shard_map/ppermute | solution.py:569
  204.0 1.2 fusion.6
  205.9 0.8 pad_maximum_fusion.5
  (146 shorter events, 8.0 us)
Async XLA Ops:
  0.7 18.5 %collective-permute-start = (s32[4,6]{0,1:T(8,128)S(1)}, s32[4,6]{0,1:T(8,128)S(1)}, u32[]{:S(2)}, u32[]{:S(2)}) collective-permute-start(s32[4,6]{0,1:T(8,128)S(1)} %pad_add_fusion), channel_id=1, source_target_pairs={{0,12},{4,0},{8,4},{12,8},{1,13},{5,1},{9,5},{13,9},{2,14},{6,2},{... | collective-permute-start | bytes 296 | tf_op jit(solution)/shard_map/ppermute | solution.py:427
  3.2 16.2 %collective-permute-start.1 = (s32[4,6]{0,1:T(8,128)S(1)}, s32[4,6]{0,1:T(8,128)S(1)}, u32[]{:S(2)}, u32[]{:S(2)}) collective-permute-start(s32[4,6]{0,1:T(8,128)S(1)} %pad_add_fusion), channel_id=1, source_target_pairs={{0,8},{4,12},{8,0},{12,4},{1,9},{5,13},{9,1},{13,5},{2,10},{6,14},... | collective-permute-start | bytes 296 | tf_op jit(solution)/shard_map/ppermute | solution.py:427
  3.8 15.8 %collective-permute-start.2 = (s32[4,6]{0,1:T(8,128)S(1)}, s32[4,6]{0,1:T(8,128)S(1)}, u32[]{:S(2)}, u32[]{:S(2)}) collective-permute-start(s32[4,6]{0,1:T(8,128)S(1)} %pad_add_fusion), channel_id=1, source_target_pairs={{0,4},{4,8},{8,12},{12,0},{1,5},{5,9},{9,13},{13,1},{2,6},{6,10},{... | collective-permute-start | bytes 296 | tf_op jit(solution)/shard_map/ppermute | solution.py:427
  5.0 15.4 %collective-permute-start.4 = (bf16[4,256,256]{2,1,0:T(8,128)(2,1)S(1)}, bf16[4,256,256]{2,1,0:T(8,128)(2,1)}, u32[]{:S(2)}, u32[]{:S(2)}) collective-permute-start(bf16[4,256,256]{2,1,0:T(8,128)(2,1)S(1)} %constant_dynamic-slice_fusion), channel_id=1, source_target_pairs={{0,8},{4,12},{8,0},{12,4},{1,9},{5,13},{9,1},{13,5},{2,10},{6,14},... | collective-permute-start | bytes 1572872 | tf_op jit(solution)/shard_map/ppermute | solution.py:399
  6.9 11.3 %copy-start.35 = (s32[512]{0:T(512)S(1)}, s32[512]{0:T(512)}, u32[]{:S(2)}) copy-start(s32[512]{0:T(512)} %param.24) | copy-start | bytes 6148
  6.9 11.3 %copy-start.36 = (s32[16]{0:T(128)S(1)}, s32[16]{0:T(128)}, u32[]{:S(2)}) copy-start(s32[16]{0:T(128)} %param.25) | copy-start | bytes 196
  17.6 14.8 %collective-permute-start.3 = (f32[2,128,2048]{2,1,0:T(8,128)}, f32[2,128,2048]{2,1,0:T(8,128)}, u32[]{:S(2)}, u32[]{:S(2)}) collective-permute-start(f32[2,128,2048]{2,1,0:T(8,128)} %get-tuple-element.51), channel_id=1, source_target_pairs={{0,4},{4,0},{8,12},{12,8},{1,5},{5,1},{9,13},{13,9},{2,6},{6,2},{1... | collective-permute-start | bytes 6291464 | tf_op jit(solution)/shard_map/ppermute | solution.py:396
  18.2 2.2 %copy-start.26 = (s32[24]{0:T(128)}, s32[24]{0:T(128)S(1)}, u32[]{:S(2)}) copy-start(s32[24]{0:T(128)S(1)} %reshape.233) | copy-start | bytes 292
  18.3 2.1 %copy-start.25 = (s32[512]{0:T(512)}, s32[512]{0:T(512)S(1)}, u32[]{:S(2)}) copy-start(s32[512]{0:T(512)S(1)} %select_reduce_fusion.1) | copy-start | bytes 6148
  20.5 11.9 %copy-start.4 = (f32[2,128,2048]{2,1,0:T(8,128)S(1)}, f32[2,128,2048]{2,1,0:T(8,128)}, u32[]{:S(2)}) copy-start(f32[2,128,2048]{2,1,0:T(8,128)} %get-tuple-element.50.keep) | copy-start | bytes 6291460
  27.6 2.1 %collective-permute-start.5 = (bf16[2,128,1024]{2,1,0:T(8,128)(2,1)}, bf16[2,128,1024]{2,1,0:T(8,128)(2,1)S(1)}, u32[]{:S(2)}, u32[]{:S(2)}) collective-permute-start(bf16[2,128,1024]{2,1,0:T(8,128)(2,1)} %bitcast.111), channel_id=1, source_target_pairs={{0,4},{4,0},{8,12},{12,8},{1,5},{5,1},{9,13},{13,9},{2,6},{6,2},{1... | collective-permute-start | bytes 1572872 | tf_op jit(solution)/shard_map/ppermute | solution.py:396
  29.7 15.3 %copy-start.22 = (bf16[2,128,1024]{2,1,0:T(8,128)(2,1)}, bf16[2,128,1024]{2,1,0:T(8,128)(2,1)S(1)}, u32[]{:S(2)}) copy-start(bf16[2,128,1024]{2,1,0:T(8,128)(2,1)S(1)} %collective-permute-done.5.core) | copy-start | bytes 1572868
  30.9 19.7 %collective-permute-start.7 = (bf16[128,1024]{1,0:T(8,128)(2,1)S(1)}, bf16[128,1024]{1,0:T(8,128)(2,1)S(1)}, u32[]{:S(2)}, u32[]{:S(2)}) collective-permute-start(bf16[128,1024]{1,0:T(8,128)(2,1)S(1)} %fusion.18), channel_id=1, source_target_pairs={{0,8},{4,12},{8,0},{12,4},{1,9},{5,13},{9,1},{13,5},{2,10},{6,14},... | collective-permute-start | bytes 786440 | tf_op jit(solution)/shard_map/ppermute | solution.py:399
  33.7 11.4 %copy-start.34 = (s32[1,512]{1,0:T(1,128)S(1)}, s32[1,512]{1,0:T(1,128)}, u32[]{:S(2)}) copy-start(s32[1,512]{1,0:T(1,128)} %get-tuple-element.63) | copy-start | bytes 6148
  33.7 16.8 %collective-permute-start.6 = (bf16[2,64,2048]{2,1,0:T(8,128)(2,1)S(1)}, bf16[2,64,2048]{2,1,0:T(8,128)(2,1)S(1)}, u32[]{:S(2)}, u32[]{:S(2)}) collective-permute-start(bf16[2,64,2048]{2,1,0:T(8,128)(2,1)S(1)} %fusion.3), channel_id=1, source_target_pairs={{0,8},{4,12},{8,0},{12,4},{1,9},{5,13},{9,1},{13,5},{2,10},{6,14},... | collective-permute-start | bytes 1572872 | tf_op jit(solution)/shard_map/ppermute | solution.py:399
  45.0 9.7 %collective-permute-start.8 = (f32[2,128,2048]{2,1,0:T(8,128)}, f32[2,128,2048]{2,1,0:T(8,128)S(1)}, u32[]{:S(2)}, u32[]{:S(2)}) collective-permute-start(f32[2,128,2048]{2,1,0:T(8,128)} %get-tuple-element.60), channel_id=1, source_target_pairs={{0,4},{4,0},{8,12},{12,8},{1,5},{5,1},{9,13},{13,9},{2,6},{6,2},{1... | collective-permute-start | bytes 6291464 | tf_op jit(solution)/shard_map/ppermute | solution.py:396
  52.0 2.7 %copy-start.17 = (f32[2,128,2048]{2,1,0:T(8,128)S(1)}, f32[2,128,2048]{2,1,0:T(8,128)}, u32[]{:S(2)}) copy-start(f32[2,128,2048]{2,1,0:T(8,128)} %get-tuple-element.59.keep) | copy-start | bytes 6291460
  54.7 4.8 %copy-start.18 = (f32[2,128,2048]{2,1,0:T(8,128)}, f32[2,128,2048]{2,1,0:T(8,128)S(1)}, u32[]{:S(2)}) copy-start(f32[2,128,2048]{2,1,0:T(8,128)S(1)} %collective-permute-done.8.core) | copy-start | bytes 6291460
  54.8 4.7 %copy-start.24 = (s32[512]{0:T(512)S(1)}, s32[512]{0:T(512)}, u32[]{:S(2)}) copy-start(s32[512]{0:T(512)} %select_reduce_fusion) | copy-start | bytes 6148
  59.5 3.1 %collective-permute-start.9 = (bf16[2,128,1024]{2,1,0:T(8,128)(2,1)}, bf16[2,128,1024]{2,1,0:T(8,128)(2,1)S(1)}, u32[]{:S(2)}, u32[]{:S(2)}) collective-permute-start(bf16[2,128,1024]{2,1,0:T(8,128)(2,1)} %get-tuple-element.65), channel_id=1, source_target_pairs={{0,4},{4,0},{8,12},{12,8},{1,5},{5,1},{9,13},{13,9},{2,6},{6,2},{1... | collective-permute-start | bytes 1572872 | tf_op jit(solution)/shard_map/ppermute | solution.py:396
  59.7 30.7 %collective-permute-start.15 = (bf16[4,256,256]{2,1,0:T(8,128)(2,1)}, bf16[4,256,256]{2,1,0:T(8,128)(2,1)S(1)}, u32[]{:S(2)}, u32[]{:S(2)}) collective-permute-start(bf16[4,256,256]{2,1,0:T(8,128)(2,1)} %collective-permute-done.4.refs_5_), channel_id=1, source_target_pairs={{0,16},{16,0},{1,17},{17,1},{2,18},{18,2},{3,19},{19,3},{4,20},{20... | collective-permute-start | bytes 1572872 | tf_op jit(solution)/shard_map/ppermute | solution.py:504
  61.2 29.2 %collective-permute-start.12 = (bf16[2,64,2048]{2,1,0:T(8,128)(2,1)S(1)}, bf16[2,64,2048]{2,1,0:T(8,128)(2,1)S(1)}, u32[]{:S(2)}, u32[]{:S(2)}) collective-permute-start(bf16[2,64,2048]{2,1,0:T(8,128)(2,1)S(1)} %fusion.2), channel_id=1, source_target_pairs={{0,8},{4,12},{8,0},{12,4},{1,9},{5,13},{9,1},{13,5},{2,10},{6,14},... | collective-permute-start | bytes 1572872 | tf_op jit(solution)/shard_map/ppermute | solution.py:399
  62.6 12.4 %copy-start.23 = (bf16[2,128,1024]{2,1,0:T(8,128)(2,1)}, bf16[2,128,1024]{2,1,0:T(8,128)(2,1)S(1)}, u32[]{:S(2)}) copy-start(bf16[2,128,1024]{2,1,0:T(8,128)(2,1)S(1)} %collective-permute-done.9.core) | copy-start | bytes 1572868
  63.8 17.1 %collective-permute-start.10 = (bf16[128,1024]{1,0:T(8,128)(2,1)S(1)}, bf16[128,1024]{1,0:T(8,128)(2,1)S(1)}, u32[]{:S(2)}, u32[]{:S(2)}) collective-permute-start(bf16[128,1024]{1,0:T(8,128)(2,1)S(1)} %fusion.17), channel_id=1, source_target_pairs={{0,8},{4,12},{8,0},{12,4},{1,9},{5,13},{9,1},{13,5},{2,10},{6,14},... | collective-permute-start | bytes 786440 | tf_op jit(solution)/shard_map/ppermute | solution.py:399
  75.0 9.1 %copy-start.7 = (f32[2,128,2048]{2,1,0:T(8,128)S(1)}, f32[2,128,2048]{2,1,0:T(8,128)}, u32[]{:S(2)}) copy-start(f32[2,128,2048]{2,1,0:T(8,128)} %get-tuple-element.69.keep) | copy-start | bytes 6291460
  75.1 9.1 %collective-permute-start.11 = (f32[2,128,2048]{2,1,0:T(8,128)}, f32[2,128,2048]{2,1,0:T(8,128)S(1)}, u32[]{:S(2)}, u32[]{:S(2)}) collective-permute-start(f32[2,128,2048]{2,1,0:T(8,128)} %get-tuple-element.70), channel_id=1, source_target_pairs={{0,4},{4,0},{8,12},{12,8},{1,5},{5,1},{9,13},{13,9},{2,6},{6,2},{1... | collective-permute-start | bytes 6291464 | tf_op jit(solution)/shard_map/ppermute | solution.py:396
  84.1 5.6 %copy-start.8 = (f32[2,128,2048]{2,1,0:T(8,128)}, f32[2,128,2048]{2,1,0:T(8,128)S(1)}, u32[]{:S(2)}) copy-start(f32[2,128,2048]{2,1,0:T(8,128)S(1)} %collective-permute-done.11.core) | copy-start | bytes 6291460
  84.3 18.9 %collective-permute-start.13 = (bf16[2,64,2048]{2,1,0:T(8,128)(2,1)S(1)}, bf16[2,64,2048]{2,1,0:T(8,128)(2,1)S(1)}, u32[]{:S(2)}, u32[]{:S(2)}) collective-permute-start(bf16[2,64,2048]{2,1,0:T(8,128)(2,1)S(1)} %fusion.1), channel_id=1, source_target_pairs={{0,8},{4,12},{8,0},{12,4},{1,9},{5,13},{9,1},{13,5},{2,10},{6,14},... | collective-permute-start | bytes 1572872 | tf_op jit(solution)/shard_map/ppermute | solution.py:399
  89.8 13.4 %copy-start = (bf16[4,2,256,256]{3,2,1,0:T(8,128)(2,1)S(1)}, bf16[4,2,256,256]{3,2,1,0:T(8,128)(2,1)}, u32[]{:S(2)}) copy-start(bf16[4,2,256,256]{3,2,1,0:T(8,128)(2,1)} %param.20) | copy-start | bytes 3145732
  89.8 13.4 %collective-permute-start.14 = (bf16[64,2048]{1,0:T(8,128)(2,1)}, bf16[64,2048]{1,0:T(8,128)(2,1)S(1)}, u32[]{:S(2)}, u32[]{:S(2)}) collective-permute-start(bf16[64,2048]{1,0:T(8,128)(2,1)} %shard_map.126), channel_id=1, source_target_pairs={{0,8},{4,12},{8,0},{12,4},{1,9},{5,13},{9,1},{13,5},{2,10},{6,14},... | collective-permute-start | bytes 786440 | tf_op jit(solution)/shard_map/ppermute | solution.py:399
  90.4 10.7 %copy-start.2 = (bf16[4,256,256]{2,1,0:T(8,128)(2,1)}, bf16[4,256,256]{2,1,0:T(8,128)(2,1)S(1)}, u32[]{:S(2)}) copy-start(bf16[4,256,256]{2,1,0:T(8,128)(2,1)S(1)} %collective-permute-done.15.refs_6_) | copy-start | bytes 1572868
  90.4 27.7 %collective-permute-start.21 = (bf16[4,256,256]{2,1,0:T(8,128)(2,1)S(1)}, bf16[4,256,256]{2,1,0:T(8,128)(2,1)S(1)}, u32[]{:S(2)}, u32[]{:S(2)}) collective-permute-start(bf16[4,256,256]{2,1,0:T(8,128)(2,1)S(1)} %collective-permute-done.15.refs_6_), channel_id=1, source_target_pairs={{0,4},{4,0},{8,12},{12,8},{1,5},{5,1},{9,13},{13,9},{2,6},{6,2},{1... | collective-permute-start | bytes 1572872 | tf_op jit(solution)/shard_map/ppermute | solution.py:396
  90.4 10.6 %copy-start.37 = (bf16[2,64,2048]{2,1,0:T(8,128)(2,1)}, bf16[2,64,2048]{2,1,0:T(8,128)(2,1)S(1)}, u32[]{:S(2)}) copy-start(bf16[2,64,2048]{2,1,0:T(8,128)(2,1)S(1)} %collective-permute-done.12.refs_0_) | copy-start | bytes 1572868
  101.1 16.4 %collective-permute-start.17 = (f32[2,128,2048]{2,1,0:T(8,128)}, f32[2,128,2048]{2,1,0:T(8,128)S(1)}, u32[]{:S(2)}, u32[]{:S(2)}) collective-permute-start(f32[2,128,2048]{2,1,0:T(8,128)} %get-tuple-element.79), channel_id=1, source_target_pairs={{0,4},{4,0},{8,12},{12,8},{1,5},{5,1},{9,13},{13,9},{2,6},{6,2},{1... | collective-permute-start | bytes 6291464 | tf_op jit(solution)/shard_map/ppermute | solution.py:396
  101.6 18.6 %collective-permute-start.20 = (bf16[4,256,256]{2,1,0:T(8,128)(2,1)}, bf16[4,256,256]{2,1,0:T(8,128)(2,1)}, u32[]{:S(2)}, u32[]{:S(2)}) collective-permute-start(bf16[4,256,256]{2,1,0:T(8,128)(2,1)} %collective-permute-done.4.refs_5_), channel_id=1, source_target_pairs={{0,4},{4,0},{8,12},{12,8},{1,5},{5,1},{9,13},{13,9},{2,6},{6,2},{1... | collective-permute-start | bytes 1572872 | tf_op jit(solution)/shard_map/ppermute | solution.py:396
  103.2 22.0 %collective-permute-start.22 = (bf16[8,256,256]{2,1,0:T(8,128)(2,1)S(1)}, bf16[8,256,256]{2,1,0:T(8,128)(2,1)S(1)}, u32[]{:S(2)}, u32[]{:S(2)}) collective-permute-start(bf16[8,256,256]{2,1,0:T(8,128)(2,1)S(1)} %bitcast.98), channel_id=1, source_target_pairs={{0,4},{4,0},{8,12},{12,8},{1,5},{5,1},{9,13},{13,9},{2,6},{6,2},{1... | collective-permute-start | bytes 3145736 | tf_op jit(solution)/shard_map/ppermute | solution.py:396
  103.2 3.4 %copy-start.20 = (bf16[2,64,2048]{2,1,0:T(8,128)(2,1)}, bf16[2,64,2048]{2,1,0:T(8,128)(2,1)S(1)}, u32[]{:S(2)}) copy-start(bf16[2,64,2048]{2,1,0:T(8,128)(2,1)S(1)} %collective-permute-done.13.refs_0_) | copy-start | bytes 1572868
  106.6 4.8 %copy-start.13 = (bf16[64,2048]{1,0:T(8,128)(2,1)S(1)}, bf16[64,2048]{1,0:T(8,128)(2,1)}, u32[]{:S(2)}) copy-start(bf16[64,2048]{1,0:T(8,128)(2,1)} %shard_map.126) | copy-start | bytes 786436
  106.6 9.1 %copy-start.21 = (bf16[64,2048]{1,0:T(8,128)(2,1)S(1)}, bf16[64,2048]{1,0:T(8,128)(2,1)}, u32[]{:S(2)}) copy-start(bf16[64,2048]{1,0:T(8,128)(2,1)} %shard_map.128) | copy-start | bytes 786436
  106.6 9.1 %collective-permute-start.16 = (bf16[64,2048]{1,0:T(8,128)(2,1)}, bf16[64,2048]{1,0:T(8,128)(2,1)}, u32[]{:S(2)}, u32[]{:S(2)}) collective-permute-start(bf16[64,2048]{1,0:T(8,128)(2,1)} %shard_map.128), channel_id=1, source_target_pairs={{0,8},{4,12},{8,0},{12,4},{1,9},{5,13},{9,1},{13,5},{2,10},{6,14},... | collective-permute-start | bytes 786440 | tf_op jit(solution)/shard_map/ppermute | solution.py:399
  108.0 10.0 %copy-start.5 = (f32[2,128,2048]{2,1,0:T(8,128)S(1)}, f32[2,128,2048]{2,1,0:T(8,128)}, u32[]{:S(2)}) copy-start(f32[2,128,2048]{2,1,0:T(8,128)} %get-tuple-element.78.keep) | copy-start | bytes 6291460
  112.2 8.0 %copy-start.12 = (bf16[64,2048]{1,0:T(8,128)(2,1)S(1)}, bf16[64,2048]{1,0:T(8,128)(2,1)}, u32[]{:S(2)}) copy-start(bf16[64,2048]{1,0:T(8,128)(2,1)} %shard_map.129) | copy-start | bytes 786436
  112.2 8.7 %copy-start.27 = (s32[24]{0:T(128)S(1)}, s32[24]{0:T(128)}, u32[]{:S(2)}) copy-start(s32[24]{0:T(128)} %copy-done.26) | copy-start | bytes 292
  112.2 8.7 %copy-start.29 = (s32[24]{0:T(128)S(1)}, s32[24]{0:T(128)}, u32[]{:S(2)}) copy-start(s32[24]{0:T(128)} %copy-done.28) | copy-start | bytes 292
  112.2 8.7 %copy-start.31 = (s32[24]{0:T(128)S(1)}, s32[24]{0:T(128)}, u32[]{:S(2)}) copy-start(s32[24]{0:T(128)} %copy-done.30) | copy-start | bytes 292
  112.2 8.8 %copy-start.33 = (s32[24]{0:T(128)S(1)}, s32[24]{0:T(128)}, u32[]{:S(2)}) copy-start(s32[24]{0:T(128)} %copy-done.32) | copy-start | bytes 292
  115.7 9.5 %collective-permute-start.18 = (bf16[128,2048]{1,0:T(8,128)(2,1)}, bf16[128,2048]{1,0:T(8,128)(2,1)}, u32[]{:S(2)}, u32[]{:S(2)}) collective-permute-start(bf16[128,2048]{1,0:T(8,128)(2,1)} %pad_maximum_fusion.1.refs_2_), channel_id=1, source_target_pairs={{0,4},{4,0},{8,12},{12,8},{1,5},{5,1},{9,13},{13,9},{2,6},{6,2},{1... | collective-permute-start | bytes 1572872 | tf_op jit(solution)/shard_map/ppermute | solution.py:396
  117.5 7.7 %collective-permute-start.19 = (bf16[128,2048]{1,0:T(8,128)(2,1)}, bf16[128,2048]{1,0:T(8,128)(2,1)}, u32[]{:S(2)}, u32[]{:S(2)}) collective-permute-start(bf16[128,2048]{1,0:T(8,128)(2,1)} %pad_maximum_fusion.2.refs_3_), channel_id=1, source_target_pairs={{0,4},{4,0},{8,12},{12,8},{1,5},{5,1},{9,13},{13,9},{2,6},{6,2},{1... | collective-permute-start | bytes 1572872 | tf_op jit(solution)/shard_map/ppermute | solution.py:396
  118.9 6.3 %copy-start.3 = (bf16[4,256,256]{2,1,0:T(8,128)(2,1)}, bf16[4,256,256]{2,1,0:T(8,128)(2,1)S(1)}, u32[]{:S(2)}) copy-start(bf16[4,256,256]{2,1,0:T(8,128)(2,1)S(1)} %collective-permute-done.21.refs_9_) | copy-start | bytes 1572868
  118.9 16.4 %collective-permute-start.23 = (bf16[2,64,2048]{2,1,0:T(8,128)(2,1)S(1)}, bf16[2,64,2048]{2,1,0:T(8,128)(2,1)}, u32[]{:S(2)}, u32[]{:S(2)}) collective-permute-start(bf16[2,64,2048]{2,1,0:T(8,128)(2,1)S(1)} %fusion), channel_id=1, source_target_pairs={{0,8},{4,12},{8,0},{12,4},{1,9},{5,13},{9,1},{13,5},{2,10},{6,14},... | collective-permute-start | bytes 1572872 | tf_op jit(solution)/shard_map/ppermute | solution.py:399
  120.3 20.5 %collective-permute-start.27 = (bf16[64,2048]{1,0:T(8,128)(2,1)S(1)}, bf16[64,2048]{1,0:T(8,128)(2,1)}, u32[]{:S(2)}, u32[]{:S(2)}) collective-permute-start(bf16[64,2048]{1,0:T(8,128)(2,1)S(1)} %copy-done.12), channel_id=1, source_target_pairs={{0,8},{4,12},{8,0},{12,4},{1,9},{5,13},{9,1},{13,5},{2,10},{6,14},... | collective-permute-start | bytes 786440 | tf_op jit(solution)/shard_map/ppermute | solution.py:399
  138.4 13.7 %collective-permute-start.29 = (bf16[64,2048]{1,0:T(8,128)(2,1)}, bf16[64,2048]{1,0:T(8,128)(2,1)S(1)}, u32[]{:S(2)}, u32[]{:S(2)}) collective-permute-start(bf16[64,2048]{1,0:T(8,128)(2,1)} %shard_map.131), channel_id=1, source_target_pairs={{0,8},{4,12},{8,0},{12,4},{1,9},{5,13},{9,1},{13,5},{2,10},{6,14},... | collective-permute-start | bytes 786440 | tf_op jit(solution)/shard_map/ppermute | solution.py:399
  141.8 10.3 %copy-start.10 = (bf16[128,2048]{1,0:T(8,128)(2,1)}, bf16[128,2048]{1,0:T(8,128)(2,1)S(1)}, u32[]{:S(2)}) copy-start(bf16[128,2048]{1,0:T(8,128)(2,1)S(1)} %pad_maximum_fusion.3.refs_2_) | copy-start | bytes 1572868
  141.8 10.3 %copy-start.14 = (bf16[64,2048]{1,0:T(8,128)(2,1)S(1)}, bf16[64,2048]{1,0:T(8,128)(2,1)}, u32[]{:S(2)}) copy-start(bf16[64,2048]{1,0:T(8,128)(2,1)} %shard_map.131) | copy-start | bytes 786436
  141.8 10.5 %copy-start.9 = (f32[256,1024]{1,0:T(8,128)S(1)}, f32[256,1024]{1,0:T(8,128)}, u32[]{:S(2)}) copy-start(f32[256,1024]{1,0:T(8,128)} %shard_map.130) | copy-start | bytes 3145732
  141.8 17.8 %collective-permute-start.28 = (bf16[128,2048]{1,0:T(8,128)(2,1)S(1)}, bf16[128,2048]{1,0:T(8,128)(2,1)S(1)}, u32[]{:S(2)}, u32[]{:S(2)}) collective-permute-start(bf16[128,2048]{1,0:T(8,128)(2,1)S(1)} %pad_maximum_fusion.3.refs_2_), channel_id=1, source_target_pairs={{0,4},{4,0},{8,12},{12,8},{1,5},{5,1},{9,13},{13,9},{2,6},{6,2},{1... | collective-permute-start | bytes 1572872 | tf_op jit(solution)/shard_map/ppermute | solution.py:396
  152.2 1.6 copy-start.11
  152.2 7.5 %collective-permute-start.30 = (bf16[128,2048]{1,0:T(8,128)(2,1)S(1)}, bf16[128,2048]{1,0:T(8,128)(2,1)S(1)}, u32[]{:S(2)}, u32[]{:S(2)}) collective-permute-start(bf16[128,2048]{1,0:T(8,128)(2,1)S(1)} %pad_maximum_fusion.4.refs_3_), channel_id=1, source_target_pairs={{0,4},{4,0},{8,12},{12,8},{1,5},{5,1},{9,13},{13,9},{2,6},{6,2},{1... | collective-permute-start | bytes 1572872 | tf_op jit(solution)/shard_map/ppermute | solution.py:396
  153.9 23.0 %collective-permute-start.24 = (bf16[4,16,2048]{2,1,0:T(8,128)(2,1)S(1)}, bf16[4,16,2048]{2,1,0:T(8,128)(2,1)S(1)}, u32[]{:S(2)}, u32[]{:S(2)}) collective-permute-start(bf16[4,16,2048]{2,1,0:T(8,128)(2,1)S(1)} %get-tuple-element.98), channel_id=1, source_target_pairs={{0,1},{1,2},{2,3},{3,0},{4,5},{5,6},{6,7},{7,4},{8,9},{9,10},{10,1... | collective-permute-start | bytes 786440 | tf_op jit(solution)/shard_map/ppermute | solution.py:569
  154.8 22.2 %collective-permute-start.25 = (bf16[4,16,2048]{2,1,0:T(8,128)(2,1)S(1)}, bf16[4,16,2048]{2,1,0:T(8,128)(2,1)S(1)}, u32[]{:S(2)}, u32[]{:S(2)}) collective-permute-start(bf16[4,16,2048]{2,1,0:T(8,128)(2,1)S(1)} %get-tuple-element.100), channel_id=1, source_target_pairs={{0,2},{1,3},{2,0},{3,1},{4,6},{5,7},{6,4},{7,5},{8,10},{9,11},{10,... | collective-permute-start | bytes 786440 | tf_op jit(solution)/shard_map/ppermute | solution.py:569
  158.4 19.6 %collective-permute-start.26 = (bf16[4,16,2048]{2,1,0:T(8,128)(2,1)S(1)}, bf16[4,16,2048]{2,1,0:T(8,128)(2,1)S(1)}, u32[]{:S(2)}, u32[]{:S(2)}) collective-permute-start(bf16[4,16,2048]{2,1,0:T(8,128)(2,1)S(1)} %get-tuple-element.99), channel_id=1, source_target_pairs={{0,3},{1,0},{2,1},{3,2},{4,7},{5,4},{6,5},{7,6},{8,11},{9,8},{10,9... | collective-permute-start | bytes 786440 | tf_op jit(solution)/shard_map/ppermute | solution.py:569
  176.9 11.2 %collective-permute-start.31 = (bf16[4,16,2048]{2,1,0:T(8,128)(2,1)S(1)}, bf16[4,16,2048]{2,1,0:T(8,128)(2,1)S(1)}, u32[]{:S(2)}, u32[]{:S(2)}) collective-permute-start(bf16[4,16,2048]{2,1,0:T(8,128)(2,1)S(1)} %get-tuple-element.91), channel_id=1, source_target_pairs={{0,1},{1,2},{2,3},{3,0},{4,5},{5,6},{6,7},{7,4},{8,9},{9,10},{10,1... | collective-permute-start | bytes 786440 | tf_op jit(solution)/shard_map/ppermute | solution.py:569
  177.0 21.5 %collective-permute-start.32 = (bf16[4,16,2048]{2,1,0:T(8,128)(2,1)S(1)}, bf16[4,16,2048]{2,1,0:T(8,128)(2,1)S(1)}, u32[]{:S(2)}, u32[]{:S(2)}) collective-permute-start(bf16[4,16,2048]{2,1,0:T(8,128)(2,1)S(1)} %get-tuple-element.92), channel_id=1, source_target_pairs={{0,2},{1,3},{2,0},{3,1},{4,6},{5,7},{6,4},{7,5},{8,10},{9,11},{10,... | collective-permute-start | bytes 786440 | tf_op jit(solution)/shard_map/ppermute | solution.py:569
  177.9 26.1 %collective-permute-start.33 = (bf16[4,16,2048]{2,1,0:T(8,128)(2,1)S(1)}, bf16[4,16,2048]{2,1,0:T(8,128)(2,1)S(1)}, u32[]{:S(2)}, u32[]{:S(2)}) collective-permute-start(bf16[4,16,2048]{2,1,0:T(8,128)(2,1)S(1)} %get-tuple-element.93), channel_id=1, source_target_pairs={{0,3},{1,0},{2,1},{3,2},{4,7},{5,4},{6,5},{7,6},{8,11},{9,8},{10,9... | collective-permute-start | bytes 786440 | tf_op jit(solution)/shard_map/ppermute | solution.py:569
  (10 other events, 8.8 us)

commit v10 on v9

--- a/solution.py
+++ b/solution.py
@@ -291,7 +291,7 @@
     )(scal)
 
 
-def down_body(arrays, steps, skip, start, listed, *refs):
+def down_body(arrays, steps, start, listed, *refs):
     fars, nears, (w, *refs) = refs[:PARTS], refs[PARTS : 2 * PARTS], refs[2 * PARTS :]
     sources, (slot, out, hid, *refs) = refs[:arrays], refs[arrays:]
     tiles, arrived = refs[:arrays], refs[arrays]
@@ -317,7 +317,7 @@
             copy.wait()
 
     for r in range(arrays):
-        entry = r * steps + skip + step
+        entry = r * steps + step
 
         def add(n, carry):
             i = listed[entry, 4 * n]
@@ -332,20 +332,18 @@
         lax.fori_loop(0, listed[entry, last], add, 0)
 
 
-def down(listed, fars, nears, w, tiles, slot, start, parts, part):
+def down(listed, fars, nears, w, tiles, slot, start):
     rows, depth = 2 * fars[0].shape[0], w.shape[0]
     block = min(512, w.shape[1])
     steps = w.shape[1] // block
-    here = steps // parts
-    skip = part * here
     return pl.pallas_call(
-        functools.partial(down_body, len(tiles), steps, skip, start),
+        functools.partial(down_body, len(tiles), steps, start),
         grid_spec=pltpu.PrefetchScalarGridSpec(
             num_scalar_prefetch=1,
-            grid=(here,),
+            grid=(steps,),
             in_specs=[
                 *[whole(f.shape) for f in (*fars, *nears)],
-                pl.BlockSpec((depth, block), lambda i, s: (0, skip + i)),
+                pl.BlockSpec((depth, block), lambda i, s: (0, i)),
                 *[pl.BlockSpec(memory_space=pl.ANY)] * len(tiles),
                 whole(slot.shape),
             ],
@@ -356,7 +354,7 @@
                 pltpu.SemaphoreType.DMA((len(tiles),)),
             ],
         ),
-        out_shape=jax.ShapeDtypeStruct((rows, here * block), F32),
+        out_shape=jax.ShapeDtypeStruct((rows, w.shape[1]), F32),
         compiler_params=pltpu.CompilerParams(vmem_limit_bytes=VMEM),
         cost_estimate=cost(1e9, 1e6),
     )(listed, *fars, *nears, w, *tiles, slot)
@@ -513,7 +511,11 @@
     )
     ss_q = slot_q[:, None]
 
-    features = finish(packed, packed_core, packed_sends, kept[second], *gots[ahead])
+    counts = [t.shape[0] for t in [*tiles, flat_tiles]] * 2
+    listed = hits(
+        after(down_scal, kept[second]), shard_width, width_tiles, plan, counts, owners, per_owner, per_slot
+    )
+    features = finish(packed, packed_core, packed_sends, listed, *gots[ahead])
     exchange(second, features)
     send, spread = product(
         after(scal, *sends[second]),
@@ -528,7 +530,11 @@
     spread_core = core_swap(send)
     spread_sends = [spread[k - 1] + spread_core[k - 1] for k in range(1, ys)]
     multiply(third, *sends[second], *spread_sends)
-    home_delta = finish(spread, spread_core, spread_sends, kept[third])
+    far_tiles = {0: core_swap(after(from_y, kept[second])), len(tiles): core_swap(after(flat_tiles, kept[second]))}
+    home_delta = finish(spread, spread_core, spread_sends, kept[third], *tiles[1:], *far_tiles.values())
+    if len(tiles) == 2:
+        far_tiles[1] = core_swap(after(tiles[1], home_delta))
+    all_tiles = [*tiles, flat_tiles] + [far_tiles[i] for i in range(len(far_tiles))]
     exchange(third, home_delta)
 
     def finish_hidden(u, flops, *earlier):
@@ -552,13 +558,11 @@
     def join(hid, moved, *earlier):
         return jnp.concatenate([after(m, *earlier) for m in moved] + [hid])
 
-    def multiply_down(i, chips, fars, parts, part, *earlier):
-        return down(
-            after(listed, *earlier), fars, chips, down_weight, all_tiles, ss_q, starts[i], parts, part
-        )
-
-    def finish_down(i, outs, sent=None):
-        out = outs[0] if len(outs) == 1 else jnp.concatenate(outs, axis=1)
+    def multiply_down(i, chips, *earlier):
+        fars = [core_swap(c) for c in chips]
+        return down(after(listed, *earlier), fars, chips, down_weight, all_tiles, ss_q, starts[i])
+
+    def finish_down(i, out, sent=None):
         blocks = out.reshape(owners, shift, sizes[i] // (owners * shift), shard_width).transpose(1, 0, 2, 3)
         total = lax.dynamic_index_in_dim(blocks, here_t, 0, keepdims=False)
         came = []
@@ -571,34 +575,18 @@
         return came, total.astype(BF)
 
     hid_a, moved_a = finish_hidden(ahead, 1e9, *sends[third])
-    near_tiles = [*tiles, flat_tiles]
-    all_tiles = near_tiles + [core_swap(after(t, hid_a)) for t in near_tiles]
-    listed = hits(
-        after(down_scal, kept[second]),
-        shard_width,
-        width_tiles,
-        plan,
-        [t.shape[0] for t in all_tiles],
-        owners,
-        per_owner,
-        per_slot,
-    )
     multiply(fourth, *sends[third], hid_a, *gots[second])
-    hid_b, moved_b = finish_hidden(second, SHORT, kept[fourth], *gots[third], *moved_a, *tiles[1:])
-    hid_c, moved_c = finish_hidden(third, 1e9, hid_b)
-    exchange(fourth, hid_c, *moved_b)
-    first = [join(hid_a, moved_a, hid_b), join(hid_b, moved_b, hid_c)]
-    fars = [core_swap(c) for c in first]
-    split = 2 if shard_width >= 1024 else 1
-    outs = [multiply_down(0, first, fars, split, 0, *sends[fourth])]
-    hid_d, moved_d = finish_hidden(fourth, 1e9, outs[0])
-    if split == 2:
-        outs.append(multiply_down(0, first, fars, split, 1, hid_d))
-    came, total = finish_down(0, outs)
+    hid_b, moved_b = finish_hidden(second, SHORT, kept[fourth], *gots[third], *moved_a, *all_tiles)
+    exchange(fourth, hid_b)
+    hid_c, moved_c = finish_hidden(third, 1e9, hid_b, *sends[fourth])
+    hid_d, moved_d = finish_hidden(fourth, 1e9, hid_c)
+    first = [join(hid_a, moved_a, hid_b), join(hid_b, moved_b, *sends[fourth])]
+    out = multiply_down(0, first, hid_d)
+    came, total = finish_down(0, out)
     result = [total]
-    last = [join(hid_c, moved_c, hid_d), join(hid_d, moved_d, *outs[1:])]
-    outs = [multiply_down(1, last, [core_swap(c) for c in last], 1, 0, *outs)]
-    came, total = finish_down(1, outs, came)
+    last = [join(hid_c, moved_c, out), join(hid_d, moved_d, out)]
+    out = multiply_down(1, last, out)
+    came, total = finish_down(1, out, came)
     result.append(total)
 
     placed = [jnp.take(r, at_home, axis=0).reshape(-1, shard_width) for r in result]

time: 207 us -> 205 us (level)
  Pallas kernels: 109 us -> 105 us
  other arithmetic: 14.6 us -> 10.8 us
  starting transfers between devices: 32.7 us -> 36.1 us
  waiting for transfers between devices: 36.7 us -> 39.8 us
    ppermute x11, waiting for transfers between devices: 15.3 us -> 23.9 us  [y_move(): lax.ppermute(x, 'delta', [(i, (i + 2 * k) % owners) for i in range(owners)])]
    ppermute x6, waiting for transfers between devices: 19.6 us -> 14.7 us  [finish_down(): lax.ppermute(gone, 'tensor', [(j, (j + k) % shift) for j in range(shift)])]
    pallas_call x3 -> x2, Pallas kernels: 33.4 us -> 28.8 us  [down(): pl.pallas_call(functools.partial(down_body, len(tiles), steps, start), gr...]
    ppermute x6, starting transfers between devices: 12.5 us -> 16.7 us  [finish_down(): lax.ppermute(gone, 'tensor', [(j, (j + k) % shift) for j in range(shift)])]
    concatenate x4, other arithmetic: 3.68 us -> 0.15 us  [join(): return jnp.concatenate([after(m, *earlier) for m in moved] + [hid])]
    unnamed x80 -> x68, local copies, waits for them, and re-layouts: 5.62 us -> 5.6 us
  transfers between devices with their start and end apart: 34 -> 34, of which waited for: 8 -> 8; matrix products, arithmetic and copies ran while one was open for 9% -> 6% of each run, Pallas kernels for 51% -> 49%
where the time goes in v10:
time: 205 us
  Pallas kernels  105 us (51%)
  waiting for transfers between devices  39.8 us (19%)
  starting transfers between devices  36.1 us (18%)
  local copies, waits for them, and re-layouts  12.5 us (6%)
  other arithmetic  10.8 us (5%)
    pallas_call x4, Pallas kernels, gate_up(): pl.pallas_call(functools.partial(gate_up_body, owners), grid_spec=pltpu.P...  42.5 us
    pallas_call x2, Pallas kernels, down(): pl.pallas_call(functools.partial(down_body, len(tiles), steps, start), gr...  28.8 us
    ppermute x11, waiting for transfers between devices, y_move(): lax.ppermute(x, 'delta', [(i, (i + 2 * k) % owners) for i in range(owners)])  23.9 us
    ppermute x6, starting transfers between devices, finish_down(): lax.ppermute(gone, 'tensor', [(j, (j + k) % shift) for j in range(shift)])  16.7 us
    ppermute x6, waiting for transfers between devices, finish_down(): lax.ppermute(gone, 'tensor', [(j, (j + k) % shift) for j in range(shift)])  14.7 us
    pallas_call x4, Pallas kernels, activate(): pl.pallas_call(functools.partial(activate_body, per_slot, start, each, ro...  13.1 us
    ppermute x11, starting transfers between devices, y_move(): lax.ppermute(x, 'delta', [(i, (i + 2 * k) % owners) for i in range(owners)])  12.7 us
    pallas_call x1, Pallas kernels, pack(): pl.pallas_call(functools.partial(pack_body, owners, per_owner, kinds, str...  7.13 us
  transfers between devices with their start and end apart: 34, of which 8 were waited for; matrix products, arithmetic and copies ran while one was open for 6% of the time, Pallas kernels for 49%

profile of v10, /device:TPU:0, one launch (start us, length us, event | category | flops | bytes accessed | tf_op | source)
XLA Modules:
  0.0 204.5 jit_solution(9610448228397627553)
XLA Ops:
  0.0 0.7 pad_add_fusion
  0.7 2.4 %collective-permute-start = (s32[4,6]{0,1:T(8,128)S(1)}, s32[4,6]{0,1:T(8,128)S(1)}, u32[]{:S(2)}, u32[]{:S(2)}) collective-permute-start(s32[4,6]{0,1:T(8,128)S(1)} %pad_add_fusion), channel_id=1, source_target_pairs={{0,12},{4,0},{8,4},{12,8},{1,13},{5,1},{9,5},{13,9},{2,14},{6,2},{... | collective-permute-start | bytes 296 | tf_op jit(solution)/shard_map/ppermute | solution.py:425
  3.2 0.6 collective-permute-start.1
  4.0 1.1 constant_dynamic-slice_fusion
  5.0 1.3 collective-permute-start.4
  6.3 0.7 broadcast_multiply_fusion
  7.0 10.6 %shard_map.118 = (f32[2,128,2048]{2,1,0:T(8,128)}, f32[2,128,2048]{2,1,0:T(8,128)}) custom-call(s32[4]{0:T(128)} %get-tuple-element.73.scal.order, bf16[4,16,8,2048]{3,2,1,0:T(8,128)(2,1)} %bitcast.78, bf16[4,16,8,2048]{3,2,1,0:T(8,128)(2,1)} %bitcast.79, bf16[4,16,8,2048]{3,2,1,0:T(8,128)(2,1)} %bitcast.80, bf16[4,16,8,2048]{3,2,1,0:T(8,128)(2,1)} %bitcast.81, ...), custom_call_target="tpu_custom_call" | custom-call | flops 4294967296 | bytes 16777216 | tf_op jit(solution)/shard_map/pallas_call | solution.py:165
  18.4 0.8 copy.38.ss
  19.8 0.6 concatenate.36.scal
  20.4 0.8 copy-done.8
  21.2 7.1 %shard_map.119 = (bf16[256,1024]{1,0:T(8,128)(2,1)}, bf16[256,1024]{1,0:T(8,128)(2,1)}, s32[1,512]{1,0:T(1,128)}, bf16[128,128]{1,0:T(8,128)(2,1)}) custom-call(s32[101]{0:T(128)} %concatenate.36.scal, bf16[512,2048]{1,0:T(8,128)(2,1)} %x.1, s32[1,512]{1,0:T(1,128)} %bitcast.108, s32[512,1]{1,0:T(8,128)} %copy.38.ss), custom_call_target="tpu_custom_call" | custom-call | flops 120000004096 | bytes 4000000 | tf_op jit(solution)/shard_map/pallas_call | solution.py:73
  28.7 0.6 concatenate.35.scal
  29.3 1.1 collective-permute-done.5.core
  30.5 1.1 fusion.18
  31.6 1.5 collective-permute-start.7
  33.1 1.3 fusion.3
  34.4 0.7 collective-permute-start.6
  35.1 10.6 %shard_map.120 = (f32[2,128,2048]{2,1,0:T(8,128)}, f32[2,128,2048]{2,1,0:T(8,128)}) custom-call(s32[4]{0:T(128)} %get-tuple-element.73.scal.order, bf16[4,16,8,2048]{3,2,1,0:T(8,128)(2,1)} %bitcast.82, bf16[4,16,8,2048]{3,2,1,0:T(8,128)(2,1)} %bitcast.83, bf16[4,16,8,2048]{3,2,1,0:T(8,128)(2,1)} %bitcast.84, bf16[4,16,8,2048]{3,2,1,0:T(8,128)(2,1)} %bitcast.85, ...), custom_call_target="tpu_custom_call" | custom-call | flops 4294967296 | bytes 16777216 | tf_op jit(solution)/shard_map/pallas_call | solution.py:165
  45.7 3.5 %shard_map.121.listed = s32[24,33]{1,0:T(8,128)} custom-call(s32[103]{0:T(128)} %concatenate.35.scal), custom_call_target="tpu_custom_call" | custom-call | flops 1000000 | bytes 10000 | tf_op jit(solution)/shard_map/pallas_call | solution.py:283
  49.2 0.8 select_reduce_fusion
  50.0 1.2 collective-permute-done.6.refs_0_
  51.3 2.7 %shard_map.122.x = bf16[128,1024]{1,0:T(8,128)(2,1)} custom-call(s32[4]{0:T(128)} %get-tuple-element.73.scal.order, bf16[2,128,1024]{2,1,0:T(8,128)(2,1)} %bitcast.104, bf16[2,128,1024]{2,1,0:T(8,128)(2,1)} %copy-done.27, bf16[128,1024]{1,0:T(8,128)(2,1)} %collective-permute-done.7.refs_0_), custom_call_target="tpu_custom_call" | custom-call | flops 120000004096 | bytes 1000000 | tf_op jit(solution)/shard_map/pallas_call | solution.py:191
  54.0 1.1 fusion.2
  55.5 4.6 %shard_map.123 = (bf16[2,128,1024]{2,1,0:T(8,128)(2,1)}, bf16[2,128,1024]{2,1,0:T(8,128)(2,1)}) custom-call(s32[101]{0:T(128)} %concatenate.36.scal, bf16[128,1024]{1,0:T(8,128)(2,1)} %shard_map.122.x, bf16[4,2,256,256]{3,2,1,0:T(8,128)(2,1)} %gt.1, bf16[4,2,256,256]{3,2,1,0:T(8,128)(2,1)} %ut.1, s32[1,512]{1,0:T(1,128)} %bitcast.105), custom_call_target="tpu_custom_call" | custom-call | flops 120000004096 | bytes 4000000 | tf_op jit(solution)/shard_map/pallas_call | solution.py:120
  60.7 1.5 collective-permute-start.10
  62.3 1.5 collective-permute-start.15
  63.8 1.1 fusion.17
  64.9 0.7 collective-permute-start.13
  65.6 10.8 %shard_map.124 = (f32[2,128,2048]{2,1,0:T(8,128)}, f32[2,128,2048]{2,1,0:T(8,128)}) custom-call(s32[4]{0:T(128)} %get-tuple-element.73.scal.order, bf16[4,16,8,2048]{3,2,1,0:T(8,128)(2,1)} %bitcast.86, bf16[4,16,8,2048]{3,2,1,0:T(8,128)(2,1)} %bitcast.87, bf16[4,16,8,2048]{3,2,1,0:T(8,128)(2,1)} %bitcast.88, bf16[4,16,8,2048]{3,2,1,0:T(8,128)(2,1)} %bitcast.89, ...), custom_call_target="tpu_custom_call" | custom-call | flops 4294967296 | bytes 16777216 | tf_op jit(solution)/shard_map/pallas_call | solution.py:165
  76.5 6.1 %collective-permute-done.13.refs_0_ = bf16[128,1024]{1,0:T(8,128)(2,1)S(1)} collective-permute-done((bf16[128,1024]{1,0:T(8,128)(2,1)S(1)}, bf16[128,1024]{1,0:T(8,128)(2,1)S(1)}, u32[]{:S(2)}, u32[]{:S(2)}) %collective-permute-start.13) | collective-permute-done | bytes 262176 | tf_op jit(solution)/shard_map/ppermute | solution.py:397
  82.6 0.7 copy-done.33
  83.3 2.5 %shard_map.125.refs_1_ = bf16[128,1024]{1,0:T(8,128)(2,1)} custom-call(s32[4]{0:T(128)} %get-tuple-element.73.scal.order, bf16[2,128,1024]{2,1,0:T(8,128)(2,1)} %get-tuple-element.62.keep, bf16[2,128,1024]{2,1,0:T(8,128)(2,1)} %collective-permute-done.9.core, bf16[128,1024]{1,0:T(8,128)(2,1)} %copy-done.33), custom_call_target="tpu_custom_call" | custom-call | flops 120000004096 | bytes 1000000 | tf_op jit(solution)/shard_map/pallas_call | solution.py:191
  85.9 1.5 collective-permute-start.17
  87.4 0.8 add_select_fusion.refs_2_.refs_11_
  88.2 3.2 %shard_map.126 = bf16[64,2048]{1,0:T(8,128)(2,1)} custom-call(f32[2,128,2048]{2,1,0:T(8,128)} %get-tuple-element.48.keep, f32[2,128,2048]{2,1,0:T(8,128)} %collective-permute-done.3.core, bf16[2,64,2048]{2,1,0:T(8,128)(2,1)} %copy-done.23, bf16[128,1024]{1,0:T(8,128)(2,1)} %shard_map.125.refs_1_, s32[512,1]{1,0:T(8,128)} %add_select_fusion.refs_2_.refs_11_, ...), custom_call_target="tpu_custom_call" | custom-call | flops 1000000000 | bytes 3145728 | tf_op jit(solution)/shard_map/pallas_call | solution.py:236
  91.4 0.7 collective-permute-start.18
  92.1 10.5 %shard_map.127 = (f32[2,128,2048]{2,1,0:T(8,128)}, f32[2,128,2048]{2,1,0:T(8,128)}) custom-call(s32[4]{0:T(128)} %get-tuple-element.73.scal.order, bf16[4,16,8,2048]{3,2,1,0:T(8,128)(2,1)} %bitcast.90, bf16[4,16,8,2048]{3,2,1,0:T(8,128)(2,1)} %bitcast.91, bf16[4,16,8,2048]{3,2,1,0:T(8,128)(2,1)} %bitcast.92, bf16[4,16,8,2048]{3,2,1,0:T(8,128)(2,1)} %bitcast.93, ...), custom_call_target="tpu_custom_call" | custom-call | flops 4294967296 | bytes 16777216 | tf_op jit(solution)/shard_map/pallas_call | solution.py:165
  102.7 3.2 %collective-permute-done.18 = bf16[64,2048]{1,0:T(8,128)(2,1)S(1)} collective-permute-done((bf16[64,2048]{1,0:T(8,128)(2,1)}, bf16[64,2048]{1,0:T(8,128)(2,1)S(1)}, u32[]{:S(2)}, u32[]{:S(2)}) %collective-permute-start.18) | collective-permute-done | bytes 262176 | tf_op jit(solution)/shard_map/ppermute | solution.py:397
  105.9 3.4 %shard_map.128 = bf16[64,2048]{1,0:T(8,128)(2,1)} custom-call(f32[2,128,2048]{2,1,0:T(8,128)} %get-tuple-element.57.keep, f32[2,128,2048]{2,1,0:T(8,128)} %copy-done.22, bf16[2,64,2048]{2,1,0:T(8,128)(2,1)} %collective-permute-done.15.refs_0_, bf16[128,1024]{1,0:T(8,128)(2,1)} %shard_map.125.refs_1_, s32[512,1]{1,0:T(8,128)} %add_select_fusion.refs_2_.refs_11_, ...), custom_call_target="tpu_custom_call" | custom-call | flops 120000004096 | bytes 3145728 | tf_op jit(solution)/shard_map/pallas_call | solution.py:236
  109.4 1.5 collective-permute-start.22
  111.1 0.7 collective-permute-start.20
  111.8 7.0 %collective-permute-done.22 = bf16[64,2048]{1,0:T(8,128)(2,1)S(1)} collective-permute-done((bf16[64,2048]{1,0:T(8,128)(2,1)}, bf16[64,2048]{1,0:T(8,128)(2,1)S(1)}, u32[]{:S(2)}, u32[]{:S(2)}) %collective-permute-start.22) | collective-permute-done | bytes 262176 | tf_op jit(solution)/shard_map/ppermute | solution.py:397
  119.0 3.3 %shard_map.129 = bf16[64,2048]{1,0:T(8,128)(2,1)} custom-call(f32[2,128,2048]{2,1,0:T(8,128)} %get-tuple-element.69.keep, f32[2,128,2048]{2,1,0:T(8,128)} %copy-done.4, bf16[2,64,2048]{2,1,0:T(8,128)(2,1)} %copy-done.24, bf16[128,1024]{1,0:T(8,128)(2,1)} %shard_map.125.refs_1_, s32[512,1]{1,0:T(8,128)} %add_select_fusion.refs_2_.refs_11_, ...), custom_call_target="tpu_custom_call" | custom-call | flops 1000000000 | bytes 3145728 | tf_op jit(solution)/shard_map/pallas_call | solution.py:236
  122.3 1.5 collective-permute-start.27
  123.8 6.3 %collective-permute-done.20.refs_0_ = bf16[2,64,2048]{2,1,0:T(8,128)(2,1)S(1)} collective-permute-done((bf16[2,64,2048]{2,1,0:T(8,128)(2,1)S(1)}, bf16[2,64,2048]{2,1,0:T(8,128)(2,1)S(1)}, u32[]{:S(2)}, u32[]{:S(2)}) %collective-permute-start.20) | collective-permute-done | bytes 524320 | tf_op jit(solution)/shard_map/ppermute | solution.py:397
  130.1 0.8 copy-done.25
  130.9 3.2 %shard_map.130 = bf16[64,2048]{1,0:T(8,128)(2,1)} custom-call(f32[2,128,2048]{2,1,0:T(8,128)} %get-tuple-element.78.keep, f32[2,128,2048]{2,1,0:T(8,128)} %copy-done.6, bf16[2,64,2048]{2,1,0:T(8,128)(2,1)} %copy-done.25, bf16[128,1024]{1,0:T(8,128)(2,1)} %shard_map.125.refs_1_, s32[512,1]{1,0:T(8,128)} %add_select_fusion.refs_2_.refs_11_, ...), custom_call_target="tpu_custom_call" | custom-call | flops 1000000000 | bytes 3145728 | tf_op jit(solution)/shard_map/pallas_call | solution.py:236
  134.1 1.4 collective-permute-start.29
  135.5 0.8 copy-done.19
  136.3 0.8 copy-done.20
  137.1 14.4 %shard_map.131 = f32[256,2048]{1,0:T(8,128)} custom-call(s32[24,33]{1,0:T(8,128)} %shard_map.121.listed, bf16[128,2048]{1,0:T(8,128)(2,1)} %copy-done.19, bf16[128,2048]{1,0:T(8,128)(2,1)} %copy-done.20, bf16[128,2048]{1,0:T(8,128)(2,1)} %copy-done.14, bf16[128,2048]{1,0:T(8,128)(2,1)} %copy-done.15, bf16[4096,2048]{1,0:T(8,128)(2,1)} %refs_4_.11, ...), custom_call_target="tpu_custom_call" | custom-call | flops 1000000000 | bytes 1000000 | tf_op jit(solution)/shard_map/pallas_call | solution.py:339
  151.8 0.5 collective-permute-start.30
  152.4 1.1 copy-done.1
  153.6 3.2 %collective-permute-start.26 = (bf16[4,16,2048]{2,1,0:T(8,128)(2,1)S(1)}, bf16[4,16,2048]{2,1,0:T(8,128)(2,1)S(1)}, u32[]{:S(2)}, u32[]{:S(2)}) collective-permute-start(bf16[4,16,2048]{2,1,0:T(8,128)(2,1)S(1)} %get-tuple-element.95), channel_id=1, source_target_pairs={{0,3},{1,0},{2,1},{3,2},{4,7},{5,4},{6,5},{7,6},{8,11},{9,8},{10,9... | collective-permute-start | bytes 786440 | tf_op jit(solution)/shard_map/ppermute | solution.py:573
  157.5 14.4 %shard_map.132 = f32[256,2048]{1,0:T(8,128)} custom-call(s32[24,33]{1,0:T(8,128)} %shard_map.121.listed, bf16[128,2048]{1,0:T(8,128)(2,1)} %collective-permute-done.28.refs_0_, bf16[128,2048]{1,0:T(8,128)(2,1)} %collective-permute-done.30.refs_1_, bf16[128,2048]{1,0:T(8,128)(2,1)} %copy-done.12, bf16[128,2048]{1,0:T(8,128)(2,1)} %copy-done.13, ...), custom_call_target="tpu_custom_call" | custom-call | flops 1000000000 | bytes 1000000 | tf_op jit(solution)/shard_map/pallas_call | solution.py:339
  171.9 1.5 fusion.15
  173.4 3.0 %collective-permute-start.33 = (bf16[4,16,2048]{2,1,0:T(8,128)(2,1)S(1)}, bf16[4,16,2048]{2,1,0:T(8,128)(2,1)S(1)}, u32[]{:S(2)}, u32[]{:S(2)}) collective-permute-start(bf16[4,16,2048]{2,1,0:T(8,128)(2,1)S(1)} %get-tuple-element.89), channel_id=1, source_target_pairs={{0,3},{1,0},{2,1},{3,2},{4,7},{5,4},{6,5},{7,6},{8,11},{9,8},{10,9... | collective-permute-start | bytes 786440 | tf_op jit(solution)/shard_map/ppermute | solution.py:573
  176.4 5.0 %collective-permute-done.25 = bf16[4,16,2048]{2,1,0:T(8,128)(2,1)S(1)} collective-permute-done((bf16[4,16,2048]{2,1,0:T(8,128)(2,1)S(1)}, bf16[4,16,2048]{2,1,0:T(8,128)(2,1)S(1)}, u32[]{:S(2)}, u32[]{:S(2)}) %collective-permute-start.25) | collective-permute-done | bytes 262176 | tf_op jit(solution)/shard_map/ppermute | solution.py:573
  181.4 9.9 %collective-permute-start.31 = (bf16[4,16,2048]{2,1,0:T(8,128)(2,1)S(1)}, bf16[4,16,2048]{2,1,0:T(8,128)(2,1)}, u32[]{:S(2)}, u32[]{:S(2)}) collective-permute-start(bf16[4,16,2048]{2,1,0:T(8,128)(2,1)S(1)} %get-tuple-element.87), channel_id=1, source_target_pairs={{0,1},{1,2},{2,3},{3,0},{4,5},{5,6},{6,7},{7,4},{8,9},{9,10},{10,1... | collective-permute-start | bytes 786440 | tf_op jit(solution)/shard_map/ppermute | solution.py:573
  191.4 0.6 gather_fusion
  192.0 9.7 %collective-permute-done.32 = bf16[4,16,2048]{2,1,0:T(8,128)(2,1)} collective-permute-done((bf16[4,16,2048]{2,1,0:T(8,128)(2,1)S(1)}, bf16[4,16,2048]{2,1,0:T(8,128)(2,1)}, u32[]{:S(2)}, u32[]{:S(2)}) %collective-permute-start.32) | collective-permute-done | bytes 262176 | tf_op jit(solution)/shard_map/ppermute | solution.py:573
  201.7 1.3 fusion.6
  203.0 0.6 gather_fusion.1
  203.7 0.8 pad_maximum_fusion.4
  (132 shorter events, 5.0 us)
Async XLA Ops:
  0.7 18.5 %collective-permute-start = (s32[4,6]{0,1:T(8,128)S(1)}, s32[4,6]{0,1:T(8,128)S(1)}, u32[]{:S(2)}, u32[]{:S(2)}) collective-permute-start(s32[4,6]{0,1:T(8,128)S(1)} %pad_add_fusion), channel_id=1, source_target_pairs={{0,12},{4,0},{8,4},{12,8},{1,13},{5,1},{9,5},{13,9},{2,14},{6,2},{... | collective-permute-start | bytes 296 | tf_op jit(solution)/shard_map/ppermute | solution.py:425
  3.2 16.3 %collective-permute-start.1 = (s32[4,6]{0,1:T(8,128)S(1)}, s32[4,6]{0,1:T(8,128)S(1)}, u32[]{:S(2)}, u32[]{:S(2)}) collective-permute-start(s32[4,6]{0,1:T(8,128)S(1)} %pad_add_fusion), channel_id=1, source_target_pairs={{0,8},{4,12},{8,0},{12,4},{1,9},{5,13},{9,1},{13,5},{2,10},{6,14},... | collective-permute-start | bytes 296 | tf_op jit(solution)/shard_map/ppermute | solution.py:425
  3.8 15.8 %collective-permute-start.2 = (s32[4,6]{0,1:T(8,128)S(1)}, s32[4,6]{0,1:T(8,128)S(1)}, u32[]{:S(2)}, u32[]{:S(2)}) collective-permute-start(s32[4,6]{0,1:T(8,128)S(1)} %pad_add_fusion), channel_id=1, source_target_pairs={{0,4},{4,8},{8,12},{12,0},{1,5},{5,9},{9,13},{13,1},{2,6},{6,10},{... | collective-permute-start | bytes 296 | tf_op jit(solution)/shard_map/ppermute | solution.py:425
  5.0 15.4 %collective-permute-start.4 = (bf16[4,256,256]{2,1,0:T(8,128)(2,1)S(1)}, bf16[4,256,256]{2,1,0:T(8,128)(2,1)S(1)}, u32[]{:S(2)}, u32[]{:S(2)}) collective-permute-start(bf16[4,256,256]{2,1,0:T(8,128)(2,1)S(1)} %constant_dynamic-slice_fusion), channel_id=1, source_target_pairs={{0,8},{4,12},{8,0},{12,4},{1,9},{5,13},{9,1},{13,5},{2,10},{6,14},... | collective-permute-start | bytes 1572872 | tf_op jit(solution)/shard_map/ppermute | solution.py:397
  7.0 11.3 %copy-start.31 = (s32[512]{0:T(512)S(1)}, s32[512]{0:T(512)}, u32[]{:S(2)}) copy-start(s32[512]{0:T(512)} %param.24) | copy-start | bytes 6148
  7.0 11.3 %copy-start.32 = (s32[16]{0:T(128)S(1)}, s32[16]{0:T(128)}, u32[]{:S(2)}) copy-start(s32[16]{0:T(128)} %param.25) | copy-start | bytes 196
  17.7 15.4 %collective-permute-start.3 = (f32[2,128,2048]{2,1,0:T(8,128)}, f32[2,128,2048]{2,1,0:T(8,128)}, u32[]{:S(2)}, u32[]{:S(2)}) collective-permute-start(f32[2,128,2048]{2,1,0:T(8,128)} %get-tuple-element.49), channel_id=1, source_target_pairs={{0,4},{4,0},{8,12},{12,8},{1,5},{5,1},{9,13},{13,9},{2,6},{6,2},{1... | collective-permute-start | bytes 6291464 | tf_op jit(solution)/shard_map/ppermute | solution.py:394
  18.4 2.8 %copy-start.29 = (s32[512]{0:T(512)}, s32[512]{0:T(512)S(1)}, u32[]{:S(2)}) copy-start(s32[512]{0:T(512)S(1)} %select_reduce_fusion.1) | copy-start | bytes 6148
  21.2 11.9 %copy-start.2 = (f32[2,128,2048]{2,1,0:T(8,128)S(1)}, f32[2,128,2048]{2,1,0:T(8,128)}, u32[]{:S(2)}) copy-start(f32[2,128,2048]{2,1,0:T(8,128)} %get-tuple-element.48.keep) | copy-start | bytes 6291460
  28.3 2.1 %collective-permute-start.5 = (bf16[2,128,1024]{2,1,0:T(8,128)(2,1)}, bf16[2,128,1024]{2,1,0:T(8,128)(2,1)S(1)}, u32[]{:S(2)}, u32[]{:S(2)}) collective-permute-start(bf16[2,128,1024]{2,1,0:T(8,128)(2,1)} %bitcast.110), channel_id=1, source_target_pairs={{0,4},{4,0},{8,12},{12,8},{1,5},{5,1},{9,13},{13,9},{2,6},{6,2},{1... | collective-permute-start | bytes 1572872 | tf_op jit(solution)/shard_map/ppermute | solution.py:394
  30.5 2.6 %copy-start.27 = (bf16[2,128,1024]{2,1,0:T(8,128)(2,1)}, bf16[2,128,1024]{2,1,0:T(8,128)(2,1)S(1)}, u32[]{:S(2)}) copy-start(bf16[2,128,1024]{2,1,0:T(8,128)(2,1)S(1)} %collective-permute-done.5.core) | copy-start | bytes 1572868
  31.6 19.7 %collective-permute-start.7 = (bf16[128,1024]{1,0:T(8,128)(2,1)S(1)}, bf16[128,1024]{1,0:T(8,128)(2,1)}, u32[]{:S(2)}, u32[]{:S(2)}) collective-permute-start(bf16[128,1024]{1,0:T(8,128)(2,1)S(1)} %fusion.18), channel_id=1, source_target_pairs={{0,8},{4,12},{8,0},{12,4},{1,9},{5,13},{9,1},{13,5},{2,10},{6,14},... | collective-permute-start | bytes 786440 | tf_op jit(solution)/shard_map/ppermute | solution.py:397
  34.4 14.8 %copy-start.30 = (s32[1,512]{1,0:T(1,128)S(1)}, s32[1,512]{1,0:T(1,128)}, u32[]{:S(2)}) copy-start(s32[1,512]{1,0:T(1,128)} %get-tuple-element.61) | copy-start | bytes 6148
  34.4 16.8 %collective-permute-start.6 = (bf16[2,64,2048]{2,1,0:T(8,128)(2,1)S(1)}, bf16[2,64,2048]{2,1,0:T(8,128)(2,1)S(1)}, u32[]{:S(2)}, u32[]{:S(2)}) collective-permute-start(bf16[2,64,2048]{2,1,0:T(8,128)(2,1)S(1)} %fusion.3), channel_id=1, source_target_pairs={{0,8},{4,12},{8,0},{12,4},{1,9},{5,13},{9,1},{13,5},{2,10},{6,14},... | collective-permute-start | bytes 1572872 | tf_op jit(solution)/shard_map/ppermute | solution.py:397
  45.7 8.2 %collective-permute-start.8 = (f32[2,128,2048]{2,1,0:T(8,128)}, f32[2,128,2048]{2,1,0:T(8,128)S(1)}, u32[]{:S(2)}, u32[]{:S(2)}) collective-permute-start(f32[2,128,2048]{2,1,0:T(8,128)} %get-tuple-element.58), channel_id=1, source_target_pairs={{0,4},{4,0},{8,12},{12,8},{1,5},{5,1},{9,13},{13,9},{2,6},{6,2},{1... | collective-permute-start | bytes 6291464 | tf_op jit(solution)/shard_map/ppermute | solution.py:394
  51.3 2.7 %copy-start.23 = (bf16[2,64,2048]{2,1,0:T(8,128)(2,1)}, bf16[2,64,2048]{2,1,0:T(8,128)(2,1)S(1)}, u32[]{:S(2)}) copy-start(bf16[2,64,2048]{2,1,0:T(8,128)(2,1)S(1)} %collective-permute-done.6.refs_0_) | copy-start | bytes 1572868
  51.3 2.7 %copy-start.21 = (f32[2,128,2048]{2,1,0:T(8,128)S(1)}, f32[2,128,2048]{2,1,0:T(8,128)}, u32[]{:S(2)}) copy-start(f32[2,128,2048]{2,1,0:T(8,128)} %get-tuple-element.57.keep) | copy-start | bytes 6291460
  54.0 1.6 copy-start.22
  55.5 4.7 %copy-start = (bf16[4,2,256,256]{3,2,1,0:T(8,128)(2,1)S(1)}, bf16[4,2,256,256]{3,2,1,0:T(8,128)(2,1)}, u32[]{:S(2)}) copy-start(bf16[4,2,256,256]{3,2,1,0:T(8,128)(2,1)} %param.20) | copy-start | bytes 3145732
  55.5 5.2 %copy-start.9 = (bf16[4,256,256]{2,1,0:T(8,128)(2,1)S(1)}, bf16[4,256,256]{2,1,0:T(8,128)(2,1)}, u32[]{:S(2)}) copy-start(bf16[4,256,256]{2,1,0:T(8,128)(2,1)} %copy-done.8) | copy-start | bytes 1572868
  55.5 6.7 %copy-start.28 = (s32[512]{0:T(512)S(1)}, s32[512]{0:T(512)}, u32[]{:S(2)}) copy-start(s32[512]{0:T(512)} %select_reduce_fusion) | copy-start | bytes 6148
  60.2 3.6 %collective-permute-start.9 = (bf16[2,128,1024]{2,1,0:T(8,128)(2,1)}, bf16[2,128,1024]{2,1,0:T(8,128)(2,1)}, u32[]{:S(2)}, u32[]{:S(2)}) collective-permute-start(bf16[2,128,1024]{2,1,0:T(8,128)(2,1)} %get-tuple-element.63), channel_id=1, source_target_pairs={{0,4},{4,0},{8,12},{12,8},{1,5},{5,1},{9,13},{13,9},{2,6},{6,2},{1... | collective-permute-start | bytes 1572872 | tf_op jit(solution)/shard_map/ppermute | solution.py:394
  60.2 16.3 %collective-permute-start.12 = (bf16[8,256,256]{2,1,0:T(8,128)(2,1)S(1)}, bf16[8,256,256]{2,1,0:T(8,128)(2,1)S(1)}, u32[]{:S(2)}, u32[]{:S(2)}) collective-permute-start(bf16[8,256,256]{2,1,0:T(8,128)(2,1)S(1)} %bitcast.97), channel_id=1, source_target_pairs={{0,4},{4,0},{8,12},{12,8},{1,5},{5,1},{9,13},{13,9},{2,6},{6,2},{1... | collective-permute-start | bytes 3145736 | tf_op jit(solution)/shard_map/ppermute | solution.py:394
  60.7 15.7 %collective-permute-start.10 = (bf16[4,256,256]{2,1,0:T(8,128)(2,1)S(1)}, bf16[4,256,256]{2,1,0:T(8,128)(2,1)S(1)}, u32[]{:S(2)}, u32[]{:S(2)}) collective-permute-start(bf16[4,256,256]{2,1,0:T(8,128)(2,1)S(1)} %copy-done.9), channel_id=1, source_target_pairs={{0,16},{16,0},{1,17},{17,1},{2,18},{18,2},{3,19},{19,3},{4,20},{20... | collective-permute-start | bytes 1572872 | tf_op jit(solution)/shard_map/ppermute | solution.py:502
  62.2 14.3 %collective-permute-start.11 = (bf16[4,256,256]{2,1,0:T(8,128)(2,1)S(1)}, bf16[4,256,256]{2,1,0:T(8,128)(2,1)}, u32[]{:S(2)}, u32[]{:S(2)}) collective-permute-start(bf16[4,256,256]{2,1,0:T(8,128)(2,1)S(1)} %copy-done.9), channel_id=1, source_target_pairs={{0,4},{4,0},{8,12},{12,8},{1,5},{5,1},{9,13},{13,9},{2,6},{6,2},{1... | collective-permute-start | bytes 1572872 | tf_op jit(solution)/shard_map/ppermute | solution.py:394
  62.3 29.8 %collective-permute-start.15 = (bf16[2,64,2048]{2,1,0:T(8,128)(2,1)}, bf16[2,64,2048]{2,1,0:T(8,128)(2,1)}, u32[]{:S(2)}, u32[]{:S(2)}) collective-permute-start(bf16[2,64,2048]{2,1,0:T(8,128)(2,1)} %fusion.2), channel_id=1, source_target_pairs={{0,8},{4,12},{8,0},{12,4},{1,9},{5,13},{9,1},{13,5},{2,10},{6,14},... | collective-permute-start | bytes 1572872 | tf_op jit(solution)/shard_map/ppermute | solution.py:397
  64.9 17.7 %collective-permute-start.13 = (bf16[128,1024]{1,0:T(8,128)(2,1)S(1)}, bf16[128,1024]{1,0:T(8,128)(2,1)S(1)}, u32[]{:S(2)}, u32[]{:S(2)}) collective-permute-start(bf16[128,1024]{1,0:T(8,128)(2,1)S(1)} %fusion.17), channel_id=1, source_target_pairs={{0,8},{4,12},{8,0},{12,4},{1,9},{5,13},{9,1},{13,5},{2,10},{6,14},... | collective-permute-start | bytes 786440 | tf_op jit(solution)/shard_map/ppermute | solution.py:397
  76.3 9.4 %copy-start.10 = (bf16[4,256,256]{2,1,0:T(8,128)(2,1)}, bf16[4,256,256]{2,1,0:T(8,128)(2,1)S(1)}, u32[]{:S(2)}) copy-start(bf16[4,256,256]{2,1,0:T(8,128)(2,1)S(1)} %collective-permute-done.10.refs_6_) | copy-start | bytes 1572868
  76.4 9.4 %collective-permute-start.14 = (f32[2,128,2048]{2,1,0:T(8,128)}, f32[2,128,2048]{2,1,0:T(8,128)S(1)}, u32[]{:S(2)}, u32[]{:S(2)}) collective-permute-start(f32[2,128,2048]{2,1,0:T(8,128)} %get-tuple-element.70), channel_id=1, source_target_pairs={{0,4},{4,0},{8,12},{12,8},{1,5},{5,1},{9,13},{13,9},{2,6},{6,2},{1... | collective-permute-start | bytes 6291464 | tf_op jit(solution)/shard_map/ppermute | solution.py:394
  76.5 9.3 %copy-start.7 = (bf16[8,256,256]{2,1,0:T(8,128)(2,1)}, bf16[8,256,256]{2,1,0:T(8,128)(2,1)S(1)}, u32[]{:S(2)}) copy-start(bf16[8,256,256]{2,1,0:T(8,128)(2,1)S(1)} %collective-permute-done.12.refs_10_) | copy-start | bytes 3145732
  76.5 9.3 %copy-start.3 = (f32[2,128,2048]{2,1,0:T(8,128)S(1)}, f32[2,128,2048]{2,1,0:T(8,128)}, u32[]{:S(2)}) copy-start(f32[2,128,2048]{2,1,0:T(8,128)} %get-tuple-element.69.keep) | copy-start | bytes 6291460
  85.8 16.9 %collective-permute-start.19 = (bf16[4,256,256]{2,1,0:T(8,128)(2,1)S(1)}, bf16[4,256,256]{2,1,0:T(8,128)(2,1)S(1)}, u32[]{:S(2)}, u32[]{:S(2)}) collective-permute-start(bf16[4,256,256]{2,1,0:T(8,128)(2,1)S(1)} %collective-permute-done.10.refs_6_), channel_id=1, source_target_pairs={{0,4},{4,0},{8,12},{12,8},{1,5},{5,1},{9,13},{13,9},{2,6},{6,2},{1... | collective-permute-start | bytes 1572872 | tf_op jit(solution)/shard_map/ppermute | solution.py:394
  85.8 5.6 %copy-start.4 = (f32[2,128,2048]{2,1,0:T(8,128)}, f32[2,128,2048]{2,1,0:T(8,128)S(1)}, u32[]{:S(2)}) copy-start(f32[2,128,2048]{2,1,0:T(8,128)S(1)} %collective-permute-done.14.core) | copy-start | bytes 6291460
  85.9 20.0 %collective-permute-start.17 = (bf16[2,64,2048]{2,1,0:T(8,128)(2,1)S(1)}, bf16[2,64,2048]{2,1,0:T(8,128)(2,1)S(1)}, u32[]{:S(2)}, u32[]{:S(2)}) collective-permute-start(bf16[2,64,2048]{2,1,0:T(8,128)(2,1)S(1)} %fusion.1), channel_id=1, source_target_pairs={{0,8},{4,12},{8,0},{12,4},{1,9},{5,13},{9,1},{13,5},{2,10},{6,14},... | collective-permute-start | bytes 1572872 | tf_op jit(solution)/shard_map/ppermute | solution.py:397
  91.4 14.5 %collective-permute-start.18 = (bf16[64,2048]{1,0:T(8,128)(2,1)}, bf16[64,2048]{1,0:T(8,128)(2,1)S(1)}, u32[]{:S(2)}, u32[]{:S(2)}) collective-permute-start(bf16[64,2048]{1,0:T(8,128)(2,1)} %shard_map.126), channel_id=1, source_target_pairs={{0,8},{4,12},{8,0},{12,4},{1,9},{5,13},{9,1},{13,5},{2,10},{6,14},... | collective-permute-start | bytes 786440 | tf_op jit(solution)/shard_map/ppermute | solution.py:397
  102.6 8.4 %collective-permute-start.16 = (f32[2,128,2048]{2,1,0:T(8,128)}, f32[2,128,2048]{2,1,0:T(8,128)S(1)}, u32[]{:S(2)}, u32[]{:S(2)}) collective-permute-start(f32[2,128,2048]{2,1,0:T(8,128)} %get-tuple-element.75), channel_id=1, source_target_pairs={{0,4},{4,0},{8,12},{12,8},{1,5},{5,1},{9,13},{13,9},{2,6},{6,2},{1... | collective-permute-start | bytes 6291464 | tf_op jit(solution)/shard_map/ppermute | solution.py:394
  102.7 6.7 %copy-start.11 = (bf16[4,256,256]{2,1,0:T(8,128)(2,1)}, bf16[4,256,256]{2,1,0:T(8,128)(2,1)S(1)}, u32[]{:S(2)}) copy-start(bf16[4,256,256]{2,1,0:T(8,128)(2,1)S(1)} %collective-permute-done.19.refs_9_) | copy-start | bytes 1572868
  105.9 3.4 %copy-start.24 = (bf16[2,64,2048]{2,1,0:T(8,128)(2,1)}, bf16[2,64,2048]{2,1,0:T(8,128)(2,1)S(1)}, u32[]{:S(2)}) copy-start(bf16[2,64,2048]{2,1,0:T(8,128)(2,1)S(1)} %collective-permute-done.17.refs_0_) | copy-start | bytes 1572868
  105.9 4.9 %copy-start.16 = (bf16[64,2048]{1,0:T(8,128)(2,1)S(1)}, bf16[64,2048]{1,0:T(8,128)(2,1)}, u32[]{:S(2)}) copy-start(bf16[64,2048]{1,0:T(8,128)(2,1)} %shard_map.126) | copy-start | bytes 786436
  105.9 5.1 %copy-start.5 = (f32[2,128,2048]{2,1,0:T(8,128)S(1)}, f32[2,128,2048]{2,1,0:T(8,128)}, u32[]{:S(2)}) copy-start(f32[2,128,2048]{2,1,0:T(8,128)} %get-tuple-element.78.keep) | copy-start | bytes 6291460
  109.4 9.5 %copy-start.26 = (bf16[64,2048]{1,0:T(8,128)(2,1)S(1)}, bf16[64,2048]{1,0:T(8,128)(2,1)}, u32[]{:S(2)}) copy-start(bf16[64,2048]{1,0:T(8,128)(2,1)} %shard_map.128) | copy-start | bytes 786436
  109.4 9.5 %collective-permute-start.22 = (bf16[64,2048]{1,0:T(8,128)(2,1)}, bf16[64,2048]{1,0:T(8,128)(2,1)S(1)}, u32[]{:S(2)}, u32[]{:S(2)}) collective-permute-start(bf16[64,2048]{1,0:T(8,128)(2,1)} %shard_map.128), channel_id=1, source_target_pairs={{0,8},{4,12},{8,0},{12,4},{1,9},{5,13},{9,1},{13,5},{2,10},{6,14},... | collective-permute-start | bytes 786440 | tf_op jit(solution)/shard_map/ppermute | solution.py:397
  110.9 11.4 %copy-start.14 = (bf16[128,2048]{1,0:T(8,128)(2,1)}, bf16[128,2048]{1,0:T(8,128)(2,1)S(1)}, u32[]{:S(2)}) copy-start(bf16[128,2048]{1,0:T(8,128)(2,1)S(1)} %pad_maximum_fusion.refs_2_) | copy-start | bytes 1572868
  110.9 24.6 %collective-permute-start.21 = (bf16[128,2048]{1,0:T(8,128)(2,1)S(1)}, bf16[128,2048]{1,0:T(8,128)(2,1)S(1)}, u32[]{:S(2)}, u32[]{:S(2)}) collective-permute-start(bf16[128,2048]{1,0:T(8,128)(2,1)S(1)} %pad_maximum_fusion.refs_2_), channel_id=1, source_target_pairs={{0,4},{4,0},{8,12},{12,8},{1,5},{5,1},{9,13},{13,9},{2,6},{6,2},{1... | collective-permute-start | bytes 1572872 | tf_op jit(solution)/shard_map/ppermute | solution.py:394
  111.0 11.3 %copy-start.6 = (f32[2,128,2048]{2,1,0:T(8,128)}, f32[2,128,2048]{2,1,0:T(8,128)S(1)}, u32[]{:S(2)}) copy-start(f32[2,128,2048]{2,1,0:T(8,128)S(1)} %collective-permute-done.16.core) | copy-start | bytes 6291460
  111.1 19.0 %collective-permute-start.20 = (bf16[2,64,2048]{2,1,0:T(8,128)(2,1)S(1)}, bf16[2,64,2048]{2,1,0:T(8,128)(2,1)S(1)}, u32[]{:S(2)}, u32[]{:S(2)}) collective-permute-start(bf16[2,64,2048]{2,1,0:T(8,128)(2,1)S(1)} %fusion), channel_id=1, source_target_pairs={{0,8},{4,12},{8,0},{12,4},{1,9},{5,13},{9,1},{13,5},{2,10},{6,14},... | collective-permute-start | bytes 1572872 | tf_op jit(solution)/shard_map/ppermute | solution.py:397
  118.9 3.4 %copy-start.15 = (bf16[128,2048]{1,0:T(8,128)(2,1)}, bf16[128,2048]{1,0:T(8,128)(2,1)S(1)}, u32[]{:S(2)}) copy-start(bf16[128,2048]{1,0:T(8,128)(2,1)S(1)} %pad_maximum_fusion.1.refs_3_) | copy-start | bytes 1572868
  118.9 16.6 %collective-permute-start.23 = (bf16[128,2048]{1,0:T(8,128)(2,1)S(1)}, bf16[128,2048]{1,0:T(8,128)(2,1)S(1)}, u32[]{:S(2)}, u32[]{:S(2)}) collective-permute-start(bf16[128,2048]{1,0:T(8,128)(2,1)S(1)} %pad_maximum_fusion.1.refs_3_), channel_id=1, source_target_pairs={{0,4},{4,0},{8,12},{12,8},{1,5},{5,1},{9,13},{13,9},{2,6},{6,2},{1... | collective-permute-start | bytes 1572872 | tf_op jit(solution)/shard_map/ppermute | solution.py:394
  122.3 29.2 %collective-permute-start.27 = (bf16[64,2048]{1,0:T(8,128)(2,1)}, bf16[64,2048]{1,0:T(8,128)(2,1)S(1)}, u32[]{:S(2)}, u32[]{:S(2)}) collective-permute-start(bf16[64,2048]{1,0:T(8,128)(2,1)} %shard_map.129), channel_id=1, source_target_pairs={{0,8},{4,12},{8,0},{12,4},{1,9},{5,13},{9,1},{13,5},{2,10},{6,14},... | collective-permute-start | bytes 786440 | tf_op jit(solution)/shard_map/ppermute | solution.py:397
  134.1 17.5 %copy-start.17 = (bf16[64,2048]{1,0:T(8,128)(2,1)S(1)}, bf16[64,2048]{1,0:T(8,128)(2,1)}, u32[]{:S(2)}) copy-start(bf16[64,2048]{1,0:T(8,128)(2,1)} %shard_map.129) | copy-start | bytes 786436
  134.1 17.6 %copy-start.18 = (bf16[64,2048]{1,0:T(8,128)(2,1)S(1)}, bf16[64,2048]{1,0:T(8,128)(2,1)}, u32[]{:S(2)}) copy-start(bf16[64,2048]{1,0:T(8,128)(2,1)} %shard_map.130) | copy-start | bytes 786436
  134.1 17.6 %collective-permute-start.29 = (bf16[64,2048]{1,0:T(8,128)(2,1)}, bf16[64,2048]{1,0:T(8,128)(2,1)S(1)}, u32[]{:S(2)}, u32[]{:S(2)}) collective-permute-start(bf16[64,2048]{1,0:T(8,128)(2,1)} %shard_map.130), channel_id=1, source_target_pairs={{0,8},{4,12},{8,0},{12,4},{1,9},{5,13},{9,1},{13,5},{2,10},{6,14},... | collective-permute-start | bytes 786440 | tf_op jit(solution)/shard_map/ppermute | solution.py:397
  136.3 0.8 copy-start.20
  151.5 2.0 copy-start.1
  151.6 5.9 %copy-start.12 = (bf16[128,2048]{1,0:T(8,128)(2,1)}, bf16[128,2048]{1,0:T(8,128)(2,1)S(1)}, u32[]{:S(2)}) copy-start(bf16[128,2048]{1,0:T(8,128)(2,1)S(1)} %pad_maximum_fusion.2.refs_2_) | copy-start | bytes 1572868
  151.6 5.8 %collective-permute-start.28 = (bf16[128,2048]{1,0:T(8,128)(2,1)S(1)}, bf16[128,2048]{1,0:T(8,128)(2,1)}, u32[]{:S(2)}, u32[]{:S(2)}) collective-permute-start(bf16[128,2048]{1,0:T(8,128)(2,1)S(1)} %pad_maximum_fusion.2.refs_2_), channel_id=1, source_target_pairs={{0,4},{4,0},{8,12},{12,8},{1,5},{5,1},{9,13},{13,9},{2,6},{6,2},{1... | collective-permute-start | bytes 1572872 | tf_op jit(solution)/shard_map/ppermute | solution.py:394
  151.8 5.7 %copy-start.13 = (bf16[128,2048]{1,0:T(8,128)(2,1)}, bf16[128,2048]{1,0:T(8,128)(2,1)S(1)}, u32[]{:S(2)}) copy-start(bf16[128,2048]{1,0:T(8,128)(2,1)S(1)} %pad_maximum_fusion.3.refs_3_) | copy-start | bytes 1572868
  151.8 5.7 %collective-permute-start.30 = (bf16[128,2048]{1,0:T(8,128)(2,1)S(1)}, bf16[128,2048]{1,0:T(8,128)(2,1)}, u32[]{:S(2)}, u32[]{:S(2)}) collective-permute-start(bf16[128,2048]{1,0:T(8,128)(2,1)S(1)} %pad_maximum_fusion.3.refs_3_), channel_id=1, source_target_pairs={{0,4},{4,0},{8,12},{12,8},{1,5},{5,1},{9,13},{13,9},{2,6},{6,2},{1... | collective-permute-start | bytes 1572872 | tf_op jit(solution)/shard_map/ppermute | solution.py:394
  153.6 19.8 %collective-permute-start.26 = (bf16[4,16,2048]{2,1,0:T(8,128)(2,1)S(1)}, bf16[4,16,2048]{2,1,0:T(8,128)(2,1)S(1)}, u32[]{:S(2)}, u32[]{:S(2)}) collective-permute-start(bf16[4,16,2048]{2,1,0:T(8,128)(2,1)S(1)} %get-tuple-element.95), channel_id=1, source_target_pairs={{0,3},{1,0},{2,1},{3,2},{4,7},{5,4},{6,5},{7,6},{8,11},{9,8},{10,9... | collective-permute-start | bytes 786440 | tf_op jit(solution)/shard_map/ppermute | solution.py:573
  156.8 24.6 %collective-permute-start.25 = (bf16[4,16,2048]{2,1,0:T(8,128)(2,1)S(1)}, bf16[4,16,2048]{2,1,0:T(8,128)(2,1)S(1)}, u32[]{:S(2)}, u32[]{:S(2)}) collective-permute-start(bf16[4,16,2048]{2,1,0:T(8,128)(2,1)S(1)} %get-tuple-element.96), channel_id=1, source_target_pairs={{0,2},{1,3},{2,0},{3,1},{4,6},{5,7},{6,4},{7,5},{8,10},{9,11},{10,... | collective-permute-start | bytes 786440 | tf_op jit(solution)/shard_map/ppermute | solution.py:573
  157.0 24.4 %collective-permute-start.24 = (bf16[4,16,2048]{2,1,0:T(8,128)(2,1)S(1)}, bf16[4,16,2048]{2,1,0:T(8,128)(2,1)S(1)}, u32[]{:S(2)}, u32[]{:S(2)}) collective-permute-start(bf16[4,16,2048]{2,1,0:T(8,128)(2,1)S(1)} %get-tuple-element.94), channel_id=1, source_target_pairs={{0,1},{1,2},{2,3},{3,0},{4,5},{5,6},{6,7},{7,4},{8,9},{9,10},{10,1... | collective-permute-start | bytes 786440 | tf_op jit(solution)/shard_map/ppermute | solution.py:573
  173.4 18.5 %collective-permute-start.33 = (bf16[4,16,2048]{2,1,0:T(8,128)(2,1)S(1)}, bf16[4,16,2048]{2,1,0:T(8,128)(2,1)S(1)}, u32[]{:S(2)}, u32[]{:S(2)}) collective-permute-start(bf16[4,16,2048]{2,1,0:T(8,128)(2,1)S(1)} %get-tuple-element.89), channel_id=1, source_target_pairs={{0,3},{1,0},{2,1},{3,2},{4,7},{5,4},{6,5},{7,6},{8,11},{9,8},{10,9... | collective-permute-start | bytes 786440 | tf_op jit(solution)/shard_map/ppermute | solution.py:573
  181.4 20.3 %collective-permute-start.32 = (bf16[4,16,2048]{2,1,0:T(8,128)(2,1)S(1)}, bf16[4,16,2048]{2,1,0:T(8,128)(2,1)}, u32[]{:S(2)}, u32[]{:S(2)}) collective-permute-start(bf16[4,16,2048]{2,1,0:T(8,128)(2,1)S(1)} %get-tuple-element.88), channel_id=1, source_target_pairs={{0,2},{1,3},{2,0},{3,1},{4,6},{5,7},{6,4},{7,5},{8,10},{9,11},{10,... | collective-permute-start | bytes 786440 | tf_op jit(solution)/shard_map/ppermute | solution.py:573
  181.4 20.3 %collective-permute-start.31 = (bf16[4,16,2048]{2,1,0:T(8,128)(2,1)S(1)}, bf16[4,16,2048]{2,1,0:T(8,128)(2,1)}, u32[]{:S(2)}, u32[]{:S(2)}) collective-permute-start(bf16[4,16,2048]{2,1,0:T(8,128)(2,1)S(1)} %get-tuple-element.87), channel_id=1, source_target_pairs={{0,1},{1,2},{2,3},{3,0},{4,5},{5,6},{6,7},{7,4},{8,9},{9,10},{10,1... | collective-permute-start | bytes 786440 | tf_op jit(solution)/shard_map/ppermute | solution.py:573
  (4 other events, 3.1 us)

commit v11 on v10

--- a/solution.py
+++ b/solution.py
@@ -291,6 +291,16 @@
     )(scal)
 
 
+def copy_body(x, out):
+    out[...] = x[...]
+
+
+def copied(x):
+    return pl.pallas_call(
+        copy_body, out_shape=jax.ShapeDtypeStruct(x.shape, x.dtype), cost_estimate=cost(SHORT, 1e3)
+    )(x)
+
+
 def down_body(arrays, steps, start, listed, *refs):
     fars, nears, (w, *refs) = refs[:PARTS], refs[PARTS : 2 * PARTS], refs[2 * PARTS :]
     sources, (slot, out, hid, *refs) = refs[:arrays], refs[arrays:]
@@ -558,7 +568,7 @@
     def join(hid, moved, *earlier):
         return jnp.concatenate([after(m, *earlier) for m in moved] + [hid])
 
-    def multiply_down(i, chips, *earlier):
+    def multiply_down(i, chips, listed, *earlier):
         fars = [core_swap(c) for c in chips]
         return down(after(listed, *earlier), fars, chips, down_weight, all_tiles, ss_q, starts[i])
 
@@ -579,13 +589,15 @@
     hid_b, moved_b = finish_hidden(second, SHORT, kept[fourth], *gots[third], *moved_a, *all_tiles)
     exchange(fourth, hid_b)
     hid_c, moved_c = finish_hidden(third, 1e9, hid_b, *sends[fourth])
-    hid_d, moved_d = finish_hidden(fourth, 1e9, hid_c)
     first = [join(hid_a, moved_a, hid_b), join(hid_b, moved_b, *sends[fourth])]
-    out = multiply_down(0, first, hid_d)
+    out = multiply_down(0, first, listed, hid_c)
     came, total = finish_down(0, out)
     result = [total]
-    last = [join(hid_c, moved_c, out), join(hid_d, moved_d, out)]
-    out = multiply_down(1, last, out)
+    hid_d, moved_d = finish_hidden(fourth, 1e9, out)
+    beside = copied(after(listed, hid_d))
+    last = [join(hid_c, moved_c, out), join(hid_d, moved_d, beside)]
+    beside = copied(after(beside, last[1]))
+    out = multiply_down(1, last, beside, out)
     came, total = finish_down(1, out, came)
     result.append(total)
 

time: 205 us -> 203 us (level)
  starting transfers between devices: 36.1 us -> 27.9 us
  local copies, waits for them, and re-layouts: 12.5 us -> 17.1 us
  waiting for transfers between devices: 39.8 us -> 36.8 us
    ppermute x11, waiting for transfers between devices: 23.9 us -> 14.5 us  [y_move(): lax.ppermute(x, 'delta', [(i, (i + 2 * k) % owners) for i in range(owners)])]
    ppermute x6, starting transfers between devices: 16.7 us -> 8.2 us  [finish_down(): lax.ppermute(gone, 'tensor', [(j, (j + k) % shift) for j in range(shift)])]
    ppermute x6, waiting for transfers between devices: 14.7 us -> 20.4 us  [finish_down(): lax.ppermute(gone, 'tensor', [(j, (j + k) % shift) for j in range(shift)])]
    pallas_call x0 -> x2, Pallas kernels: none -> 2.61 us  [copied(): pl.pallas_call(copy_body, out_shape=jax.ShapeDtypeStruct(x.shape, x.dtype...]
    convert_element_type x2, local copies, waits for them, and re-layouts: 1.57 us -> 3.75 us  [finish_down(): lax.dynamic_index_in_dim(blocks, (here_t + k) % shift, 0, keepdims=False)]
    unnamed x68 -> x72, local copies, waits for them, and re-layouts: 5.6 us -> 7.7 us
  transfers between devices with their start and end apart: 34 -> 34, of which waited for: 8 -> 8; matrix products, arithmetic and copies ran while one was open for 6% -> 9% of each run, Pallas kernels for 49% -> 51%
where the time goes in v11:
time: 203 us; the launch traced here: 202 us
  Pallas kernels  107 us (53%)
  waiting for transfers between devices  36.8 us (18%)
  starting transfers between devices  27.9 us (14%)
  local copies, waits for them, and re-layouts  17.1 us (8%)
  other arithmetic  12.8 us (6%)
    pallas_call x4, Pallas kernels, gate_up(): pl.pallas_call(functools.partial(gate_up_body, owners), grid_spec=pltpu.P...  42.6 us
    pallas_call x2, Pallas kernels, down(): pl.pallas_call(functools.partial(down_body, len(tiles), steps, start), gr...  28 us
    ppermute x6, waiting for transfers between devices, finish_down(): lax.ppermute(gone, 'tensor', [(j, (j + k) % shift) for j in range(shift)])  20.4 us
    ppermute x11, waiting for transfers between devices, y_move(): lax.ppermute(x, 'delta', [(i, (i + 2 * k) % owners) for i in range(owners)])  14.5 us
    pallas_call x4, Pallas kernels, activate(): pl.pallas_call(functools.partial(activate_body, per_slot, start, each, ro...  13 us
    ppermute x11, starting transfers between devices, y_move(): lax.ppermute(x, 'delta', [(i, (i + 2 * k) % owners) for i in range(owners)])  13 us
    ppermute x6, starting transfers between devices, finish_down(): lax.ppermute(gone, 'tensor', [(j, (j + k) % shift) for j in range(shift)])  8.2 us
    unnamed x72, local copies, waits for them, and re-layouts  7.7 us
  transfers between devices with their start and end apart: 34, of which 8 were waited for; matrix products, arithmetic and copies ran while one was open for 9% of the time, Pallas kernels for 51%

profile of v11, /device:TPU:0, one launch (start us, length us, event | category | flops | bytes accessed | tf_op | source)
XLA Modules:
  0.0 201.8 jit_solution(6041637103953519462)
XLA Ops:
  0.0 0.7 pad_add_fusion
  0.7 2.4 %collective-permute-start = (s32[4,6]{0,1:T(8,128)S(1)}, s32[4,6]{0,1:T(8,128)S(1)}, u32[]{:S(2)}, u32[]{:S(2)}) collective-permute-start(s32[4,6]{0,1:T(8,128)S(1)} %pad_add_fusion), channel_id=1, source_target_pairs={{0,12},{4,0},{8,4},{12,8},{1,13},{5,1},{9,5},{13,9},{2,14},{6,2},{... | collective-permute-start | bytes 296 | tf_op jit(solution)/shard_map/ppermute | solution.py:435
  4.0 1.1 constant_dynamic-slice_fusion
  5.0 1.3 collective-permute-start.4
  6.9 10.7 %shard_map.118 = (f32[2,128,2048]{2,1,0:T(8,128)}, f32[2,128,2048]{2,1,0:T(8,128)}) custom-call(s32[4]{0:T(128)} %get-tuple-element.75.scal.order, bf16[4,16,8,2048]{3,2,1,0:T(8,128)(2,1)} %bitcast.78, bf16[4,16,8,2048]{3,2,1,0:T(8,128)(2,1)} %bitcast.79, bf16[4,16,8,2048]{3,2,1,0:T(8,128)(2,1)} %bitcast.80, bf16[4,16,8,2048]{3,2,1,0:T(8,128)(2,1)} %bitcast.81, ...), custom_call_target="tpu_custom_call" | custom-call | flops 4294967296 | bytes 16777216 | tf_op jit(solution)/shard_map/pallas_call | solution.py:165
  18.3 0.8 copy.38.ss
  20.4 0.8 copy-done.7
  21.2 7.1 %shard_map.119 = (bf16[256,1024]{1,0:T(8,128)(2,1)}, bf16[256,1024]{1,0:T(8,128)(2,1)}, s32[1,512]{1,0:T(1,128)}, bf16[128,128]{1,0:T(8,128)(2,1)}) custom-call(s32[101]{0:T(128)} %concatenate.36.scal, bf16[512,2048]{1,0:T(8,128)(2,1)} %x.1, s32[1,512]{1,0:T(1,128)} %bitcast.108, s32[512,1]{1,0:T(8,128)} %copy.38.ss), custom_call_target="tpu_custom_call" | custom-call | flops 120000004096 | bytes 4000000 | tf_op jit(solution)/shard_map/pallas_call | solution.py:73
  29.4 1.1 collective-permute-done.5.core
  30.4 1.1 fusion.18
  31.6 1.5 collective-permute-start.7
  33.1 1.3 fusion.3
  34.4 0.7 collective-permute-start.6
  35.1 10.6 %shard_map.120 = (f32[2,128,2048]{2,1,0:T(8,128)}, f32[2,128,2048]{2,1,0:T(8,128)}) custom-call(s32[4]{0:T(128)} %get-tuple-element.75.scal.order, bf16[4,16,8,2048]{3,2,1,0:T(8,128)(2,1)} %bitcast.82, bf16[4,16,8,2048]{3,2,1,0:T(8,128)(2,1)} %bitcast.83, bf16[4,16,8,2048]{3,2,1,0:T(8,128)(2,1)} %bitcast.84, bf16[4,16,8,2048]{3,2,1,0:T(8,128)(2,1)} %bitcast.85, ...), custom_call_target="tpu_custom_call" | custom-call | flops 4294967296 | bytes 16777216 | tf_op jit(solution)/shard_map/pallas_call | solution.py:165
  45.7 3.5 %shard_map.121.listed.x = s32[24,33]{1,0:T(8,128)} custom-call(s32[103]{0:T(128)} %concatenate.35.scal), custom_call_target="tpu_custom_call" | custom-call | flops 1000000 | bytes 10000 | tf_op jit(solution)/shard_map/pallas_call | solution.py:283
  49.2 0.8 select_reduce_fusion
  50.0 1.2 collective-permute-done.6.refs_0_
  51.2 2.7 %shard_map.122.x = bf16[128,1024]{1,0:T(8,128)(2,1)} custom-call(s32[4]{0:T(128)} %get-tuple-element.75.scal.order, bf16[2,128,1024]{2,1,0:T(8,128)(2,1)} %bitcast.104, bf16[2,128,1024]{2,1,0:T(8,128)(2,1)} %copy-done.28, bf16[128,1024]{1,0:T(8,128)(2,1)} %collective-permute-done.7.refs_0_), custom_call_target="tpu_custom_call" | custom-call | flops 120000004096 | bytes 1000000 | tf_op jit(solution)/shard_map/pallas_call | solution.py:191
  53.9 1.0 fusion.2
  55.4 4.6 %shard_map.123 = (bf16[2,128,1024]{2,1,0:T(8,128)(2,1)}, bf16[2,128,1024]{2,1,0:T(8,128)(2,1)}) custom-call(s32[101]{0:T(128)} %concatenate.36.scal, bf16[128,1024]{1,0:T(8,128)(2,1)} %shard_map.122.x, bf16[4,2,256,256]{3,2,1,0:T(8,128)(2,1)} %gt.1, bf16[4,2,256,256]{3,2,1,0:T(8,128)(2,1)} %ut.1, s32[1,512]{1,0:T(1,128)} %bitcast.105), custom_call_target="tpu_custom_call" | custom-call | flops 120000004096 | bytes 4000000 | tf_op jit(solution)/shard_map/pallas_call | solution.py:120
  60.6 1.5 collective-permute-start.11
  62.2 1.5 collective-permute-start.16
  63.7 1.1 fusion.17
  64.7 0.7 collective-permute-start.14
  65.4 10.7 %shard_map.124 = (f32[2,128,2048]{2,1,0:T(8,128)}, f32[2,128,2048]{2,1,0:T(8,128)}) custom-call(s32[4]{0:T(128)} %get-tuple-element.75.scal.order, bf16[4,16,8,2048]{3,2,1,0:T(8,128)(2,1)} %bitcast.86, bf16[4,16,8,2048]{3,2,1,0:T(8,128)(2,1)} %bitcast.87, bf16[4,16,8,2048]{3,2,1,0:T(8,128)(2,1)} %bitcast.88, bf16[4,16,8,2048]{3,2,1,0:T(8,128)(2,1)} %bitcast.89, ...), custom_call_target="tpu_custom_call" | custom-call | flops 4294967296 | bytes 16777216 | tf_op jit(solution)/shard_map/pallas_call | solution.py:165
  76.3 1.1 copy-done.6
  77.4 5.1 %collective-permute-done.14.refs_0_ = bf16[128,1024]{1,0:T(8,128)(2,1)S(1)} collective-permute-done((bf16[128,1024]{1,0:T(8,128)(2,1)S(1)}, bf16[128,1024]{1,0:T(8,128)(2,1)S(1)}, u32[]{:S(2)}, u32[]{:S(2)}) %collective-permute-start.14) | collective-permute-done | bytes 262176 | tf_op jit(solution)/shard_map/ppermute | solution.py:407
  82.5 0.7 copy-done.35
  83.2 2.5 %shard_map.125.refs_1_ = bf16[128,1024]{1,0:T(8,128)(2,1)} custom-call(s32[4]{0:T(128)} %get-tuple-element.75.scal.order, bf16[2,128,1024]{2,1,0:T(8,128)(2,1)} %get-tuple-element.64.keep, bf16[2,128,1024]{2,1,0:T(8,128)(2,1)} %collective-permute-done.9.core, bf16[128,1024]{1,0:T(8,128)(2,1)} %copy-done.35), custom_call_target="tpu_custom_call" | custom-call | flops 120000004096 | bytes 1000000 | tf_op jit(solution)/shard_map/pallas_call | solution.py:191
  85.8 1.5 collective-permute-start.15
  87.3 0.8 add_select_fusion.refs_2_.refs_11_
  88.1 3.2 %shard_map.126 = bf16[64,2048]{1,0:T(8,128)(2,1)} custom-call(f32[2,128,2048]{2,1,0:T(8,128)} %get-tuple-element.50.keep, f32[2,128,2048]{2,1,0:T(8,128)} %collective-permute-done.3.core, bf16[2,64,2048]{2,1,0:T(8,128)(2,1)} %copy-done.26, bf16[128,1024]{1,0:T(8,128)(2,1)} %shard_map.125.refs_1_, s32[512,1]{1,0:T(8,128)} %add_select_fusion.refs_2_.refs_11_, ...), custom_call_target="tpu_custom_call" | custom-call | flops 1000000000 | bytes 3145728 | tf_op jit(solution)/shard_map/pallas_call | solution.py:236
  92.0 10.6 %shard_map.127 = (f32[2,128,2048]{2,1,0:T(8,128)}, f32[2,128,2048]{2,1,0:T(8,128)}) custom-call(s32[4]{0:T(128)} %get-tuple-element.75.scal.order, bf16[4,16,8,2048]{3,2,1,0:T(8,128)(2,1)} %bitcast.90, bf16[4,16,8,2048]{3,2,1,0:T(8,128)(2,1)} %bitcast.91, bf16[4,16,8,2048]{3,2,1,0:T(8,128)(2,1)} %bitcast.92, bf16[4,16,8,2048]{3,2,1,0:T(8,128)(2,1)} %bitcast.93, ...), custom_call_target="tpu_custom_call" | custom-call | flops 4294967296 | bytes 16777216 | tf_op jit(solution)/shard_map/pallas_call | solution.py:165
  102.7 3.1 %collective-permute-done.17 = bf16[64,2048]{1,0:T(8,128)(2,1)S(1)} collective-permute-done((bf16[64,2048]{1,0:T(8,128)(2,1)}, bf16[64,2048]{1,0:T(8,128)(2,1)S(1)}, u32[]{:S(2)}, u32[]{:S(2)}) %collective-permute-start.17) | collective-permute-done | bytes 262176 | tf_op jit(solution)/shard_map/ppermute | solution.py:407
  105.8 3.4 %shard_map.128 = bf16[64,2048]{1,0:T(8,128)(2,1)} custom-call(f32[2,128,2048]{2,1,0:T(8,128)} %get-tuple-element.59.keep, f32[2,128,2048]{2,1,0:T(8,128)} %copy-done.23, bf16[2,64,2048]{2,1,0:T(8,128)(2,1)} %collective-permute-done.16.refs_0_, bf16[128,1024]{1,0:T(8,128)(2,1)} %shard_map.125.refs_1_, s32[512,1]{1,0:T(8,128)} %add_select_fusion.refs_2_.refs_11_, ...), custom_call_target="tpu_custom_call" | custom-call | flops 120000004096 | bytes 3145728 | tf_op jit(solution)/shard_map/pallas_call | solution.py:236
  109.3 1.5 collective-permute-start.21
  111.0 1.3 copy-done.5
  112.4 5.1 %collective-permute-done.21 = bf16[64,2048]{1,0:T(8,128)(2,1)S(1)} collective-permute-done((bf16[64,2048]{1,0:T(8,128)(2,1)}, bf16[64,2048]{1,0:T(8,128)(2,1)S(1)}, u32[]{:S(2)}, u32[]{:S(2)}) %collective-permute-start.21) | collective-permute-done | bytes 262176 | tf_op jit(solution)/shard_map/ppermute | solution.py:407
  117.6 1.5 collective-permute-start.26
  120.2 3.2 %shard_map.129 = bf16[64,2048]{1,0:T(8,128)(2,1)} custom-call(f32[2,128,2048]{2,1,0:T(8,128)} %get-tuple-element.72.keep, f32[2,128,2048]{2,1,0:T(8,128)} %copy-done.3, bf16[2,64,2048]{2,1,0:T(8,128)(2,1)} %copy-done.24, bf16[128,1024]{1,0:T(8,128)(2,1)} %shard_map.125.refs_1_, s32[512,1]{1,0:T(8,128)} %add_select_fusion.refs_2_.refs_11_, ...), custom_call_target="tpu_custom_call" | custom-call | flops 1000000000 | bytes 3145728 | tf_op jit(solution)/shard_map/pallas_call | solution.py:236
  124.1 0.8 copy-done.18
  124.9 0.8 copy-done.19
  125.7 14.0 %shard_map.130 = f32[256,2048]{1,0:T(8,128)} custom-call(s32[24,33]{1,0:T(8,128)} %shard_map.121.listed.x, bf16[128,2048]{1,0:T(8,128)(2,1)} %copy-done.18, bf16[128,2048]{1,0:T(8,128)(2,1)} %copy-done.19, bf16[128,2048]{1,0:T(8,128)(2,1)} %copy-done.11, bf16[128,2048]{1,0:T(8,128)(2,1)} %copy-done.12, bf16[4096,2048]{1,0:T(8,128)(2,1)} %refs_4_.11, ...), custom_call_target="tpu_custom_call" | custom-call | flops 1000000000 | bytes 1000000 | tf_op jit(solution)/shard_map/pallas_call | solution.py:349
  139.7 0.8 copy-done.25
  140.5 3.2 %shard_map.131 = bf16[64,2048]{1,0:T(8,128)(2,1)} custom-call(f32[2,128,2048]{2,1,0:T(8,128)} %get-tuple-element.79.keep, f32[2,128,2048]{2,1,0:T(8,128)} %copy-done.5, bf16[2,64,2048]{2,1,0:T(8,128)(2,1)} %copy-done.25, bf16[128,1024]{1,0:T(8,128)(2,1)} %shard_map.125.refs_1_, s32[512,1]{1,0:T(8,128)} %add_select_fusion.refs_2_.refs_11_, ...), custom_call_target="tpu_custom_call" | custom-call | flops 1000000000 | bytes 3145728 | tf_op jit(solution)/shard_map/pallas_call | solution.py:236
  143.7 1.7 collective-permute-start.27
  145.4 2.3 %fusion.13 = (bf16[4,16,2048]{2,1,0:T(8,128)(2,1)}, bf16[4,16,2048]{2,1,0:T(8,128)(2,1)}, bf16[4,16,2048]{2,1,0:T(8,128)(2,1)}) fusion(f32[4,4,16,2048]{3,2,1,0:T(8,128)} %bitcast.98, s32[]{:T(128)S(6)} %select_n.114, s32[]{:T(128)S(6)} %select_n.118, s32[]{:T(128)S(6)} %select_n.116), kind=kLoop, calls=%fused_computation.38 | loop fusion | bytes 1572876 | tf_op jit(solution)/shard_map/convert_element_type | solution.py:580
  147.7 2.9 %collective-permute-start.25 = (bf16[4,16,2048]{2,1,0:T(8,128)(2,1)}, bf16[4,16,2048]{2,1,0:T(8,128)(2,1)}, u32[]{:S(2)}, u32[]{:S(2)}) collective-permute-start(bf16[4,16,2048]{2,1,0:T(8,128)(2,1)} %get-tuple-element.99), channel_id=1, source_target_pairs={{0,3},{1,0},{2,1},{3,2},{4,7},{5,4},{6,5},{7,6},{8,11},{9,8},{10,9... | collective-permute-start | bytes 786440 | tf_op jit(solution)/shard_map/ppermute | solution.py:583
  150.6 1.4 collective-permute-start.23
  152.0 1.3 shard_map.132.x
  154.1 1.3 shard_map.133.listed
  155.4 0.7 collective-permute-done.30.refs_1_
  156.2 0.8 copy-done.21
  157.0 14.0 %shard_map.134 = f32[256,2048]{1,0:T(8,128)} custom-call(s32[24,33]{1,0:T(8,128)} %shard_map.133.listed, bf16[128,2048]{1,0:T(8,128)(2,1)} %copy-done.20, bf16[128,2048]{1,0:T(8,128)(2,1)} %copy-done.21, bf16[128,2048]{1,0:T(8,128)(2,1)} %copy-done.13, bf16[128,2048]{1,0:T(8,128)(2,1)} %copy-done.14, bf16[4096,2048]{1,0:T(8,128)(2,1)} %refs_4_.11, ...), custom_call_target="tpu_custom_call" | custom-call | flops 1000000000 | bytes 1000000 | tf_op jit(solution)/shard_map/pallas_call | solution.py:349
  171.0 1.5 fusion.15
  172.5 2.4 %collective-permute-start.33 = (bf16[4,16,2048]{2,1,0:T(8,128)(2,1)S(1)}, bf16[4,16,2048]{2,1,0:T(8,128)(2,1)S(1)}, u32[]{:S(2)}, u32[]{:S(2)}) collective-permute-start(bf16[4,16,2048]{2,1,0:T(8,128)(2,1)S(1)} %get-tuple-element.93), channel_id=1, source_target_pairs={{0,3},{1,0},{2,1},{3,2},{4,7},{5,4},{6,5},{7,6},{8,11},{9,8},{10,9... | collective-permute-start | bytes 786440 | tf_op jit(solution)/shard_map/ppermute | solution.py:583
  174.9 0.9 collective-permute-start.32
  176.4 1.4 fusion.9
  177.8 0.7 gather_fusion
  178.5 3.2 %collective-permute-done.33 = bf16[4,16,2048]{2,1,0:T(8,128)(2,1)S(1)} collective-permute-done((bf16[4,16,2048]{2,1,0:T(8,128)(2,1)S(1)}, bf16[4,16,2048]{2,1,0:T(8,128)(2,1)S(1)}, u32[]{:S(2)}, u32[]{:S(2)}) %collective-permute-start.33) | collective-permute-done | bytes 262176 | tf_op jit(solution)/shard_map/ppermute | solution.py:583
  181.7 17.2 %collective-permute-done.32 = bf16[4,16,2048]{2,1,0:T(8,128)(2,1)S(1)} collective-permute-done((bf16[4,16,2048]{2,1,0:T(8,128)(2,1)S(1)}, bf16[4,16,2048]{2,1,0:T(8,128)(2,1)S(1)}, u32[]{:S(2)}, u32[]{:S(2)}) %collective-permute-start.32) | collective-permute-done | bytes 262176 | tf_op jit(solution)/shard_map/ppermute | solution.py:583
  198.9 1.2 fusion.6
  200.1 0.7 gather_fusion.1
  200.9 0.8 pad_maximum_fusion.4
  (138 shorter events, 10.2 us)
Async XLA Ops:
  0.7 18.5 %collective-permute-start = (s32[4,6]{0,1:T(8,128)S(1)}, s32[4,6]{0,1:T(8,128)S(1)}, u32[]{:S(2)}, u32[]{:S(2)}) collective-permute-start(s32[4,6]{0,1:T(8,128)S(1)} %pad_add_fusion), channel_id=1, source_target_pairs={{0,12},{4,0},{8,4},{12,8},{1,13},{5,1},{9,5},{13,9},{2,14},{6,2},{... | collective-permute-start | bytes 296 | tf_op jit(solution)/shard_map/ppermute | solution.py:435
  3.2 16.2 %collective-permute-start.1 = (s32[4,6]{0,1:T(8,128)S(1)}, s32[4,6]{0,1:T(8,128)S(1)}, u32[]{:S(2)}, u32[]{:S(2)}) collective-permute-start(s32[4,6]{0,1:T(8,128)S(1)} %pad_add_fusion), channel_id=1, source_target_pairs={{0,8},{4,12},{8,0},{12,4},{1,9},{5,13},{9,1},{13,5},{2,10},{6,14},... | collective-permute-start | bytes 296 | tf_op jit(solution)/shard_map/ppermute | solution.py:435
  3.8 15.7 %collective-permute-start.2 = (s32[4,6]{0,1:T(8,128)S(1)}, s32[4,6]{0,1:T(8,128)S(1)}, u32[]{:S(2)}, u32[]{:S(2)}) collective-permute-start(s32[4,6]{0,1:T(8,128)S(1)} %pad_add_fusion), channel_id=1, source_target_pairs={{0,4},{4,8},{8,12},{12,0},{1,5},{5,9},{9,13},{13,1},{2,6},{6,10},{... | collective-permute-start | bytes 296 | tf_op jit(solution)/shard_map/ppermute | solution.py:435
  5.0 15.3 %collective-permute-start.4 = (bf16[4,256,256]{2,1,0:T(8,128)(2,1)S(1)}, bf16[4,256,256]{2,1,0:T(8,128)(2,1)S(1)}, u32[]{:S(2)}, u32[]{:S(2)}) collective-permute-start(bf16[4,256,256]{2,1,0:T(8,128)(2,1)S(1)} %constant_dynamic-slice_fusion), channel_id=1, source_target_pairs={{0,8},{4,12},{8,0},{12,4},{1,9},{5,13},{9,1},{13,5},{2,10},{6,14},... | collective-permute-start | bytes 1572872 | tf_op jit(solution)/shard_map/ppermute | solution.py:407
  6.9 11.3 %copy-start.33 = (s32[512]{0:T(512)S(1)}, s32[512]{0:T(512)}, u32[]{:S(2)}) copy-start(s32[512]{0:T(512)} %param.24) | copy-start | bytes 6148
  6.9 11.3 %copy-start.34 = (s32[16]{0:T(128)S(1)}, s32[16]{0:T(128)}, u32[]{:S(2)}) copy-start(s32[16]{0:T(128)} %param.25) | copy-start | bytes 196
  17.6 15.5 %collective-permute-start.3 = (f32[2,128,2048]{2,1,0:T(8,128)}, f32[2,128,2048]{2,1,0:T(8,128)}, u32[]{:S(2)}, u32[]{:S(2)}) collective-permute-start(f32[2,128,2048]{2,1,0:T(8,128)} %get-tuple-element.51), channel_id=1, source_target_pairs={{0,4},{4,0},{8,12},{12,8},{1,5},{5,1},{9,13},{13,9},{2,6},{6,2},{1... | collective-permute-start | bytes 6291464 | tf_op jit(solution)/shard_map/ppermute | solution.py:404
  18.3 2.9 %copy-start.30 = (s32[512]{0:T(512)}, s32[512]{0:T(512)S(1)}, u32[]{:S(2)}) copy-start(s32[512]{0:T(512)S(1)} %select_reduce_fusion.1) | copy-start | bytes 6148
  21.2 11.9 %copy-start.1 = (f32[2,128,2048]{2,1,0:T(8,128)S(1)}, f32[2,128,2048]{2,1,0:T(8,128)}, u32[]{:S(2)}) copy-start(f32[2,128,2048]{2,1,0:T(8,128)} %get-tuple-element.50.keep) | copy-start | bytes 6291460
  28.3 2.1 %collective-permute-start.5 = (bf16[2,128,1024]{2,1,0:T(8,128)(2,1)}, bf16[2,128,1024]{2,1,0:T(8,128)(2,1)S(1)}, u32[]{:S(2)}, u32[]{:S(2)}) collective-permute-start(bf16[2,128,1024]{2,1,0:T(8,128)(2,1)} %bitcast.110), channel_id=1, source_target_pairs={{0,4},{4,0},{8,12},{12,8},{1,5},{5,1},{9,13},{13,9},{2,6},{6,2},{1... | collective-permute-start | bytes 1572872 | tf_op jit(solution)/shard_map/ppermute | solution.py:404
  30.4 2.6 %copy-start.28 = (bf16[2,128,1024]{2,1,0:T(8,128)(2,1)}, bf16[2,128,1024]{2,1,0:T(8,128)(2,1)S(1)}, u32[]{:S(2)}) copy-start(bf16[2,128,1024]{2,1,0:T(8,128)(2,1)S(1)} %collective-permute-done.5.core) | copy-start | bytes 1572868
  31.6 19.7 %collective-permute-start.7 = (bf16[128,1024]{1,0:T(8,128)(2,1)S(1)}, bf16[128,1024]{1,0:T(8,128)(2,1)}, u32[]{:S(2)}, u32[]{:S(2)}) collective-permute-start(bf16[128,1024]{1,0:T(8,128)(2,1)S(1)} %fusion.18), channel_id=1, source_target_pairs={{0,8},{4,12},{8,0},{12,4},{1,9},{5,13},{9,1},{13,5},{2,10},{6,14},... | collective-permute-start | bytes 786440 | tf_op jit(solution)/shard_map/ppermute | solution.py:407
  34.4 14.8 %copy-start.32 = (s32[1,512]{1,0:T(1,128)S(1)}, s32[1,512]{1,0:T(1,128)}, u32[]{:S(2)}) copy-start(s32[1,512]{1,0:T(1,128)} %get-tuple-element.63) | copy-start | bytes 6148
  34.4 16.8 %collective-permute-start.6 = (bf16[2,64,2048]{2,1,0:T(8,128)(2,1)S(1)}, bf16[2,64,2048]{2,1,0:T(8,128)(2,1)S(1)}, u32[]{:S(2)}, u32[]{:S(2)}) collective-permute-start(bf16[2,64,2048]{2,1,0:T(8,128)(2,1)S(1)} %fusion.3), channel_id=1, source_target_pairs={{0,8},{4,12},{8,0},{12,4},{1,9},{5,13},{9,1},{13,5},{2,10},{6,14},... | collective-permute-start | bytes 1572872 | tf_op jit(solution)/shard_map/ppermute | solution.py:407
  45.7 8.2 %collective-permute-start.8 = (f32[2,128,2048]{2,1,0:T(8,128)}, f32[2,128,2048]{2,1,0:T(8,128)S(1)}, u32[]{:S(2)}, u32[]{:S(2)}) collective-permute-start(f32[2,128,2048]{2,1,0:T(8,128)} %get-tuple-element.60), channel_id=1, source_target_pairs={{0,4},{4,0},{8,12},{12,8},{1,5},{5,1},{9,13},{13,9},{2,6},{6,2},{1... | collective-permute-start | bytes 6291464 | tf_op jit(solution)/shard_map/ppermute | solution.py:404
  51.2 2.7 %copy-start.26 = (bf16[2,64,2048]{2,1,0:T(8,128)(2,1)}, bf16[2,64,2048]{2,1,0:T(8,128)(2,1)S(1)}, u32[]{:S(2)}) copy-start(bf16[2,64,2048]{2,1,0:T(8,128)(2,1)S(1)} %collective-permute-done.6.refs_0_) | copy-start | bytes 1572868
  51.2 2.7 %copy-start.22 = (f32[2,128,2048]{2,1,0:T(8,128)S(1)}, f32[2,128,2048]{2,1,0:T(8,128)}, u32[]{:S(2)}) copy-start(f32[2,128,2048]{2,1,0:T(8,128)} %get-tuple-element.59.keep) | copy-start | bytes 6291460
  53.9 1.5 copy-start.23
  55.4 4.6 %copy-start = (bf16[4,2,256,256]{3,2,1,0:T(8,128)(2,1)S(1)}, bf16[4,2,256,256]{3,2,1,0:T(8,128)(2,1)}, u32[]{:S(2)}) copy-start(bf16[4,2,256,256]{3,2,1,0:T(8,128)(2,1)} %param.20) | copy-start | bytes 3145732
  55.4 5.2 %copy-start.8 = (bf16[4,256,256]{2,1,0:T(8,128)(2,1)S(1)}, bf16[4,256,256]{2,1,0:T(8,128)(2,1)}, u32[]{:S(2)}) copy-start(bf16[4,256,256]{2,1,0:T(8,128)(2,1)} %copy-done.7) | copy-start | bytes 1572868
  55.4 6.7 %copy-start.29 = (s32[512]{0:T(512)S(1)}, s32[512]{0:T(512)}, u32[]{:S(2)}) copy-start(s32[512]{0:T(512)} %select_reduce_fusion) | copy-start | bytes 6148
  60.0 3.6 %collective-permute-start.9 = (bf16[2,128,1024]{2,1,0:T(8,128)(2,1)}, bf16[2,128,1024]{2,1,0:T(8,128)(2,1)}, u32[]{:S(2)}, u32[]{:S(2)}) collective-permute-start(bf16[2,128,1024]{2,1,0:T(8,128)(2,1)} %get-tuple-element.65), channel_id=1, source_target_pairs={{0,4},{4,0},{8,12},{12,8},{1,5},{5,1},{9,13},{13,9},{2,6},{6,2},{1... | collective-permute-start | bytes 1572872 | tf_op jit(solution)/shard_map/ppermute | solution.py:404
  60.1 16.2 %collective-permute-start.13 = (bf16[8,256,256]{2,1,0:T(8,128)(2,1)S(1)}, bf16[8,256,256]{2,1,0:T(8,128)(2,1)S(1)}, u32[]{:S(2)}, u32[]{:S(2)}) collective-permute-start(bf16[8,256,256]{2,1,0:T(8,128)(2,1)S(1)} %bitcast.97), channel_id=1, source_target_pairs={{0,4},{4,0},{8,12},{12,8},{1,5},{5,1},{9,13},{13,9},{2,6},{6,2},{1... | collective-permute-start | bytes 3145736 | tf_op jit(solution)/shard_map/ppermute | solution.py:404
  60.6 15.6 %collective-permute-start.11 = (bf16[4,256,256]{2,1,0:T(8,128)(2,1)S(1)}, bf16[4,256,256]{2,1,0:T(8,128)(2,1)S(1)}, u32[]{:S(2)}, u32[]{:S(2)}) collective-permute-start(bf16[4,256,256]{2,1,0:T(8,128)(2,1)S(1)} %copy-done.8), channel_id=1, source_target_pairs={{0,16},{16,0},{1,17},{17,1},{2,18},{18,2},{3,19},{19,3},{4,20},{20... | collective-permute-start | bytes 1572872 | tf_op jit(solution)/shard_map/ppermute | solution.py:512
  62.1 14.2 %collective-permute-start.12 = (bf16[4,256,256]{2,1,0:T(8,128)(2,1)S(1)}, bf16[4,256,256]{2,1,0:T(8,128)(2,1)}, u32[]{:S(2)}, u32[]{:S(2)}) collective-permute-start(bf16[4,256,256]{2,1,0:T(8,128)(2,1)S(1)} %copy-done.8), channel_id=1, source_target_pairs={{0,4},{4,0},{8,12},{12,8},{1,5},{5,1},{9,13},{13,9},{2,6},{6,2},{1... | collective-permute-start | bytes 1572872 | tf_op jit(solution)/shard_map/ppermute | solution.py:404
  62.2 29.7 %collective-permute-start.16 = (bf16[2,64,2048]{2,1,0:T(8,128)(2,1)}, bf16[2,64,2048]{2,1,0:T(8,128)(2,1)}, u32[]{:S(2)}, u32[]{:S(2)}) collective-permute-start(bf16[2,64,2048]{2,1,0:T(8,128)(2,1)} %fusion.2), channel_id=1, source_target_pairs={{0,8},{4,12},{8,0},{12,4},{1,9},{5,13},{9,1},{13,5},{2,10},{6,14},... | collective-permute-start | bytes 1572872 | tf_op jit(solution)/shard_map/ppermute | solution.py:407
  64.7 17.7 %collective-permute-start.14 = (bf16[128,1024]{1,0:T(8,128)(2,1)S(1)}, bf16[128,1024]{1,0:T(8,128)(2,1)S(1)}, u32[]{:S(2)}, u32[]{:S(2)}) collective-permute-start(bf16[128,1024]{1,0:T(8,128)(2,1)S(1)} %fusion.17), channel_id=1, source_target_pairs={{0,8},{4,12},{8,0},{12,4},{1,9},{5,13},{9,1},{13,5},{2,10},{6,14},... | collective-permute-start | bytes 786440 | tf_op jit(solution)/shard_map/ppermute | solution.py:407
  76.2 9.5 %copy-start.9 = (bf16[4,256,256]{2,1,0:T(8,128)(2,1)}, bf16[4,256,256]{2,1,0:T(8,128)(2,1)S(1)}, u32[]{:S(2)}) copy-start(bf16[4,256,256]{2,1,0:T(8,128)(2,1)S(1)} %collective-permute-done.11.refs_6_) | copy-start | bytes 1572868
  76.2 9.5 %collective-permute-start.10 = (f32[2,128,2048]{2,1,0:T(8,128)}, f32[2,128,2048]{2,1,0:T(8,128)S(1)}, u32[]{:S(2)}, u32[]{:S(2)}) collective-permute-start(f32[2,128,2048]{2,1,0:T(8,128)} %get-tuple-element.68), channel_id=1, source_target_pairs={{0,4},{4,0},{8,12},{12,8},{1,5},{5,1},{9,13},{13,9},{2,6},{6,2},{1... | collective-permute-start | bytes 6291464 | tf_op jit(solution)/shard_map/ppermute | solution.py:404
  76.3 1.1 copy-start.6
  77.4 8.3 %copy-start.2 = (f32[2,128,2048]{2,1,0:T(8,128)S(1)}, f32[2,128,2048]{2,1,0:T(8,128)}, u32[]{:S(2)}) copy-start(f32[2,128,2048]{2,1,0:T(8,128)} %get-tuple-element.72.keep) | copy-start | bytes 6291460
  85.7 17.0 %collective-permute-start.18 = (bf16[4,256,256]{2,1,0:T(8,128)(2,1)S(1)}, bf16[4,256,256]{2,1,0:T(8,128)(2,1)S(1)}, u32[]{:S(2)}, u32[]{:S(2)}) collective-permute-start(bf16[4,256,256]{2,1,0:T(8,128)(2,1)S(1)} %collective-permute-done.11.refs_6_), channel_id=1, source_target_pairs={{0,4},{4,0},{8,12},{12,8},{1,5},{5,1},{9,13},{13,9},{2,6},{6,2},{1... | collective-permute-start | bytes 1572872 | tf_op jit(solution)/shard_map/ppermute | solution.py:404
  85.7 5.6 %copy-start.3 = (f32[2,128,2048]{2,1,0:T(8,128)}, f32[2,128,2048]{2,1,0:T(8,128)S(1)}, u32[]{:S(2)}) copy-start(f32[2,128,2048]{2,1,0:T(8,128)S(1)} %collective-permute-done.10.core) | copy-start | bytes 6291460
  85.8 20.0 %collective-permute-start.15 = (bf16[2,64,2048]{2,1,0:T(8,128)(2,1)S(1)}, bf16[2,64,2048]{2,1,0:T(8,128)(2,1)S(1)}, u32[]{:S(2)}, u32[]{:S(2)}) collective-permute-start(bf16[2,64,2048]{2,1,0:T(8,128)(2,1)S(1)} %fusion.1), channel_id=1, source_target_pairs={{0,8},{4,12},{8,0},{12,4},{1,9},{5,13},{9,1},{13,5},{2,10},{6,14},... | collective-permute-start | bytes 1572872 | tf_op jit(solution)/shard_map/ppermute | solution.py:407
  91.3 14.5 %collective-permute-start.17 = (bf16[64,2048]{1,0:T(8,128)(2,1)}, bf16[64,2048]{1,0:T(8,128)(2,1)S(1)}, u32[]{:S(2)}, u32[]{:S(2)}) collective-permute-start(bf16[64,2048]{1,0:T(8,128)(2,1)} %shard_map.126), channel_id=1, source_target_pairs={{0,8},{4,12},{8,0},{12,4},{1,9},{5,13},{9,1},{13,5},{2,10},{6,14},... | collective-permute-start | bytes 786440 | tf_op jit(solution)/shard_map/ppermute | solution.py:407
  102.6 8.3 %collective-permute-start.19 = (f32[2,128,2048]{2,1,0:T(8,128)}, f32[2,128,2048]{2,1,0:T(8,128)S(1)}, u32[]{:S(2)}, u32[]{:S(2)}) collective-permute-start(f32[2,128,2048]{2,1,0:T(8,128)} %get-tuple-element.80), channel_id=1, source_target_pairs={{0,4},{4,0},{8,12},{12,8},{1,5},{5,1},{9,13},{13,9},{2,6},{6,2},{1... | collective-permute-start | bytes 6291464 | tf_op jit(solution)/shard_map/ppermute | solution.py:404
  102.7 6.6 %copy-start.10 = (bf16[4,256,256]{2,1,0:T(8,128)(2,1)}, bf16[4,256,256]{2,1,0:T(8,128)(2,1)S(1)}, u32[]{:S(2)}) copy-start(bf16[4,256,256]{2,1,0:T(8,128)(2,1)S(1)} %collective-permute-done.18.refs_9_) | copy-start | bytes 1572868
  105.8 3.4 %copy-start.24 = (bf16[2,64,2048]{2,1,0:T(8,128)(2,1)}, bf16[2,64,2048]{2,1,0:T(8,128)(2,1)S(1)}, u32[]{:S(2)}) copy-start(bf16[2,64,2048]{2,1,0:T(8,128)(2,1)S(1)} %collective-permute-done.15.refs_0_) | copy-start | bytes 1572868
  105.8 4.9 %copy-start.17 = (bf16[64,2048]{1,0:T(8,128)(2,1)S(1)}, bf16[64,2048]{1,0:T(8,128)(2,1)}, u32[]{:S(2)}) copy-start(bf16[64,2048]{1,0:T(8,128)(2,1)} %shard_map.126) | copy-start | bytes 786436
  105.8 5.1 %copy-start.4 = (f32[2,128,2048]{2,1,0:T(8,128)S(1)}, f32[2,128,2048]{2,1,0:T(8,128)}, u32[]{:S(2)}) copy-start(f32[2,128,2048]{2,1,0:T(8,128)} %get-tuple-element.79.keep) | copy-start | bytes 6291460
  109.3 8.2 %copy-start.27 = (bf16[64,2048]{1,0:T(8,128)(2,1)S(1)}, bf16[64,2048]{1,0:T(8,128)(2,1)}, u32[]{:S(2)}) copy-start(bf16[64,2048]{1,0:T(8,128)(2,1)} %shard_map.128) | copy-start | bytes 786436
  109.3 8.2 %collective-permute-start.21 = (bf16[64,2048]{1,0:T(8,128)(2,1)}, bf16[64,2048]{1,0:T(8,128)(2,1)S(1)}, u32[]{:S(2)}, u32[]{:S(2)}) collective-permute-start(bf16[64,2048]{1,0:T(8,128)(2,1)} %shard_map.128), channel_id=1, source_target_pairs={{0,8},{4,12},{8,0},{12,4},{1,9},{5,13},{9,1},{13,5},{2,10},{6,14},... | collective-permute-start | bytes 786440 | tf_op jit(solution)/shard_map/ppermute | solution.py:407
  110.8 12.6 %copy-start.11 = (bf16[128,2048]{1,0:T(8,128)(2,1)}, bf16[128,2048]{1,0:T(8,128)(2,1)S(1)}, u32[]{:S(2)}) copy-start(bf16[128,2048]{1,0:T(8,128)(2,1)S(1)} %pad_maximum_fusion.refs_2_) | copy-start | bytes 1572868
  110.8 13.3 %collective-permute-start.20 = (bf16[128,2048]{1,0:T(8,128)(2,1)S(1)}, bf16[128,2048]{1,0:T(8,128)(2,1)S(1)}, u32[]{:S(2)}, u32[]{:S(2)}) collective-permute-start(bf16[128,2048]{1,0:T(8,128)(2,1)S(1)} %pad_maximum_fusion.refs_2_), channel_id=1, source_target_pairs={{0,4},{4,0},{8,12},{12,8},{1,5},{5,1},{9,13},{13,9},{2,6},{6,2},{1... | collective-permute-start | bytes 1572872 | tf_op jit(solution)/shard_map/ppermute | solution.py:404
  110.9 1.5 copy-start.5
  117.5 5.9 %copy-start.12 = (bf16[128,2048]{1,0:T(8,128)(2,1)}, bf16[128,2048]{1,0:T(8,128)(2,1)S(1)}, u32[]{:S(2)}) copy-start(bf16[128,2048]{1,0:T(8,128)(2,1)S(1)} %pad_maximum_fusion.1.refs_3_) | copy-start | bytes 1572868
  117.5 6.5 %collective-permute-start.22 = (bf16[128,2048]{1,0:T(8,128)(2,1)S(1)}, bf16[128,2048]{1,0:T(8,128)(2,1)S(1)}, u32[]{:S(2)}, u32[]{:S(2)}) collective-permute-start(bf16[128,2048]{1,0:T(8,128)(2,1)S(1)} %pad_maximum_fusion.1.refs_3_), channel_id=1, source_target_pairs={{0,4},{4,0},{8,12},{12,8},{1,5},{5,1},{9,13},{13,9},{2,6},{6,2},{1... | collective-permute-start | bytes 1572872 | tf_op jit(solution)/shard_map/ppermute | solution.py:404
  117.6 22.0 %collective-permute-start.26 = (bf16[2,64,2048]{2,1,0:T(8,128)(2,1)S(1)}, bf16[2,64,2048]{2,1,0:T(8,128)(2,1)S(1)}, u32[]{:S(2)}, u32[]{:S(2)}) collective-permute-start(bf16[2,64,2048]{2,1,0:T(8,128)(2,1)S(1)} %fusion), channel_id=1, source_target_pairs={{0,8},{4,12},{8,0},{12,4},{1,9},{5,13},{9,1},{13,5},{2,10},{6,14},... | collective-permute-start | bytes 1572872 | tf_op jit(solution)/shard_map/ppermute | solution.py:407
  123.4 29.9 %collective-permute-start.28 = (bf16[64,2048]{1,0:T(8,128)(2,1)}, bf16[64,2048]{1,0:T(8,128)(2,1)S(1)}, u32[]{:S(2)}, u32[]{:S(2)}) collective-permute-start(bf16[64,2048]{1,0:T(8,128)(2,1)} %shard_map.129), channel_id=1, source_target_pairs={{0,8},{4,12},{8,0},{12,4},{1,9},{5,13},{9,1},{13,5},{2,10},{6,14},... | collective-permute-start | bytes 786440 | tf_op jit(solution)/shard_map/ppermute | solution.py:407
  143.7 9.8 %collective-permute-start.27 = (bf16[64,2048]{1,0:T(8,128)(2,1)}, bf16[64,2048]{1,0:T(8,128)(2,1)S(1)}, u32[]{:S(2)}, u32[]{:S(2)}) collective-permute-start(bf16[64,2048]{1,0:T(8,128)(2,1)} %shard_map.131), channel_id=1, source_target_pairs={{0,8},{4,12},{8,0},{12,4},{1,9},{5,13},{9,1},{13,5},{2,10},{6,14},... | collective-permute-start | bytes 786440 | tf_op jit(solution)/shard_map/ppermute | solution.py:407
  147.7 24.9 %collective-permute-start.25 = (bf16[4,16,2048]{2,1,0:T(8,128)(2,1)}, bf16[4,16,2048]{2,1,0:T(8,128)(2,1)}, u32[]{:S(2)}, u32[]{:S(2)}) collective-permute-start(bf16[4,16,2048]{2,1,0:T(8,128)(2,1)} %get-tuple-element.99), channel_id=1, source_target_pairs={{0,3},{1,0},{2,1},{3,2},{4,7},{5,4},{6,5},{7,6},{8,11},{9,8},{10,9... | collective-permute-start | bytes 786440 | tf_op jit(solution)/shard_map/ppermute | solution.py:583
  150.6 24.3 %collective-permute-start.24 = (bf16[4,16,2048]{2,1,0:T(8,128)(2,1)}, bf16[4,16,2048]{2,1,0:T(8,128)(2,1)}, u32[]{:S(2)}, u32[]{:S(2)}) collective-permute-start(bf16[4,16,2048]{2,1,0:T(8,128)(2,1)} %get-tuple-element.100), channel_id=1, source_target_pairs={{0,2},{1,3},{2,0},{3,1},{4,6},{5,7},{6,4},{7,5},{8,10},{9,11},{10,... | collective-permute-start | bytes 786440 | tf_op jit(solution)/shard_map/ppermute | solution.py:583
  150.6 2.7 %copy-start.15 = (bf16[64,2048]{1,0:T(8,128)(2,1)S(1)}, bf16[64,2048]{1,0:T(8,128)(2,1)}, u32[]{:S(2)}) copy-start(bf16[64,2048]{1,0:T(8,128)(2,1)} %shard_map.129) | copy-start | bytes 786436
  150.6 2.9 %copy-start.16 = (bf16[64,2048]{1,0:T(8,128)(2,1)S(1)}, bf16[64,2048]{1,0:T(8,128)(2,1)}, u32[]{:S(2)}) copy-start(bf16[64,2048]{1,0:T(8,128)(2,1)} %shard_map.131) | copy-start | bytes 786436
  150.6 25.2 %collective-permute-start.23 = (bf16[4,16,2048]{2,1,0:T(8,128)(2,1)}, bf16[4,16,2048]{2,1,0:T(8,128)(2,1)}, u32[]{:S(2)}, u32[]{:S(2)}) collective-permute-start(bf16[4,16,2048]{2,1,0:T(8,128)(2,1)} %get-tuple-element.98), channel_id=1, source_target_pairs={{0,1},{1,2},{2,3},{3,0},{4,5},{5,6},{6,7},{7,4},{8,9},{9,10},{10,1... | collective-permute-start | bytes 786440 | tf_op jit(solution)/shard_map/ppermute | solution.py:583
  153.4 2.0 %copy-start.13 = (bf16[128,2048]{1,0:T(8,128)(2,1)}, bf16[128,2048]{1,0:T(8,128)(2,1)S(1)}, u32[]{:S(2)}) copy-start(bf16[128,2048]{1,0:T(8,128)(2,1)S(1)} %pad_maximum_fusion.3.refs_2_) | copy-start | bytes 1572868
  153.4 2.0 %collective-permute-start.29 = (bf16[128,2048]{1,0:T(8,128)(2,1)S(1)}, bf16[128,2048]{1,0:T(8,128)(2,1)S(1)}, u32[]{:S(2)}, u32[]{:S(2)}) collective-permute-start(bf16[128,2048]{1,0:T(8,128)(2,1)S(1)} %pad_maximum_fusion.3.refs_2_), channel_id=1, source_target_pairs={{0,4},{4,0},{8,12},{12,8},{1,5},{5,1},{9,13},{13,9},{2,6},{6,2},{1... | collective-permute-start | bytes 1572872 | tf_op jit(solution)/shard_map/ppermute | solution.py:404
  153.5 1.9 copy-start.14
  153.6 2.6 %collective-permute-start.30 = (bf16[128,2048]{1,0:T(8,128)(2,1)S(1)}, bf16[128,2048]{1,0:T(8,128)(2,1)S(1)}, u32[]{:S(2)}, u32[]{:S(2)}) collective-permute-start(bf16[128,2048]{1,0:T(8,128)(2,1)S(1)} %pad_maximum_fusion.2.refs_3_), channel_id=1, source_target_pairs={{0,4},{4,0},{8,12},{12,8},{1,5},{5,1},{9,13},{13,9},{2,6},{6,2},{1... | collective-permute-start | bytes 1572872 | tf_op jit(solution)/shard_map/ppermute | solution.py:404
  156.2 0.8 copy-start.21
  172.5 9.2 %collective-permute-start.33 = (bf16[4,16,2048]{2,1,0:T(8,128)(2,1)S(1)}, bf16[4,16,2048]{2,1,0:T(8,128)(2,1)S(1)}, u32[]{:S(2)}, u32[]{:S(2)}) collective-permute-start(bf16[4,16,2048]{2,1,0:T(8,128)(2,1)S(1)} %get-tuple-element.93), channel_id=1, source_target_pairs={{0,3},{1,0},{2,1},{3,2},{4,7},{5,4},{6,5},{7,6},{8,11},{9,8},{10,9... | collective-permute-start | bytes 786440 | tf_op jit(solution)/shard_map/ppermute | solution.py:583
  174.9 24.0 %collective-permute-start.32 = (bf16[4,16,2048]{2,1,0:T(8,128)(2,1)S(1)}, bf16[4,16,2048]{2,1,0:T(8,128)(2,1)S(1)}, u32[]{:S(2)}, u32[]{:S(2)}) collective-permute-start(bf16[4,16,2048]{2,1,0:T(8,128)(2,1)S(1)} %get-tuple-element.92), channel_id=1, source_target_pairs={{0,2},{1,3},{2,0},{3,1},{4,6},{5,7},{6,4},{7,5},{8,10},{9,11},{10,... | collective-permute-start | bytes 786440 | tf_op jit(solution)/shard_map/ppermute | solution.py:583
  175.8 25.0 %copy-start.31 = (pred[4]{0:T(512)(128)(4,1)S(1)}, pred[4]{0:T(512)(128)(4,1)}, u32[]{:S(2)}) copy-start(pred[4]{0:T(512)(128)(4,1)} %get-tuple-element.94) | copy-start | bytes 16
  175.8 23.1 %collective-permute-start.31 = (bf16[4,16,2048]{2,1,0:T(8,128)(2,1)S(1)}, bf16[4,16,2048]{2,1,0:T(8,128)(2,1)S(1)}, u32[]{:S(2)}, u32[]{:S(2)}) collective-permute-start(bf16[4,16,2048]{2,1,0:T(8,128)(2,1)S(1)} %get-tuple-element.91), channel_id=1, source_target_pairs={{0,1},{1,2},{2,3},{3,0},{4,5},{5,6},{6,7},{7,4},{8,9},{9,10},{10,1... | collective-permute-start | bytes 786440 | tf_op jit(solution)/shard_map/ppermute | solution.py:583
  (6 other events, 4.7 us)
